TPU v7x, 32 devices: a whole 2x2x4 slice. The times are simulated.
32 devices in a mesh: seq: 16 (over z, x, core), fsdp: 2 (over y).
Axes of the slice: x: 2, y: 2, z: 4, core: 2. Of those that a mesh axis runs over, the one named last changes fastest.
Arguments:
- tokens: bfloat16 [8192, 640], P(('seq', 'fsdp')), may hold values from -6 to 6
- positions: int32 [8192], P(('seq', 'fsdp')), may hold values from 0 to 7935, as said below
- cotangent: bfloat16 [8192, 640], P(('seq', 'fsdp')), may hold values from -6 to 6
- in_gain: bfloat16 [640], P('fsdp'), may hold values from 0.25 to 1.75
- w_query: bfloat16 [640, 1024], P('fsdp'), may hold values from -0.25 to 0.25
- w_key: bfloat16 [640, 256], P('fsdp'), may hold values from -0.25 to 0.25
- w_value: bfloat16 [640, 256], P('fsdp'), may hold values from -0.25 to 0.25
- query_gain: bfloat16 [256], P('fsdp'), may hold values from 0.25 to 1.75
- key_gain: bfloat16 [256], P('fsdp'), may hold values from 0.25 to 1.75
- w_out: bfloat16 [1024, 640], P('fsdp'), may hold values from -0.1875 to 0.1875
- attn_gain: bfloat16 [640], P('fsdp'), may hold values from 0.25 to 1.75
- ffn_gain_in: bfloat16 [640], P('fsdp'), may hold values from 0.25 to 1.75
- w_gate: bfloat16 [640, 2048], P('fsdp'), may hold values from -0.25 to 0.25
- w_up: bfloat16 [640, 2048], P('fsdp'), may hold values from -0.25 to 0.25
- w_down: bfloat16 [2048, 640], P('fsdp'), may hold values from -0.125 to 0.125
- ffn_gain_out: bfloat16 [640], P('fsdp'), may hold values from 0.25 to 1.75
Outputs:
- layer_out: bfloat16 [8192, 640], P(('seq', 'fsdp'))
- grad_tokens: float32 [8192, 640], P(('seq', 'fsdp'))
- grad_in_gain: float32 [640], P('fsdp')
- grad_query: float32 [640, 1024], P('fsdp')
- grad_key: float32 [640, 256], P('fsdp')
- grad_value: float32 [640, 256], P('fsdp')
- grad_query_gain: float32 [256], P('fsdp')
- grad_key_gain: float32 [256], P('fsdp')
- grad_w_out: float32 [1024, 640], P('fsdp')
- grad_attn_gain: float32 [640], P('fsdp')
- grad_ffn_gain_in: float32 [640], P('fsdp')
- grad_gate: float32 [640, 2048], P('fsdp')
- grad_up: float32 [640, 2048], P('fsdp')
- grad_down: float32 [2048, 640], P('fsdp')
- grad_ffn_gain_out: float32 [640], P('fsdp')
Inputs may be any that keep to these rules, and one draw needn't show every extreme that they name: Sequences lie end to end: one holds 7936 tokens and begins within the first 256 tokens; the others, before and after it, hold 256 tokens together; positions count from 0 in each sequence.
All inputs are finite; a program needn't handle non-finite values.
Results may differ from a plain program's by a relative error of at most 0.017.
Values may be sent and summed in bfloat16 or wider, within the bound.
No kernel may reach another device: no remote copies, remote signals or barrier semaphores. Data moves between devices by JAX's collectives and lax.ppermute only.
A program may use at most 128 MiB of HBM per device.

v0:
```python
import jax
import jax.numpy as jnp
from jax import lax
from jax.sharding import PartitionSpec as P

WINDOW = 512


EPSILON = 1e-06
ROPE_BASE = 10000.0
MASKED = -1e30


def shifted(array, axis, by):
    length = lax.axis_size(axis)
    pairs = [(i, i + by) for i in range(length) if 0 <= i + by < length]
    return lax.ppermute(array, axis, pairs)


def norm_scale(values, scales):
    return values * lax.rsqrt(jnp.mean(values * values, axis=-1, keepdims=True) + EPSILON) * scales


def rotate(values, places):
    half_dim = values.shape[-1] // 2
    frequency = ROPE_BASE ** (-(jnp.arange(half_dim, dtype=jnp.float32) * 2.0 / values.shape[-1]))
    angles = places.astype(jnp.float32)[:, None] * frequency[None, :]
    cosine = jnp.cos(angles)[:, None, :]
    sine_part = jnp.sin(angles)[:, None, :]
    first_half = values[..., :half_dim]
    second_half = values[..., half_dim:]
    return jnp.concatenate(
        [
            first_half * cosine - second_half * sine_part,
            second_half * cosine + first_half * sine_part,
        ],
        axis=-1,
    )


def gelu_gate(gate_vals, up_vals):
    return jax.nn.gelu(gate_vals, approximate=True) * up_vals


def on_device(
    tokens,
    positions,
    cotangent,
    in_gain,
    w_query,
    w_key,
    w_value,
    query_gain,
    key_gain,
    w_out,
    attn_gain,
    ffn_gain_in,
    w_gate,
    w_up,
    w_down,
    ffn_gain_out,
):
    gathered = (
        lax.all_gather(in_gain, "fsdp", axis=0, tiled=True),
        lax.all_gather(w_query, "fsdp", axis=0, tiled=True),
        lax.all_gather(w_key, "fsdp", axis=0, tiled=True),
        lax.all_gather(w_value, "fsdp", axis=0, tiled=True),
        lax.all_gather(query_gain, "fsdp", axis=0, tiled=True),
        lax.all_gather(key_gain, "fsdp", axis=0, tiled=True),
        lax.all_gather(w_out, "fsdp", axis=0, tiled=True),
        lax.all_gather(attn_gain, "fsdp", axis=0, tiled=True),
        lax.all_gather(ffn_gain_in, "fsdp", axis=0, tiled=True),
        lax.all_gather(w_gate, "fsdp", axis=0, tiled=True),
        lax.all_gather(w_up, "fsdp", axis=0, tiled=True),
        lax.all_gather(w_down, "fsdp", axis=0, tiled=True),
        lax.all_gather(ffn_gain_out, "fsdp", axis=0, tiled=True),
    )
    (
        gain_in,
        full_query,
        full_key,
        full_value,
        gain_query,
        gain_key,
        full_out,
        gain_attn,
        gain_ffn_in,
        full_gate,
        full_up,
        full_down,
        gain_ffn_out,
    ) = gathered
    token_rows = tokens.shape[0]
    head_dim = full_key.shape[1]
    head_count = full_query.shape[1] // head_dim
    keep_rows = min(token_rows, WINDOW)
    hop_count = (WINDOW + token_rows - 1) // token_rows
    block_rows = min(token_rows, 512)
    score_scale = head_dim ** (-0.5)
    tokens_f = tokens.astype(jnp.float32)
    normed_f, pull_in = jax.vjp(norm_scale, tokens_f, gain_in.astype(jnp.float32))
    normed = normed_f.astype(jnp.bfloat16)
    query_raw = jnp.dot(normed, full_query, preferred_element_type=jnp.float32).reshape(
        token_rows, head_count, head_dim
    )
    key_raw = jnp.dot(normed, full_key, preferred_element_type=jnp.float32).reshape(
        token_rows, 1, head_dim
    )
    value_raw = jnp.dot(normed, full_value, preferred_element_type=jnp.float32)

    def prepare(values, scales):
        return rotate(norm_scale(values, scales), positions)

    queries_f, pull_query = jax.vjp(prepare, query_raw, gain_query.astype(jnp.float32))
    keys_f, pull_key = jax.vjp(prepare, key_raw, gain_key.astype(jnp.float32))
    queries = queries_f.astype(jnp.bfloat16)
    keys_own = keys_f.reshape(token_rows, head_dim).astype(jnp.bfloat16)
    values_own = value_raw.astype(jnp.bfloat16)
    halo_key = keys_own
    halo_value = values_own
    key_parts = [keys_own]
    value_parts = [values_own]
    for hop_index in range(hop_count):
        halo_key, halo_value = shifted((halo_key, halo_value), ("seq", "fsdp"), 1)
        key_parts.insert(0, halo_key)
        value_parts.insert(0, halo_value)
    keys_all = jnp.concatenate(key_parts, axis=0)
    values_all = jnp.concatenate(value_parts, axis=0)
    distance = jnp.arange(block_rows)[:, None] + WINDOW - jnp.arange(block_rows + WINDOW)[None, :]

    def block_scores(block_index):
        lower = block_index * block_rows
        allowed = (distance >= 0) & (distance < WINDOW) & (distance <= positions[:, None])
        raw_scores = jnp.einsum(
            "qhd,kd->hqk", queries, keys_all, preferred_element_type=jnp.float32
        )
        return jnp.where(allowed[None], raw_scores * score_scale, MASKED)

    block_index = 0
    scores = block_scores(block_index)
    top_score = jnp.max(scores, axis=-1, keepdims=True)
    logsum = top_score + jnp.log(jnp.sum(jnp.exp(scores - top_score), axis=-1, keepdims=True))
    attn_probs = jnp.exp(scores - logsum).astype(jnp.bfloat16)
    attended_parts = jnp.einsum(
        "hqk,kd->qhd", attn_probs, values_all, preferred_element_type=jnp.float32
    )
    logsums = [logsum]
    attended = attended_parts.reshape(token_rows, head_count * head_dim).astype(jnp.bfloat16)
    projected = jnp.dot(attended, full_out, preferred_element_type=jnp.float32)
    branch_attn, pull_attn = jax.vjp(norm_scale, projected, gain_attn.astype(jnp.float32))
    residual = tokens_f + branch_attn
    ffn_in_f, pull_ffn_in = jax.vjp(norm_scale, residual, gain_ffn_in.astype(jnp.float32))
    ffn_in = ffn_in_f.astype(jnp.bfloat16)
    gate_vals = jnp.dot(ffn_in, full_gate, preferred_element_type=jnp.float32)
    up_vals = jnp.dot(ffn_in, full_up, preferred_element_type=jnp.float32)
    mixed_f, pull_mixed = jax.vjp(gelu_gate, gate_vals, up_vals)
    mixed_vals = mixed_f.astype(jnp.bfloat16)
    down_vals = jnp.dot(mixed_vals, full_down, preferred_element_type=jnp.float32)
    branch_ffn, pull_ffn_out = jax.vjp(norm_scale, down_vals, gain_ffn_out.astype(jnp.float32))
    layer_out = (residual + branch_ffn).astype(jnp.bfloat16)
    full_query, full_key, full_value, full_out, full_gate, full_up, full_down = (
        lax.all_gather(w_query, "fsdp", axis=0, tiled=True),
        lax.all_gather(w_key, "fsdp", axis=0, tiled=True),
        lax.all_gather(w_value, "fsdp", axis=0, tiled=True),
        lax.all_gather(w_out, "fsdp", axis=0, tiled=True),
        lax.all_gather(w_gate, "fsdp", axis=0, tiled=True),
        lax.all_gather(w_up, "fsdp", axis=0, tiled=True),
        lax.all_gather(w_down, "fsdp", axis=0, tiled=True),
    )
    upstream = cotangent.astype(jnp.float32)
    d_down_f, grad_ffn_out = pull_ffn_out(upstream)
    d_down = d_down_f.astype(jnp.bfloat16)
    grad_down = jnp.einsum("tf,td->fd", mixed_vals, d_down, preferred_element_type=jnp.float32)
    d_mixed = jnp.einsum("td,fd->tf", d_down, full_down, preferred_element_type=jnp.float32)
    d_gate_f, d_up_f = pull_mixed(d_mixed)
    d_gate = d_gate_f.astype(jnp.bfloat16)
    d_up = d_up_f.astype(jnp.bfloat16)
    grad_gate = jnp.einsum("td,tf->df", ffn_in, d_gate, preferred_element_type=jnp.float32)
    grad_up = jnp.einsum("td,tf->df", ffn_in, d_up, preferred_element_type=jnp.float32)
    d_ffn_in = jnp.einsum(
        "tf,df->td", d_gate, full_gate, preferred_element_type=jnp.float32
    ) + jnp.einsum("tf,df->td", d_up, full_up, preferred_element_type=jnp.float32)
    d_resid_part, grad_ffn_in = pull_ffn_in(d_ffn_in)
    d_residual = upstream + d_resid_part
    d_proj_f, grad_attn = pull_attn(d_residual)
    d_proj = d_proj_f.astype(jnp.bfloat16)
    grad_out = jnp.einsum("tq,td->qd", attended, d_proj, preferred_element_type=jnp.float32)
    d_attended = (
        jnp.einsum("td,qd->tq", d_proj, full_out, preferred_element_type=jnp.float32)
        .astype(jnp.bfloat16)
        .reshape(token_rows, head_count, head_dim)
    )
    key_grads = jnp.zeros((WINDOW + token_rows, head_dim), jnp.float32)
    value_grads = jnp.zeros((WINDOW + token_rows, head_dim), jnp.float32)
    block_index = 0
    lower = block_index * block_rows
    scores = block_scores(block_index)
    probs_f = jnp.exp(scores - logsums[block_index])
    attn_probs = probs_f.astype(jnp.bfloat16)
    d_probs = jnp.einsum("qhd,kd->hqk", d_attended, values_all, preferred_element_type=jnp.float32)
    row_terms = jnp.sum(probs_f * d_probs, axis=-1, keepdims=True)
    d_scores = (probs_f * (d_probs - row_terms) * score_scale).astype(jnp.bfloat16)
    query_grad_parts = jnp.einsum(
        "hqk,kd->qhd", d_scores, keys_all, preferred_element_type=jnp.float32
    )
    key_grads = key_grads.at[lower : lower + block_rows + WINDOW].add(
        jnp.einsum("hqk,qhd->kd", d_scores, queries, preferred_element_type=jnp.float32)
    )
    value_grads = value_grads.at[lower : lower + block_rows + WINDOW].add(
        jnp.einsum("hqk,qhd->kd", attn_probs, d_attended, preferred_element_type=jnp.float32)
    )
    carry_key = key_grads[0:keep_rows]
    carry_value = value_grads[0:keep_rows]
    for hop_index in range(hop_count):
        carry_key, carry_value = shifted((carry_key, carry_value), ("seq", "fsdp"), -1)
        if hop_index + 1 < hop_count:
            start_row = (hop_index + 1) * keep_rows
            carry_key = carry_key + key_grads[start_row : start_row + keep_rows]
            carry_value = carry_value + value_grads[start_row : start_row + keep_rows]
    own_key = key_grads[WINDOW:].at[token_rows - keep_rows :].add(carry_key)
    own_value = value_grads[WINDOW:].at[token_rows - keep_rows :].add(carry_value)
    d_query_f, grad_query_gain = pull_query(query_grad_parts)
    d_key_f, grad_key_gain = pull_key(own_key.reshape(token_rows, 1, head_dim))
    d_query_raw = d_query_f.reshape(token_rows, head_count * head_dim).astype(jnp.bfloat16)
    d_key_raw = d_key_f.reshape(token_rows, head_dim).astype(jnp.bfloat16)
    d_value_raw = own_value.astype(jnp.bfloat16)
    grad_query = jnp.einsum("td,tq->dq", normed, d_query_raw, preferred_element_type=jnp.float32)
    grad_key = jnp.einsum("td,tq->dq", normed, d_key_raw, preferred_element_type=jnp.float32)
    grad_value = jnp.einsum("td,tq->dq", normed, d_value_raw, preferred_element_type=jnp.float32)
    d_normed = (
        jnp.einsum("tq,dq->td", d_query_raw, full_query, preferred_element_type=jnp.float32)
        + jnp.einsum("tq,dq->td", d_key_raw, full_key, preferred_element_type=jnp.float32)
        + jnp.einsum("tq,dq->td", d_value_raw, full_value, preferred_element_type=jnp.float32)
    )
    d_tokens, grad_in = pull_in(d_normed)
    grad_tokens = d_residual + d_tokens
    shards = (
        lax.psum_scatter(grad_in, "fsdp", scatter_dimension=0, tiled=True),
        lax.psum_scatter(grad_query, "fsdp", scatter_dimension=0, tiled=True),
        lax.psum_scatter(grad_key, "fsdp", scatter_dimension=0, tiled=True),
        lax.psum_scatter(grad_value, "fsdp", scatter_dimension=0, tiled=True),
        lax.psum_scatter(grad_query_gain, "fsdp", scatter_dimension=0, tiled=True),
        lax.psum_scatter(grad_key_gain, "fsdp", scatter_dimension=0, tiled=True),
        lax.psum_scatter(grad_out, "fsdp", scatter_dimension=0, tiled=True),
        lax.psum_scatter(grad_attn, "fsdp", scatter_dimension=0, tiled=True),
        lax.psum_scatter(grad_ffn_in, "fsdp", scatter_dimension=0, tiled=True),
        lax.psum_scatter(grad_gate, "fsdp", scatter_dimension=0, tiled=True),
        lax.psum_scatter(grad_up, "fsdp", scatter_dimension=0, tiled=True),
        lax.psum_scatter(grad_down, "fsdp", scatter_dimension=0, tiled=True),
        lax.psum_scatter(grad_ffn_out, "fsdp", scatter_dimension=0, tiled=True),
    )
    (
        part_one,
        part_two,
        part_three,
        part_four,
        part_five,
        part_six,
        part_seven,
        part_eight,
        part_nine,
        part_ten,
        part_eleven,
        part_twelve,
        part_thirteen,
    ) = shards
    totals = lax.psum(
        (
            part_one,
            part_two,
            part_three,
            part_four,
            part_five,
            part_six,
            part_seven,
            part_eight,
            part_nine,
            part_ten,
            part_eleven,
            part_twelve,
            part_thirteen,
        ),
        "seq",
    )
    return (
        layer_out,
        grad_tokens,
        totals[0],
        totals[1],
        totals[2],
        totals[3],
        totals[4],
        totals[5],
        totals[6],
        totals[7],
        totals[8],
        totals[9],
        totals[10],
        totals[11],
        totals[12],
    )


def solution(mesh):
    return jax.shard_map(
        on_device,
        mesh=mesh,
        in_specs=(
            P(("seq", "fsdp"), None),
            P(("seq", "fsdp")),
            P(("seq", "fsdp"), None),
            P("fsdp"),
            P("fsdp", None),
            P("fsdp", None),
            P("fsdp", None),
            P("fsdp"),
            P("fsdp"),
            P("fsdp", None),
            P("fsdp"),
            P("fsdp"),
            P("fsdp", None),
            P("fsdp", None),
            P("fsdp", None),
            P("fsdp"),
        ),
        out_specs=(
            P(("seq", "fsdp"), None),
            P(("seq", "fsdp"), None),
            P("fsdp"),
            P("fsdp", None),
            P("fsdp", None),
            P("fsdp", None),
            P("fsdp"),
            P("fsdp"),
            P("fsdp", None),
            P("fsdp"),
            P("fsdp"),
            P("fsdp", None),
            P("fsdp", None),
            P("fsdp", None),
            P("fsdp"),
        ),
        check_vma=False,
    )
```

profile of v0, /device:TPU:1, one launch (start us, length us, event | category | flops | bytes accessed | tf_op | source)
XLA Modules:
  0.0 813.9 jit_solution(15814652024248788954)
XLA Ops:
  12.4 4.4 all-reduce.17
  16.8 3.1 all-gather
  19.9 9.1 %all_gather.48 = bf16[640,256]{1,0:T(8,128)(2,1)S(1)} all-gather(bf16[320,256]{1,0:T(8,128)(2,1)S(1)} %copy-done.50), channel_id=1, replica_groups=mesh['seq'=16,'fsdp'=2] {'fsdp'}, dimensions={0}, use_global_device_ids=true | all-gather | bytes 491520 | tf_op jit(solution)/shard_map/all_gather | solution.py:66
  31.0 3.6 collective-permute-start.2
  34.7 9.4 %all_gather.47 = bf16[640,256]{1,0:T(8,128)(2,1)S(1)} all-gather(bf16[320,256]{1,0:T(8,128)(2,1)S(1)} %copy-done.51), channel_id=1, replica_groups=mesh['seq'=16,'fsdp'=2] {'fsdp'}, dimensions={0}, use_global_device_ids=true | all-gather | bytes 491520 | tf_op jit(solution)/shard_map/all_gather | solution.py:67
  45.1 4.1 collective-permute-start
  49.9 4.5 all-gather.1
  55.3 3.4 collective-permute-start.3
  58.7 5.0 collective-permute-start.1
  63.8 2.0 fusion.86
  67.9 1.7 fusion.92
  70.5 2.4 convolution_convert_fusion.1
  72.9 2.2 multiply_reduce_fusion.8
  77.9 36.7 %all-gather.12.cloned.1.call-done = bf16[640,2048]{1,0:T(8,128)(2,1)} async-done(((bf16[320,2048]{1,0:T(8,128)(2,1)}), bf16[640,2048]{1,0:T(8,128)(2,1)}) %all-gather.12.cloned.1.call-update) | async-done | bytes 2621456 | tf_op jit(solution)/shard_map/all_gather | solution.py:73
  114.6 4.2 fusion.93
  118.8 36.3 %all-gather.14.cloned.1.call-done = bf16[640,2048]{1,0:T(8,128)(2,1)} async-done(((bf16[320,2048]{1,0:T(8,128)(2,1)}), bf16[640,2048]{1,0:T(8,128)(2,1)}) %all-gather.14.cloned.1.call-update) | async-done | bytes 2621456 | tf_op jit(solution)/shard_map/all_gather | solution.py:74
  155.1 5.3 multiply_convert_fusion.1
  160.4 35.1 %all-gather.16.cloned.1.call-done = bf16[2048,640]{1,0:T(8,128)(2,1)} async-done(((bf16[1024,640]{1,0:T(8,128)(2,1)}), bf16[2048,640]{1,0:T(8,128)(2,1)}) %all-gather.16.cloned.1.call-update) | async-done | bytes 2621456 | tf_op jit(solution)/shard_map/all_gather | solution.py:75
  195.5 3.3 multiply_reduce_fusion.6
  200.6 2.3 multiply_convert_fusion
  209.6 3.2 fusion.39
  212.8 5.3 fusion.16
  219.1 2.5 collective-permute-start.4
  221.6 6.6 collective-permute-done.4
  229.2 3.9 collective-permute-start.5
  233.1 6.1 collective-permute-done.5
  243.1 1.6 convolution_bitcast_fusion
  244.7 4.4 collective-permute-start.6
  249.1 10.8 %collective-permute-done.6 = f32[256,256]{1,0:T(8,128)S(1)} collective-permute-done((f32[256,256]{1,0:T(8,128)S(1)}, f32[256,256]{1,0:T(8,128)S(1)}, u32[]{:S(2)}, u32[]{:S(2)}) %collective-permute-start.6) | collective-permute-done | bytes 262176 | tf_op jit(solution)/shard_map/ppermute | solution.py:17
  259.9 4.4 collective-permute-start.7
  264.3 4.5 collective-permute-done.7
  270.8 5.6 fusion.15
  279.0 2.2 fusion.84
  281.5 2.1 fusion.96
  283.7 3.2 fusion.97
  288.1 3.3 fusion.98
  292.6 3.3 fusion.99
  296.1 34.2 %reduce-scatter.8.cloned.1.call-done = f32[320,1024]{1,0:T(8,128)} async-done(((f32[640,1024]{1,0:T(8,128)}), f32[320,1024]{1,0:T(8,128)}) %reduce-scatter.8.cloned.1.call-update) | async-done | bytes 1310736 | tf_op jit(solution)/shard_map/reduce_scatter | solution.py:239
  330.3 40.6 %reduce-scatter.14.cloned.1.call-done = f32[512,640]{1,0:T(8,128)} async-done(((f32[1024,640]{1,0:T(8,128)}), f32[512,640]{1,0:T(8,128)}) %reduce-scatter.14.cloned.1.call-update) | async-done | bytes 1310736 | tf_op jit(solution)/shard_map/reduce_scatter | solution.py:244
  370.9 67.8 %reduce-scatter.16.cloned.1.call-done = f32[320,2048]{1,0:T(8,128)} async-done(((f32[640,2048]{1,0:T(8,128)}), f32[320,2048]{1,0:T(8,128)}) %reduce-scatter.16.cloned.1.call-update) | async-done | bytes 2621456 | tf_op jit(solution)/shard_map/reduce_scatter | solution.py:247
  438.7 68.1 %reduce-scatter.18.cloned.1.call-done = f32[320,2048]{1,0:T(8,128)} async-done(((f32[640,2048]{1,0:T(8,128)}), f32[320,2048]{1,0:T(8,128)}) %reduce-scatter.18.cloned.1.call-update) | async-done | bytes 2621456 | tf_op jit(solution)/shard_map/reduce_scatter | solution.py:248
  506.8 67.8 %reduce-scatter.20.cloned.1.call-done = f32[1024,640]{1,0:T(8,128)} async-done(((f32[2048,640]{1,0:T(8,128)}), f32[1024,640]{1,0:T(8,128)}) %reduce-scatter.20.cloned.1.call-update) | async-done | bytes 2621456 | tf_op jit(solution)/shard_map/reduce_scatter | solution.py:249
  577.6 5.5 all-reduce.16
  583.5 35.1 %all-reduce.14 = (f32[320]{0:T(512)}, f32[128]{0:T(128)}, f32[128]{0:T(128)}, f32[320]{0:T(512)}, f32[320]{0:T(512)}, /*index=5*/f32[320]{0:T(512)}) all-reduce(f32[320]{0:T(512)S(1)} %dynamic-slice.25, f32[128]{0:T(128)S(1)} %dynamic-slice.27, f32[128]{0:T(128)S(1)} %dynamic-slice.29, ...), channel_id=1, replica_groups=mesh['seq'=16,'fsdp'=2] {'seq'}, use_global_device_ids=true, to_apply=%region_17.18 | all-reduce | flops 1536 | bytes 12288 | tf_op jit(solution)/shard_map/psum | solution.py:267
  619.8 175.5 %all-reduce.20.cloned.1.call-done = (f32[320,1024]{1,0:T(8,128)}, f32[320,256]{1,0:T(8,128)}, f32[320,256]{1,0:T(8,128)}, f32[512,640]{1,0:T(8,128)}, f32[320,20...) async-done(((f32[320,1024]{1,0:T(8,128)}, f32[320,256]{1,0:T(8,128)}, f32[320,256]{1,0:T(8,128)}, f32[512,640]{1,0:T(8,128)}, f32[320,2048]{1,0:T(8,128)}, ...) | async-done | bytes 11141136 | tf_op jit(solution)/shard_map/psum | solution.py:267
  795.3 2.7 copy.143
  800.5 1.5 copy.147
  803.2 1.5 copy.148
  (251 shorter events, 45.7 us)
Async XLA Ops:
  7.2 3.0 copy-start.55
  7.2 4.2 copy-start.56
  7.2 4.4 copy-start.57
  7.2 4.7 copy-start.58
  7.2 4.9 copy-start.59
  7.2 9.5 %copy-start.54 = (s32[256]{0:T(256)S(1)}, s32[256]{0:T(256)}, u32[]{:S(2)}) copy-start(s32[256]{0:T(256)} %param.33) | copy-start | bytes 3076
  7.2 9.5 %copy-start.64 = (bf16[128]{0:T(256)(128)(2,1)S(1)}, bf16[128]{0:T(256)(128)(2,1)}, u32[]{:S(2)}) copy-start(bf16[128]{0:T(256)(128)(2,1)} %param.40) | copy-start | bytes 772
  7.3 12.6 %copy-start.50 = (bf16[320,256]{1,0:T(8,128)(2,1)S(1)}, bf16[320,256]{1,0:T(8,128)(2,1)}, u32[]{:S(2)}) copy-start(bf16[320,256]{1,0:T(8,128)(2,1)} %param.37) | copy-start | bytes 491524
  7.3 21.7 %copy-start.2 = (bf16[256,640]{1,0:T(8,128)(2,1)S(1)}, bf16[256,640]{1,0:T(8,128)(2,1)}, u32[]{:S(2)}) copy-start(bf16[256,640]{1,0:T(8,128)(2,1)} %param.32) | copy-start | bytes 983044
  7.3 56.5 %all-gather.8.cloned.1.call-start = ((), (), s32[]{:S(2)}) async-start(), calls=%async_computation.7 | async-start | bytes 1966080 | tf_op jit(solution)/shard_map/all_gather | solution.py:65
  8.0 64.9 %all-gather.10.cloned.1.call-start = ((), (), s32[]{:S(2)}) async-start(), calls=%async_computation.8 | async-start | bytes 1966080 | tf_op jit(solution)/shard_map/all_gather | solution.py:70
  8.8 25.9 %copy-start.51 = (bf16[320,256]{1,0:T(8,128)(2,1)S(1)}, bf16[320,256]{1,0:T(8,128)(2,1)}, u32[]{:S(2)}) copy-start(bf16[320,256]{1,0:T(8,128)(2,1)} %param.38) | copy-start | bytes 491524
  8.8 105.8 %all-gather.12.cloned.1.call-start = ((), (), s32[]{:S(2)}) async-start(), calls=%async_computation.9 | async-start | bytes 3932160 | tf_op jit(solution)/shard_map/all_gather | solution.py:73
  9.5 145.6 %all-gather.14.cloned.1.call-start = ((), (), s32[]{:S(2)}) async-start(), calls=%async_computation.10 | async-start | bytes 3932160 | tf_op jit(solution)/shard_map/all_gather | solution.py:74
  10.1 185.4 %all-gather.16.cloned.1.call-start = ((), (), s32[]{:S(2)}) async-start(), calls=%async_computation.11 | async-start | bytes 3932160 | tf_op jit(solution)/shard_map/all_gather | solution.py:75
  29.2 20.7 %copy-start.65 = (bf16[128]{0:T(256)(128)(2,1)S(1)}, bf16[128]{0:T(256)(128)(2,1)}, u32[]{:S(2)}) copy-start(bf16[128]{0:T(256)(128)(2,1)} %param.39) | copy-start | bytes 772
  31.0 34.7 %copy-start.52 = (bf16[256,256]{0,1:T(8,128)(2,1)}, bf16[256,256]{0,1:T(8,128)(2,1)S(1)}, u32[]{:S(2)}) copy-start(bf16[256,256]{0,1:T(8,128)(2,1)S(1)} %maximum_bitcast_fusion.6) | copy-start | bytes 393220
  31.0 24.3 %collective-permute-start.2 = (bf16[256,256]{0,1:T(8,128)(2,1)S(1)}, bf16[256,256]{0,1:T(8,128)(2,1)S(1)}, u32[]{:S(2)}, u32[]{:S(2)}) collective-permute-start(bf16[256,256]{0,1:T(8,128)(2,1)S(1)} %maximum_bitcast_fusion.6), channel_id=1, source_target_pairs={{0,1},{1,2},{2,3},{3,4},{4,5},{5,6},{6,7},{7,8},{8,9},{9,10},{10,1... | collective-permute-start | bytes 393224 | tf_op jit(solution)/shard_map/ppermute | solution.py:17
  45.1 18.6 %copy-start.43 = (bf16[256,256]{1,0:T(8,128)(2,1)}, bf16[256,256]{1,0:T(8,128)(2,1)S(1)}, u32[]{:S(2)}) copy-start(bf16[256,256]{1,0:T(8,128)(2,1)S(1)} %convolution_convert_fusion.2) | copy-start | bytes 393220
  45.1 13.6 %collective-permute-start = (bf16[256,256]{1,0:T(8,128)(2,1)S(1)}, bf16[256,256]{1,0:T(8,128)(2,1)}, u32[]{:S(2)}, u32[]{:S(2)}) collective-permute-start(bf16[256,256]{1,0:T(8,128)(2,1)S(1)} %convolution_convert_fusion.2), channel_id=1, source_target_pairs={{0,1},{1,2},{2,3},{3,4},{4,5},{5,6},{6,7},{7,8},{8,9},{9,10},{10,1... | collective-permute-start | bytes 393224 | tf_op jit(solution)/shard_map/ppermute | solution.py:17
  49.3 246.8 %reduce-scatter.10.cloned.1.call-start = ((), (), s32[]{:S(2)}) async-start(), calls=%async_computation.13 | async-start | bytes 983040 | tf_op jit(solution)/shard_map/reduce_scatter | solution.py:240
  49.9 17.1 %copy-start.35 = (f32[256,128]{1,0:T(8,128)}, f32[256,128]{1,0:T(8,128)S(1)}, u32[]{:S(2)}) copy-start(f32[256,128]{1,0:T(8,128)S(1)} %get-tuple-element.145) | copy-start | bytes 393220
  49.9 17.1 %copy-start.36 = (f32[256,128]{1,0:T(8,128)}, f32[256,128]{1,0:T(8,128)S(1)}, u32[]{:S(2)}) copy-start(f32[256,128]{1,0:T(8,128)S(1)} %get-tuple-element.146) | copy-start | bytes 393220
  55.3 11.3 %copy-start.61 = (bf16[256,256]{0,1:T(8,128)(2,1)}, bf16[256,256]{0,1:T(8,128)(2,1)S(1)}, u32[]{:S(2)}) copy-start(bf16[256,256]{0,1:T(8,128)(2,1)S(1)} %collective-permute-done.2) | copy-start | bytes 393220
  55.3 11.8 %collective-permute-start.3 = (bf16[256,256]{0,1:T(8,128)(2,1)S(1)}, bf16[256,256]{0,1:T(8,128)(2,1)S(1)}, u32[]{:S(2)}, u32[]{:S(2)}) collective-permute-start(bf16[256,256]{0,1:T(8,128)(2,1)S(1)} %collective-permute-done.2), channel_id=1, source_target_pairs={{0,1},{1,2},{2,3},{3,4},{4,5},{5,6},{6,7},{7,8},{8,9},{9,10},{10,1... | collective-permute-start | bytes 393224 | tf_op jit(solution)/shard_map/ppermute | solution.py:17
  58.7 11.3 %collective-permute-start.1 = (bf16[256,256]{1,0:T(8,128)(2,1)}, bf16[256,256]{1,0:T(8,128)(2,1)}, u32[]{:S(2)}, u32[]{:S(2)}) collective-permute-start(bf16[256,256]{1,0:T(8,128)(2,1)} %collective-permute-done), channel_id=1, source_target_pairs={{0,1},{1,2},{2,3},{3,4},{4,5},{5,6},{6,7},{7,8},{8,9},{9,10},{10,1... | collective-permute-start | bytes 393224 | tf_op jit(solution)/shard_map/ppermute | solution.py:17
  195.5 3.3 copy-start.16
  195.5 3.6 copy-start.4
  195.5 4.6 copy-start.60
  195.5 4.6 copy-start.66
  202.9 3.8 copy-start.14
  202.9 3.8 copy-start.41
  218.1 22.7 %copy-start.26 = (f32[256,256]{0,1:T(8,128)S(1)}, f32[256,256]{0,1:T(8,128)}, u32[]{:S(2)}) copy-start(f32[256,256]{0,1:T(8,128)} %copy-done.25) | copy-start | bytes 786436
  219.1 9.1 %collective-permute-start.4 = (f32[256,256]{0,1:T(8,128)S(1)}, f32[256,256]{0,1:T(8,128)S(1)}, u32[]{:S(2)}, u32[]{:S(2)}) collective-permute-start(f32[256,256]{0,1:T(8,128)S(1)} %slice.103), channel_id=1, source_target_pairs={{1,0},{2,1},{3,2},{4,3},{5,4},{6,5},{7,6},{8,7},{9,8},{10,9},{11,1... | collective-permute-start | bytes 786440 | tf_op jit(solution)/shard_map/ppermute | solution.py:17
  229.2 10.0 %collective-permute-start.5 = (f32[256,256]{0,1:T(8,128)S(1)}, f32[256,256]{0,1:T(8,128)S(1)}, u32[]{:S(2)}, u32[]{:S(2)}) collective-permute-start(f32[256,256]{0,1:T(8,128)S(1)} %slice_add_fusion.2), channel_id=1, source_target_pairs={{1,0},{2,1},{3,2},{4,3},{5,4},{6,5},{7,6},{8,7},{9,8},{10,9},{11,1... | collective-permute-start | bytes 786440 | tf_op jit(solution)/shard_map/ppermute | solution.py:17
  243.0 53.1 %reduce-scatter.12.cloned.1.call-start = ((), (), s32[]{:S(2)}) async-start(), calls=%async_computation.14 | async-start | bytes 983040 | tf_op jit(solution)/shard_map/reduce_scatter | solution.py:241
  244.7 15.2 %collective-permute-start.6 = (f32[256,256]{1,0:T(8,128)S(1)}, f32[256,256]{1,0:T(8,128)S(1)}, u32[]{:S(2)}, u32[]{:S(2)}) collective-permute-start(f32[256,256]{1,0:T(8,128)S(1)} %slice.106), channel_id=1, source_target_pairs={{1,0},{2,1},{3,2},{4,3},{5,4},{6,5},{7,6},{8,7},{9,8},{10,9},{11,1... | collective-permute-start | bytes 786440 | tf_op jit(solution)/shard_map/ppermute | solution.py:17
  259.9 8.9 %collective-permute-start.7 = (f32[256,256]{1,0:T(8,128)S(1)}, f32[256,256]{1,0:T(8,128)S(1)}, u32[]{:S(2)}, u32[]{:S(2)}) collective-permute-start(f32[256,256]{1,0:T(8,128)S(1)} %slice_add_fusion), channel_id=1, source_target_pairs={{1,0},{2,1},{3,2},{4,3},{5,4},{6,5},{7,6},{8,7},{9,8},{10,9},{11,1... | collective-permute-start | bytes 786440 | tf_op jit(solution)/shard_map/ppermute | solution.py:17
  270.7 59.6 %reduce-scatter.8.cloned.1.call-start = ((), (), s32[]{:S(2)}) async-start(), calls=%async_computation.12 | async-start | bytes 3932160 | tf_op jit(solution)/shard_map/reduce_scatter | solution.py:239
  281.2 89.7 %reduce-scatter.14.cloned.1.call-start = ((), (), s32[]{:S(2)}) async-start(), calls=%async_computation.15 | async-start | bytes 3932160 | tf_op jit(solution)/shard_map/reduce_scatter | solution.py:244
  283.6 155.1 %reduce-scatter.16.cloned.1.call-start = ((), (), s32[]{:S(2)}) async-start(), calls=%async_computation.16 | async-start | bytes 7864320 | tf_op jit(solution)/shard_map/reduce_scatter | solution.py:247
  286.9 219.9 %reduce-scatter.18.cloned.1.call-start = ((), (), s32[]{:S(2)}) async-start(), calls=%async_computation.17 | async-start | bytes 7864320 | tf_op jit(solution)/shard_map/reduce_scatter | solution.py:248
  291.4 283.3 %reduce-scatter.20.cloned.1.call-start = ((), (), s32[]{:S(2)}) async-start(), calls=%async_computation.18 | async-start | bytes 7864320 | tf_op jit(solution)/shard_map/reduce_scatter | solution.py:249
  296.0 499.3 %all-reduce.20.cloned.1.call-start = ((), (), s32[]{:S(2)}) async-start(), calls=%async_computation.19 | async-start | bytes 22282240 | tf_op jit(solution)/shard_map/psum | solution.py:267
  576.5 42.2 %copy-start.9 = (f32[256,640]{1,0:T(8,128)S(1)}, f32[256,640]{1,0:T(8,128)}, u32[]{:S(2)}) copy-start(f32[256,640]{1,0:T(8,128)} %copy-done.8) | copy-start | bytes 1966084
  795.3 3.4 copy-start.46
  795.3 4.1 copy-start.30
  795.3 5.2 copy-start.24
  (40 other events, 66.5 us)
Sparse Core Ops, SparseCore 0:
  9.7 29.8 all-gather.7
  41.1 31.1 all-gather.9
  73.9 40.6 all-gather.11
  116.0 39.0 all-gather.13
  156.5 39.0 all-gather.15
  243.1 19.7 reduce-scatter.9
  270.9 18.9 reduce-scatter.11
  292.7 37.5 reduce-scatter.7
  333.2 37.5 reduce-scatter.13
  373.0 65.6 reduce-scatter.15
  441.1 65.6 reduce-scatter.17
  509.0 65.6 reduce-scatter.19
  580.1 215.1 all-reduce.19
where the time goes:
time: 815 us; the launch traced here: 814 us
  waiting for transfers between devices  593 us (73%)
  blocking collectives  71.1 us (9%)
  matrix products  60.4 us (7%)
  starting transfers between devices  32.1 us (4%)
  local copies, waits for them, and re-layouts  27.5 us (3%)
  between operations  17.1 us (2%)
  other arithmetic  12.8 us (2%)
    psum x1, waiting for transfers between devices, on_device(): lax.psum((part_one, part_two, part_three, part_four, part_five, part_six,...  176 us
    reduce_scatter x1, waiting for transfers between devices, on_device(): lax.psum_scatter(grad_up, 'fsdp', scatter_dimension=0, tiled=True)  68.1 us
    reduce_scatter x1, waiting for transfers between devices, on_device(): lax.psum_scatter(grad_down, 'fsdp', scatter_dimension=0, tiled=True)  67.8 us
    reduce_scatter x1, waiting for transfers between devices, on_device(): lax.psum_scatter(grad_gate, 'fsdp', scatter_dimension=0, tiled=True)  67.8 us
    reduce_scatter x1, waiting for transfers between devices, on_device(): lax.psum_scatter(grad_out, 'fsdp', scatter_dimension=0, tiled=True)  40.6 us
    all_gather x1, waiting for transfers between devices, on_device(): lax.all_gather(w_gate, 'fsdp', axis=0, tiled=True)  36.7 us
    all_gather x1, waiting for transfers between devices, on_device(): lax.all_gather(w_up, 'fsdp', axis=0, tiled=True)  36.3 us
    psum x1, blocking collectives, on_device(): lax.psum((part_one, part_two, part_three, part_four, part_five, part_six,...  35.1 us
  transfers between devices with their start and end apart: 21, of which 13 were waited for; matrix products, arithmetic and copies ran while one was open for 7% of the time, Pallas kernels for 0%

commit v1 on v0

v1 whole, which is shorter than its diff:
```python
import jax
import jax.numpy as jnp
from jax import lax
from jax.sharding import PartitionSpec as P

WINDOW = 512
EPSILON = 1e-06
ROPE_BASE = 10000.0
MASKED = -1e30
LANES = 128
BF16 = jnp.bfloat16
F32 = jnp.float32


def norm_scale(values, scales):
    return values * lax.rsqrt(jnp.mean(values * values, axis=-1, keepdims=True) + EPSILON) * scales


def rotate(values, places):
    half_dim = values.shape[-1] // 2
    frequency = ROPE_BASE ** (-(jnp.arange(half_dim, dtype=F32) * 2.0 / values.shape[-1]))
    angles = places.astype(F32)[:, None] * frequency[None, :]
    cosine = jnp.cos(angles)[:, None, :]
    sine_part = jnp.sin(angles)[:, None, :]
    first_half = values[..., :half_dim]
    second_half = values[..., half_dim:]
    return jnp.concatenate(
        [first_half * cosine - second_half * sine_part, second_half * cosine + first_half * sine_part], axis=-1
    )


def gelu_gate(gate_vals, up_vals):
    return jax.nn.gelu(gate_vals, approximate=True) * up_vals


class Places:
    def __init__(self):
        self.seq = lax.axis_size("seq")
        self.fsdp = lax.axis_size("fsdp")
        self.outer = self.seq // 4
        index = lax.axis_index("seq")
        self.core_at = index % 2
        self.mid_at = (index // 2) % 2
        self.outer_at = index // 4
        self.fsdp_at = lax.axis_index("fsdp")

    def core_swap(self, array):
        return lax.ppermute(array, "seq", [(i, i ^ 1) for i in range(self.seq)])

    def mid_swap(self, array):
        return lax.ppermute(array, "seq", [(i, i ^ 2) for i in range(self.seq)])

    def outer_shift(self, array, by):
        return lax.ppermute(array, "seq", [(i, (i + 4 * by) % self.seq) for i in range(self.seq)])

    def fsdp_shift(self, array, by):
        return lax.ppermute(array, "fsdp", [(i, (i + by) % self.fsdp) for i in range(self.fsdp)])


def pick(array, at):
    return lax.dynamic_index_in_dim(array, at, 0, keepdims=False)


def ordered(pieces, at):
    count = len(pieces)
    if count == 2:
        own, other = pieces
        return jnp.where(at == 0, jnp.stack([own, other]), jnp.stack([other, own]))
    stacked = jnp.stack(pieces)
    return jnp.stack([pick(stacked, (at - j) % count) for j in range(count)])


def gather_rows(here, shard):
    rows = shard.shape[0]
    half_rows = rows // 2
    half = lax.dynamic_slice_in_dim(shard, here.core_at * half_rows, half_rows, 0)
    pieces = [shard]
    for by in range(1, here.fsdp):
        mine = here.fsdp_shift(half, by)
        pieces.append(ordered([mine, here.core_swap(mine)], here.core_at).reshape(shard.shape))
    return ordered(pieces, here.fsdp_at).reshape((here.fsdp * rows,) + shard.shape[1:])


def pack_columns(here, grad):
    rows, columns = grad.shape
    tall, wide = rows // (here.fsdp * here.outer), columns // (4 * LANES)
    cut = grad.astype(BF16).reshape(here.fsdp, here.outer, tall, 2, 2, wide, LANES)
    return cut.transpose(3, 0, 4, 1, 5, 2, 6).reshape(2, here.fsdp, 2, here.outer, wide * tall, LANES)


def unpack_columns(here, packed, rows, columns):
    tall, wide = rows // here.outer, columns // (4 * LANES)
    cut = packed.reshape(2, 2, here.outer, wide, tall, LANES)
    return cut.transpose(2, 4, 0, 1, 3, 5).reshape(rows, columns).astype(F32)


def pack_rows(here, grad):
    rows, columns = grad.shape
    tall, wide = rows // (here.fsdp * here.outer * 4), columns // LANES
    cut = grad.astype(BF16).reshape(here.fsdp, 2, 2, here.outer, tall, wide, LANES)
    return cut.transpose(1, 0, 2, 3, 5, 4, 6).reshape(2, here.fsdp, 2, here.outer, wide * tall, LANES)


def unpack_rows(here, packed, rows, columns):
    tall, wide = rows // (here.outer * 4), columns // LANES
    cut = packed.reshape(2, 2, here.outer, wide, tall, LANES)
    return cut.transpose(0, 1, 2, 4, 3, 5).reshape(rows, columns).astype(F32)


def total(terms):
    out = terms[0].astype(F32)
    for term in terms[1:]:
        out = out + term.astype(F32)
    return out.astype(BF16)


def reduce_chunk(here, packed):
    kept = pick(packed, here.core_at)
    packed = total([kept, here.core_swap(pick(packed, 1 - here.core_at))])
    terms = [pick(packed, here.fsdp_at)]
    for by in range(1, here.fsdp):
        terms.append(here.fsdp_shift(pick(packed, (here.fsdp_at + by) % here.fsdp), by))
    packed = total(terms)
    kept = pick(packed, here.mid_at)
    packed = total([kept, here.mid_swap(pick(packed, 1 - here.mid_at))])
    terms = [pick(packed, here.outer_at)]
    for by in range(1, here.outer):
        terms.append(here.outer_shift(pick(packed, (here.outer_at + by) % here.outer), by))
    own = total(terms)
    packed = ordered([own] + [here.outer_shift(own, by) for by in range(1, here.outer)], here.outer_at)
    packed = ordered([packed, here.mid_swap(packed)], here.mid_at)
    return ordered([packed, here.core_swap(packed)], here.core_at)


def linear_shift(array, by):
    count = lax.axis_size("seq") * lax.axis_size("fsdp")
    return lax.ppermute(array, ("seq", "fsdp"), [(i, i + by) for i in range(count) if 0 <= i + by < count])


def on_device(
    tokens, positions, cotangent, in_gain, w_query, w_key, w_value, query_gain, key_gain, w_out, attn_gain,
    ffn_gain_in, w_gate, w_up, w_down, ffn_gain_out,
):
    here = Places()
    rows = tokens.shape[0]
    head_dim = w_key.shape[1]
    query_cols = w_query.shape[1]
    head_count = query_cols // head_dim
    hops = (WINDOW + rows - 1) // rows
    halo = hops * rows
    gains = (in_gain, query_gain, key_gain, attn_gain, ffn_gain_in, ffn_gain_out)
    cuts = [0]
    for gain in gains:
        cuts.append(cuts[-1] + gain.shape[0])

    qkv_shard = jnp.concatenate([w_query, w_key, w_value], axis=1)
    shard_rows, qkv_cols = qkv_shard.shape
    padded = (shard_rows + 1 + 31) // 32 * 32
    gain_row = jnp.pad(jnp.concatenate(gains), (0, qkv_cols - cuts[-1]))[None]
    first = jnp.concatenate([qkv_shard, jnp.pad(gain_row, ((0, padded - shard_rows - 1), (0, 0)))], axis=0)
    first = gather_rows(here, first).reshape(here.fsdp, padded, qkv_cols)
    full_qkv = first[:, :shard_rows].reshape(-1, qkv_cols)
    gain_rows = first[:, shard_rows].astype(F32)
    gain_in, gain_query, gain_key, gain_attn, gain_ffn_in, gain_ffn_out = (
        gain_rows[:, cuts[i] : cuts[i + 1]].reshape(-1) for i in range(6)
    )
    all_tokens = jnp.concatenate([linear_shift(tokens, by) for by in range(hops, 0, -1)] + [tokens], axis=0)
    full_out = gather_rows(here, w_out)
    full_gate = gather_rows(here, w_gate)
    full_up = gather_rows(here, w_up)
    full_down = gather_rows(here, w_down)

    score_scale = head_dim ** (-0.5)
    tokens_f = tokens.astype(F32)
    all_positions = jnp.concatenate([positions[0] - halo + jnp.arange(halo, dtype=jnp.int32), positions])
    normed_f, pull_in = jax.vjp(norm_scale, all_tokens.astype(F32), gain_in)
    normed_all = normed_f.astype(BF16)
    normed = normed_all[halo:]
    query_raw = jnp.dot(normed, full_qkv[:, :query_cols], preferred_element_type=F32).reshape(
        rows, head_count, head_dim
    )
    kv_raw = jnp.dot(normed_all, full_qkv[:, query_cols:], preferred_element_type=F32)
    key_raw = kv_raw[:, :head_dim].reshape(halo + rows, 1, head_dim)
    values_all = kv_raw[:, head_dim:].astype(BF16)

    queries_f, pull_query = jax.vjp(lambda v, g: rotate(norm_scale(v, g), positions), query_raw, gain_query)
    keys_f, pull_key = jax.vjp(lambda v, g: rotate(norm_scale(v, g), all_positions), key_raw, gain_key)
    queries = queries_f.astype(BF16)
    keys_all = keys_f.reshape(halo + rows, head_dim).astype(BF16)
    distance = jnp.arange(rows)[:, None] + halo - jnp.arange(halo + rows)[None, :]
    allowed = (distance >= 0) & (distance < WINDOW) & (distance <= positions[:, None])
    raw_scores = jnp.einsum("qhd,kd->hqk", queries, keys_all, preferred_element_type=F32)
    scores = jnp.where(allowed[None], raw_scores * score_scale, MASKED)
    top_score = jnp.max(scores, axis=-1, keepdims=True)
    weights = jnp.exp(scores - top_score)
    probs_f = weights / jnp.sum(weights, axis=-1, keepdims=True)
    attn_probs = probs_f.astype(BF16)
    attended = (
        jnp.einsum("hqk,kd->qhd", attn_probs, values_all, preferred_element_type=F32)
        .reshape(rows, query_cols)
        .astype(BF16)
    )
    projected = jnp.dot(attended, full_out, preferred_element_type=F32)
    branch_attn, pull_attn = jax.vjp(norm_scale, projected, gain_attn)
    residual = tokens_f + branch_attn
    ffn_in_f, pull_ffn_in = jax.vjp(norm_scale, residual, gain_ffn_in)
    ffn_in = ffn_in_f.astype(BF16)
    gate_vals = jnp.dot(ffn_in, full_gate, preferred_element_type=F32)
    up_vals = jnp.dot(ffn_in, full_up, preferred_element_type=F32)
    mixed_f, pull_mixed = jax.vjp(gelu_gate, gate_vals, up_vals)
    mixed_vals = mixed_f.astype(BF16)
    down_vals = jnp.dot(mixed_vals, full_down, preferred_element_type=F32)
    branch_ffn, pull_ffn_out = jax.vjp(norm_scale, down_vals, gain_ffn_out)
    layer_out = (residual + branch_ffn).astype(BF16)

    upstream = cotangent.astype(F32)
    d_down_f, grad_ffn_out = pull_ffn_out(upstream)
    d_down = d_down_f.astype(BF16)
    grad_down = jnp.einsum("tf,td->fd", mixed_vals, d_down, preferred_element_type=F32)
    down_chunk = reduce_chunk(here, pack_rows(here, grad_down))
    d_mixed = jnp.einsum("td,fd->tf", d_down, full_down, preferred_element_type=F32)
    d_gate_f, d_up_f = pull_mixed(d_mixed)
    d_gate = d_gate_f.astype(BF16)
    d_up = d_up_f.astype(BF16)
    grad_gate = jnp.einsum("td,tf->df", ffn_in, d_gate, preferred_element_type=F32)
    grad_up = jnp.einsum("td,tf->df", ffn_in, d_up, preferred_element_type=F32)
    gate_chunk = reduce_chunk(
        here, jnp.concatenate([pack_columns(here, grad_gate), pack_columns(here, grad_up)], axis=-2)
    )
    d_ffn_in = jnp.einsum("tf,df->td", d_gate, full_gate, preferred_element_type=F32) + jnp.einsum(
        "tf,df->td", d_up, full_up, preferred_element_type=F32
    )
    d_resid_part, grad_ffn_in = pull_ffn_in(d_ffn_in)
    d_residual = upstream + d_resid_part
    d_proj_f, grad_attn = pull_attn(d_residual)
    d_proj = d_proj_f.astype(BF16)
    grad_out = jnp.einsum("tq,td->qd", attended, d_proj, preferred_element_type=F32)
    d_attended = (
        jnp.einsum("td,qd->tq", d_proj, full_out, preferred_element_type=F32)
        .astype(BF16)
        .reshape(rows, head_count, head_dim)
    )
    d_probs = jnp.einsum("qhd,kd->hqk", d_attended, values_all, preferred_element_type=F32)
    row_terms = jnp.sum(probs_f * d_probs, axis=-1, keepdims=True)
    d_scores = (probs_f * (d_probs - row_terms) * score_scale).astype(BF16)
    d_queries = jnp.einsum("hqk,kd->qhd", d_scores, keys_all, preferred_element_type=F32)
    d_keys = jnp.einsum("hqk,qhd->kd", d_scores, queries, preferred_element_type=F32)
    d_values = jnp.einsum("hqk,qhd->kd", attn_probs, d_attended, preferred_element_type=F32)
    d_query_f, grad_query_gain = pull_query(d_queries)
    d_key_f, grad_key_gain = pull_key(d_keys.reshape(halo + rows, 1, head_dim))
    d_query_raw = d_query_f.reshape(rows, query_cols).astype(BF16)
    d_kv_raw = jnp.concatenate([d_key_f.reshape(halo + rows, head_dim), d_values], axis=1).astype(BF16)
    grad_q = jnp.einsum("td,tq->dq", normed, d_query_raw, preferred_element_type=F32)
    grad_kv = jnp.einsum("td,tq->dq", normed_all, d_kv_raw, preferred_element_type=F32)
    d_normed = jnp.einsum("tq,dq->td", d_kv_raw, full_qkv[:, query_cols:], preferred_element_type=F32)
    d_normed_q = jnp.einsum("tq,dq->td", d_query_raw, full_qkv[:, :query_cols], preferred_element_type=F32)
    d_normed = jnp.concatenate([d_normed[:halo], d_normed[halo:] + d_normed_q], axis=0)
    d_tokens, grad_in = pull_in(d_normed)
    gain_grads = (grad_in, grad_query_gain, grad_key_gain, grad_attn, grad_ffn_in, grad_ffn_out)
    gain_pack = jnp.concatenate([g.reshape(here.fsdp, -1) for g in gain_grads], axis=1)
    gain_piece = cuts[-1] // (4 * here.outer)
    gain_pack = gain_pack.reshape(here.fsdp, 2, 2, here.outer, 1, gain_piece).transpose(1, 0, 2, 3, 4, 5)
    gain_pack = jnp.pad(gain_pack.astype(BF16), ((0, 0),) * 4 + ((0, 15), (0, LANES - gain_piece)))
    out_pack = pack_rows(here, grad_out)
    qkv_pack = pack_columns(here, jnp.concatenate([grad_q, grad_kv], axis=1))
    last_chunk = reduce_chunk(here, jnp.concatenate([out_pack, qkv_pack, gain_pack], axis=-2))

    grad_tokens = d_residual + d_tokens[halo:]
    for by in range(1, hops + 1):
        start = halo - by * rows
        grad_tokens = grad_tokens + linear_shift(d_tokens[start : start + rows].astype(BF16), -by).astype(F32)

    gate_rows = gate_chunk.shape[-2] // 2
    out_rows, qkv_rows = out_pack.shape[-2], qkv_pack.shape[-2]
    total_out = unpack_rows(here, last_chunk[..., :out_rows, :], *w_out.shape)
    total_qkv = unpack_columns(here, last_chunk[..., out_rows : out_rows + qkv_rows, :], shard_rows, qkv_cols)
    total_gains = last_chunk[..., out_rows + qkv_rows, :gain_piece].reshape(-1).astype(F32)
    g = [total_gains[cuts[i] : cuts[i + 1]] for i in range(6)]
    return (
        layer_out,
        grad_tokens,
        g[0],
        total_qkv[:, :query_cols],
        total_qkv[:, query_cols : query_cols + head_dim],
        total_qkv[:, query_cols + head_dim :],
        g[1],
        g[2],
        total_out,
        g[3],
        g[4],
        unpack_columns(here, gate_chunk[..., :gate_rows, :], *w_gate.shape),
        unpack_columns(here, gate_chunk[..., gate_rows:, :], *w_up.shape),
        unpack_rows(here, down_chunk, *w_down.shape),
        g[5],
    )


def solution(mesh):
    tok = P(("seq", "fsdp"), None)
    mat = P("fsdp", None)
    vec = P("fsdp")
    return jax.shard_map(
        on_device,
        mesh=mesh,
        in_specs=(
            tok, P(("seq", "fsdp")), tok, vec, mat, mat, mat, vec, vec, mat, vec, vec, mat, mat, mat, vec,
        ),
        out_specs=(tok, tok, vec, mat, mat, mat, vec, vec, mat, vec, vec, mat, mat, mat, vec),
        check_vma=False,
    )
```

time: 815 us -> 409 us (0.50)
  waiting for transfers between devices: 593 us -> 129 us
  local copies, waits for them, and re-layouts: 27.5 us -> 104 us
  blocking collectives: 71.1 us -> 0 us
  other arithmetic: 12.8 us -> 60.2 us
  starting transfers between devices: 32.1 us -> 56.7 us
  between operations: 17.1 us -> 3.14 us
  matrix products: 60.4 us -> 48.4 us
    reduce_scatter x7 -> x0, waiting for transfers between devices: 279 us -> none  [the longest x1 68.1 us: on_device(): lax.psum_scatter(grad_up, 'fsdp', scatter_dimension=0, tiled=True)]
    psum x1 -> x0, waiting for transfers between devices: 176 us -> none  [on_device(): lax.psum((part_one, part_two, part_three, part_four, part_five, part_six,...]
    all_gather x5 -> x0, waiting for transfers between devices: 108 us -> none  [the longest x1 36.7 us: on_device(): lax.all_gather(w_gate, 'fsdp', axis=0, tiled=True)]
    ppermute x8 -> x47, waiting for transfers between devices: 27.9 us -> 129 us  [the longest x8 79.2 us: fsdp_shift(): lax.ppermute(array, 'fsdp', [(i, (i + by) % self.fsdp) for i in range(sel...]
    psum x1 -> x0, blocking collectives: 35.1 us -> none  [on_device(): lax.psum((part_one, part_two, part_three, part_four, part_five, part_six,...]
    reshape x1 -> x12, local copies, waits for them, and re-layouts: 0.5 us -> 28 us  [the longest x4 14 us: pack_columns(): grad.astype(BF16).reshape(here.fsdp, here.outer, tall, 2, 2, wide, LANES)]
    all_gather x4 -> x0, blocking collectives: 26.1 us -> none  [the longest x1 9.42 us: on_device(): lax.all_gather(w_value, 'fsdp', axis=0, tiled=True)]
    ppermute x8 -> x47, starting transfers between devices: 31.3 us -> 56.7 us  [the longest x18 23 us: outer_shift(): lax.ppermute(array, 'seq', [(i, (i + 4 * by) % self.seq) for i in range(s...]
  transfers between devices with their start and end apart: 21 -> 47, of which waited for: 13 -> 18; matrix products, arithmetic and copies ran while one was open for 7% -> 29% of each run, Pallas kernels for 0% -> 0%
where the time goes in v1:
time: 409 us; the launch traced here: 402 us
  waiting for transfers between devices  129 us (32%)
  local copies, waits for them, and re-layouts  104 us (25%)
  other arithmetic  60.2 us (15%)
  starting transfers between devices  56.7 us (14%)
  matrix products  48.4 us (12%)
    ppermute x8, waiting for transfers between devices, fsdp_shift(): lax.ppermute(array, 'fsdp', [(i, (i + by) % self.fsdp) for i in range(sel...  79.2 us
    ppermute x6, waiting for transfers between devices, mid_swap(): return lax.ppermute(array, 'seq', [(i, i ^ 2) for i in range(self.seq)])  25.4 us
    ppermute x18, starting transfers between devices, outer_shift(): lax.ppermute(array, 'seq', [(i, (i + 4 * by) % self.seq) for i in range(s...  23 us
    ppermute x18, waiting for transfers between devices, outer_shift(): lax.ppermute(array, 'seq', [(i, (i + 4 * by) % self.seq) for i in range(s...  20.7 us
    select_n x18, other arithmetic, ordered(): return jnp.where(at == 0, jnp.stack([own, other]), jnp.stack([other, own]))  19.1 us
    unnamed x187, local copies, waits for them, and re-layouts  18.2 us
    ppermute x4, starting transfers between devices, linear_shift(): lax.ppermute(array, ('seq', 'fsdp'), [(i, i + by) for i in range(count) i...  17.5 us
    reshape x4, local copies, waits for them, and re-layouts, pack_columns(): grad.astype(BF16).reshape(here.fsdp, here.outer, tall, 2, 2, wide, LANES)  14 us
  transfers between devices with their start and end apart: 47, of which 18 were waited for; matrix products, arithmetic and copies ran while one was open for 29% of the time, Pallas kernels for 0%

profile of v1, /device:TPU:1, one launch (start us, length us, event | category | flops | bytes accessed | tf_op | source)
XLA Modules:
  0.0 401.7 jit_solution(692546264552026303)
XLA Ops:
  0.7 4.1 %collective-permute-start.1 = (bf16[256,640]{1,0:T(8,128)(2,1)}, bf16[256,640]{1,0:T(8,128)(2,1)S(1)}, u32[]{:S(2)}, u32[]{:S(2)}) collective-permute-start(bf16[256,640]{1,0:T(8,128)(2,1)} %param.16), channel_id=1, source_target_pairs={{0,1},{1,2},{2,3},{3,4},{4,5},{5,6},{6,7},{7,8},{8,9},{9,10},{10,1... | collective-permute-start | bytes 983048 | tf_op jit(solution)/shard_map/ppermute | solution.py:137
  4.8 4.0 collective-permute-start
  8.8 4.2 %concatenate.96 = bf16[1536]{0:T(1024)(128)(2,1)S(1)} concatenate(bf16[320]{0:T(512)(128)(2,1)} %param.19, bf16[128]{0:T(256)(128)(2,1)} %param.23, bf16[128]{0:T(256)(128)(2,1)} %param.24, bf16[320]{0:T(512)(128)(2,1)} %param.26, bf16[320]{0:T(512)(128)(2,1)} %param.27, bf16[320]{0:T(512)(128)(2,1)} %param.31), dimensions={0} | concatenate | bytes 6144 | tf_op jit(solution)/shard_map/concatenate | solution.py:159
  26.8 10.0 %collective-permute-done.4 = bf16[256,640]{1,0:T(8,128)(2,1)} collective-permute-done((bf16[256,640]{1,0:T(8,128)(2,1)}, bf16[256,640]{1,0:T(8,128)(2,1)}, u32[]{:S(2)}, u32[]{:S(2)}) %collective-permute-start.4) | collective-permute-done | bytes 327712 | tf_op jit(solution)/shard_map/ppermute | solution.py:57
  37.7 13.1 %collective-permute-done.6 = bf16[160,2048]{1,0:T(8,128)(2,1)} collective-permute-done((bf16[160,2048]{1,0:T(8,128)(2,1)}, bf16[160,2048]{1,0:T(8,128)(2,1)}, u32[]{:S(2)}, u32[]{:S(2)}) %collective-permute-start.6) | collective-permute-done | bytes 655392 | tf_op jit(solution)/shard_map/ppermute | solution.py:57
  50.9 14.0 %collective-permute-done.8 = bf16[160,2048]{1,0:T(8,128)(2,1)} collective-permute-done((bf16[160,2048]{1,0:T(8,128)(2,1)}, bf16[160,2048]{1,0:T(8,128)(2,1)}, u32[]{:S(2)}, u32[]{:S(2)}) %collective-permute-start.8) | collective-permute-done | bytes 655392 | tf_op jit(solution)/shard_map/ppermute | solution.py:57
  64.9 12.7 %collective-permute-done.10 = bf16[512,640]{1,0:T(8,128)(2,1)} collective-permute-done((bf16[512,640]{1,0:T(8,128)(2,1)}, bf16[512,640]{1,0:T(8,128)(2,1)}, u32[]{:S(2)}, u32[]{:S(2)}) %collective-permute-start.10) | collective-permute-done | bytes 655392 | tf_op jit(solution)/shard_map/ppermute | solution.py:57
  119.1 2.6 multiply_convert_fusion
  134.1 7.1 %fusion.37 = f32[256,4,256]{2,0,1:T(8,128)} fusion(f32[768,256,4]{1,0,2:T(8,128)} %fusion.101, bf16[768,1,128]{0,2,1:T(8,128)(2,1)} %copy-done.56, bf16[768,1,128]{0,2,1:T(8,128)(2,1)} %copy-done.55, f32[4,256,768]{1,2,0:T(8,128)} %copy-done.88, f32[4,256]{1,0:T(4,128)S(1)} %copy-done.91), kind=kOutput, calls=%fused_computation.83 | convolution fusion | flops 408946432 | bytes 7737344 | tf_op jit(solution)/shard_map/hqk,kd->qhd/dot_general | solution.py:246
  141.2 6.8 %fusion.40 = f32[768,1,256]{0,2,1:T(8,128)} fusion(f32[768,256,4]{1,0,2:T(8,128)} %fusion.101, bf16[256,4,128]{2,0,1:T(8,128)(2,1)S(1)} %copy-done.49, bf16[256,4,128]{2,0,1:T(8,128)(2,1)S(1)} %copy-done.47, f32[4,256,768]{1,2,0:T(8,128)} %copy-done.88, f32[4,256]{1,0:T(4,128)S(1)} %copy-done.91), kind=kOutput, calls=%fused_computation.100 | convolution fusion | flops 409208576 | bytes 7606272 | tf_op jit(solution)/shard_map/hqk,qhd->kd/dot_general | solution.py:247
  148.0 3.1 fusion.85
  152.1 3.3 fusion.69
  158.2 2.6 slice.170
  160.7 2.6 convolution_add_fusion
  163.4 2.7 convolution_convert_fusion.3
  169.1 2.5 convolution_convert_fusion
  171.6 7.0 %reshape.841 = bf16[2,2,2,4,64,5,128]{6,5,4,3,2,1,0:T(8,128)(2,1)} reshape(bf16[2048,640]{1,0:T(8,128)(2,1)} %convolution_convert_fusion) | data formatting | bytes 5242880 | tf_op jit(solution)/shard_map/reshape | solution.py:100
  178.6 3.0 copy.178
  187.4 6.8 %convert_element_type.370 = bf16[2,4,80,2,2,3,128]{6,5,4,3,2,1,0:T(4,128)(2,1)} reshape(bf16[640,1536]{1,0:T(8,128)(2,1)} %pad_maximum_fusion.1) | data formatting | bytes 3932160 | tf_op jit(solution)/shard_map/convert_element_type | solution.py:87
  194.2 3.6 copy.170
  197.8 4.1 %reshape.828 = bf16[2,2,2,4,32,5,128]{6,5,4,3,2,1,0:T(8,128)(2,1)} reshape(bf16[1024,640]{1,0:T(8,128)(2,1)} %convolution_convert_fusion.4) | data formatting | bytes 2621440 | tf_op jit(solution)/shard_map/reshape | solution.py:100
  201.9 2.9 copy.168
  204.8 3.6 reshape.837
  208.5 2.5 copy.174
  211.0 2.4 convolution_convert_fusion.1
  213.4 5.4 %reshape.839 = bf16[2,4,80,2,2,4,128]{6,5,4,3,2,1,0:T(4,128)(2,1)} reshape(bf16[640,2048]{1,0:T(8,128)(2,1)} %convolution_convert_fusion.1) | data formatting | bytes 5242880 | tf_op jit(solution)/shard_map/reshape | solution.py:87
  218.8 2.4 copy.175
  236.5 13.1 %collective-permute-done.37 = bf16[2,4,320,128]{3,2,1,0:T(8,128)(2,1)} collective-permute-done((bf16[2,4,320,128]{3,2,1,0:T(8,128)(2,1)}, bf16[2,4,320,128]{3,2,1,0:T(8,128)(2,1)}, u32[]{:S(2)}, u32[]{:S(2)}) %collective-permute-start.37) | collective-permute-done | bytes 655392 | tf_op jit(solution)/shard_map/ppermute | solution.py:57
  255.0 4.7 %collective-permute-done.38 = bf16[4,320,128]{2,1,0:T(8,128)(2,1)S(1)} collective-permute-done((bf16[4,320,128]{2,1,0:T(8,128)(2,1)S(1)}, bf16[4,320,128]{2,1,0:T(8,128)(2,1)S(1)}, u32[]{:S(2)}, u32[]{:S(2)}) %collective-permute-start.38) | collective-permute-done | bytes 327712 | tf_op jit(solution)/shard_map/ppermute | solution.py:51
  259.9 3.1 collective-permute-start.41
  263.7 2.4 fusion.3
  266.4 3.8 collective-permute-done.40
  275.2 4.9 %collective-permute-start.13 = (bf16[256,640]{1,0:T(8,128)(2,1)S(1)}, bf16[256,640]{1,0:T(8,128)(2,1)S(1)}, u32[]{:S(2)}, u32[]{:S(2)}) collective-permute-start(bf16[256,640]{1,0:T(8,128)(2,1)S(1)} %get-tuple-element.43), channel_id=1, source_target_pairs={{2,0},{3,1},{4,2},{5,3},{6,4},{7,5},{8,6},{9,7},{10,8},{11,9},{12,... | collective-permute-start | bytes 983048 | tf_op jit(solution)/shard_map/ppermute | solution.py:137
  282.1 2.6 collective-permute-start.19
  286.0 16.1 %collective-permute-done.26 = bf16[2,4,640,128]{3,2,1,0:T(8,128)(2,1)S(1)} collective-permute-done((bf16[2,4,640,128]{3,2,1,0:T(8,128)(2,1)S(1)}, bf16[2,4,640,128]{3,2,1,0:T(8,128)(2,1)S(1)}, u32[]{:S(2)}, u32[]{:S(2)}) %collective-permute-start.26) | collective-permute-done | bytes 1310752 | tf_op jit(solution)/shard_map/ppermute | solution.py:57
  302.9 3.1 collective-permute-start.22
  308.1 7.6 %collective-permute-done.21 = bf16[416,128]{1,0:T(8,128)(2,1)S(1)} collective-permute-done((bf16[416,128]{1,0:T(8,128)(2,1)S(1)}, bf16[416,128]{1,0:T(8,128)(2,1)S(1)}, u32[]{:S(2)}, u32[]{:S(2)}) %collective-permute-start.21) | collective-permute-done | bytes 106528 | tf_op jit(solution)/shard_map/ppermute | solution.py:54
  317.0 2.4 collective-permute-start.30
  319.5 4.2 %collective-permute-done.45 = bf16[4,320,128]{2,1,0:T(8,128)(2,1)S(1)} collective-permute-done((bf16[4,320,128]{2,1,0:T(8,128)(2,1)S(1)}, bf16[4,320,128]{2,1,0:T(8,128)(2,1)S(1)}, u32[]{:S(2)}, u32[]{:S(2)}) %collective-permute-start.45) | collective-permute-done | bytes 327712 | tf_op jit(solution)/shard_map/ppermute | solution.py:51
  325.2 7.7 %collective-permute-done.23 = bf16[4,416,128]{2,1,0:T(8,128)(2,1)S(1)} collective-permute-done((bf16[4,416,128]{2,1,0:T(8,128)(2,1)S(1)}, bf16[4,416,128]{2,1,0:T(8,128)(2,1)S(1)}, u32[]{:S(2)}, u32[]{:S(2)}) %collective-permute-start.23) | collective-permute-done | bytes 426016 | tf_op jit(solution)/shard_map/ppermute | solution.py:51
  332.9 4.6 %collective-permute-start.12 = (bf16[256,640]{1,0:T(8,128)(2,1)S(1)}, bf16[256,640]{1,0:T(8,128)(2,1)S(1)}, u32[]{:S(2)}, u32[]{:S(2)}) collective-permute-start(bf16[256,640]{1,0:T(8,128)(2,1)S(1)} %get-tuple-element.42), channel_id=1, source_target_pairs={{1,0},{2,1},{3,2},{4,3},{5,4},{6,5},{7,6},{8,7},{9,8},{10,9},{11,1... | collective-permute-start | bytes 983048 | tf_op jit(solution)/shard_map/ppermute | solution.py:137
  338.3 2.4 collective-permute-start.33
  340.9 4.1 %collective-permute-done.12 = bf16[256,640]{1,0:T(8,128)(2,1)S(1)} collective-permute-done((bf16[256,640]{1,0:T(8,128)(2,1)S(1)}, bf16[256,640]{1,0:T(8,128)(2,1)S(1)}, u32[]{:S(2)}, u32[]{:S(2)}) %collective-permute-start.12) | collective-permute-done | bytes 327712 | tf_op jit(solution)/shard_map/ppermute | solution.py:137
  347.5 8.3 %collective-permute-done.32 = bf16[640,128]{1,0:T(8,128)(2,1)S(1)} collective-permute-done((bf16[640,128]{1,0:T(8,128)(2,1)S(1)}, bf16[640,128]{1,0:T(8,128)(2,1)S(1)}, u32[]{:S(2)}, u32[]{:S(2)}) %collective-permute-start.32) | collective-permute-done | bytes 163872 | tf_op jit(solution)/shard_map/ppermute | solution.py:54
  363.1 6.8 %collective-permute-done.34 = bf16[4,640,128]{2,1,0:T(8,128)(2,1)} collective-permute-done((bf16[4,640,128]{2,1,0:T(8,128)(2,1)}, bf16[4,640,128]{2,1,0:T(8,128)(2,1)}, u32[]{:S(2)}, u32[]{:S(2)}) %collective-permute-start.34) | collective-permute-done | bytes 655392 | tf_op jit(solution)/shard_map/ppermute | solution.py:51
  369.9 2.5 maximum_select_fusion.11
  372.5 4.5 %collective-permute-start.35 = (bf16[2,4,640,128]{3,2,1,0:T(8,128)(2,1)}, bf16[2,4,640,128]{3,2,1,0:T(8,128)(2,1)}, u32[]{:S(2)}, u32[]{:S(2)}) collective-permute-start(bf16[2,4,640,128]{3,2,1,0:T(8,128)(2,1)} %maximum_select_fusion.11), channel_id=1, source_target_pairs={{0,2},{2,0},{4,6},{6,4},{8,10},{10,8},{12,14},{14,12},{16,18},{18,... | collective-permute-start | bytes 3932168 | tf_op jit(solution)/shard_map/ppermute | solution.py:48
  380.2 2.6 slice.178
  (417 shorter events, 147.8 us)
Async XLA Ops:
  0.7 24.0 %collective-permute-start.1 = (bf16[256,640]{1,0:T(8,128)(2,1)}, bf16[256,640]{1,0:T(8,128)(2,1)S(1)}, u32[]{:S(2)}, u32[]{:S(2)}) collective-permute-start(bf16[256,640]{1,0:T(8,128)(2,1)} %param.16), channel_id=1, source_target_pairs={{0,1},{1,2},{2,3},{3,4},{4,5},{5,6},{6,7},{7,8},{8,9},{9,10},{10,1... | collective-permute-start | bytes 983048 | tf_op jit(solution)/shard_map/ppermute | solution.py:137
  4.8 21.3 %collective-permute-start = (bf16[256,640]{1,0:T(8,128)(2,1)}, bf16[256,640]{1,0:T(8,128)(2,1)S(1)}, u32[]{:S(2)}, u32[]{:S(2)}) collective-permute-start(bf16[256,640]{1,0:T(8,128)(2,1)} %param.16), channel_id=1, source_target_pairs={{0,2},{1,3},{2,4},{3,5},{4,6},{5,7},{6,8},{7,9},{8,10},{9,11},{10,... | collective-permute-start | bytes 983048 | tf_op jit(solution)/shard_map/ppermute | solution.py:137
  15.2 21.7 %collective-permute-start.2 = (bf16[176,1536]{1,0:T(8,128)(2,1)}, bf16[176,1536]{1,0:T(8,128)(2,1)}, u32[]{:S(2)}, u32[]{:S(2)}) collective-permute-start(bf16[176,1536]{1,0:T(8,128)(2,1)} %constant_dynamic-slice_fusion.16), channel_id=1, source_target_pairs={{0,1},{1,0},{2,3},{3,2},{4,5},{5,4},{6,7},{7,6},{8,9},{9,8},{10,11... | collective-permute-start | bytes 1622024 | tf_op jit(solution)/shard_map/ppermute | solution.py:57
  15.9 20.9 %collective-permute-start.4 = (bf16[256,640]{1,0:T(8,128)(2,1)}, bf16[256,640]{1,0:T(8,128)(2,1)}, u32[]{:S(2)}, u32[]{:S(2)}) collective-permute-start(bf16[256,640]{1,0:T(8,128)(2,1)} %constant_dynamic-slice_fusion.15), channel_id=1, source_target_pairs={{0,1},{1,0},{2,3},{3,2},{4,5},{5,4},{6,7},{7,6},{8,9},{9,8},{10,11... | collective-permute-start | bytes 983048 | tf_op jit(solution)/shard_map/ppermute | solution.py:57
  18.3 32.6 %collective-permute-start.6 = (bf16[160,2048]{1,0:T(8,128)(2,1)}, bf16[160,2048]{1,0:T(8,128)(2,1)}, u32[]{:S(2)}, u32[]{:S(2)}) collective-permute-start(bf16[160,2048]{1,0:T(8,128)(2,1)} %constant_dynamic-slice_fusion.14), channel_id=1, source_target_pairs={{0,1},{1,0},{2,3},{3,2},{4,5},{5,4},{6,7},{7,6},{8,9},{9,8},{10,11... | collective-permute-start | bytes 1966088 | tf_op jit(solution)/shard_map/ppermute | solution.py:57
  24.7 59.6 %copy-start.22 = (bf16[256,640]{1,0:T(8,128)(2,1)}, bf16[256,640]{1,0:T(8,128)(2,1)S(1)}, u32[]{:S(2)}) copy-start(bf16[256,640]{1,0:T(8,128)(2,1)S(1)} %collective-permute-done.1) | copy-start | bytes 983044
  24.7 40.2 %collective-permute-start.8 = (bf16[160,2048]{1,0:T(8,128)(2,1)}, bf16[160,2048]{1,0:T(8,128)(2,1)}, u32[]{:S(2)}, u32[]{:S(2)}) collective-permute-start(bf16[160,2048]{1,0:T(8,128)(2,1)} %constant_dynamic-slice_fusion.13), channel_id=1, source_target_pairs={{0,1},{1,0},{2,3},{3,2},{4,5},{5,4},{6,7},{7,6},{8,9},{9,8},{10,11... | collective-permute-start | bytes 1966088 | tf_op jit(solution)/shard_map/ppermute | solution.py:57
  26.1 51.5 %collective-permute-start.10 = (bf16[512,640]{1,0:T(8,128)(2,1)}, bf16[512,640]{1,0:T(8,128)(2,1)}, u32[]{:S(2)}, u32[]{:S(2)}) collective-permute-start(bf16[512,640]{1,0:T(8,128)(2,1)} %constant_dynamic-slice_fusion.12), channel_id=1, source_target_pairs={{0,1},{1,0},{2,3},{3,2},{4,5},{5,4},{6,7},{7,6},{8,9},{9,8},{10,11... | collective-permute-start | bytes 1966088 | tf_op jit(solution)/shard_map/ppermute | solution.py:57
  36.8 40.8 %collective-permute-start.5 = (bf16[256,640]{1,0:T(8,128)(2,1)}, bf16[256,640]{1,0:T(8,128)(2,1)}, u32[]{:S(2)}, u32[]{:S(2)}) collective-permute-start(bf16[256,640]{1,0:T(8,128)(2,1)} %collective-permute-done.4), channel_id=1, source_target_pairs={{0,2},{2,0},{4,6},{6,4},{8,10},{10,8},{12,14},{14,12},{16,18},{18,... | collective-permute-start | bytes 983048 | tf_op jit(solution)/shard_map/ppermute | solution.py:48
  36.9 43.5 %collective-permute-start.3 = (bf16[176,1536]{1,0:T(8,128)(2,1)}, bf16[176,1536]{1,0:T(8,128)(2,1)S(1)}, u32[]{:S(2)}, u32[]{:S(2)}) collective-permute-start(bf16[176,1536]{1,0:T(8,128)(2,1)} %collective-permute-done.2), channel_id=1, source_target_pairs={{0,2},{2,0},{4,6},{6,4},{8,10},{10,8},{12,14},{14,12},{16,18},{18,... | collective-permute-start | bytes 1622024 | tf_op jit(solution)/shard_map/ppermute | solution.py:48
  50.9 54.9 %collective-permute-start.7 = (bf16[160,2048]{1,0:T(8,128)(2,1)}, bf16[160,2048]{1,0:T(8,128)(2,1)}, u32[]{:S(2)}, u32[]{:S(2)}) collective-permute-start(bf16[160,2048]{1,0:T(8,128)(2,1)} %collective-permute-done.6), channel_id=1, source_target_pairs={{0,2},{2,0},{4,6},{6,4},{8,10},{10,8},{12,14},{14,12},{16,18},{18,... | collective-permute-start | bytes 1966088 | tf_op jit(solution)/shard_map/ppermute | solution.py:48
  64.9 44.5 %collective-permute-start.9 = (bf16[160,2048]{1,0:T(8,128)(2,1)}, bf16[160,2048]{1,0:T(8,128)(2,1)}, u32[]{:S(2)}, u32[]{:S(2)}) collective-permute-start(bf16[160,2048]{1,0:T(8,128)(2,1)} %collective-permute-done.8), channel_id=1, source_target_pairs={{0,2},{2,0},{4,6},{6,4},{8,10},{10,8},{12,14},{14,12},{16,18},{18,... | collective-permute-start | bytes 1966088 | tf_op jit(solution)/shard_map/ppermute | solution.py:48
  77.6 35.6 %collective-permute-start.11 = (bf16[512,640]{1,0:T(8,128)(2,1)}, bf16[512,640]{1,0:T(8,128)(2,1)}, u32[]{:S(2)}, u32[]{:S(2)}) collective-permute-start(bf16[512,640]{1,0:T(8,128)(2,1)} %collective-permute-done.10), channel_id=1, source_target_pairs={{0,2},{2,0},{4,6},{6,4},{8,10},{10,8},{12,14},{14,12},{16,18},{18,... | collective-permute-start | bytes 1966088 | tf_op jit(solution)/shard_map/ppermute | solution.py:48
  182.8 46.1 %collective-permute-start.36 = (bf16[2,2,4,320,128]{4,3,2,1,0:T(8,128)(2,1)}, bf16[2,2,4,320,128]{4,3,2,1,0:T(8,128)(2,1)}, u32[]{:S(2)}, u32[]{:S(2)}) collective-permute-start(bf16[2,2,4,320,128]{4,3,2,1,0:T(8,128)(2,1)} %dynamic-slice_bitcast_fusion.1), channel_id=1, source_target_pairs={{0,2},{2,0},{4,6},{6,4},{8,10},{10,8},{12,14},{14,12},{16,18},{18,... | collective-permute-start | bytes 3932168 | tf_op jit(solution)/shard_map/ppermute | solution.py:48
  223.9 39.9 %collective-permute-start.25 = (bf16[2,2,4,640,128]{4,3,2,1,0:T(8,128)(2,1)}, bf16[2,2,4,640,128]{4,3,2,1,0:T(8,128)(2,1)}, u32[]{:S(2)}, u32[]{:S(2)}) collective-permute-start(bf16[2,2,4,640,128]{4,3,2,1,0:T(8,128)(2,1)} %fusion.10), channel_id=1, source_target_pairs={{0,2},{2,0},{4,6},{6,4},{8,10},{10,8},{12,14},{14,12},{16,18},{18,... | collective-permute-start | bytes 7864328 | tf_op jit(solution)/shard_map/ppermute | solution.py:48
  228.4 24.2 %collective-permute-start.14 = (bf16[2,2,4,416,128]{4,3,2,1,0:T(8,128)(2,1)}, bf16[2,2,4,416,128]{4,3,2,1,0:T(8,128)(2,1)}, u32[]{:S(2)}, u32[]{:S(2)}) collective-permute-start(bf16[2,2,4,416,128]{4,3,2,1,0:T(8,128)(2,1)} %dynamic-slice_bitcast_fusion), channel_id=1, source_target_pairs={{0,2},{2,0},{4,6},{6,4},{8,10},{10,8},{12,14},{14,12},{16,18},{18,... | collective-permute-start | bytes 5111816 | tf_op jit(solution)/shard_map/ppermute | solution.py:48
  232.9 16.6 %collective-permute-start.37 = (bf16[2,4,320,128]{3,2,1,0:T(8,128)(2,1)}, bf16[2,4,320,128]{3,2,1,0:T(8,128)(2,1)}, u32[]{:S(2)}, u32[]{:S(2)}) collective-permute-start(bf16[2,4,320,128]{3,2,1,0:T(8,128)(2,1)} %dynamic-slice_bitcast_fusion.4), channel_id=1, source_target_pairs={{0,1},{1,0},{2,3},{3,2},{4,5},{5,4},{6,7},{7,6},{8,9},{9,8},{10,11... | collective-permute-start | bytes 1966088 | tf_op jit(solution)/shard_map/ppermute | solution.py:57
  250.9 8.9 %collective-permute-start.38 = (bf16[4,320,128]{2,1,0:T(8,128)(2,1)S(1)}, bf16[4,320,128]{2,1,0:T(8,128)(2,1)S(1)}, u32[]{:S(2)}, u32[]{:S(2)}) collective-permute-start(bf16[4,320,128]{2,1,0:T(8,128)(2,1)S(1)} %dynamic-slice_bitcast_fusion.7), channel_id=1, source_target_pairs={{0,4},{2,6},{4,0},{6,2},{8,12},{10,14},{12,8},{14,10},{16,20},{18,... | collective-permute-start | bytes 983048 | tf_op jit(solution)/shard_map/ppermute | solution.py:51
  254.6 19.4 %collective-permute-start.15 = (bf16[2,4,416,128]{3,2,1,0:T(8,128)(2,1)S(1)}, bf16[2,4,416,128]{3,2,1,0:T(8,128)(2,1)S(1)}, u32[]{:S(2)}, u32[]{:S(2)}) collective-permute-start(bf16[2,4,416,128]{3,2,1,0:T(8,128)(2,1)S(1)} %dynamic-slice_bitcast_fusion.3), channel_id=1, source_target_pairs={{0,1},{1,0},{2,3},{3,2},{4,5},{5,4},{6,7},{7,6},{8,9},{9,8},{10,11... | collective-permute-start | bytes 2555912 | tf_op jit(solution)/shard_map/ppermute | solution.py:57
  259.9 6.4 %collective-permute-start.41 = (bf16[320,128]{1,0:T(8,128)(2,1)S(1)}, bf16[320,128]{1,0:T(8,128)(2,1)S(1)}, u32[]{:S(2)}, u32[]{:S(2)}) collective-permute-start(bf16[320,128]{1,0:T(8,128)(2,1)S(1)} %get-tuple-element.77), channel_id=1, source_target_pairs={{0,24},{2,26},{4,28},{6,30},{8,0},{10,2},{12,4},{14,6},{16,8},{18,... | collective-permute-start | bytes 245768 | tf_op jit(solution)/shard_map/ppermute | solution.py:54
  263.0 7.1 %collective-permute-start.40 = (bf16[320,128]{1,0:T(8,128)(2,1)S(1)}, bf16[320,128]{1,0:T(8,128)(2,1)S(1)}, u32[]{:S(2)}, u32[]{:S(2)}) collective-permute-start(bf16[320,128]{1,0:T(8,128)(2,1)S(1)} %get-tuple-element.78), channel_id=1, source_target_pairs={{0,16},{2,18},{4,20},{6,22},{8,24},{10,26},{12,28},{14,30},{16,0},... | collective-permute-start | bytes 245768 | tf_op jit(solution)/shard_map/ppermute | solution.py:54
  263.0 7.1 %collective-permute-start.39 = (bf16[320,128]{1,0:T(8,128)(2,1)S(1)}, bf16[320,128]{1,0:T(8,128)(2,1)S(1)}, u32[]{:S(2)}, u32[]{:S(2)}) collective-permute-start(bf16[320,128]{1,0:T(8,128)(2,1)S(1)} %get-tuple-element.76), channel_id=1, source_target_pairs={{0,8},{2,10},{4,12},{6,14},{8,16},{10,18},{12,20},{14,22},{16,24},... | collective-permute-start | bytes 245768 | tf_op jit(solution)/shard_map/ppermute | solution.py:54
  266.3 35.8 %collective-permute-start.26 = (bf16[2,4,640,128]{3,2,1,0:T(8,128)(2,1)S(1)}, bf16[2,4,640,128]{3,2,1,0:T(8,128)(2,1)S(1)}, u32[]{:S(2)}, u32[]{:S(2)}) collective-permute-start(bf16[2,4,640,128]{3,2,1,0:T(8,128)(2,1)S(1)} %dynamic-slice_bitcast_fusion.2), channel_id=1, source_target_pairs={{0,1},{1,0},{2,3},{3,2},{4,5},{5,4},{6,7},{7,6},{8,9},{9,8},{10,11... | collective-permute-start | bytes 3932168 | tf_op jit(solution)/shard_map/ppermute | solution.py:57
  270.2 5.0 %collective-permute-start.44 = (bf16[320,128]{1,0:T(8,128)(2,1)S(1)}, bf16[320,128]{1,0:T(8,128)(2,1)S(1)}, u32[]{:S(2)}, u32[]{:S(2)}) collective-permute-start(bf16[320,128]{1,0:T(8,128)(2,1)S(1)} %fusion.100), channel_id=1, source_target_pairs={{0,24},{2,26},{4,28},{6,30},{8,0},{10,2},{12,4},{14,6},{16,8},{18,... | collective-permute-start | bytes 245768 | tf_op jit(solution)/shard_map/ppermute | solution.py:54
  270.3 9.8 %collective-permute-start.43 = (bf16[320,128]{1,0:T(8,128)(2,1)S(1)}, bf16[320,128]{1,0:T(8,128)(2,1)S(1)}, u32[]{:S(2)}, u32[]{:S(2)}) collective-permute-start(bf16[320,128]{1,0:T(8,128)(2,1)S(1)} %fusion.100), channel_id=1, source_target_pairs={{0,16},{2,18},{4,20},{6,22},{8,24},{10,26},{12,28},{14,30},{16,0},... | collective-permute-start | bytes 245768 | tf_op jit(solution)/shard_map/ppermute | solution.py:54
  272.5 7.5 %collective-permute-start.42 = (bf16[320,128]{1,0:T(8,128)(2,1)S(1)}, bf16[320,128]{1,0:T(8,128)(2,1)S(1)}, u32[]{:S(2)}, u32[]{:S(2)}) collective-permute-start(bf16[320,128]{1,0:T(8,128)(2,1)S(1)} %fusion.100), channel_id=1, source_target_pairs={{0,8},{2,10},{4,12},{6,14},{8,16},{10,18},{12,20},{14,22},{16,24},... | collective-permute-start | bytes 245768 | tf_op jit(solution)/shard_map/ppermute | solution.py:54
  274.3 7.7 %collective-permute-start.16 = (bf16[4,416,128]{2,1,0:T(8,128)(2,1)S(1)}, bf16[4,416,128]{2,1,0:T(8,128)(2,1)S(1)}, u32[]{:S(2)}, u32[]{:S(2)}) collective-permute-start(bf16[4,416,128]{2,1,0:T(8,128)(2,1)S(1)} %dynamic-slice_bitcast_fusion.6), channel_id=1, source_target_pairs={{0,4},{2,6},{4,0},{6,2},{8,12},{10,14},{12,8},{14,10},{16,20},{18,... | collective-permute-start | bytes 1277960 | tf_op jit(solution)/shard_map/ppermute | solution.py:51
  275.2 65.6 %collective-permute-start.13 = (bf16[256,640]{1,0:T(8,128)(2,1)S(1)}, bf16[256,640]{1,0:T(8,128)(2,1)S(1)}, u32[]{:S(2)}, u32[]{:S(2)}) collective-permute-start(bf16[256,640]{1,0:T(8,128)(2,1)S(1)} %get-tuple-element.43), channel_id=1, source_target_pairs={{2,0},{3,1},{4,2},{5,3},{6,4},{7,5},{8,6},{9,7},{10,8},{11,9},{12,... | collective-permute-start | bytes 983048 | tf_op jit(solution)/shard_map/ppermute | solution.py:137
  282.1 20.7 %collective-permute-start.19 = (bf16[416,128]{1,0:T(8,128)(2,1)S(1)}, bf16[416,128]{1,0:T(8,128)(2,1)S(1)}, u32[]{:S(2)}, u32[]{:S(2)}) collective-permute-start(bf16[416,128]{1,0:T(8,128)(2,1)S(1)} %get-tuple-element.68), channel_id=1, source_target_pairs={{0,24},{2,26},{4,28},{6,30},{8,0},{10,2},{12,4},{14,6},{16,8},{18,... | collective-permute-start | bytes 319496 | tf_op jit(solution)/shard_map/ppermute | solution.py:54
  284.7 18.1 %collective-permute-start.18 = (bf16[416,128]{1,0:T(8,128)(2,1)S(1)}, bf16[416,128]{1,0:T(8,128)(2,1)S(1)}, u32[]{:S(2)}, u32[]{:S(2)}) collective-permute-start(bf16[416,128]{1,0:T(8,128)(2,1)S(1)} %get-tuple-element.69), channel_id=1, source_target_pairs={{0,16},{2,18},{4,20},{6,22},{8,24},{10,26},{12,28},{14,30},{16,0},... | collective-permute-start | bytes 319496 | tf_op jit(solution)/shard_map/ppermute | solution.py:54
  284.7 18.1 %collective-permute-start.17 = (bf16[416,128]{1,0:T(8,128)(2,1)S(1)}, bf16[416,128]{1,0:T(8,128)(2,1)S(1)}, u32[]{:S(2)}, u32[]{:S(2)}) collective-permute-start(bf16[416,128]{1,0:T(8,128)(2,1)S(1)} %get-tuple-element.67), channel_id=1, source_target_pairs={{0,8},{2,10},{4,12},{6,14},{8,16},{10,18},{12,20},{14,22},{16,24},... | collective-permute-start | bytes 319496 | tf_op jit(solution)/shard_map/ppermute | solution.py:54
  302.5 14.3 %collective-permute-start.27 = (bf16[4,640,128]{2,1,0:T(8,128)(2,1)S(1)}, bf16[4,640,128]{2,1,0:T(8,128)(2,1)S(1)}, u32[]{:S(2)}, u32[]{:S(2)}) collective-permute-start(bf16[4,640,128]{2,1,0:T(8,128)(2,1)S(1)} %dynamic-slice_bitcast_fusion.5), channel_id=1, source_target_pairs={{0,4},{2,6},{4,0},{6,2},{8,12},{10,14},{12,8},{14,10},{16,20},{18,... | collective-permute-start | bytes 1966088 | tf_op jit(solution)/shard_map/ppermute | solution.py:51
  302.9 4.8 %collective-permute-start.22 = (bf16[416,128]{1,0:T(8,128)(2,1)S(1)}, bf16[416,128]{1,0:T(8,128)(2,1)S(1)}, u32[]{:S(2)}, u32[]{:S(2)}) collective-permute-start(bf16[416,128]{1,0:T(8,128)(2,1)S(1)} %fusion.97), channel_id=1, source_target_pairs={{0,24},{2,26},{4,28},{6,30},{8,0},{10,2},{12,4},{14,6},{16,8},{18,... | collective-permute-start | bytes 319496 | tf_op jit(solution)/shard_map/ppermute | solution.py:54
  306.0 9.6 %collective-permute-start.21 = (bf16[416,128]{1,0:T(8,128)(2,1)S(1)}, bf16[416,128]{1,0:T(8,128)(2,1)S(1)}, u32[]{:S(2)}, u32[]{:S(2)}) collective-permute-start(bf16[416,128]{1,0:T(8,128)(2,1)S(1)} %fusion.97), channel_id=1, source_target_pairs={{0,16},{2,18},{4,20},{6,22},{8,24},{10,26},{12,28},{14,30},{16,0},... | collective-permute-start | bytes 319496 | tf_op jit(solution)/shard_map/ppermute | solution.py:54
  306.0 9.6 %collective-permute-start.20 = (bf16[416,128]{1,0:T(8,128)(2,1)S(1)}, bf16[416,128]{1,0:T(8,128)(2,1)S(1)}, u32[]{:S(2)}, u32[]{:S(2)}) collective-permute-start(bf16[416,128]{1,0:T(8,128)(2,1)S(1)} %fusion.97), channel_id=1, source_target_pairs={{0,8},{2,10},{4,12},{6,14},{8,16},{10,18},{12,20},{14,22},{16,24},... | collective-permute-start | bytes 319496 | tf_op jit(solution)/shard_map/ppermute | solution.py:54
  307.7 16.0 %collective-permute-start.45 = (bf16[4,320,128]{2,1,0:T(8,128)(2,1)S(1)}, bf16[4,320,128]{2,1,0:T(8,128)(2,1)S(1)}, u32[]{:S(2)}, u32[]{:S(2)}) collective-permute-start(bf16[4,320,128]{2,1,0:T(8,128)(2,1)S(1)} %get-tuple-element.71), channel_id=1, source_target_pairs={{0,4},{2,6},{4,0},{6,2},{8,12},{10,14},{12,8},{14,10},{16,20},{18,... | collective-permute-start | bytes 983048 | tf_op jit(solution)/shard_map/ppermute | solution.py:51
  315.9 17.0 %collective-permute-start.23 = (bf16[4,416,128]{2,1,0:T(8,128)(2,1)S(1)}, bf16[4,416,128]{2,1,0:T(8,128)(2,1)S(1)}, u32[]{:S(2)}, u32[]{:S(2)}) collective-permute-start(bf16[4,416,128]{2,1,0:T(8,128)(2,1)S(1)} %get-tuple-element.62), channel_id=1, source_target_pairs={{0,4},{2,6},{4,0},{6,2},{8,12},{10,14},{12,8},{14,10},{16,20},{18,... | collective-permute-start | bytes 1277960 | tf_op jit(solution)/shard_map/ppermute | solution.py:51
  317.0 20.7 %collective-permute-start.30 = (bf16[640,128]{1,0:T(8,128)(2,1)S(1)}, bf16[640,128]{1,0:T(8,128)(2,1)S(1)}, u32[]{:S(2)}, u32[]{:S(2)}) collective-permute-start(bf16[640,128]{1,0:T(8,128)(2,1)S(1)} %get-tuple-element.58), channel_id=1, source_target_pairs={{0,24},{2,26},{4,28},{6,30},{8,0},{10,2},{12,4},{14,6},{16,8},{18,... | collective-permute-start | bytes 491528 | tf_op jit(solution)/shard_map/ppermute | solution.py:54
  319.4 18.3 %collective-permute-start.29 = (bf16[640,128]{1,0:T(8,128)(2,1)S(1)}, bf16[640,128]{1,0:T(8,128)(2,1)S(1)}, u32[]{:S(2)}, u32[]{:S(2)}) collective-permute-start(bf16[640,128]{1,0:T(8,128)(2,1)S(1)} %get-tuple-element.59), channel_id=1, source_target_pairs={{0,16},{2,18},{4,20},{6,22},{8,24},{10,26},{12,28},{14,30},{16,0},... | collective-permute-start | bytes 491528 | tf_op jit(solution)/shard_map/ppermute | solution.py:54
  323.8 14.5 %collective-permute-start.28 = (bf16[640,128]{1,0:T(8,128)(2,1)S(1)}, bf16[640,128]{1,0:T(8,128)(2,1)S(1)}, u32[]{:S(2)}, u32[]{:S(2)}) collective-permute-start(bf16[640,128]{1,0:T(8,128)(2,1)S(1)} %get-tuple-element.57), channel_id=1, source_target_pairs={{0,8},{2,10},{4,12},{6,14},{8,16},{10,18},{12,20},{14,22},{16,24},... | collective-permute-start | bytes 491528 | tf_op jit(solution)/shard_map/ppermute | solution.py:54
  332.9 12.1 %collective-permute-start.12 = (bf16[256,640]{1,0:T(8,128)(2,1)S(1)}, bf16[256,640]{1,0:T(8,128)(2,1)S(1)}, u32[]{:S(2)}, u32[]{:S(2)}) collective-permute-start(bf16[256,640]{1,0:T(8,128)(2,1)S(1)} %get-tuple-element.42), channel_id=1, source_target_pairs={{1,0},{2,1},{3,2},{4,3},{5,4},{6,5},{7,6},{8,7},{9,8},{10,9},{11,1... | collective-permute-start | bytes 983048 | tf_op jit(solution)/shard_map/ppermute | solution.py:137
  337.7 19.6 %collective-permute-start.46 = (bf16[2,4,320,128]{3,2,1,0:T(8,128)(2,1)S(1)}, bf16[2,4,320,128]{3,2,1,0:T(8,128)(2,1)S(1)}, u32[]{:S(2)}, u32[]{:S(2)}) collective-permute-start(bf16[2,4,320,128]{3,2,1,0:T(8,128)(2,1)S(1)} %maximum_select_fusion.18), channel_id=1, source_target_pairs={{0,2},{2,0},{4,6},{6,4},{8,10},{10,8},{12,14},{14,12},{16,18},{18,... | collective-permute-start | bytes 1966088 | tf_op jit(solution)/shard_map/ppermute | solution.py:48
  337.8 23.8 %collective-permute-start.24 = (bf16[2,4,416,128]{3,2,1,0:T(8,128)(2,1)S(1)}, bf16[2,4,416,128]{3,2,1,0:T(8,128)(2,1)S(1)}, u32[]{:S(2)}, u32[]{:S(2)}) collective-permute-start(bf16[2,4,416,128]{3,2,1,0:T(8,128)(2,1)S(1)} %maximum_select_fusion.15), channel_id=1, source_target_pairs={{0,2},{2,0},{4,6},{6,4},{8,10},{10,8},{12,14},{14,12},{16,18},{18,... | collective-permute-start | bytes 2555912 | tf_op jit(solution)/shard_map/ppermute | solution.py:48
  338.3 9.2 %collective-permute-start.33 = (bf16[640,128]{1,0:T(8,128)(2,1)S(1)}, bf16[640,128]{1,0:T(8,128)(2,1)S(1)}, u32[]{:S(2)}, u32[]{:S(2)}) collective-permute-start(bf16[640,128]{1,0:T(8,128)(2,1)S(1)} %fusion.92), channel_id=1, source_target_pairs={{0,24},{2,26},{4,28},{6,30},{8,0},{10,2},{12,4},{14,6},{16,8},{18,... | collective-permute-start | bytes 491528 | tf_op jit(solution)/shard_map/ppermute | solution.py:54
  340.8 15.1 %collective-permute-start.32 = (bf16[640,128]{1,0:T(8,128)(2,1)S(1)}, bf16[640,128]{1,0:T(8,128)(2,1)S(1)}, u32[]{:S(2)}, u32[]{:S(2)}) collective-permute-start(bf16[640,128]{1,0:T(8,128)(2,1)S(1)} %fusion.92), channel_id=1, source_target_pairs={{0,16},{2,18},{4,20},{6,22},{8,24},{10,26},{12,28},{14,30},{16,0},... | collective-permute-start | bytes 491528 | tf_op jit(solution)/shard_map/ppermute | solution.py:54
  345.0 10.8 %collective-permute-start.31 = (bf16[640,128]{1,0:T(8,128)(2,1)S(1)}, bf16[640,128]{1,0:T(8,128)(2,1)S(1)}, u32[]{:S(2)}, u32[]{:S(2)}) collective-permute-start(bf16[640,128]{1,0:T(8,128)(2,1)S(1)} %fusion.92), channel_id=1, source_target_pairs={{0,8},{2,10},{4,12},{6,14},{8,16},{10,18},{12,20},{14,22},{16,24},... | collective-permute-start | bytes 491528 | tf_op jit(solution)/shard_map/ppermute | solution.py:54
  357.0 12.9 %collective-permute-start.34 = (bf16[4,640,128]{2,1,0:T(8,128)(2,1)}, bf16[4,640,128]{2,1,0:T(8,128)(2,1)}, u32[]{:S(2)}, u32[]{:S(2)}) collective-permute-start(bf16[4,640,128]{2,1,0:T(8,128)(2,1)} %get-tuple-element.52), channel_id=1, source_target_pairs={{0,4},{2,6},{4,0},{6,2},{8,12},{10,14},{12,8},{14,10},{16,20},{18,... | collective-permute-start | bytes 1966088 | tf_op jit(solution)/shard_map/ppermute | solution.py:51
  372.5 17.4 %collective-permute-start.35 = (bf16[2,4,640,128]{3,2,1,0:T(8,128)(2,1)}, bf16[2,4,640,128]{3,2,1,0:T(8,128)(2,1)}, u32[]{:S(2)}, u32[]{:S(2)}) collective-permute-start(bf16[2,4,640,128]{3,2,1,0:T(8,128)(2,1)} %maximum_select_fusion.11), channel_id=1, source_target_pairs={{0,2},{2,0},{4,6},{6,4},{8,10},{10,8},{12,14},{14,12},{16,18},{18,... | collective-permute-start | bytes 3932168 | tf_op jit(solution)/shard_map/ppermute | solution.py:48
  (92 other events, 622.2 us)

commit v2 on v1

v2 whole, which is shorter than its diff:
```python
import functools
import math

import jax
import jax.numpy as jnp
from jax import lax
from jax.experimental import pallas as pl
from jax.experimental.pallas import tpu as pltpu
from jax.sharding import PartitionSpec as P

WINDOW = 512
EPSILON = 1e-06
ROPE_BASE = 10000.0
MASKED = -1e30
BF16 = jnp.bfloat16
F32 = jnp.float32
QBLOCK = 128
GELU_A = math.sqrt(2.0 / math.pi)
GELU_B = 0.044715

VMEM = pl.BlockSpec(memory_space=pltpu.VMEM)
SMEM = pl.BlockSpec(memory_space=pltpu.SMEM)
ANY = pl.BlockSpec(memory_space=pl.ANY)


class Places:
    def __init__(self):
        self.seq = lax.axis_size("seq")
        self.fsdp = lax.axis_size("fsdp")
        self.outer = self.seq // 4
        index = lax.axis_index("seq")
        self.core_at = index % 2
        self.mid_at = (index // 2) % 2
        self.outer_at = index // 4
        self.fsdp_at = lax.axis_index("fsdp")
        self.vector = jnp.stack([self.core_at, self.mid_at, self.fsdp_at]).astype(jnp.int32)

    def core_swap(self, array):
        return lax.ppermute(array, "seq", [(i, i ^ 1) for i in range(self.seq)])

    def mid_swap(self, array):
        return lax.ppermute(array, "seq", [(i, i ^ 2) for i in range(self.seq)])

    def outer_shift(self, array, by):
        return lax.ppermute(array, "seq", [(i, (i + 4 * by) % self.seq) for i in range(self.seq)])

    def fsdp_shift(self, array, by):
        return lax.ppermute(array, "fsdp", [(i, (i + by) % self.fsdp) for i in range(self.fsdp)])


def linear_shift(array, by):
    count = lax.axis_size("seq") * lax.axis_size("fsdp")
    return lax.ppermute(array, ("seq", "fsdp"), [(i, i + by) for i in range(count) if 0 <= i + by < count])


def pick(array, at):
    return lax.dynamic_index_in_dim(array, at, 0, keepdims=False)


def ordered(pieces, at):
    count = len(pieces)
    if count == 2:
        own, other = pieces
        return jnp.where(at == 0, jnp.stack([own, other]), jnp.stack([other, own]))
    stacked = jnp.stack(pieces)
    return jnp.stack([pick(stacked, (at - j) % count) for j in range(count)])


def fetch(here, shard, axis):
    half = shard.shape[axis] // 2
    part = lax.dynamic_slice_in_dim(shard, here.core_at * half, half, axis)
    pieces = [shard]
    for by in range(1, here.fsdp):
        mine = here.fsdp_shift(part, by)
        pieces += [mine, here.core_swap(mine)]
    return pieces


def multiple(value, of):
    return pl.multiple_of(value, of)


def place_copies(pieces, whole, sems, at, axis):
    core, fsdp = at[0], at[2]
    count = (len(pieces) + 1) // 2
    rows, columns = pieces[0].shape
    copies = []
    for k, piece in enumerate(pieces):
        by = (k + 1) // 2
        row = multiple(lax.rem(fsdp + (count - by), count) * rows, 16)
        if k == 0:
            target = whole.at[pl.ds(row, rows), :]
        else:
            half = core if k % 2 == 1 else 1 - core
            if axis == 0:
                target = whole.at[pl.ds(multiple(row + half * (rows // 2), 16), rows // 2), :]
            else:
                target = whole.at[pl.ds(row, rows), pl.ds(multiple(half * (columns // 2), 128), columns // 2)]
        copies.append(pltpu.make_async_copy(piece, target, sems.at[k]))
    return copies


def dot(a, b):
    return lax.dot_general(a, b, (((1,), (0,)), ((), ())), preferred_element_type=F32)


def dot_nt(a, b):
    return lax.dot_general(a, b, (((1,), (1,)), ((), ())), preferred_element_type=F32)


def dot_tn(a, b):
    return lax.dot_general(a, b, (((0,), (0,)), ((), ())), preferred_element_type=F32)


def inverse_rms(u):
    return lax.rsqrt(jnp.mean(u * u, axis=-1, keepdims=True) + EPSILON)


def norm_back(u, g, dz):
    r = inverse_rms(u)
    ur = u * r
    gdz = g * dz
    du = r * (gdz - ur * jnp.mean(gdz * ur, axis=-1, keepdims=True))
    return du, jnp.sum(dz * ur, axis=0, keepdims=True)


def params(megabytes=56):
    return pltpu.CompilerParams(vmem_limit_bytes=megabytes * 1024 * 1024)


def cost(flops, bytes_accessed):
    return pl.CostEstimate(flops=int(flops), bytes_accessed=int(bytes_accessed), transcendentals=0)


def shape(dims, kind):
    return jax.ShapeDtypeStruct(tuple(dims), kind)


def attend_kernel(n_tok, n_qkv, heads, *refs):
    at = refs[0]
    toks = refs[1 : 1 + n_tok]
    pos, cosine, sine, gain_in, gain_q, gain_k = refs[1 + n_tok : 7 + n_tok]
    qkv = refs[7 + n_tok : 7 + n_tok + n_qkv]
    normed, q_raw, k_raw, q_st, keys, values, probs, attended, w_full, sems = refs[7 + n_tok + n_qkv :]
    copies = place_copies(qkv, w_full, sems, at, 1)
    for copy in copies:
        copy.start()
    rows = toks[0].shape[0]
    dim = keys.shape[1]
    half = dim // 2
    halo = (n_tok - 1) * rows
    gain = gain_in[...]
    for i, tok in enumerate(toks):
        u = tok[...].astype(F32)
        normed[i * rows : (i + 1) * rows, :] = (u * inverse_rms(u) * gain).astype(BF16)
    for copy in copies:
        copy.wait()

    def turned(u, g, cos, sin):
        u = u * inverse_rms(u) * g
        first, second = u[:, :half], u[:, half:]
        return (first * cos - second * sin).astype(BF16), (second * cos + first * sin).astype(BF16)

    for i in range(n_tok):
        here = slice(i * rows, (i + 1) * rows)
        kv = dot(normed[here, :], w_full[:, heads * dim :])
        k_raw[here, :] = kv[:, :dim]
        values[here, :] = kv[:, dim:].astype(BF16)
        first, second = turned(kv[:, :dim], gain_k[...], cosine[here, :], sine[here, :])
        keys[here, :half] = first
        keys[here, half:] = second
    blocks = rows // QBLOCK
    for h in range(heads):
        u = dot(normed[halo:, :], w_full[:, h * dim : (h + 1) * dim])
        q_raw[:, h * dim : (h + 1) * dim] = u
        first, second = turned(u, gain_q[...], cosine[halo:, :], sine[halo:, :])
        for b in range(blocks):
            start = (b * heads + h) * QBLOCK
            q_st[start : start + QBLOCK, :half] = first[b * QBLOCK : (b + 1) * QBLOCK, :]
            q_st[start : start + QBLOCK, half:] = second[b * QBLOCK : (b + 1) * QBLOCK, :]
    span = WINDOW + QBLOCK
    distance = (
        lax.broadcasted_iota(jnp.int32, (QBLOCK, span), 0)
        + WINDOW
        - lax.broadcasted_iota(jnp.int32, (QBLOCK, span), 1)
    )
    scale = dim ** (-0.5)
    for b in range(blocks):
        first_key = halo - WINDOW + b * QBLOCK
        limit = jnp.minimum(pos[b * QBLOCK : (b + 1) * QBLOCK, :], WINDOW - 1)
        allowed = (distance >= 0) & (distance <= limit)
        for h in range(heads):
            start = (b * heads + h) * QBLOCK
            scores = dot_nt(q_st[start : start + QBLOCK, :], keys[first_key : first_key + span, :]) * scale
            scores = jnp.where(allowed, scores, MASKED)
            weights = jnp.exp(scores - jnp.max(scores, axis=-1, keepdims=True))
            weights = (weights * (1.0 / jnp.sum(weights, axis=-1, keepdims=True))).astype(BF16)
            probs[start : start + QBLOCK, :] = weights
            attended[b * QBLOCK : (b + 1) * QBLOCK, h * dim : (h + 1) * dim] = dot(
                weights, values[first_key : first_key + span, :]
            ).astype(BF16)


def gate_kernel(n_out, n_gate, n_up, *refs):
    at, attended, tokens, gain_attn, gain_ffn = refs[:5]
    refs = refs[5:]
    out_w, gate_w, up_w, refs = (
        refs[:n_out],
        refs[n_out : n_out + n_gate],
        refs[n_out + n_gate : n_out + n_gate + n_up],
        refs[n_out + n_gate + n_up :],
    )
    projected_ref, residual_ref, ffn_in_ref, mixed, gelu_out, gate_slope = refs[:6]
    out_full, gate_full, up_full, out_sems, gate_sems, up_sems = refs[6:]
    groups = (
        place_copies(out_w, out_full, out_sems, at, 0),
        place_copies(gate_w, gate_full, gate_sems, at, 1),
        place_copies(up_w, up_full, up_sems, at, 1),
    )
    for group in groups:
        for copy in group:
            copy.start()
    for copy in groups[0]:
        copy.wait()
    projected = dot(attended[...], out_full[...])
    projected_ref[...] = projected
    residual = tokens[...].astype(F32) + projected * inverse_rms(projected) * gain_attn[...]
    residual_ref[...] = residual
    ffn_in_ref[...] = (residual * inverse_rms(residual) * gain_ffn[...]).astype(BF16)
    for group in groups[1:]:
        for copy in group:
            copy.wait()
    width = 256

    def step(i, _):
        cut = pl.ds(multiple(i * width, width), width)
        gate = dot(ffn_in_ref[...], gate_full[:, cut])
        up = dot(ffn_in_ref[...], up_full[:, cut])
        square = gate * gate
        t = jnp.tanh(GELU_A * gate * (1.0 + GELU_B * square))
        cdf = 0.5 * (1.0 + t)
        act = gate * cdf
        slope = cdf + 0.5 * gate * (1.0 - t * t) * (GELU_A * (1.0 + 3.0 * GELU_B * square))
        mixed[:, cut] = (act * up).astype(BF16)
        gelu_out[:, cut] = act.astype(BF16)
        gate_slope[:, cut] = (up * slope).astype(BF16)
        return 0

    lax.fori_loop(0, gate_full.shape[1] // width, step, 0)


def relative_blocks(at, fsdp):
    for c in range(2):
        core = c + at[0] - 2 * c * at[0]
        for f in range(fsdp):
            row = lax.rem(at[2] + f, fsdp)
            for x in range(2):
                mid = x + at[1] - 2 * x * at[1]
                yield c, f, x, core, row, mid


def down_kernel(n_down, fsdp, *refs):
    at, mixed, residual, cotangent, gain_out = refs[:5]
    down_w = refs[5 : 5 + n_down]
    layer_out, d_down, grad_gain, keep, send = refs[5 + n_down : 10 + n_down]
    down_full, mixed_t, sems = refs[10 + n_down :]
    copies = place_copies(down_w, down_full, sems, at, 0)
    for copy in copies:
        copy.start()
    mixed_t[...] = mixed[...].T
    for copy in copies:
        copy.wait()
    down = dot(mixed[...], down_full[...])
    r = inverse_rms(down)
    gain = gain_out[...]
    layer_out[...] = (residual[...] + down * r * gain).astype(BF16)
    du, dg = norm_back(down, gain, cotangent[...].astype(F32))
    grad_gain[...] = dg
    d_down[...] = du.astype(BF16)
    block = keep.shape[2]
    for c, f, x, core, row, mid in relative_blocks(at, fsdp):
        start = multiple(((row * 2 + core) * 2 + mid) * block, 16)
        target = keep if c == 0 else send
        target[f, x] = dot(mixed_t[pl.ds(start, block), :], d_down[...]).astype(BF16)


def gate_back_kernel(n_down, fsdp, *refs):
    at, d_down, gelu_out, gate_slope, ffn_in = refs[:5]
    down_w = refs[5 : 5 + n_down]
    d_gate, d_up, keep, send = refs[5 + n_down : 9 + n_down]
    down_full, ffn_t, sems = refs[9 + n_down :]
    copies = place_copies(down_w, down_full, sems, at, 0)
    for copy in copies:
        copy.start()
    ffn_t[...] = ffn_in[...].T
    for copy in copies:
        copy.wait()
    width = 256

    def step(i, _):
        cut = pl.ds(multiple(i * width, width), width)
        d_mixed = dot_nt(d_down[...], down_full[cut, :])
        d_gate[:, cut] = (d_mixed * gate_slope[:, cut].astype(F32)).astype(BF16)
        d_up[:, cut] = (d_mixed * gelu_out[:, cut].astype(F32)).astype(BF16)
        return 0

    lax.fori_loop(0, d_gate.shape[1] // width, step, 0)
    tall, wide = keep.shape[2] // 2, keep.shape[3]
    for c, f, x, core, row, mid in relative_blocks(at, fsdp):
        cut = pl.ds(multiple((core * 2 + mid) * wide, 128), wide)
        left = ffn_t[pl.ds(multiple(row * tall, 16), tall), :]
        target = keep if c == 0 else send
        target[f, x, :tall, :] = dot(left, d_gate[:, cut]).astype(BF16)
        target[f, x, tall:, :] = dot(left, d_up[:, cut]).astype(BF16)


def last_kernel(n_out, n_gate, n_up, n_qkv, n_tok, fsdp, heads, *refs):
    (
        at, d_gate, d_up, residual, projected, cotangent, gain_ffn, gain_attn, attended,
        q_raw, k_raw, q_st, keys, values, probs, cosine, sine, gain_q, gain_k, gain_in, normed,
    ) = refs[:21]
    toks = refs[21 : 21 + n_tok]
    refs = refs[21 + n_tok :]
    out_w, gate_w, up_w, qkv_w, refs = (
        refs[:n_out],
        refs[n_out : n_out + n_gate],
        refs[n_out + n_gate : n_out + n_gate + n_up],
        refs[n_out + n_gate + n_up : n_out + n_gate + n_up + n_qkv],
        refs[n_out + n_gate + n_up + n_qkv :],
    )
    grad_tokens, d_halo, g_ffn, g_attn, g_q, g_k, g_in, keep, send = refs[:9]
    (
        out_full, gate_full, up_full, w_full, att_t, normed_t, d_att, d_scores, d_q, d_k, d_v, d_qkv,
        out_sems, gate_sems, up_sems, qkv_sems,
    ) = refs[9:]
    groups = (
        place_copies(gate_w, gate_full, gate_sems, at, 1),
        place_copies(up_w, up_full, up_sems, at, 1),
        place_copies(out_w, out_full, out_sems, at, 0),
        place_copies(qkv_w, w_full, qkv_sems, at, 1),
    )
    for group in groups:
        for copy in group:
            copy.start()
    att_t[...] = attended[...].T
    normed_t[...] = normed[...].T
    for copy in groups[0] + groups[1]:
        copy.wait()
    d_ffn_in = dot_nt(d_gate[...], gate_full[...]) + dot_nt(d_up[...], up_full[...])
    du, dg = norm_back(residual[...], gain_ffn[...], d_ffn_in)
    g_ffn[...] = dg
    d_residual = cotangent[...].astype(F32) + du
    grad_tokens[...] = d_residual
    du, dg = norm_back(projected[...], gain_attn[...], d_residual)
    g_attn[...] = dg
    d_proj = du.astype(BF16)
    rows = toks[0].shape[0]
    halo = (n_tok - 1) * rows
    dim = keys.shape[1]
    half = dim // 2
    blocks = rows // QBLOCK
    span = WINDOW + QBLOCK
    for copy in groups[2]:
        copy.wait()
    for h in range(heads):
        part = dot_nt(d_proj, out_full[h * dim : (h + 1) * dim, :]).astype(BF16)
        for b in range(blocks):
            start = (b * heads + h) * QBLOCK
            d_att[start : start + QBLOCK, :] = part[b * QBLOCK : (b + 1) * QBLOCK, :]
    out_block = att_t.shape[0] // (4 * fsdp)
    tall, wide = normed_t.shape[0] // fsdp, keep.shape[3]
    columns = d_proj.shape[1]
    for c, f, x, core, row, mid in relative_blocks(at, fsdp):
        start = multiple(((row * 2 + core) * 2 + mid) * out_block, 16)
        part = dot(att_t[pl.ds(start, out_block), :], d_proj).astype(BF16)
        target = keep if c == 0 else send
        target[f, x, tall : tall + out_block, :] = part[:, :wide]
        target[f, x, tall + out_block :, : columns - wide] = part[:, wide:]
        target[f, x, tall + out_block :, columns - wide :] = jnp.zeros((out_block, 2 * wide - columns), BF16)
    scale = dim ** (-0.5)
    d_k[...] = jnp.zeros(d_k.shape, F32)
    d_v[...] = jnp.zeros(d_v.shape, F32)
    for b in range(blocks):
        first_key = halo - WINDOW + b * QBLOCK
        here = slice(first_key, first_key + span)
        for h in range(heads):
            start = (b * heads + h) * QBLOCK
            stack = slice(start, start + QBLOCK)
            d_probs = dot_nt(d_att[stack, :], values[here, :])
            p = probs[stack, :].astype(F32)
            row_terms = jnp.sum(p * d_probs, axis=-1, keepdims=True)
            ds = (p * (d_probs - row_terms) * scale).astype(BF16)
            d_scores[h * QBLOCK : (h + 1) * QBLOCK, :] = ds
            d_q[b * QBLOCK : (b + 1) * QBLOCK, h * dim : (h + 1) * dim] = dot(ds, keys[here, :])
        stack = slice(b * heads * QBLOCK, (b + 1) * heads * QBLOCK)
        d_k[here, :] += dot_tn(d_scores[...], q_st[stack, :])
        d_v[here, :] += dot_tn(probs[stack, :], d_att[stack, :])

    def turned_back(u, g, dz, cos, sin):
        first, second = dz[:, :half], dz[:, half:]
        dz = jnp.concatenate([first * cos + second * sin, second * cos - first * sin], axis=1)
        return norm_back(u, g, dz)

    total_q = jnp.zeros((1, dim), F32)
    if halo:
        d_qkv[:halo, : heads * dim] = jnp.zeros((halo, heads * dim), BF16)
    for h in range(heads):
        cut = slice(h * dim, (h + 1) * dim)
        du, dg = turned_back(q_raw[:, cut], gain_q[...], d_q[:, cut], cosine[halo:, :], sine[halo:, :])
        total_q += dg
        d_qkv[halo:, cut] = du.astype(BF16)
    g_q[...] = total_q
    total_k = jnp.zeros((1, dim), F32)
    for i in range(n_tok):
        here = slice(i * rows, (i + 1) * rows)
        du, dg = turned_back(k_raw[here, :], gain_k[...], d_k[here, :], cosine[here, :], sine[here, :])
        total_k += dg
        d_qkv[here, heads * dim : (heads + 1) * dim] = du.astype(BF16)
        d_qkv[here, (heads + 1) * dim :] = d_v[here, :].astype(BF16)
    g_k[...] = total_k
    for c, f, x, core, row, mid in relative_blocks(at, fsdp):
        cut = pl.ds(multiple((core * 2 + mid) * wide, 128), wide)
        left = normed_t[pl.ds(multiple(row * tall, 16), tall), :]
        target = keep if c == 0 else send
        target[f, x, :tall, :] = dot(left, d_qkv[:, cut]).astype(BF16)
    for copy in groups[3]:
        copy.wait()
    total_in = jnp.zeros(g_in.shape, F32)
    for i in range(n_tok):
        here = slice(i * rows, (i + 1) * rows)
        if i < n_tok - 1:
            d_normed = dot_nt(d_qkv[here, heads * dim :], w_full[:, heads * dim :])
        else:
            d_normed = dot_nt(d_qkv[here, :], w_full[...])
        du, dg = norm_back(toks[i][...].astype(F32), gain_in[...], d_normed)
        total_in += dg
        if i < n_tok - 1:
            d_halo[here, :] = du.astype(BF16)
        else:
            grad_tokens[...] += du
    g_in[...] = total_in


def add(*terms):
    out = terms[0].astype(F32)
    for term in terms[1:]:
        out = out + term.astype(F32)
    return out


def reduce_chunk(here, keep, send):
    other = here.core_swap(send)
    n, w = keep.shape[2:]
    arrived = []
    for by in range(1, here.fsdp):
        arrived.append(here.fsdp_shift(add(keep[by], other[by]).astype(BF16), by))
    across = here.mid_swap(add(keep[0, 1], other[0, 1], *[a[1] for a in arrived]).astype(BF16))
    mine = add(keep[0, 0], other[0, 0], *[a[0] for a in arrived], across).astype(BF16)
    mine = mine.reshape(here.outer, n // here.outer, w)
    terms = [pick(mine, here.outer_at)]
    for by in range(1, here.outer):
        terms.append(here.outer_shift(pick(mine, (here.outer_at + by) % here.outer), by))
    own = add(*terms).astype(BF16)
    block = ordered([own] + [here.outer_shift(own, by) for by in range(1, here.outer)], here.outer_at).reshape(n, w)
    across = here.mid_swap(block)
    return [[block, across], [here.core_swap(block), here.core_swap(across)]]


def by_place(here, blocks):
    own = [jnp.where(here.mid_at == 0, a, b) for a, b in blocks]
    other = [jnp.where(here.mid_at == 0, b, a) for a, b in blocks]
    pairs = list(zip(own, other))
    first = [jnp.where(here.core_at == 0, a, b) for a, b in zip(pairs[0], pairs[1])]
    second = [jnp.where(here.core_at == 0, b, a) for a, b in zip(pairs[0], pairs[1])]
    return first + second


def on_device(
    tokens, positions, cotangent, in_gain, w_query, w_key, w_value, query_gain, key_gain, w_out, attn_gain,
    ffn_gain_in, w_gate, w_up, w_down, ffn_gain_out,
):
    here = Places()
    fsdp = here.fsdp
    rows, width = tokens.shape
    dim = w_key.shape[1]
    query_cols = w_query.shape[1]
    heads = query_cols // dim
    hidden = w_gate.shape[1]
    hops = (WINDOW + rows - 1) // rows
    n_tok = hops + 1
    halo = hops * rows
    every = halo + rows
    at = here.vector

    gains = (in_gain, query_gain, key_gain, attn_gain, ffn_gain_in, ffn_gain_out)
    cuts = [0]
    for gain in gains:
        cuts.append(cuts[-1] + gain.shape[0])
    gain_row = jnp.concatenate(gains)
    qkv_w = fetch(here, jnp.concatenate([w_query, w_key, w_value], axis=1), 1)
    gain_rows = ordered([gain_row] + [here.fsdp_shift(gain_row, by) for by in range(1, fsdp)], here.fsdp_at)
    gain_rows = gain_rows.astype(F32)
    gain_in, gain_q, gain_k, gain_attn, gain_ffn, gain_out = (
        gain_rows[:, cuts[i] : cuts[i + 1]].reshape(1, -1) for i in range(6)
    )
    toks = [linear_shift(tokens, by) for by in range(hops, 0, -1)] + [tokens]
    out_w = fetch(here, w_out, 0)
    gate_w = fetch(here, w_gate, 1)
    up_w = fetch(here, w_up, 1)
    down_w = fetch(here, w_down, 0)

    all_positions = jnp.concatenate([positions[0] - halo + jnp.arange(halo, dtype=jnp.int32), positions])
    frequency = ROPE_BASE ** (-(jnp.arange(dim // 2, dtype=F32) * 2.0 / dim))
    angles = all_positions.astype(F32)[:, None] * frequency[None, :]
    cosine, sine = jnp.cos(angles), jnp.sin(angles)

    span = WINDOW + QBLOCK
    weight_bytes = 2 * fsdp * w_gate.size
    normed, q_raw, k_raw, q_st, keys, values, probs, attended = pl.pallas_call(
        functools.partial(attend_kernel, n_tok, len(qkv_w), heads),
        out_shape=(
            shape((every, width), BF16),
            shape((rows, query_cols), F32),
            shape((every, dim), F32),
            shape((heads * rows, dim), BF16),
            shape((every, dim), BF16),
            shape((every, dim), BF16),
            shape((heads * rows, span), BF16),
            shape((rows, query_cols), BF16),
        ),
        in_specs=[SMEM] + [VMEM] * (n_tok + 6) + [ANY] * len(qkv_w),
        out_specs=(VMEM,) * 8,
        scratch_shapes=[
            pltpu.VMEM((width, query_cols + 2 * dim), BF16),
            pltpu.SemaphoreType.DMA((len(qkv_w),)),
        ],
        compiler_params=params(),
        cost_estimate=cost(4e9, 1e7),
        name="attend",
    )(at, *toks, positions[:, None], cosine, sine, gain_in, gain_q, gain_k, *qkv_w)

    projected, residual, ffn_in, mixed, gelu_out, gate_slope = pl.pallas_call(
        functools.partial(gate_kernel, len(out_w), len(gate_w), len(up_w)),
        out_shape=(
            shape((rows, width), F32),
            shape((rows, width), F32),
            shape((rows, width), BF16),
            shape((rows, hidden), BF16),
            shape((rows, hidden), BF16),
            shape((rows, hidden), BF16),
        ),
        in_specs=[SMEM] + [VMEM] * 4 + [ANY] * (len(out_w) + len(gate_w) + len(up_w)),
        out_specs=(VMEM,) * 6,
        scratch_shapes=[
            pltpu.VMEM((query_cols, width), BF16),
            pltpu.VMEM((width, hidden), BF16),
            pltpu.VMEM((width, hidden), BF16),
            pltpu.SemaphoreType.DMA((len(out_w),)),
            pltpu.SemaphoreType.DMA((len(gate_w),)),
            pltpu.SemaphoreType.DMA((len(up_w),)),
        ],
        compiler_params=params(),
        cost_estimate=cost(4e9, 2 * weight_bytes),
        name="gate",
    )(at, attended, tokens, gain_attn, gain_ffn, *out_w, *gate_w, *up_w)

    down_block = w_down.shape[0] // 4
    down_shape = shape((fsdp, 2, down_block, width), BF16)
    layer_out, d_down, g_ffn_out, down_keep, down_send = pl.pallas_call(
        functools.partial(down_kernel, len(down_w), fsdp),
        out_shape=(
            shape((rows, width), BF16),
            shape((rows, width), BF16),
            shape((1, width), F32),
            down_shape,
            down_shape,
        ),
        in_specs=[SMEM] + [VMEM] * 4 + [ANY] * len(down_w),
        out_specs=(VMEM,) * 5,
        scratch_shapes=[
            pltpu.VMEM((hidden, width), BF16),
            pltpu.VMEM((hidden, rows), BF16),
            pltpu.SemaphoreType.DMA((len(down_w),)),
        ],
        compiler_params=params(),
        cost_estimate=cost(4e9, 2 * weight_bytes),
        name="down",
    )(at, mixed, residual, cotangent, gain_out, *down_w)

    gate_shape = shape((fsdp, 2, 2 * w_gate.shape[0], hidden // 4), BF16)
    d_gate, d_up, gate_keep, gate_send = pl.pallas_call(
        functools.partial(gate_back_kernel, len(down_w), fsdp),
        out_shape=(
            shape((rows, hidden), BF16),
            shape((rows, hidden), BF16),
            gate_shape,
            gate_shape,
        ),
        in_specs=[SMEM] + [VMEM] * 4 + [ANY] * len(down_w),
        out_specs=(VMEM,) * 4,
        scratch_shapes=[
            pltpu.VMEM((hidden, width), BF16),
            pltpu.VMEM((width, rows), BF16),
            pltpu.SemaphoreType.DMA((len(down_w),)),
        ],
        compiler_params=params(),
        cost_estimate=cost(6e9, 3 * weight_bytes),
        name="gate_back",
    )(at, d_down, gelu_out, gate_slope, ffn_in, *down_w)

    qkv_cols = query_cols + 2 * dim
    last_wide = qkv_cols // 4
    shard_rows = w_query.shape[0]
    out_block = w_out.shape[0] // 4
    last_shape = shape((fsdp, 2, shard_rows + 2 * out_block, last_wide), BF16)
    grad_tokens, d_halo, g_ffn, g_attn, g_q, g_k, g_in, last_keep, last_send = pl.pallas_call(
        functools.partial(
            last_kernel, len(out_w), len(gate_w), len(up_w), len(qkv_w), n_tok, fsdp, heads
        ),
        out_shape=(
            shape((rows, width), F32),
            shape((halo, width), BF16),
            shape((1, width), F32),
            shape((1, width), F32),
            shape((1, dim), F32),
            shape((1, dim), F32),
            shape((1, width), F32),
            last_shape,
            last_shape,
        ),
        in_specs=[SMEM]
        + [VMEM] * (20 + n_tok)
        + [ANY] * (len(out_w) + len(gate_w) + len(up_w) + len(qkv_w)),
        out_specs=(VMEM,) * 9,
        scratch_shapes=[
            pltpu.VMEM((query_cols, width), BF16),
            pltpu.VMEM((width, hidden), BF16),
            pltpu.VMEM((width, hidden), BF16),
            pltpu.VMEM((width, qkv_cols), BF16),
            pltpu.VMEM((query_cols, rows), BF16),
            pltpu.VMEM((width, every), BF16),
            pltpu.VMEM((heads * rows, dim), BF16),
            pltpu.VMEM((heads * QBLOCK, span), BF16),
            pltpu.VMEM((rows, query_cols), F32),
            pltpu.VMEM((every, dim), F32),
            pltpu.VMEM((every, dim), F32),
            pltpu.VMEM((every, qkv_cols), BF16),
            pltpu.SemaphoreType.DMA((len(out_w),)),
            pltpu.SemaphoreType.DMA((len(gate_w),)),
            pltpu.SemaphoreType.DMA((len(up_w),)),
            pltpu.SemaphoreType.DMA((len(qkv_w),)),
        ],
        compiler_params=params(),
        cost_estimate=cost(15e9, 4 * weight_bytes),
        name="last",
    )(
        at, d_gate, d_up, residual, projected, cotangent, gain_ffn, gain_attn, attended,
        q_raw, k_raw, q_st, keys, values, probs, cosine, sine, gain_q, gain_k, gain_in, normed,
        *toks, *out_w, *gate_w, *up_w, *qkv_w,
    )

    gain_grads = (g_in, g_q, g_k, g_attn, g_ffn, g_ffn_out)
    packed = jnp.concatenate([g.reshape(fsdp, -1) for g in gain_grads], axis=1).astype(BF16)
    corner = 2 * last_wide - width
    per_block = cuts[-1] // 4
    deep = -(-per_block // corner)
    packed = jnp.pad(packed.reshape(fsdp, 4, per_block), ((0, 0), (0, 0), (0, deep * corner - per_block)))
    packed = packed.reshape(fsdp, 2, 2, deep, corner)
    packed = jnp.stack([pick(packed, (here.fsdp_at + f) % fsdp) for f in range(fsdp)])
    packed = jnp.where(here.mid_at == 0, packed, packed[:, :, ::-1])
    corner_at = (0, 0, shard_rows + out_block, width - last_wide)
    last_keep = lax.dynamic_update_slice(last_keep, jnp.where(here.core_at == 0, packed[:, 0], packed[:, 1]), corner_at)
    last_send = lax.dynamic_update_slice(last_send, jnp.where(here.core_at == 0, packed[:, 1], packed[:, 0]), corner_at)

    down_blocks = by_place(here, reduce_chunk(here, down_keep, down_send))
    gate_blocks = by_place(here, reduce_chunk(here, gate_keep, gate_send))
    last_blocks = by_place(here, reduce_chunk(here, last_keep, last_send))

    for by in range(1, hops + 1):
        start = halo - by * rows
        grad_tokens = grad_tokens + linear_shift(d_halo[start : start + rows], -by).astype(F32)

    total_down = jnp.concatenate(down_blocks, axis=0).astype(F32)
    total_gate = jnp.concatenate([b[:shard_rows] for b in gate_blocks], axis=1).astype(F32)
    total_up = jnp.concatenate([b[shard_rows:] for b in gate_blocks], axis=1).astype(F32)
    total_qkv = jnp.concatenate([b[:shard_rows] for b in last_blocks], axis=1).astype(F32)
    middle = shard_rows + out_block
    total_out = jnp.concatenate(
        [jnp.concatenate([b[shard_rows:middle], b[middle:, : width - last_wide]], axis=1) for b in last_blocks],
        axis=0,
    ).astype(F32)
    total_gains = jnp.concatenate(
        [b[middle : middle + deep, width - last_wide :].reshape(-1)[:per_block] for b in last_blocks]
    ).astype(F32)
    g = [total_gains[cuts[i] : cuts[i + 1]] for i in range(6)]
    return (
        layer_out, grad_tokens, g[0],
        total_qkv[:, :query_cols],
        total_qkv[:, query_cols : query_cols + dim],
        total_qkv[:, query_cols + dim :],
        g[1], g[2], total_out, g[3], g[4], total_gate, total_up, total_down, g[5],
    )


def solution(mesh):
    tok = P(("seq", "fsdp"), None)
    mat = P("fsdp", None)
    vec = P("fsdp")
    return jax.shard_map(
        on_device,
        mesh=mesh,
        in_specs=(tok, P(("seq", "fsdp")), tok, vec, mat, mat, mat, vec, vec, mat, vec, vec, mat, mat, mat, vec),
        out_specs=(tok, tok, vec, mat, mat, mat, vec, vec, mat, vec, vec, mat, mat, mat, vec),
        check_vma=False,
    )
```

time: 409 us -> 328 us (0.80); the launches traced: 402 us -> 327 us
  local copies, waits for them, and re-layouts: 104 us -> 23.7 us
  Pallas kernels: 0 us -> 56.4 us
  matrix products: 48.4 us -> 0 us
  other arithmetic: 60.2 us -> 26.6 us
  waiting for transfers between devices: 129 us -> 146 us
  starting transfers between devices: 56.7 us -> 72.1 us
    pallas_call x0 -> x5, Pallas kernels: none -> 56.4 us  [the longest x1 20.8 us: on_device(): pl.pallas_call(functools.partial(last_kernel, len(out_w), len(gate_w), le...]
    dot_general x24 -> x0, matrix products: 48.4 us -> none  [the longest x1 7.09 us: on_device(): jnp.einsum('hqk,kd->qhd', d_scores, keys_all, preferred_element_type=F32)]
    ppermute x8 -> x9, waiting for transfers between devices: 79.2 us -> 31.5 us  [fsdp_shift(): lax.ppermute(array, 'fsdp', [(i, (i + by) % self.fsdp) for i in range(sel...]
    ppermute x4, waiting for transfers between devices: 4.12 us -> 33.3 us  [linear_shift(): lax.ppermute(array, ('seq', 'fsdp'), [(i, i + by) for i in range(count) i...]
    reshape x12, local copies, waits for them, and re-layouts: 28 us -> 3 us  [the longest x4 2.65 us: on_device(): gain_rows[:, cuts[i]:cuts[i + 1]].reshape(1, -1)]
    ppermute x18, waiting for transfers between devices: 20.7 us -> 40 us  [outer_shift(): lax.ppermute(array, 'seq', [(i, (i + 4 * by) % self.seq) for i in range(s...]
    convert_element_type x13 -> x1, local copies, waits for them, and re-layouts: 19.2 us -> 0.02 us  [on_device(): jnp.concatenate([g.reshape(fsdp, -1) for g in gain_grads], axis=1)]
    select_n x18 -> x5, other arithmetic: 19.1 us -> 0.78 us  [the longest x3 0.76 us: by_place(): jnp.where(here.core_at == 0, a, b)]
  transfers between devices with their start and end apart: 47 -> 51, of which waited for: 18 -> 22; matrix products, arithmetic and copies ran while one was open for 29% -> 12% of each run, Pallas kernels for 0% -> 6%
where the time goes in v2:
time: 328 us; the launch traced here: 327 us
  waiting for transfers between devices  146 us (45%)
  starting transfers between devices  72.1 us (22%)
  Pallas kernels  56.4 us (17%)
  other arithmetic  26.6 us (8%)
  local copies, waits for them, and re-layouts  23.7 us (7%)
    ppermute x6, waiting for transfers between devices, mid_swap(): return lax.ppermute(array, 'seq', [(i, i ^ 2) for i in range(self.seq)])  40.8 us
    ppermute x18, waiting for transfers between devices, outer_shift(): lax.ppermute(array, 'seq', [(i, (i + 4 * by) % self.seq) for i in range(s...  40 us
    ppermute x4, waiting for transfers between devices, linear_shift(): lax.ppermute(array, ('seq', 'fsdp'), [(i, i + by) for i in range(count) i...  33.3 us
    ppermute x9, waiting for transfers between devices, fsdp_shift(): lax.ppermute(array, 'fsdp', [(i, (i + by) % self.fsdp) for i in range(sel...  31.5 us
    ppermute x18, starting transfers between devices, outer_shift(): lax.ppermute(array, 'seq', [(i, (i + 4 * by) % self.seq) for i in range(s...  21.3 us
    pallas_call x1, Pallas kernels, on_device(): pl.pallas_call(functools.partial(last_kernel, len(out_w), len(gate_w), le...  20.8 us
    ppermute x4, starting transfers between devices, linear_shift(): lax.ppermute(array, ('seq', 'fsdp'), [(i, i + by) for i in range(count) i...  20.2 us
    ppermute x14, starting transfers between devices, core_swap(): return lax.ppermute(array, 'seq', [(i, i ^ 1) for i in range(self.seq)])  15.5 us
  transfers between devices with their start and end apart: 51, of which 22 were waited for; matrix products, arithmetic and copies ran while one was open for 12% of the time, Pallas kernels for 6%

profile of v2, /device:TPU:1, one launch (start us, length us, event | category | flops | bytes accessed | tf_op | source)
XLA Modules:
  0.0 326.7 jit_solution(16977159910112620673)
XLA Ops:
  0.7 4.6 %collective-permute-start = (bf16[256,640]{1,0:T(8,128)(2,1)}, bf16[256,640]{1,0:T(8,128)(2,1)}, u32[]{:S(2)}, u32[]{:S(2)}) collective-permute-start(bf16[256,640]{1,0:T(8,128)(2,1)} %refs_23_.1), channel_id=1, source_target_pairs={{0,2},{1,3},{2,4},{3,5},{4,6},{5,7},{6,8},{7,9},{8,10},{9,11},{10,... | collective-permute-start | bytes 983048 | tf_op jit(solution)/shard_map/ppermute | solution.py:53
  5.3 4.2 %concatenate.48 = bf16[1536]{0:T(1024)(128)(2,1)S(1)} concatenate(bf16[320]{0:T(512)(128)(2,1)} %param.19, bf16[128]{0:T(256)(128)(2,1)} %param.23, bf16[128]{0:T(256)(128)(2,1)} %param.24, bf16[320]{0:T(512)(128)(2,1)} %param.26, bf16[320]{0:T(512)(128)(2,1)} %param.27, bf16[320]{0:T(512)(128)(2,1)} %param.31), dimensions={0} | concatenate | bytes 6144 | tf_op jit(solution)/shard_map/concatenate | solution.py:499
  17.4 2.5 multiply_sine_fusion
  22.0 3.1 collective-permute-start.1
  27.0 33.3 %collective-permute-done.1.refs_2_.refs_22_ = bf16[256,640]{1,0:T(8,128)(2,1)S(1)} collective-permute-done((bf16[256,640]{1,0:T(8,128)(2,1)}, bf16[256,640]{1,0:T(8,128)(2,1)S(1)}, u32[]{:S(2)}, u32[]{:S(2)}) %collective-permute-start.1) | collective-permute-done | bytes 327712 | tf_op jit(solution)/shard_map/ppermute | solution.py:53
  64.5 14.7 %collective-permute-done.5.refs_6_.refs_25_ = bf16[256,640]{1,0:T(8,128)(2,1)} collective-permute-done((bf16[256,640]{1,0:T(8,128)(2,1)S(1)}, bf16[256,640]{1,0:T(8,128)(2,1)}, u32[]{:S(2)}, u32[]{:S(2)}) %collective-permute-start.5) | collective-permute-done | bytes 327712 | tf_op jit(solution)/shard_map/ppermute | solution.py:48
  79.8 8.9 %attend.1 = (bf16[768,640]{1,0:T(8,128)(2,1)}, f32[256,1024]{1,0:T(8,128)}, f32[768,256]{1,0:T(8,128)}, bf16[1024,256]{1,0:T(8,128)(2,1)}, bf16[768,256]{1,0:T(8...) custom-call(s32[3]{0:T(128)} %pad_add_fusion.refs_0_, ...), custom_call_target="tpu_custom_call" | custom-call | flops 4000000000 | bytes 10000000 | tf_op jit(solution)/shard_map/attend/pallas_call | solution.py:519
  89.8 10.4 %gate.1 = (f32[256,640]{1,0:T(8,128)}, f32[256,640]{1,0:T(8,128)}, bf16[256,640]{1,0:T(8,128)(2,1)}, bf16[256,2048]{1,0:T(8,128)(2,1)}, bf16[256,2048]{1,0:T(8,128)(2,1)}, /*index=5*/bf16[256,2048]{1,0:T(8,128)(2,1)}) custom-call(s32[3]{0:T(128)} %pad_add_fusion.refs_0_, bf16[256,1024]{1,0:T(8,128)(2,1)} %get-tuple-element.47.refs_1_.refs_8_, ...), custom_call_target="tpu_custom_call" | custom-call | flops 4000000000 | bytes 5242880 | tf_op jit(solution)/shard_map/gate/pallas_call | solution.py:542
  101.1 6.7 %down.1 = (bf16[256,640]{1,0:T(8,128)(2,1)}, bf16[256,640]{1,0:T(8,128)(2,1)}, f32[1,640]{1,0:T(1,128)}, bf16[2,2,256,640]{3,2,1,0:T(8,128)(2,1)}, bf16[2,2,256,640]{3,2,1,0:T(8,128)(2,1)}) custom-call(s32[3]{0:T(128)} %pad_add_fusion.refs_0_, bf16[256,2048]{1,0:T(8,128)(2,1)} %get-tuple-element.48.refs_1_, f32[256,640]{1,0:T(8,128)} %get-tuple-element.49.refs_2_.refs_3_, ...), custom_call_target="tpu_custom_call" | custom-call | flops 4000000000 | bytes 5242880 | tf_op jit(solution)/shard_map/down/pallas_call | solution.py:569
  107.8 9.8 %gate_back.1 = (bf16[256,2048]{1,0:T(8,128)(2,1)}, bf16[256,2048]{1,0:T(8,128)(2,1)}, bf16[2,2,640,512]{3,2,1,0:T(8,128)(2,1)}, bf16[2,2,640,512]{3,2,1,0:T(8,128)(2,1)}) custom-call(s32[3]{0:T(128)} %pad_add_fusion.refs_0_, bf16[256,640]{1,0:T(8,128)(2,1)} %get-tuple-element.51.refs_1_, bf16[256,2048]{1,0:T(8,128)(2,1)} %get-tuple-element.52.refs_2_, ...), custom_call_target="tpu_custom_call" | custom-call | flops 6000000000 | bytes 7864320 | tf_op jit(solution)/shard_map/gate_back/pallas_call | solution.py:591
  117.5 20.8 %last.1 = (f32[256,640]{1,0:T(8,128)}, bf16[512,640]{1,0:T(8,128)(2,1)}, f32[1,640]{1,0:T(1,128)}, f32[1,640]{1,0:T(1,128)}, f32[1,256]{1,0:T(1,128)}, /*index=5...) custom-call(s32[3]{0:T(128)} %pad_add_fusion.refs_0_, ...), custom_call_target="tpu_custom_call" | custom-call | flops 15000000512 | bytes 10485760 | tf_op jit(solution)/shard_map/last/pallas_call | solution.py:616
  141.5 2.0 dynamic_update_slice.7
  144.0 1.4 fusion.8
  145.5 2.3 collective-permute-start.40
  147.7 15.0 %collective-permute-done.40 = bf16[2,256,640]{2,1,0:T(8,128)(2,1)S(1)} collective-permute-done((bf16[2,256,640]{2,1,0:T(8,128)(2,1)S(1)}, bf16[2,256,640]{2,1,0:T(8,128)(2,1)S(1)}, u32[]{:S(2)}, u32[]{:S(2)}) %collective-permute-start.40) | collective-permute-done | bytes 655392 | tf_op jit(solution)/shard_map/ppermute | solution.py:48
  163.6 1.9 fusion.9
  165.5 2.3 collective-permute-start.41
  167.8 2.0 dynamic_update_slice.6
  169.8 2.6 fusion.4
  172.5 2.6 collective-permute-done.41
  176.6 3.3 %collective-permute-start.44 = (bf16[64,640]{1,0:T(8,128)(2,1)S(1)}, bf16[64,640]{1,0:T(8,128)(2,1)S(1)}, u32[]{:S(2)}, u32[]{:S(2)}) collective-permute-start(bf16[64,640]{1,0:T(8,128)(2,1)S(1)} %get-tuple-element.122), channel_id=1, source_target_pairs={{0,24},{2,26},{4,28},{6,30},{8,0},{10,2},{12,4},{14,6},{16,8},{18,... | collective-permute-start | bytes 245768 | tf_op jit(solution)/shard_map/ppermute | solution.py:45
  181.4 4.9 %collective-permute-start.14 = (bf16[256,640]{1,0:T(8,128)(2,1)S(1)}, bf16[256,640]{1,0:T(8,128)(2,1)S(1)}, u32[]{:S(2)}, u32[]{:S(2)}) collective-permute-start(bf16[256,640]{1,0:T(8,128)(2,1)S(1)} %get-tuple-element.109), channel_id=1, source_target_pairs={{2,0},{3,1},{4,2},{5,3},{6,4},{7,5},{8,6},{9,7},{10,8},{11,9},{12,... | collective-permute-start | bytes 983048 | tf_op jit(solution)/shard_map/ppermute | solution.py:53
  186.8 3.8 %collective-permute-start.47 = (bf16[64,640]{1,0:T(8,128)(2,1)S(1)}, bf16[64,640]{1,0:T(8,128)(2,1)S(1)}, u32[]{:S(2)}, u32[]{:S(2)}) collective-permute-start(bf16[64,640]{1,0:T(8,128)(2,1)S(1)} %fusion.20), channel_id=1, source_target_pairs={{0,24},{2,26},{4,28},{6,30},{8,0},{10,2},{12,4},{14,6},{16,8},{18,... | collective-permute-start | bytes 245768 | tf_op jit(solution)/shard_map/ppermute | solution.py:45
  190.6 1.8 collective-permute-done.16
  196.6 1.9 collective-permute-done.45
  199.2 4.8 %collective-permute-done.17 = bf16[576,384]{1,0:T(8,128)(2,1)S(1)} collective-permute-done((bf16[576,384]{1,0:T(8,128)(2,1)S(1)}, bf16[576,384]{1,0:T(8,128)(2,1)S(1)}, u32[]{:S(2)}, u32[]{:S(2)}) %collective-permute-start.17) | collective-permute-done | bytes 442400 | tf_op jit(solution)/shard_map/ppermute | solution.py:42
  205.4 2.0 collective-permute-start.20
  209.3 4.3 %collective-permute-done.19 = bf16[144,384]{1,0:T(8,128)(2,1)S(1)} collective-permute-done((bf16[144,384]{1,0:T(8,128)(2,1)S(1)}, bf16[144,384]{1,0:T(8,128)(2,1)S(1)}, u32[]{:S(2)}, u32[]{:S(2)}) %collective-permute-start.19) | collective-permute-done | bytes 110624 | tf_op jit(solution)/shard_map/ppermute | solution.py:45
  216.6 3.2 collective-permute-done.23
  219.8 7.5 %collective-permute-start.13 = (bf16[256,640]{1,0:T(8,128)(2,1)S(1)}, bf16[256,640]{1,0:T(8,128)(2,1)S(1)}, u32[]{:S(2)}, u32[]{:S(2)}) collective-permute-start(bf16[256,640]{1,0:T(8,128)(2,1)S(1)} %get-tuple-element.108), channel_id=1, source_target_pairs={{1,0},{2,1},{3,2},{4,3},{5,4},{6,5},{7,6},{8,7},{9,8},{10,9},{11,1... | collective-permute-start | bytes 983048 | tf_op jit(solution)/shard_map/ppermute | solution.py:53
  229.1 3.1 collective-permute-start.49
  232.2 5.1 %collective-permute-done.48 = bf16[256,640]{1,0:T(8,128)(2,1)S(1)} collective-permute-done((bf16[256,640]{1,0:T(8,128)(2,1)S(1)}, bf16[256,640]{1,0:T(8,128)(2,1)S(1)}, u32[]{:S(2)}, u32[]{:S(2)}) %collective-permute-start.48) | collective-permute-done | bytes 327712 | tf_op jit(solution)/shard_map/ppermute | solution.py:42
  237.3 4.8 %collective-permute-start.50 = (bf16[256,640]{1,0:T(8,128)(2,1)S(1)}, bf16[256,640]{1,0:T(8,128)(2,1)S(1)}, u32[]{:S(2)}, u32[]{:S(2)}) collective-permute-start(bf16[256,640]{1,0:T(8,128)(2,1)S(1)} %collective-permute-done.48), channel_id=1, source_target_pairs={{0,2},{2,0},{4,6},{6,4},{8,10},{10,8},{12,14},{14,12},{16,18},{18,... | collective-permute-start | bytes 983048 | tf_op jit(solution)/shard_map/ppermute | solution.py:39
  243.1 3.7 %collective-permute-done.24 = bf16[576,384]{1,0:T(8,128)(2,1)S(1)} collective-permute-done((bf16[576,384]{1,0:T(8,128)(2,1)S(1)}, bf16[576,384]{1,0:T(8,128)(2,1)S(1)}, u32[]{:S(2)}, u32[]{:S(2)}) %collective-permute-start.24) | collective-permute-done | bytes 442400 | tf_op jit(solution)/shard_map/ppermute | solution.py:42
  246.8 2.5 collective-permute-start.26
  249.6 1.6 collective-permute-start.29
  251.4 1.7 maximum_convert_fusion.2
  253.5 12.6 %collective-permute-done.29 = bf16[640,512]{1,0:T(8,128)(2,1)S(1)} collective-permute-done((bf16[640,512]{1,0:T(8,128)(2,1)S(1)}, bf16[640,512]{1,0:T(8,128)(2,1)S(1)}, u32[]{:S(2)}, u32[]{:S(2)}) %collective-permute-start.29) | collective-permute-done | bytes 655392 | tf_op jit(solution)/shard_map/ppermute | solution.py:42
  266.5 3.0 collective-permute-start.32
  270.1 2.4 collective-permute-done.32
  272.5 11.4 %collective-permute-done.31 = bf16[160,512]{1,0:T(8,128)(2,1)S(1)} collective-permute-done((bf16[160,512]{1,0:T(8,128)(2,1)S(1)}, bf16[160,512]{1,0:T(8,128)(2,1)S(1)}, u32[]{:S(2)}, u32[]{:S(2)}) %collective-permute-start.31) | collective-permute-done | bytes 163872 | tf_op jit(solution)/shard_map/ppermute | solution.py:45
  284.1 2.1 collective-permute-start.34
  288.2 11.9 %collective-permute-done.34 = bf16[160,512]{1,0:T(8,128)(2,1)S(1)} collective-permute-done((bf16[160,512]{1,0:T(8,128)(2,1)S(1)}, bf16[160,512]{1,0:T(8,128)(2,1)S(1)}, u32[]{:S(2)}, u32[]{:S(2)}) %collective-permute-start.34) | collective-permute-done | bytes 163872 | tf_op jit(solution)/shard_map/ppermute | solution.py:45
  300.4 2.0 collective-permute-start.36
  304.0 11.9 %collective-permute-done.36 = bf16[640,512]{1,0:T(8,128)(2,1)S(1)} collective-permute-done((bf16[640,512]{1,0:T(8,128)(2,1)S(1)}, bf16[640,512]{1,0:T(8,128)(2,1)S(1)}, u32[]{:S(2)}, u32[]{:S(2)}) %collective-permute-start.36) | collective-permute-done | bytes 655392 | tf_op jit(solution)/shard_map/ppermute | solution.py:42
  315.9 2.1 collective-permute-start.38
  323.1 1.8 maximum_convert_fusion
  324.9 1.8 maximum_convert_fusion.1
  (191 shorter events, 50.3 us)
Async XLA Ops:
  0.7 25.2 %collective-permute-start = (bf16[256,640]{1,0:T(8,128)(2,1)}, bf16[256,640]{1,0:T(8,128)(2,1)}, u32[]{:S(2)}, u32[]{:S(2)}) collective-permute-start(bf16[256,640]{1,0:T(8,128)(2,1)} %refs_23_.1), channel_id=1, source_target_pairs={{0,2},{1,3},{2,4},{3,5},{4,6},{5,7},{6,8},{7,9},{8,10},{9,11},{10,... | collective-permute-start | bytes 983048 | tf_op jit(solution)/shard_map/ppermute | solution.py:53
  9.5 12.5 %collective-permute-start.2 = (bf16[1536]{0:T(1024)(128)(2,1)S(1)}, bf16[1536]{0:T(1024)(128)(2,1)S(1)}, u32[]{:S(2)}, u32[]{:S(2)}) collective-permute-start(bf16[1536]{0:T(1024)(128)(2,1)S(1)} %concatenate.48), channel_id=1, source_target_pairs={{0,1},{1,0},{2,3},{3,2},{4,5},{5,4},{6,7},{7,6},{8,9},{9,8},{10,11... | collective-permute-start | bytes 9224 | tf_op jit(solution)/shard_map/ppermute | solution.py:48
  12.0 15.0 %collective-permute-start.3 = (bf16[320,768]{1,0:T(8,128)(2,1)S(1)}, bf16[320,768]{1,0:T(8,128)(2,1)}, u32[]{:S(2)}, u32[]{:S(2)}) collective-permute-start(bf16[320,768]{1,0:T(8,128)(2,1)S(1)} %constant_dynamic-slice_fusion.18), channel_id=1, source_target_pairs={{0,1},{1,0},{2,3},{3,2},{4,5},{5,4},{6,7},{7,6},{8,9},{9,8},{10,11... | collective-permute-start | bytes 1474568 | tf_op jit(solution)/shard_map/ppermute | solution.py:48
  13.5 47.2 %collective-permute-start.7 = (bf16[320,1024]{1,0:T(8,128)(2,1)S(1)}, bf16[320,1024]{1,0:T(8,128)(2,1)}, u32[]{:S(2)}, u32[]{:S(2)}) collective-permute-start(bf16[320,1024]{1,0:T(8,128)(2,1)S(1)} %constant_dynamic-slice_fusion.16), channel_id=1, source_target_pairs={{0,1},{1,0},{2,3},{3,2},{4,5},{5,4},{6,7},{7,6},{8,9},{9,8},{10,11... | collective-permute-start | bytes 1966088 | tf_op jit(solution)/shard_map/ppermute | solution.py:48
  15.9 44.9 %collective-permute-start.9 = (bf16[320,1024]{1,0:T(8,128)(2,1)S(1)}, bf16[320,1024]{1,0:T(8,128)(2,1)}, u32[]{:S(2)}, u32[]{:S(2)}) collective-permute-start(bf16[320,1024]{1,0:T(8,128)(2,1)S(1)} %constant_dynamic-slice_fusion.15), channel_id=1, source_target_pairs={{0,1},{1,0},{2,3},{3,2},{4,5},{5,4},{6,7},{7,6},{8,9},{9,8},{10,11... | collective-permute-start | bytes 1966088 | tf_op jit(solution)/shard_map/ppermute | solution.py:48
  22.0 38.3 %collective-permute-start.1 = (bf16[256,640]{1,0:T(8,128)(2,1)}, bf16[256,640]{1,0:T(8,128)(2,1)S(1)}, u32[]{:S(2)}, u32[]{:S(2)}) collective-permute-start(bf16[256,640]{1,0:T(8,128)(2,1)} %refs_23_.1), channel_id=1, source_target_pairs={{0,1},{1,2},{2,3},{3,4},{4,5},{5,6},{6,7},{7,8},{8,9},{9,10},{10,1... | collective-permute-start | bytes 983048 | tf_op jit(solution)/shard_map/ppermute | solution.py:53
  25.8 53.5 %collective-permute-start.11 = (bf16[512,640]{1,0:T(8,128)(2,1)S(1)}, bf16[512,640]{1,0:T(8,128)(2,1)S(1)}, u32[]{:S(2)}, u32[]{:S(2)}) collective-permute-start(bf16[512,640]{1,0:T(8,128)(2,1)S(1)} %constant_dynamic-slice_fusion.14), channel_id=1, source_target_pairs={{0,1},{1,0},{2,3},{3,2},{4,5},{5,4},{6,7},{7,6},{8,9},{9,8},{10,11... | collective-permute-start | bytes 1966088 | tf_op jit(solution)/shard_map/ppermute | solution.py:48
  27.0 52.8 %collective-permute-start.4 = (bf16[320,768]{1,0:T(8,128)(2,1)}, bf16[320,768]{1,0:T(8,128)(2,1)}, u32[]{:S(2)}, u32[]{:S(2)}) collective-permute-start(bf16[320,768]{1,0:T(8,128)(2,1)} %collective-permute-done.3.refs_11_.refs_34_), channel_id=1, source_target_pairs={{0,2},{2,0},{4,6},{6,4},{8,10},{10,8},{12,14},{14,12},{16,18},{18,... | collective-permute-start | bytes 1474568 | tf_op jit(solution)/shard_map/ppermute | solution.py:39
  60.3 18.9 %collective-permute-start.5 = (bf16[256,640]{1,0:T(8,128)(2,1)S(1)}, bf16[256,640]{1,0:T(8,128)(2,1)}, u32[]{:S(2)}, u32[]{:S(2)}) collective-permute-start(bf16[256,640]{1,0:T(8,128)(2,1)S(1)} %constant_dynamic-slice_fusion.17), channel_id=1, source_target_pairs={{0,1},{1,0},{2,3},{3,2},{4,5},{5,4},{6,7},{7,6},{8,9},{9,8},{10,11... | collective-permute-start | bytes 983048 | tf_op jit(solution)/shard_map/ppermute | solution.py:48
  60.7 28.0 %collective-permute-start.8 = (bf16[320,1024]{1,0:T(8,128)(2,1)}, bf16[320,1024]{1,0:T(8,128)(2,1)S(1)}, u32[]{:S(2)}, u32[]{:S(2)}) collective-permute-start(bf16[320,1024]{1,0:T(8,128)(2,1)} %collective-permute-done.7.refs_9_.refs_28_), channel_id=1, source_target_pairs={{0,2},{2,0},{4,6},{6,4},{8,10},{10,8},{12,14},{14,12},{16,18},{18,... | collective-permute-start | bytes 1966088 | tf_op jit(solution)/shard_map/ppermute | solution.py:39
  61.1 27.6 %collective-permute-start.10 = (bf16[320,1024]{1,0:T(8,128)(2,1)}, bf16[320,1024]{1,0:T(8,128)(2,1)S(1)}, u32[]{:S(2)}, u32[]{:S(2)}) collective-permute-start(bf16[320,1024]{1,0:T(8,128)(2,1)} %collective-permute-done.9.refs_12_.refs_31_), channel_id=1, source_target_pairs={{0,2},{2,0},{4,6},{6,4},{8,10},{10,8},{12,14},{14,12},{16,18},{18,... | collective-permute-start | bytes 1966088 | tf_op jit(solution)/shard_map/ppermute | solution.py:39
  79.2 9.4 %collective-permute-start.6 = (bf16[256,640]{1,0:T(8,128)(2,1)}, bf16[256,640]{1,0:T(8,128)(2,1)S(1)}, u32[]{:S(2)}, u32[]{:S(2)}) collective-permute-start(bf16[256,640]{1,0:T(8,128)(2,1)} %collective-permute-done.5.refs_6_.refs_25_), channel_id=1, source_target_pairs={{0,2},{2,0},{4,6},{6,4},{8,10},{10,8},{12,14},{14,12},{16,18},{18,... | collective-permute-start | bytes 983048 | tf_op jit(solution)/shard_map/ppermute | solution.py:39
  79.4 20.9 %collective-permute-start.12 = (bf16[512,640]{1,0:T(8,128)(2,1)S(1)}, bf16[512,640]{1,0:T(8,128)(2,1)S(1)}, u32[]{:S(2)}, u32[]{:S(2)}) collective-permute-start(bf16[512,640]{1,0:T(8,128)(2,1)S(1)} %collective-permute-done.11.refs_6_), channel_id=1, source_target_pairs={{0,2},{2,0},{4,6},{6,4},{8,10},{10,8},{12,14},{14,12},{16,18},{18,... | collective-permute-start | bytes 1966088 | tf_op jit(solution)/shard_map/ppermute | solution.py:39
  143.5 26.3 %collective-permute-start.15 = (bf16[2,2,576,384]{3,2,1,0:T(8,128)(2,1)}, bf16[2,2,576,384]{3,2,1,0:T(8,128)(2,1)}, u32[]{:S(2)}, u32[]{:S(2)}) collective-permute-start(bf16[2,2,576,384]{3,2,1,0:T(8,128)(2,1)} %dynamic_update_slice.7), channel_id=1, source_target_pairs={{0,2},{2,0},{4,6},{6,4},{8,10},{10,8},{12,14},{14,12},{16,18},{18,... | collective-permute-start | bytes 5308424 | tf_op jit(solution)/shard_map/ppermute | solution.py:39
  143.8 54.7 %collective-permute-start.27 = (bf16[2,2,640,512]{3,2,1,0:T(8,128)(2,1)}, bf16[2,2,640,512]{3,2,1,0:T(8,128)(2,1)S(1)}, u32[]{:S(2)}, u32[]{:S(2)}) collective-permute-start(bf16[2,2,640,512]{3,2,1,0:T(8,128)(2,1)} %get-tuple-element.76), channel_id=1, source_target_pairs={{0,2},{2,0},{4,6},{6,4},{8,10},{10,8},{12,14},{14,12},{16,18},{18,... | collective-permute-start | bytes 7864328 | tf_op jit(solution)/shard_map/ppermute | solution.py:39
  145.5 17.3 %collective-permute-start.40 = (bf16[2,256,640]{2,1,0:T(8,128)(2,1)S(1)}, bf16[2,256,640]{2,1,0:T(8,128)(2,1)S(1)}, u32[]{:S(2)}, u32[]{:S(2)}) collective-permute-start(bf16[2,256,640]{2,1,0:T(8,128)(2,1)S(1)} %fusion.8), channel_id=1, source_target_pairs={{0,1},{1,0},{2,3},{3,2},{4,5},{5,4},{6,7},{7,6},{8,9},{9,8},{10,11... | collective-permute-start | bytes 1966088 | tf_op jit(solution)/shard_map/ppermute | solution.py:48
  165.5 9.6 %collective-permute-start.41 = (bf16[256,640]{1,0:T(8,128)(2,1)}, bf16[256,640]{1,0:T(8,128)(2,1)}, u32[]{:S(2)}, u32[]{:S(2)}) collective-permute-start(bf16[256,640]{1,0:T(8,128)(2,1)} %fusion.9), channel_id=1, source_target_pairs={{0,4},{2,6},{4,0},{6,2},{8,12},{10,14},{12,8},{14,10},{16,20},{18,... | collective-permute-start | bytes 983048 | tf_op jit(solution)/shard_map/ppermute | solution.py:42
  172.4 20.0 %collective-permute-start.16 = (bf16[2,576,384]{2,1,0:T(8,128)(2,1)}, bf16[2,576,384]{2,1,0:T(8,128)(2,1)S(1)}, u32[]{:S(2)}, u32[]{:S(2)}) collective-permute-start(bf16[2,576,384]{2,1,0:T(8,128)(2,1)} %fusion.4), channel_id=1, source_target_pairs={{0,1},{1,0},{2,3},{3,2},{4,5},{5,4},{6,7},{7,6},{8,9},{9,8},{10,11... | collective-permute-start | bytes 2654216 | tf_op jit(solution)/shard_map/ppermute | solution.py:48
  176.6 4.8 %collective-permute-start.44 = (bf16[64,640]{1,0:T(8,128)(2,1)S(1)}, bf16[64,640]{1,0:T(8,128)(2,1)S(1)}, u32[]{:S(2)}, u32[]{:S(2)}) collective-permute-start(bf16[64,640]{1,0:T(8,128)(2,1)S(1)} %get-tuple-element.122), channel_id=1, source_target_pairs={{0,24},{2,26},{4,28},{6,30},{8,0},{10,2},{12,4},{14,6},{16,8},{18,... | collective-permute-start | bytes 245768 | tf_op jit(solution)/shard_map/ppermute | solution.py:45
  179.9 6.8 %collective-permute-start.43 = (bf16[64,640]{1,0:T(8,128)(2,1)S(1)}, bf16[64,640]{1,0:T(8,128)(2,1)S(1)}, u32[]{:S(2)}, u32[]{:S(2)}) collective-permute-start(bf16[64,640]{1,0:T(8,128)(2,1)S(1)} %get-tuple-element.123), channel_id=1, source_target_pairs={{0,16},{2,18},{4,20},{6,22},{8,24},{10,26},{12,28},{14,30},{16,0},... | collective-permute-start | bytes 245768 | tf_op jit(solution)/shard_map/ppermute | solution.py:45
  179.9 6.8 %collective-permute-start.42 = (bf16[64,640]{1,0:T(8,128)(2,1)S(1)}, bf16[64,640]{1,0:T(8,128)(2,1)S(1)}, u32[]{:S(2)}, u32[]{:S(2)}) collective-permute-start(bf16[64,640]{1,0:T(8,128)(2,1)S(1)} %get-tuple-element.121), channel_id=1, source_target_pairs={{0,8},{2,10},{4,12},{6,14},{8,16},{10,18},{12,20},{14,22},{16,24},... | collective-permute-start | bytes 245768 | tf_op jit(solution)/shard_map/ppermute | solution.py:45
  181.4 47.7 %collective-permute-start.14 = (bf16[256,640]{1,0:T(8,128)(2,1)S(1)}, bf16[256,640]{1,0:T(8,128)(2,1)S(1)}, u32[]{:S(2)}, u32[]{:S(2)}) collective-permute-start(bf16[256,640]{1,0:T(8,128)(2,1)S(1)} %get-tuple-element.109), channel_id=1, source_target_pairs={{2,0},{3,1},{4,2},{5,3},{6,4},{7,5},{8,6},{9,7},{10,8},{11,9},{12,... | collective-permute-start | bytes 983048 | tf_op jit(solution)/shard_map/ppermute | solution.py:53
  186.8 8.1 %collective-permute-start.47 = (bf16[64,640]{1,0:T(8,128)(2,1)S(1)}, bf16[64,640]{1,0:T(8,128)(2,1)S(1)}, u32[]{:S(2)}, u32[]{:S(2)}) collective-permute-start(bf16[64,640]{1,0:T(8,128)(2,1)S(1)} %fusion.20), channel_id=1, source_target_pairs={{0,24},{2,26},{4,28},{6,30},{8,0},{10,2},{12,4},{14,6},{16,8},{18,... | collective-permute-start | bytes 245768 | tf_op jit(solution)/shard_map/ppermute | solution.py:45
  190.6 6.0 %collective-permute-start.46 = (bf16[64,640]{1,0:T(8,128)(2,1)S(1)}, bf16[64,640]{1,0:T(8,128)(2,1)S(1)}, u32[]{:S(2)}, u32[]{:S(2)}) collective-permute-start(bf16[64,640]{1,0:T(8,128)(2,1)S(1)} %fusion.20), channel_id=1, source_target_pairs={{0,16},{2,18},{4,20},{6,22},{8,24},{10,26},{12,28},{14,30},{16,0},... | collective-permute-start | bytes 245768 | tf_op jit(solution)/shard_map/ppermute | solution.py:45
  192.4 6.0 %collective-permute-start.45 = (bf16[64,640]{1,0:T(8,128)(2,1)S(1)}, bf16[64,640]{1,0:T(8,128)(2,1)S(1)}, u32[]{:S(2)}, u32[]{:S(2)}) collective-permute-start(bf16[64,640]{1,0:T(8,128)(2,1)S(1)} %fusion.20), channel_id=1, source_target_pairs={{0,8},{2,10},{4,12},{6,14},{8,16},{10,18},{12,20},{14,22},{16,24},... | collective-permute-start | bytes 245768 | tf_op jit(solution)/shard_map/ppermute | solution.py:45
  194.9 9.2 %collective-permute-start.17 = (bf16[576,384]{1,0:T(8,128)(2,1)S(1)}, bf16[576,384]{1,0:T(8,128)(2,1)S(1)}, u32[]{:S(2)}, u32[]{:S(2)}) collective-permute-start(bf16[576,384]{1,0:T(8,128)(2,1)S(1)} %fusion.5), channel_id=1, source_target_pairs={{0,4},{2,6},{4,0},{6,2},{8,12},{10,14},{12,8},{14,10},{16,20},{18,... | collective-permute-start | bytes 1327112 | tf_op jit(solution)/shard_map/ppermute | solution.py:42
  198.9 50.4 %collective-permute-start.28 = (bf16[2,640,512]{2,1,0:T(8,128)(2,1)S(1)}, bf16[2,640,512]{2,1,0:T(8,128)(2,1)S(1)}, u32[]{:S(2)}, u32[]{:S(2)}) collective-permute-start(bf16[2,640,512]{2,1,0:T(8,128)(2,1)S(1)} %fusion), channel_id=1, source_target_pairs={{0,1},{1,0},{2,3},{3,2},{4,5},{5,4},{6,7},{7,6},{8,9},{9,8},{10,11... | collective-permute-start | bytes 3932168 | tf_op jit(solution)/shard_map/ppermute | solution.py:48
  207.4 6.2 %collective-permute-start.19 = (bf16[144,384]{1,0:T(8,128)(2,1)S(1)}, bf16[144,384]{1,0:T(8,128)(2,1)S(1)}, u32[]{:S(2)}, u32[]{:S(2)}) collective-permute-start(bf16[144,384]{1,0:T(8,128)(2,1)S(1)} %get-tuple-element.116), channel_id=1, source_target_pairs={{0,16},{2,18},{4,20},{6,22},{8,24},{10,26},{12,28},{14,30},{16,0},... | collective-permute-start | bytes 331784 | tf_op jit(solution)/shard_map/ppermute | solution.py:45
  207.9 5.9 %collective-permute-start.18 = (bf16[144,384]{1,0:T(8,128)(2,1)S(1)}, bf16[144,384]{1,0:T(8,128)(2,1)S(1)}, u32[]{:S(2)}, u32[]{:S(2)}) collective-permute-start(bf16[144,384]{1,0:T(8,128)(2,1)S(1)} %get-tuple-element.114), channel_id=1, source_target_pairs={{0,8},{2,10},{4,12},{6,14},{8,16},{10,18},{12,20},{14,22},{16,24},... | collective-permute-start | bytes 331784 | tf_op jit(solution)/shard_map/ppermute | solution.py:45
  213.8 5.9 %collective-permute-start.23 = (bf16[144,384]{1,0:T(8,128)(2,1)S(1)}, bf16[144,384]{1,0:T(8,128)(2,1)S(1)}, u32[]{:S(2)}, u32[]{:S(2)}) collective-permute-start(bf16[144,384]{1,0:T(8,128)(2,1)S(1)} %fusion.17), channel_id=1, source_target_pairs={{0,24},{2,26},{4,28},{6,30},{8,0},{10,2},{12,4},{14,6},{16,8},{18,... | collective-permute-start | bytes 331784 | tf_op jit(solution)/shard_map/ppermute | solution.py:45
  214.5 12.8 %collective-permute-start.22 = (bf16[144,384]{1,0:T(8,128)(2,1)S(1)}, bf16[144,384]{1,0:T(8,128)(2,1)S(1)}, u32[]{:S(2)}, u32[]{:S(2)}) collective-permute-start(bf16[144,384]{1,0:T(8,128)(2,1)S(1)} %fusion.17), channel_id=1, source_target_pairs={{0,16},{2,18},{4,20},{6,22},{8,24},{10,26},{12,28},{14,30},{16,0},... | collective-permute-start | bytes 331784 | tf_op jit(solution)/shard_map/ppermute | solution.py:45
  215.1 12.6 %collective-permute-start.21 = (bf16[144,384]{1,0:T(8,128)(2,1)S(1)}, bf16[144,384]{1,0:T(8,128)(2,1)S(1)}, u32[]{:S(2)}, u32[]{:S(2)}) collective-permute-start(bf16[144,384]{1,0:T(8,128)(2,1)S(1)} %fusion.17), channel_id=1, source_target_pairs={{0,8},{2,10},{4,12},{6,14},{8,16},{10,18},{12,20},{14,22},{16,24},... | collective-permute-start | bytes 331784 | tf_op jit(solution)/shard_map/ppermute | solution.py:45
  219.8 22.4 %collective-permute-start.13 = (bf16[256,640]{1,0:T(8,128)(2,1)S(1)}, bf16[256,640]{1,0:T(8,128)(2,1)S(1)}, u32[]{:S(2)}, u32[]{:S(2)}) collective-permute-start(bf16[256,640]{1,0:T(8,128)(2,1)S(1)} %get-tuple-element.108), channel_id=1, source_target_pairs={{1,0},{2,1},{3,2},{4,3},{5,4},{6,5},{7,6},{8,7},{9,8},{10,9},{11,1... | collective-permute-start | bytes 983048 | tf_op jit(solution)/shard_map/ppermute | solution.py:53
  227.3 10.1 %collective-permute-start.48 = (bf16[256,640]{1,0:T(8,128)(2,1)S(1)}, bf16[256,640]{1,0:T(8,128)(2,1)S(1)}, u32[]{:S(2)}, u32[]{:S(2)}) collective-permute-start(bf16[256,640]{1,0:T(8,128)(2,1)S(1)} %bitcast.138), channel_id=1, source_target_pairs={{0,4},{2,6},{4,0},{6,2},{8,12},{10,14},{12,8},{14,10},{16,20},{18,... | collective-permute-start | bytes 983048 | tf_op jit(solution)/shard_map/ppermute | solution.py:42
  227.9 18.9 %collective-permute-start.24 = (bf16[576,384]{1,0:T(8,128)(2,1)S(1)}, bf16[576,384]{1,0:T(8,128)(2,1)S(1)}, u32[]{:S(2)}, u32[]{:S(2)}) collective-permute-start(bf16[576,384]{1,0:T(8,128)(2,1)S(1)} %bitcast.134), channel_id=1, source_target_pairs={{0,4},{2,6},{4,0},{6,2},{8,12},{10,14},{12,8},{14,10},{16,20},{18,... | collective-permute-start | bytes 1327112 | tf_op jit(solution)/shard_map/ppermute | solution.py:42
  229.1 22.0 %collective-permute-start.49 = (bf16[256,640]{1,0:T(8,128)(2,1)S(1)}, bf16[256,640]{1,0:T(8,128)(2,1)S(1)}, u32[]{:S(2)}, u32[]{:S(2)}) collective-permute-start(bf16[256,640]{1,0:T(8,128)(2,1)S(1)} %bitcast.139), channel_id=1, source_target_pairs={{0,2},{2,0},{4,6},{6,4},{8,10},{10,8},{12,14},{14,12},{16,18},{18,... | collective-permute-start | bytes 983048 | tf_op jit(solution)/shard_map/ppermute | solution.py:39
  237.3 13.8 %collective-permute-start.50 = (bf16[256,640]{1,0:T(8,128)(2,1)S(1)}, bf16[256,640]{1,0:T(8,128)(2,1)S(1)}, u32[]{:S(2)}, u32[]{:S(2)}) collective-permute-start(bf16[256,640]{1,0:T(8,128)(2,1)S(1)} %collective-permute-done.48), channel_id=1, source_target_pairs={{0,2},{2,0},{4,6},{6,4},{8,10},{10,8},{12,14},{14,12},{16,18},{18,... | collective-permute-start | bytes 983048 | tf_op jit(solution)/shard_map/ppermute | solution.py:39
  243.1 9.9 %collective-permute-start.25 = (bf16[576,384]{1,0:T(8,128)(2,1)S(1)}, bf16[576,384]{1,0:T(8,128)(2,1)S(1)}, u32[]{:S(2)}, u32[]{:S(2)}) collective-permute-start(bf16[576,384]{1,0:T(8,128)(2,1)S(1)} %bitcast.135), channel_id=1, source_target_pairs={{0,2},{2,0},{4,6},{6,4},{8,10},{10,8},{12,14},{14,12},{16,18},{18,... | collective-permute-start | bytes 1327112 | tf_op jit(solution)/shard_map/ppermute | solution.py:39
  246.8 6.2 %collective-permute-start.26 = (bf16[576,384]{1,0:T(8,128)(2,1)S(1)}, bf16[576,384]{1,0:T(8,128)(2,1)S(1)}, u32[]{:S(2)}, u32[]{:S(2)}) collective-permute-start(bf16[576,384]{1,0:T(8,128)(2,1)S(1)} %collective-permute-done.24), channel_id=1, source_target_pairs={{0,2},{2,0},{4,6},{6,4},{8,10},{10,8},{12,14},{14,12},{16,18},{18,... | collective-permute-start | bytes 1327112 | tf_op jit(solution)/shard_map/ppermute | solution.py:39
  249.6 16.5 %collective-permute-start.29 = (bf16[640,512]{1,0:T(8,128)(2,1)S(1)}, bf16[640,512]{1,0:T(8,128)(2,1)S(1)}, u32[]{:S(2)}, u32[]{:S(2)}) collective-permute-start(bf16[640,512]{1,0:T(8,128)(2,1)S(1)} %fusion.1), channel_id=1, source_target_pairs={{0,4},{2,6},{4,0},{6,2},{8,12},{10,14},{12,8},{14,10},{16,20},{18,... | collective-permute-start | bytes 1966088 | tf_op jit(solution)/shard_map/ppermute | solution.py:42
  266.5 6.0 %collective-permute-start.32 = (bf16[160,512]{1,0:T(8,128)(2,1)S(1)}, bf16[160,512]{1,0:T(8,128)(2,1)S(1)}, u32[]{:S(2)}, u32[]{:S(2)}) collective-permute-start(bf16[160,512]{1,0:T(8,128)(2,1)S(1)} %get-tuple-element.106), channel_id=1, source_target_pairs={{0,24},{2,26},{4,28},{6,30},{8,0},{10,2},{12,4},{14,6},{16,8},{18,... | collective-permute-start | bytes 491528 | tf_op jit(solution)/shard_map/ppermute | solution.py:45
  269.5 14.5 %collective-permute-start.31 = (bf16[160,512]{1,0:T(8,128)(2,1)S(1)}, bf16[160,512]{1,0:T(8,128)(2,1)S(1)}, u32[]{:S(2)}, u32[]{:S(2)}) collective-permute-start(bf16[160,512]{1,0:T(8,128)(2,1)S(1)} %get-tuple-element.107), channel_id=1, source_target_pairs={{0,16},{2,18},{4,20},{6,22},{8,24},{10,26},{12,28},{14,30},{16,0},... | collective-permute-start | bytes 491528 | tf_op jit(solution)/shard_map/ppermute | solution.py:45
  269.8 14.1 %collective-permute-start.30 = (bf16[160,512]{1,0:T(8,128)(2,1)S(1)}, bf16[160,512]{1,0:T(8,128)(2,1)S(1)}, u32[]{:S(2)}, u32[]{:S(2)}) collective-permute-start(bf16[160,512]{1,0:T(8,128)(2,1)S(1)} %get-tuple-element.105), channel_id=1, source_target_pairs={{0,8},{2,10},{4,12},{6,14},{8,16},{10,18},{12,20},{14,22},{16,24},... | collective-permute-start | bytes 491528 | tf_op jit(solution)/shard_map/ppermute | solution.py:45
  284.1 16.1 %collective-permute-start.34 = (bf16[160,512]{1,0:T(8,128)(2,1)S(1)}, bf16[160,512]{1,0:T(8,128)(2,1)S(1)}, u32[]{:S(2)}, u32[]{:S(2)}) collective-permute-start(bf16[160,512]{1,0:T(8,128)(2,1)S(1)} %fusion.14), channel_id=1, source_target_pairs={{0,16},{2,18},{4,20},{6,22},{8,24},{10,26},{12,28},{14,30},{16,0},... | collective-permute-start | bytes 491528 | tf_op jit(solution)/shard_map/ppermute | solution.py:45
  286.2 14.0 %collective-permute-start.33 = (bf16[160,512]{1,0:T(8,128)(2,1)S(1)}, bf16[160,512]{1,0:T(8,128)(2,1)S(1)}, u32[]{:S(2)}, u32[]{:S(2)}) collective-permute-start(bf16[160,512]{1,0:T(8,128)(2,1)S(1)} %fusion.14), channel_id=1, source_target_pairs={{0,8},{2,10},{4,12},{6,14},{8,16},{10,18},{12,20},{14,22},{16,24},... | collective-permute-start | bytes 491528 | tf_op jit(solution)/shard_map/ppermute | solution.py:45
  300.4 15.5 %collective-permute-start.36 = (bf16[640,512]{1,0:T(8,128)(2,1)S(1)}, bf16[640,512]{1,0:T(8,128)(2,1)S(1)}, u32[]{:S(2)}, u32[]{:S(2)}) collective-permute-start(bf16[640,512]{1,0:T(8,128)(2,1)S(1)} %bitcast.132), channel_id=1, source_target_pairs={{0,4},{2,6},{4,0},{6,2},{8,12},{10,14},{12,8},{14,10},{16,20},{18,... | collective-permute-start | bytes 1966088 | tf_op jit(solution)/shard_map/ppermute | solution.py:42
  302.6 20.0 %collective-permute-start.37 = (bf16[640,512]{1,0:T(8,128)(2,1)S(1)}, bf16[640,512]{1,0:T(8,128)(2,1)S(1)}, u32[]{:S(2)}, u32[]{:S(2)}) collective-permute-start(bf16[640,512]{1,0:T(8,128)(2,1)S(1)} %bitcast.133), channel_id=1, source_target_pairs={{0,2},{2,0},{4,6},{6,4},{8,10},{10,8},{12,14},{14,12},{16,18},{18,... | collective-permute-start | bytes 1966088 | tf_op jit(solution)/shard_map/ppermute | solution.py:39
  315.9 6.7 %collective-permute-start.38 = (bf16[640,512]{1,0:T(8,128)(2,1)S(1)}, bf16[640,512]{1,0:T(8,128)(2,1)S(1)}, u32[]{:S(2)}, u32[]{:S(2)}) collective-permute-start(bf16[640,512]{1,0:T(8,128)(2,1)S(1)} %collective-permute-done.36), channel_id=1, source_target_pairs={{0,2},{2,0},{4,6},{6,4},{8,10},{10,8},{12,14},{14,12},{16,18},{18,... | collective-permute-start | bytes 1966088 | tf_op jit(solution)/shard_map/ppermute | solution.py:39
  (20 other events, 135.7 us)

commit v3 on v2

--- a/solution.py
+++ b/solution.py
@@ -15,12 +15,18 @@
 BF16 = jnp.bfloat16
 F32 = jnp.float32
 QBLOCK = 128
+LANES = 128
+GAIN_ROWS = 32
 GELU_A = math.sqrt(2.0 / math.pi)
 GELU_B = 0.044715
 
 VMEM = pl.BlockSpec(memory_space=pltpu.VMEM)
 SMEM = pl.BlockSpec(memory_space=pltpu.SMEM)
 ANY = pl.BlockSpec(memory_space=pl.ANY)
+
+
+def wrapped(value, size):
+    return value & (size - 1) if size & (size - 1) == 0 else lax.rem(value, jnp.int32(size))
 
 
 class Places:
@@ -28,12 +34,25 @@
         self.seq = lax.axis_size("seq")
         self.fsdp = lax.axis_size("fsdp")
         self.outer = self.seq // 4
-        index = lax.axis_index("seq")
-        self.core_at = index % 2
-        self.mid_at = (index // 2) % 2
-        self.outer_at = index // 4
-        self.fsdp_at = lax.axis_index("fsdp")
-        self.vector = jnp.stack([self.core_at, self.mid_at, self.fsdp_at]).astype(jnp.int32)
+        index = lax.axis_index("seq").astype(jnp.int32)
+        fsdp_at = lax.axis_index("fsdp").astype(jnp.int32)
+        outer_at = lax.shift_right_logical(index, 2)
+        core_at, mid_at = index & 1, lax.shift_right_logical(index, 1) & 1
+        scalars = lax.optimization_barrier(
+            (
+                core_at,
+                mid_at,
+                fsdp_at,
+                core_at * 2 + mid_at,
+                tuple(wrapped(outer_at + by, self.outer) for by in range(self.outer)),
+                tuple(wrapped(outer_at - by + self.outer, self.outer) for by in range(self.outer)),
+                tuple(wrapped(fsdp_at + by, self.fsdp) for by in range(self.fsdp)),
+                tuple(wrapped(fsdp_at - by + self.fsdp, self.fsdp) for by in range(self.fsdp)),
+                jnp.stack([core_at, mid_at, fsdp_at]),
+            )
+        )
+        self.core_at, self.mid_at, self.fsdp_at, self.quarter_at = scalars[:4]
+        self.outer_ahead, self.outer_behind, self.fsdp_ahead, self.fsdp_behind, self.vector = scalars[4:]
 
     def core_swap(self, array):
         return lax.ppermute(array, "seq", [(i, i ^ 1) for i in range(self.seq)])
@@ -54,25 +73,43 @@
 
 
 def pick(array, at):
-    return lax.dynamic_index_in_dim(array, at, 0, keepdims=False)
-
-
-def ordered(pieces, at):
-    count = len(pieces)
-    if count == 2:
+    return lax.dynamic_index_in_dim(array, at, 0, keepdims=False, allow_negative_indices=False)
+
+
+def ordered(pieces, behind):
+    if len(pieces) == 2:
         own, other = pieces
-        return jnp.where(at == 0, jnp.stack([own, other]), jnp.stack([other, own]))
+        return jnp.where(behind[0] == 0, jnp.stack([own, other]), jnp.stack([other, own]))
     stacked = jnp.stack(pieces)
-    return jnp.stack([pick(stacked, (at - j) % count) for j in range(count)])
-
-
-def fetch(here, shard, axis):
-    half = shard.shape[axis] // 2
-    part = lax.dynamic_slice_in_dim(shard, here.core_at * half, half, axis)
-    pieces = [shard]
-    for by in range(1, here.fsdp):
-        mine = here.fsdp_shift(part, by)
-        pieces += [mine, here.core_swap(mine)]
+    return jnp.stack([pick(stacked, at) for at in behind])
+
+
+def own_part(here, shards, axis, ways):
+    size = sum(shard.shape[axis] for shard in shards) // ways
+    place = here.quarter_at if ways == 4 else here.core_at
+    if len(shards) == 1:
+        return lax.dynamic_slice_in_dim(shards[0], place * size, size, axis, allow_negative_indices=False)
+    joined = jnp.concatenate(shards, axis)
+    parts = [lax.slice_in_dim(joined, i * size, (i + 1) * size, axis=axis) for i in range(ways)]
+    return functools.reduce(lambda rest, i: jnp.where(place == i, parts[i], rest), range(1, ways), parts[0])
+
+
+def after(value, *earlier):
+    return lax.optimization_barrier((value, *earlier))[0]
+
+
+def over_links(here, part):
+    return [here.fsdp_shift(part, by) for by in range(1, here.fsdp)]
+
+
+def on_chips(here, arrived, ways):
+    pieces = []
+    for mine in arrived:
+        if ways == 4:
+            across = here.mid_swap(mine)
+            pieces += [mine, across, here.core_swap(mine), here.core_swap(across)]
+        else:
+            pieces += [mine, here.core_swap(mine)]
     return pieces
 
 
@@ -80,24 +117,31 @@
     return pl.multiple_of(value, of)
 
 
-def place_copies(pieces, whole, sems, at, axis):
-    core, fsdp = at[0], at[2]
-    count = (len(pieces) + 1) // 2
-    rows, columns = pieces[0].shape
+def place_copies(owned, pieces, whole, sems, at, axis, ways):
+    core, mid, fsdp = at[0], at[1], at[2]
+    count = 1 + len(pieces) // ways
+    rows = owned[0].shape[0]
     copies = []
+    column = 0
+    own_row = multiple(fsdp * rows, 16)
+    for shard in owned:
+        wide = shard.shape[1]
+        copies.append((shard, whole.at[pl.ds(own_row, rows), pl.ds(column, wide)]))
+        column += wide
     for k, piece in enumerate(pieces):
-        by = (k + 1) // 2
+        by = 1 + k // ways
         row = multiple(lax.rem(fsdp + (count - by), count) * rows, 16)
-        if k == 0:
-            target = whole.at[pl.ds(row, rows), :]
+        k = k % ways
+        if ways == 4:
+            place = (core if k < 2 else 1 - core) * 2 + (mid if k % 2 == 0 else 1 - mid)
         else:
-            half = core if k % 2 == 1 else 1 - core
-            if axis == 0:
-                target = whole.at[pl.ds(multiple(row + half * (rows // 2), 16), rows // 2), :]
-            else:
-                target = whole.at[pl.ds(row, rows), pl.ds(multiple(half * (columns // 2), 128), columns // 2)]
-        copies.append(pltpu.make_async_copy(piece, target, sems.at[k]))
-    return copies
+            place = core if k == 0 else 1 - core
+        if axis == 0:
+            target = whole.at[pl.ds(multiple(row + place * (rows // ways), 16), rows // ways), :]
+        else:
+            target = whole.at[pl.ds(row, rows), pl.ds(multiple(place * (column // ways), 128), column // ways)]
+        copies.append((piece, target))
+    return [pltpu.make_async_copy(a, b, sems.at[k]) for k, (a, b) in enumerate(copies)]
 
 
 def dot(a, b):
@@ -129,7 +173,7 @@
 
 
 def cost(flops, bytes_accessed):
-    return pl.CostEstimate(flops=int(flops), bytes_accessed=int(bytes_accessed), transcendentals=0)
+    return pl.CostEstimate(flops=int(20 * flops), bytes_accessed=int(20 * bytes_accessed), transcendentals=0)
 
 
 def shape(dims, kind):
@@ -142,7 +186,7 @@
     pos, cosine, sine, gain_in, gain_q, gain_k = refs[1 + n_tok : 7 + n_tok]
     qkv = refs[7 + n_tok : 7 + n_tok + n_qkv]
     normed, q_raw, k_raw, q_st, keys, values, probs, attended, w_full, sems = refs[7 + n_tok + n_qkv :]
-    copies = place_copies(qkv, w_full, sems, at, 1)
+    copies = place_copies(qkv[:3], qkv[3:], w_full, sems, at, 1, 4)
     for copy in copies:
         copy.start()
     rows = toks[0].shape[0]
@@ -213,9 +257,9 @@
     projected_ref, residual_ref, ffn_in_ref, mixed, gelu_out, gate_slope = refs[:6]
     out_full, gate_full, up_full, out_sems, gate_sems, up_sems = refs[6:]
     groups = (
-        place_copies(out_w, out_full, out_sems, at, 0),
-        place_copies(gate_w, gate_full, gate_sems, at, 1),
-        place_copies(up_w, up_full, up_sems, at, 1),
+        place_copies(out_w[:1], out_w[1:], out_full, out_sems, at, 0, 2),
+        place_copies(gate_w[:1], gate_w[1:], gate_full, gate_sems, at, 1, 4),
+        place_copies(up_w[:1], up_w[1:], up_full, up_sems, at, 1, 2),
     )
     for group in groups:
         for copy in group:
@@ -264,7 +308,7 @@
     down_w = refs[5 : 5 + n_down]
     layer_out, d_down, grad_gain, keep, send = refs[5 + n_down : 10 + n_down]
     down_full, mixed_t, sems = refs[10 + n_down :]
-    copies = place_copies(down_w, down_full, sems, at, 0)
+    copies = place_copies(down_w[:1], down_w[1:], down_full, sems, at, 0, 4)
     for copy in copies:
         copy.start()
     mixed_t[...] = mixed[...].T
@@ -287,9 +331,9 @@
 def gate_back_kernel(n_down, fsdp, *refs):
     at, d_down, gelu_out, gate_slope, ffn_in = refs[:5]
     down_w = refs[5 : 5 + n_down]
-    d_gate, d_up, keep, send = refs[5 + n_down : 9 + n_down]
-    down_full, ffn_t, sems = refs[9 + n_down :]
-    copies = place_copies(down_w, down_full, sems, at, 0)
+    d_gate, d_up, gate_keep, gate_send, up_keep, up_send = refs[5 + n_down : 11 + n_down]
+    down_full, ffn_t, sems = refs[11 + n_down :]
+    copies = place_copies(down_w[:1], down_w[1:], down_full, sems, at, 0, 4)
     for copy in copies:
         copy.start()
     ffn_t[...] = ffn_in[...].T
@@ -305,78 +349,83 @@
         return 0
 
     lax.fori_loop(0, d_gate.shape[1] // width, step, 0)
-    tall, wide = keep.shape[2] // 2, keep.shape[3]
-    for c, f, x, core, row, mid in relative_blocks(at, fsdp):
-        cut = pl.ds(multiple((core * 2 + mid) * wide, 128), wide)
-        left = ffn_t[pl.ds(multiple(row * tall, 16), tall), :]
-        target = keep if c == 0 else send
-        target[f, x, :tall, :] = dot(left, d_gate[:, cut]).astype(BF16)
-        target[f, x, tall:, :] = dot(left, d_up[:, cut]).astype(BF16)
-
-
-def last_kernel(n_out, n_gate, n_up, n_qkv, n_tok, fsdp, heads, *refs):
-    (
-        at, d_gate, d_up, residual, projected, cotangent, gain_ffn, gain_attn, attended,
-        q_raw, k_raw, q_st, keys, values, probs, cosine, sine, gain_q, gain_k, gain_in, normed,
-    ) = refs[:21]
-    toks = refs[21 : 21 + n_tok]
-    refs = refs[21 + n_tok :]
-    out_w, gate_w, up_w, qkv_w, refs = (
+    tall, wide = gate_keep.shape[2:]
+    for source, targets in ((d_gate, (gate_keep, gate_send)), (d_up, (up_keep, up_send))):
+        for c, f, x, core, row, mid in relative_blocks(at, fsdp):
+            cut = pl.ds(multiple((core * 2 + mid) * wide, 128), wide)
+            left = ffn_t[pl.ds(multiple(row * tall, 16), tall), :]
+            targets[c][f, x] = dot(left, source[:, cut]).astype(BF16)
+
+
+def middle_kernel(n_out, n_gate, n_up, fsdp, heads, *refs):
+    at, d_gate, d_up, residual, projected, cotangent, gain_ffn, gain_attn, attended = refs[:9]
+    refs = refs[9:]
+    out_w, gate_w, up_w, refs = (
         refs[:n_out],
         refs[n_out : n_out + n_gate],
         refs[n_out + n_gate : n_out + n_gate + n_up],
-        refs[n_out + n_gate + n_up : n_out + n_gate + n_up + n_qkv],
-        refs[n_out + n_gate + n_up + n_qkv :],
+        refs[n_out + n_gate + n_up :],
     )
-    grad_tokens, d_halo, g_ffn, g_attn, g_q, g_k, g_in, keep, send = refs[:9]
-    (
-        out_full, gate_full, up_full, w_full, att_t, normed_t, d_att, d_scores, d_q, d_k, d_v, d_qkv,
-        out_sems, gate_sems, up_sems, qkv_sems,
-    ) = refs[9:]
+    d_residual_ref, g_ffn, g_attn, d_att, keep, send = refs[:6]
+    out_full, gate_full, up_full, att_t, out_sems, gate_sems, up_sems = refs[6:]
     groups = (
-        place_copies(gate_w, gate_full, gate_sems, at, 1),
-        place_copies(up_w, up_full, up_sems, at, 1),
-        place_copies(out_w, out_full, out_sems, at, 0),
-        place_copies(qkv_w, w_full, qkv_sems, at, 1),
+        place_copies(gate_w[:1], gate_w[1:], gate_full, gate_sems, at, 1, 4),
+        place_copies(up_w[:1], up_w[1:], up_full, up_sems, at, 1, 2),
+        place_copies(out_w[:1], out_w[1:], out_full, out_sems, at, 0, 2),
     )
     for group in groups:
         for copy in group:
             copy.start()
     att_t[...] = attended[...].T
-    normed_t[...] = normed[...].T
-    for copy in groups[0] + groups[1]:
+    for copy in groups[0]:
         copy.wait()
-    d_ffn_in = dot_nt(d_gate[...], gate_full[...]) + dot_nt(d_up[...], up_full[...])
+    d_ffn_in = dot_nt(d_gate[...], gate_full[...])
+    for copy in groups[1]:
+        copy.wait()
+    d_ffn_in = d_ffn_in + dot_nt(d_up[...], up_full[...])
     du, dg = norm_back(residual[...], gain_ffn[...], d_ffn_in)
     g_ffn[...] = dg
     d_residual = cotangent[...].astype(F32) + du
-    grad_tokens[...] = d_residual
+    d_residual_ref[...] = d_residual
     du, dg = norm_back(projected[...], gain_attn[...], d_residual)
     g_attn[...] = dg
     d_proj = du.astype(BF16)
+    rows, dim = d_proj.shape[0], d_att.shape[1]
+    for copy in groups[2]:
+        copy.wait()
+    for h in range(heads):
+        part = dot_nt(d_proj, out_full[h * dim : (h + 1) * dim, :]).astype(BF16)
+        for b in range(rows // QBLOCK):
+            start = (b * heads + h) * QBLOCK
+            d_att[start : start + QBLOCK, :] = part[b * QBLOCK : (b + 1) * QBLOCK, :]
+    block = keep.shape[2]
+    for c, f, x, core, row, mid in relative_blocks(at, fsdp):
+        start = multiple(((row * 2 + core) * 2 + mid) * block, 16)
+        target = keep if c == 0 else send
+        target[f, x] = dot(att_t[pl.ds(start, block), :], d_proj).astype(BF16)
+
+
+def last_kernel(n_qkv, n_tok, fsdp, heads, *refs):
+    (
+        at, d_residual, d_att,
+        q_raw, k_raw, q_st, keys, values, probs, cosine, sine, gain_q, gain_k, gain_in, normed, g_ffn, g_attn, g_out,
+    ) = refs[:18]
+    toks = refs[18 : 18 + n_tok]
+    refs = refs[18 + n_tok :]
+    qkv_w, refs = refs[:n_qkv], refs[n_qkv:]
+    grad_tokens, d_halo, keep, send = refs[:4]
+    w_full, normed_t, d_scores, d_q, d_k, d_v, d_qkv, gain_rows, qkv_sems = refs[4:]
+    copies = place_copies(qkv_w[:3], qkv_w[3:], w_full, qkv_sems, at, 1, 4)
+    for copy in copies:
+        copy.start()
+    normed_t[...] = normed[...].T
     rows = toks[0].shape[0]
     halo = (n_tok - 1) * rows
     dim = keys.shape[1]
     half = dim // 2
     blocks = rows // QBLOCK
     span = WINDOW + QBLOCK
-    for copy in groups[2]:
-        copy.wait()
-    for h in range(heads):
-        part = dot_nt(d_proj, out_full[h * dim : (h + 1) * dim, :]).astype(BF16)
-        for b in range(blocks):
-            start = (b * heads + h) * QBLOCK
-            d_att[start : start + QBLOCK, :] = part[b * QBLOCK : (b + 1) * QBLOCK, :]
-    out_block = att_t.shape[0] // (4 * fsdp)
     tall, wide = normed_t.shape[0] // fsdp, keep.shape[3]
-    columns = d_proj.shape[1]
-    for c, f, x, core, row, mid in relative_blocks(at, fsdp):
-        start = multiple(((row * 2 + core) * 2 + mid) * out_block, 16)
-        part = dot(att_t[pl.ds(start, out_block), :], d_proj).astype(BF16)
-        target = keep if c == 0 else send
-        target[f, x, tall : tall + out_block, :] = part[:, :wide]
-        target[f, x, tall + out_block :, : columns - wide] = part[:, wide:]
-        target[f, x, tall + out_block :, columns - wide :] = jnp.zeros((out_block, 2 * wide - columns), BF16)
     scale = dim ** (-0.5)
     d_k[...] = jnp.zeros(d_k.shape, F32)
     d_v[...] = jnp.zeros(d_v.shape, F32)
@@ -409,7 +458,6 @@
         du, dg = turned_back(q_raw[:, cut], gain_q[...], d_q[:, cut], cosine[halo:, :], sine[halo:, :])
         total_q += dg
         d_qkv[halo:, cut] = du.astype(BF16)
-    g_q[...] = total_q
     total_k = jnp.zeros((1, dim), F32)
     for i in range(n_tok):
         here = slice(i * rows, (i + 1) * rows)
@@ -417,15 +465,14 @@
         total_k += dg
         d_qkv[here, heads * dim : (heads + 1) * dim] = du.astype(BF16)
         d_qkv[here, (heads + 1) * dim :] = d_v[here, :].astype(BF16)
-    g_k[...] = total_k
     for c, f, x, core, row, mid in relative_blocks(at, fsdp):
         cut = pl.ds(multiple((core * 2 + mid) * wide, 128), wide)
         left = normed_t[pl.ds(multiple(row * tall, 16), tall), :]
         target = keep if c == 0 else send
         target[f, x, :tall, :] = dot(left, d_qkv[:, cut]).astype(BF16)
-    for copy in groups[3]:
+    for copy in copies:
         copy.wait()
-    total_in = jnp.zeros(g_in.shape, F32)
+    total_in = jnp.zeros(gain_in.shape, F32)
     for i in range(n_tok):
         here = slice(i * rows, (i + 1) * rows)
         if i < n_tok - 1:
@@ -437,8 +484,18 @@
         if i < n_tok - 1:
             d_halo[here, :] = du.astype(BF16)
         else:
-            grad_tokens[...] += du
-    g_in[...] = total_in
+            grad_tokens[...] = d_residual[...] + du
+    gain_rows[...] = jnp.zeros(gain_rows.shape, F32)
+    at_row = 0
+    for total in (total_in, total_q, total_k, g_attn[...], g_ffn[...], g_out[...]):
+        for i in range(total.shape[1] // LANES):
+            gain_rows[at_row : at_row + 1, :LANES] = total[:, i * LANES : (i + 1) * LANES]
+            at_row += 1
+    packed = gain_rows[...].astype(BF16)
+    for target in (keep, send):
+        for f in range(fsdp):
+            for x in range(2):
+                target[f, x, tall:, :] = packed
 
 
 def add(*terms):
@@ -448,22 +505,33 @@
     return out
 
 
-def reduce_chunk(here, keep, send):
-    other = here.core_swap(send)
-    n, w = keep.shape[2:]
-    arrived = []
-    for by in range(1, here.fsdp):
-        arrived.append(here.fsdp_shift(add(keep[by], other[by]).astype(BF16), by))
-    across = here.mid_swap(add(keep[0, 1], other[0, 1], *[a[1] for a in arrived]).astype(BF16))
-    mine = add(keep[0, 0], other[0, 0], *[a[0] for a in arrived], across).astype(BF16)
-    mine = mine.reshape(here.outer, n // here.outer, w)
-    terms = [pick(mine, here.outer_at)]
-    for by in range(1, here.outer):
-        terms.append(here.outer_shift(pick(mine, (here.outer_at + by) % here.outer), by))
-    own = add(*terms).astype(BF16)
-    block = ordered([own] + [here.outer_shift(own, by) for by in range(1, here.outer)], here.outer_at).reshape(n, w)
-    across = here.mid_swap(block)
-    return [[block, across], [here.core_swap(block), here.core_swap(across)]]
+class Chunk:
+    def __init__(self, here, keep, send):
+        self.here, self.keep = here, keep
+        self.other = here.core_swap(send)
+
+    def over_fsdp(self, *earlier):
+        here = self.here
+        parts = [add(self.keep[by], self.other[by]).astype(BF16) for by in range(1, here.fsdp)]
+        self.arrived = [here.fsdp_shift(after(part, *earlier), by + 1) for by, part in enumerate(parts)]
+
+    def over_mid(self, *earlier):
+        terms = [self.keep[0, 1], self.other[0, 1]] + [a[1] for a in self.arrived]
+        self.across = self.here.mid_swap(after(add(*terms).astype(BF16), *earlier))
+
+    def finish(self, *earlier):
+        here = self.here
+        n, w = self.across.shape
+        terms = [self.keep[0, 0], self.other[0, 0]] + [a[0] for a in self.arrived] + [self.across]
+        mine = after(add(*terms).astype(BF16), *earlier).reshape(here.outer, n // here.outer, w)
+        terms = [pick(mine, here.outer_ahead[0])]
+        for by in range(1, here.outer):
+            terms.append(here.outer_shift(pick(mine, here.outer_ahead[by]), by))
+        own = add(*terms).astype(BF16)
+        block = ordered([own] + [here.outer_shift(own, by) for by in range(1, here.outer)], here.outer_behind)
+        block = block.reshape(n, w)
+        across = here.mid_swap(block)
+        return [[block, across], [here.core_swap(block), here.core_swap(across)]]
 
 
 def by_place(here, blocks):
@@ -497,17 +565,20 @@
     for gain in gains:
         cuts.append(cuts[-1] + gain.shape[0])
     gain_row = jnp.concatenate(gains)
-    qkv_w = fetch(here, jnp.concatenate([w_query, w_key, w_value], axis=1), 1)
-    gain_rows = ordered([gain_row] + [here.fsdp_shift(gain_row, by) for by in range(1, fsdp)], here.fsdp_at)
+    gain_rows = ordered([gain_row] + [here.fsdp_shift(gain_row, by) for by in range(1, fsdp)], here.fsdp_behind)
     gain_rows = gain_rows.astype(F32)
     gain_in, gain_q, gain_k, gain_attn, gain_ffn, gain_out = (
         gain_rows[:, cuts[i] : cuts[i + 1]].reshape(1, -1) for i in range(6)
     )
     toks = [linear_shift(tokens, by) for by in range(hops, 0, -1)] + [tokens]
-    out_w = fetch(here, w_out, 0)
-    gate_w = fetch(here, w_gate, 1)
-    up_w = fetch(here, w_up, 1)
-    down_w = fetch(here, w_down, 0)
+    qkv_w = [w_query, w_key, w_value]
+    qkv_w += on_chips(here, over_links(here, own_part(here, qkv_w, 1, 4)), 4)
+    out_part = after(own_part(here, [w_out], 0, 2), *toks[:-1])
+    out_arrived = over_links(here, out_part)
+    gate_part = after(own_part(here, [w_gate], 1, 4), qkv_w[3])
+    gate_arrived = over_links(here, gate_part)
+    up_part = after(own_part(here, [w_up], 1, 2), out_arrived[0])
+    up_arrived = over_links(here, up_part)
 
     all_positions = jnp.concatenate([positions[0] - halo + jnp.arange(halo, dtype=jnp.int32), positions])
     frequency = ROPE_BASE ** (-(jnp.arange(dim // 2, dtype=F32) * 2.0 / dim))
@@ -539,6 +610,11 @@
         name="attend",
     )(at, *toks, positions[:, None], cosine, sine, gain_in, gain_q, gain_k, *qkv_w)
 
+    down_part = after(own_part(here, [w_down], 0, 4), attended)
+    out_w = [w_out] + on_chips(here, [after(a, attended) for a in out_arrived], 2)
+    gate_w = [w_gate] + on_chips(here, [after(a, attended) for a in gate_arrived], 4)
+    up_w = [w_up] + on_chips(here, [after(a, attended) for a in up_arrived], 2)
+    down_w = [w_down] + on_chips(here, over_links(here, down_part), 4)
     projected, residual, ffn_in, mixed, gelu_out, gate_slope = pl.pallas_call(
         functools.partial(gate_kernel, len(out_w), len(gate_w), len(up_w)),
         out_shape=(
@@ -587,17 +663,21 @@
         name="down",
     )(at, mixed, residual, cotangent, gain_out, *down_w)
 
-    gate_shape = shape((fsdp, 2, 2 * w_gate.shape[0], hidden // 4), BF16)
-    d_gate, d_up, gate_keep, gate_send = pl.pallas_call(
+    down_sum = Chunk(here, down_keep, down_send)
+    d_down = after(d_down, down_sum.other)
+    gate_shape = shape((fsdp, 2, w_gate.shape[0], hidden // 4), BF16)
+    d_gate, d_up, gate_keep, gate_send, up_keep, up_send = pl.pallas_call(
         functools.partial(gate_back_kernel, len(down_w), fsdp),
         out_shape=(
             shape((rows, hidden), BF16),
             shape((rows, hidden), BF16),
             gate_shape,
             gate_shape,
+            gate_shape,
+            gate_shape,
         ),
         in_specs=[SMEM] + [VMEM] * 4 + [ANY] * len(down_w),
-        out_specs=(VMEM,) * 4,
+        out_specs=(VMEM,) * 6,
         scratch_shapes=[
             pltpu.VMEM((hidden, width), BF16),
             pltpu.VMEM((width, rows), BF16),
@@ -611,88 +691,102 @@
     qkv_cols = query_cols + 2 * dim
     last_wide = qkv_cols // 4
     shard_rows = w_query.shape[0]
-    out_block = w_out.shape[0] // 4
-    last_shape = shape((fsdp, 2, shard_rows + 2 * out_block, last_wide), BF16)
-    grad_tokens, d_halo, g_ffn, g_attn, g_q, g_k, g_in, last_keep, last_send = pl.pallas_call(
-        functools.partial(
-            last_kernel, len(out_w), len(gate_w), len(up_w), len(qkv_w), n_tok, fsdp, heads
-        ),
+    last_shape = shape((fsdp, 2, shard_rows + GAIN_ROWS, last_wide), BF16)
+    gate_sum = Chunk(here, gate_keep, gate_send)
+    up_sum = Chunk(here, up_keep, up_send)
+    down_sum.over_fsdp()
+    out_shape = shape((fsdp, 2, w_out.shape[0] // 4, width), BF16)
+    d_residual, g_ffn, g_attn, d_att, out_keep, out_send = pl.pallas_call(
+        functools.partial(middle_kernel, len(out_w), len(gate_w), len(up_w), fsdp, heads),
         out_shape=(
             shape((rows, width), F32),
-            shape((halo, width), BF16),
             shape((1, width), F32),
             shape((1, width), F32),
-            shape((1, dim), F32),
-            shape((1, dim), F32),
-            shape((1, width), F32),
-            last_shape,
-            last_shape,
+            shape((heads * rows, dim), BF16),
+            out_shape,
+            out_shape,
         ),
-        in_specs=[SMEM]
-        + [VMEM] * (20 + n_tok)
-        + [ANY] * (len(out_w) + len(gate_w) + len(up_w) + len(qkv_w)),
-        out_specs=(VMEM,) * 9,
+        in_specs=[SMEM] + [VMEM] * 8 + [ANY] * (len(out_w) + len(gate_w) + len(up_w)),
+        out_specs=(VMEM,) * 6,
         scratch_shapes=[
             pltpu.VMEM((query_cols, width), BF16),
             pltpu.VMEM((width, hidden), BF16),
             pltpu.VMEM((width, hidden), BF16),
+            pltpu.VMEM((query_cols, rows), BF16),
+            pltpu.SemaphoreType.DMA((len(out_w),)),
+            pltpu.SemaphoreType.DMA((len(gate_w),)),
+            pltpu.SemaphoreType.DMA((len(up_w),)),
+        ],
+        compiler_params=params(),
+        cost_estimate=cost(6e9, 4 * weight_bytes),
+        name="middle",
+    )(at, d_gate, d_up, residual, projected, cotangent, gain_ffn, gain_attn, attended, *out_w, *gate_w, *up_w)
+
+    gate_sum.over_fsdp()
+    out_sum = Chunk(here, out_keep, out_send)
+    d_att = after(d_att, gate_sum.other, up_sum.other, *down_sum.arrived)
+    down_sum.over_mid()
+    grad_tokens, d_halo, last_keep, last_send = pl.pallas_call(
+        functools.partial(last_kernel, len(qkv_w), n_tok, fsdp, heads),
+        out_shape=(
+            shape((rows, width), F32),
+            shape((halo, width), BF16),
+            last_shape,
+            last_shape,
+        ),
+        in_specs=[SMEM] + [VMEM] * (17 + n_tok) + [ANY] * len(qkv_w),
+        out_specs=(VMEM,) * 4,
+        scratch_shapes=[
             pltpu.VMEM((width, qkv_cols), BF16),
-            pltpu.VMEM((query_cols, rows), BF16),
             pltpu.VMEM((width, every), BF16),
-            pltpu.VMEM((heads * rows, dim), BF16),
             pltpu.VMEM((heads * QBLOCK, span), BF16),
             pltpu.VMEM((rows, query_cols), F32),
             pltpu.VMEM((every, dim), F32),
             pltpu.VMEM((every, dim), F32),
             pltpu.VMEM((every, qkv_cols), BF16),
-            pltpu.SemaphoreType.DMA((len(out_w),)),
-            pltpu.SemaphoreType.DMA((len(gate_w),)),
-            pltpu.SemaphoreType.DMA((len(up_w),)),
+            pltpu.VMEM((GAIN_ROWS, last_wide), F32),
             pltpu.SemaphoreType.DMA((len(qkv_w),)),
         ],
         compiler_params=params(),
         cost_estimate=cost(15e9, 4 * weight_bytes),
         name="last",
     )(
-        at, d_gate, d_up, residual, projected, cotangent, gain_ffn, gain_attn, attended,
+        at, d_residual, d_att,
         q_raw, k_raw, q_st, keys, values, probs, cosine, sine, gain_q, gain_k, gain_in, normed,
-        *toks, *out_w, *gate_w, *up_w, *qkv_w,
+        g_ffn, g_attn, g_ffn_out, *toks, *qkv_w,
     )
 
-    gain_grads = (g_in, g_q, g_k, g_attn, g_ffn, g_ffn_out)
-    packed = jnp.concatenate([g.reshape(fsdp, -1) for g in gain_grads], axis=1).astype(BF16)
-    corner = 2 * last_wide - width
-    per_block = cuts[-1] // 4
-    deep = -(-per_block // corner)
-    packed = jnp.pad(packed.reshape(fsdp, 4, per_block), ((0, 0), (0, 0), (0, deep * corner - per_block)))
-    packed = packed.reshape(fsdp, 2, 2, deep, corner)
-    packed = jnp.stack([pick(packed, (here.fsdp_at + f) % fsdp) for f in range(fsdp)])
-    packed = jnp.where(here.mid_at == 0, packed, packed[:, :, ::-1])
-    corner_at = (0, 0, shard_rows + out_block, width - last_wide)
-    last_keep = lax.dynamic_update_slice(last_keep, jnp.where(here.core_at == 0, packed[:, 0], packed[:, 1]), corner_at)
-    last_send = lax.dynamic_update_slice(last_send, jnp.where(here.core_at == 0, packed[:, 1], packed[:, 0]), corner_at)
-
-    down_blocks = by_place(here, reduce_chunk(here, down_keep, down_send))
-    gate_blocks = by_place(here, reduce_chunk(here, gate_keep, gate_send))
-    last_blocks = by_place(here, reduce_chunk(here, last_keep, last_send))
+    last_sum = Chunk(here, last_keep, after(last_send, down_sum.across, *gate_sum.arrived))
+    up_sum.over_fsdp()
+    gate_sum.over_mid(last_sum.other)
+    last_sum.over_fsdp()
+    out_sum.over_fsdp(last_sum.other, *up_sum.arrived)
+    down_blocks = by_place(here, down_sum.finish(last_sum.other))
+    up_sum.over_mid(last_sum.other)
+    last_sum.over_mid()
+    gate_blocks = by_place(here, gate_sum.finish(*last_sum.arrived))
+    out_sum.over_mid()
+    up_blocks = by_place(here, up_sum.finish(*out_sum.arrived))
+    last_blocks = last_sum.finish()
+    total_gains = last_blocks[0][0][shard_rows:, :LANES].astype(F32)
+    last_blocks = by_place(here, last_blocks)
+    out_blocks = by_place(here, out_sum.finish())
 
     for by in range(1, hops + 1):
         start = halo - by * rows
         grad_tokens = grad_tokens + linear_shift(d_halo[start : start + rows], -by).astype(F32)
 
     total_down = jnp.concatenate(down_blocks, axis=0).astype(F32)
-    total_gate = jnp.concatenate([b[:shard_rows] for b in gate_blocks], axis=1).astype(F32)
-    total_up = jnp.concatenate([b[shard_rows:] for b in gate_blocks], axis=1).astype(F32)
+    total_gate = jnp.concatenate(gate_blocks, axis=1).astype(F32)
+    total_up = jnp.concatenate(up_blocks, axis=1).astype(F32)
     total_qkv = jnp.concatenate([b[:shard_rows] for b in last_blocks], axis=1).astype(F32)
-    middle = shard_rows + out_block
-    total_out = jnp.concatenate(
-        [jnp.concatenate([b[shard_rows:middle], b[middle:, : width - last_wide]], axis=1) for b in last_blocks],
-        axis=0,
-    ).astype(F32)
-    total_gains = jnp.concatenate(
-        [b[middle : middle + deep, width - last_wide :].reshape(-1)[:per_block] for b in last_blocks]
-    ).astype(F32)
-    g = [total_gains[cuts[i] : cuts[i + 1]] for i in range(6)]
+    total_out = jnp.concatenate(out_blocks, axis=0).astype(F32)
+    g, at_row = [], 0
+    for gain in gains:
+        deep = fsdp * gain.shape[0] // total_gains.shape[1]
+        total = total_gains[at_row : at_row + deep].reshape(fsdp, gain.shape[0])
+        g.append(pick(total, here.fsdp_at))
+        at_row += deep
     return (
         layer_out, grad_tokens, g[0],
         total_qkv[:, :query_cols],

time: 328 us -> 289 us (0.88)
  waiting for transfers between devices: 146 us -> 75.1 us
  starting transfers between devices: 72.1 us -> 97.9 us
  Pallas kernels: 56.4 us -> 61.2 us
  local copies, waits for them, and re-layouts: 23.7 us -> 20.1 us
    ppermute x4, waiting for transfers between devices: 33.3 us -> 3.49 us  [linear_shift(): lax.ppermute(array, ('seq', 'fsdp'), [(i, i + by) for i in range(count) i...]
    ppermute x6 -> x13, waiting for transfers between devices: 40.8 us -> 19.7 us  [mid_swap(): return lax.ppermute(array, 'seq', [(i, i ^ 2) for i in range(self.seq)])]
    ppermute x18 -> x30, waiting for transfers between devices: 40 us -> 22.9 us  [outer_shift(): lax.ppermute(array, 'seq', [(i, (i + 4 * by) % self.seq) for i in range(s...]
    ppermute x14 -> x23, starting transfers between devices: 15.5 us -> 30.2 us  [core_swap(): return lax.ppermute(array, 'seq', [(i, i ^ 1) for i in range(self.seq)])]
    ppermute x18 -> x30, starting transfers between devices: 21.3 us -> 31.7 us  [outer_shift(): lax.ppermute(array, 'seq', [(i, (i + 4 * by) % self.seq) for i in range(s...]
    ppermute x4, starting transfers between devices: 20.2 us -> 11.8 us  [linear_shift(): lax.ppermute(array, ('seq', 'fsdp'), [(i, i + by) for i in range(count) i...]
    ppermute x6 -> x13, starting transfers between devices: 7.74 us -> 14.3 us  [mid_swap(): return lax.ppermute(array, 'seq', [(i, i ^ 2) for i in range(self.seq)])]
    ppermute x9 -> x11, waiting for transfers between devices: 31.5 us -> 25.8 us  [fsdp_shift(): lax.ppermute(array, 'fsdp', [(i, (i + by) % self.fsdp) for i in range(sel...]
  transfers between devices with their start and end apart: 51 -> 81, of which waited for: 22 -> 28; matrix products, arithmetic and copies ran while one was open for 12% -> 14% of each run, Pallas kernels for 6% -> 19%
where the time goes in v3:
time: 289 us; the launch traced here: 286 us
  starting transfers between devices  97.9 us (34%)
  waiting for transfers between devices  75.1 us (26%)
  Pallas kernels  61.2 us (21%)
  other arithmetic  29.7 us (10%)
  local copies, waits for them, and re-layouts  20.1 us (7%)
    ppermute x30, starting transfers between devices, outer_shift(): lax.ppermute(array, 'seq', [(i, (i + 4 * by) % self.seq) for i in range(s...  31.7 us
    ppermute x23, starting transfers between devices, core_swap(): return lax.ppermute(array, 'seq', [(i, i ^ 1) for i in range(self.seq)])  30.2 us
    ppermute x11, waiting for transfers between devices, fsdp_shift(): lax.ppermute(array, 'fsdp', [(i, (i + by) % self.fsdp) for i in range(sel...  25.8 us
    ppermute x30, waiting for transfers between devices, outer_shift(): lax.ppermute(array, 'seq', [(i, (i + 4 * by) % self.seq) for i in range(s...  22.9 us
    ppermute x13, waiting for transfers between devices, mid_swap(): return lax.ppermute(array, 'seq', [(i, i ^ 2) for i in range(self.seq)])  19.7 us
    pallas_call x1, Pallas kernels, on_device(): pl.pallas_call(functools.partial(last_kernel, len(qkv_w), n_tok, fsdp, he...  14.7 us
    ppermute x13, starting transfers between devices, mid_swap(): return lax.ppermute(array, 'seq', [(i, i ^ 2) for i in range(self.seq)])  14.3 us
    ppermute x4, starting transfers between devices, linear_shift(): lax.ppermute(array, ('seq', 'fsdp'), [(i, i + by) for i in range(count) i...  11.8 us
  transfers between devices with their start and end apart: 81, of which 28 were waited for; matrix products, arithmetic and copies ran while one was open for 14% of the time, Pallas kernels for 19%

profile of v3, /device:TPU:1, one launch (start us, length us, event | category | flops | bytes accessed | tf_op | source)
XLA Modules:
  0.0 286.3 jit_solution(10418966709967497544)
XLA Ops:
  0.7 4.0 %collective-permute-start.1 = (bf16[256,640]{1,0:T(8,128)(2,1)}, bf16[256,640]{1,0:T(8,128)(2,1)}, u32[]{:S(2)}, u32[]{:S(2)}) collective-permute-start(bf16[256,640]{1,0:T(8,128)(2,1)} %refs_20_.1), channel_id=1, source_target_pairs={{0,1},{1,2},{2,3},{3,4},{4,5},{5,6},{6,7},{7,8},{8,9},{9,10},{10,1... | collective-permute-start | bytes 983048 | tf_op jit(solution)/shard_map/ppermute | solution.py:72
  4.6 4.0 %collective-permute-start = (bf16[256,640]{1,0:T(8,128)(2,1)}, bf16[256,640]{1,0:T(8,128)(2,1)}, u32[]{:S(2)}, u32[]{:S(2)}) collective-permute-start(bf16[256,640]{1,0:T(8,128)(2,1)} %refs_20_.1), channel_id=1, source_target_pairs={{0,2},{1,3},{2,4},{3,5},{4,6},{5,7},{6,8},{7,9},{8,10},{9,11},{10,... | collective-permute-start | bytes 983048 | tf_op jit(solution)/shard_map/ppermute | solution.py:72
  8.6 4.2 %concatenate.33 = bf16[1536]{0:T(1024)(128)(2,1)S(1)} concatenate(bf16[320]{0:T(512)(128)(2,1)} %param.19, bf16[128]{0:T(256)(128)(2,1)} %param.23, bf16[128]{0:T(256)(128)(2,1)} %param.24, bf16[320]{0:T(512)(128)(2,1)} %param.26, bf16[320]{0:T(512)(128)(2,1)} %param.27, bf16[320]{0:T(512)(128)(2,1)} %param.31), dimensions={0} | concatenate | bytes 6144 | tf_op jit(solution)/shard_map/concatenate | solution.py:567
  19.8 2.5 multiply_sine_fusion
  26.7 2.3 collective-permute-done.4.refs_14_.refs_25_
  29.0 2.1 collective-permute-start.6
  32.4 1.8 collective-permute-start.9
  36.8 8.9 %attend.1 = (bf16[768,640]{1,0:T(8,128)(2,1)}, f32[256,1024]{1,0:T(8,128)}, f32[768,256]{1,0:T(8,128)}, bf16[1024,256]{1,0:T(8,128)(2,1)}, bf16[768,256]{1,0:T(8...) custom-call(s32[3]{0:T(128)} %pad_add_fusion.refs_0_, ...), custom_call_target="tpu_custom_call" | custom-call | flops 80000000000 | bytes 200000000 | tf_op jit(solution)/shard_map/attend/pallas_call | solution.py:590
  46.8 9.8 %collective-permute-done.13.refs_14_.refs_18_ = bf16[320,1024]{1,0:T(8,128)(2,1)S(1)} collective-permute-done((bf16[320,1024]{1,0:T(8,128)(2,1)S(1)}, bf16[320,1024]{1,0:T(8,128)(2,1)S(1)}, u32[]{:S(2)}, u32[]{:S(2)}) %collective-permute-start.13) | collective-permute-done | bytes 655392 | tf_op jit(solution)/shard_map/ppermute | solution.py:67
  57.5 6.2 %collective-permute-done.15.refs_6_ = bf16[256,640]{1,0:T(8,128)(2,1)} collective-permute-done((bf16[256,640]{1,0:T(8,128)(2,1)S(1)}, bf16[256,640]{1,0:T(8,128)(2,1)}, u32[]{:S(2)}, u32[]{:S(2)}) %collective-permute-start.15) | collective-permute-done | bytes 327712 | tf_op jit(solution)/shard_map/ppermute | solution.py:67
  67.8 4.8 %collective-permute-done.16.refs_7_ = bf16[256,640]{1,0:T(8,128)(2,1)} collective-permute-done((bf16[256,640]{1,0:T(8,128)(2,1)}, bf16[256,640]{1,0:T(8,128)(2,1)}, u32[]{:S(2)}, u32[]{:S(2)}) %collective-permute-start.16) | collective-permute-done | bytes 327712 | tf_op jit(solution)/shard_map/ppermute | solution.py:61
  75.8 10.5 %gate.1 = (f32[256,640]{1,0:T(8,128)}, f32[256,640]{1,0:T(8,128)}, bf16[256,640]{1,0:T(8,128)(2,1)}, bf16[256,2048]{1,0:T(8,128)(2,1)}, bf16[256,2048]{1,0:T(8,128)(2,1)}, /*index=5*/bf16[256,2048]{1,0:T(8,128)(2,1)}) custom-call(s32[3]{0:T(128)} %pad_add_fusion.refs_0_, bf16[256,1024]{1,0:T(8,128)(2,1)} %get-tuple-element.83.refs_1_.refs_8_, ...), custom_call_target="tpu_custom_call" | custom-call | flops 80000000000 | bytes 104857600 | tf_op jit(solution)/shard_map/gate/pallas_call | solution.py:618
  87.2 6.5 %down.1 = (bf16[256,640]{1,0:T(8,128)(2,1)}, bf16[256,640]{1,0:T(8,128)(2,1)}, f32[1,640]{1,0:T(1,128)}, bf16[2,2,256,640]{3,2,1,0:T(8,128)(2,1)}, bf16[2,2,256,640]{3,2,1,0:T(8,128)(2,1)}) custom-call(s32[3]{0:T(128)} %pad_add_fusion.refs_0_, bf16[256,2048]{1,0:T(8,128)(2,1)} %get-tuple-element.91.refs_1_, f32[256,640]{1,0:T(8,128)} %get-tuple-element.92.refs_2_.refs_3_, ...), custom_call_target="tpu_custom_call" | custom-call | flops 80000000000 | bytes 104857600 | tf_op jit(solution)/shard_map/down/pallas_call | solution.py:645
  93.8 3.2 %collective-permute-done.19 = bf16[2,2,256,640]{3,2,1,0:T(8,128)(2,1)S(1)} collective-permute-done((bf16[2,2,256,640]{3,2,1,0:T(8,128)(2,1)}, bf16[2,2,256,640]{3,2,1,0:T(8,128)(2,1)S(1)}, u32[]{:S(2)}, u32[]{:S(2)}) %collective-permute-start.19) | collective-permute-done | bytes 1310752 | tf_op jit(solution)/shard_map/ppermute | solution.py:58
  98.2 2.1 fusion
  101.3 10.2 %gate_back.1 = (bf16[256,2048]{1,0:T(8,128)(2,1)}, bf16[256,2048]{1,0:T(8,128)(2,1)}, bf16[2,2,320,512]{3,2,1,0:T(8,128)(2,1)}, bf16[2,2,320,512]{3,2,1,0:T(8,12...) custom-call(s32[3]{0:T(128)} %pad_add_fusion.refs_0_, ...), custom_call_target="tpu_custom_call" | custom-call | flops 120000004096 | bytes 157286400 | tf_op jit(solution)/shard_map/gate_back/pallas_call | solution.py:669
  112.1 10.4 %middle.1 = (f32[256,640]{1,0:T(8,128)}, f32[1,640]{1,0:T(1,128)}, f32[1,640]{1,0:T(1,128)}, bf16[1024,256]{1,0:T(8,128)(2,1)}, bf16[2,2,128,640]{3,2,1,0:T(8,128)(2,1)}, /*index=5*/bf16[2,2,128,640]{3,2,1,0:T(8,128)(2,1)}) custom-call(s32[3]{0:T(128)} %pad_add_fusion.refs_0_, bf16[256,2048]{1,0:T(8,128)(2,1)} %get-tuple-element.101.refs_1_, ...), custom_call_target="tpu_custom_call" | custom-call | flops 120000004096 | bytes 209715200 | tf_op jit(solution)/shard_map/middle/pallas_call | solution.py:699
  123.0 2.0 fusion.11
  126.0 2.0 fusion.16
  129.2 14.7 %last.1 = (f32[256,640]{1,0:T(8,128)}, bf16[512,640]{1,0:T(8,128)(2,1)}, bf16[2,2,352,384]{3,2,1,0:T(8,128)(2,1)}, bf16[2,2,352,384]{3,2,1,0:T(8,128)(2,1)}) custom-call(s32[3]{0:T(128)} %pad_add_fusion.refs_0_, f32[256,640]{1,0:T(8,128)} %get-tuple-element.104.refs_1_, bf16[1024,256]{1,0:T(8,128)(2,1)} %get-tuple-element.109.refs_2_, ...), custom_call_target="tpu_custom_call" | custom-call | flops 299999985664 | bytes 209715200 | tf_op jit(solution)/shard_map/last/pallas_call | solution.py:729
  147.7 1.9 collective-permute-start.23
  149.7 1.9 collective-permute-start.24
  152.9 1.8 collective-permute-start.40
  156.2 2.8 collective-permute-done.23
  163.2 2.0 collective-permute-start.74
  165.7 7.3 %collective-permute-done.40 = bf16[2,320,512]{2,1,0:T(8,128)(2,1)S(1)} collective-permute-done((bf16[2,320,512]{2,1,0:T(8,128)(2,1)S(1)}, bf16[2,320,512]{2,1,0:T(8,128)(2,1)S(1)}, u32[]{:S(2)}, u32[]{:S(2)}) %collective-permute-start.40) | collective-permute-done | bytes 655392 | tf_op jit(solution)/shard_map/ppermute | solution.py:67
  175.5 2.5 collective-permute-start.77
  180.0 5.5 %collective-permute-done.76 = bf16[64,640]{1,0:T(8,128)(2,1)S(1)} collective-permute-done((bf16[64,640]{1,0:T(8,128)(2,1)S(1)}, bf16[64,640]{1,0:T(8,128)(2,1)S(1)}, u32[]{:S(2)}, u32[]{:S(2)}) %collective-permute-start.76) | collective-permute-done | bytes 81952 | tf_op jit(solution)/shard_map/ppermute | solution.py:64
  185.6 1.9 collective-permute-start.28
  192.4 2.4 collective-permute-start.65
  198.1 3.7 %collective-permute-done.64 = bf16[80,512]{1,0:T(8,128)(2,1)S(1)} collective-permute-done((bf16[80,512]{1,0:T(8,128)(2,1)S(1)}, bf16[80,512]{1,0:T(8,128)(2,1)S(1)}, u32[]{:S(2)}, u32[]{:S(2)}) %collective-permute-start.64) | collective-permute-done | bytes 81952 | tf_op jit(solution)/shard_map/ppermute | solution.py:64
  203.5 1.7 collective-permute-done.68
  206.5 2.4 collective-permute-start.45
  210.4 3.9 %collective-permute-start.78 = (bf16[256,640]{1,0:T(8,128)(2,1)S(1)}, bf16[256,640]{1,0:T(8,128)(2,1)S(1)}, u32[]{:S(2)}, u32[]{:S(2)}) collective-permute-start(bf16[256,640]{1,0:T(8,128)(2,1)S(1)} %bitcast.189), channel_id=1, source_target_pairs={{0,4},{2,6},{4,0},{6,2},{8,12},{10,14},{12,8},{14,10},{16,20},{18,... | collective-permute-start | bytes 983048 | tf_op jit(solution)/shard_map/ppermute | solution.py:61
  214.3 3.6 %collective-permute-start.48 = (bf16[32,640]{1,0:T(8,128)(2,1)S(1)}, bf16[32,640]{1,0:T(8,128)(2,1)S(1)}, u32[]{:S(2)}, u32[]{:S(2)}) collective-permute-start(bf16[32,640]{1,0:T(8,128)(2,1)S(1)} %fusion.36), channel_id=1, source_target_pairs={{0,24},{2,26},{4,28},{6,30},{8,0},{10,2},{12,4},{14,6},{16,8},{18,... | collective-permute-start | bytes 122888 | tf_op jit(solution)/shard_map/ppermute | solution.py:64
  219.0 1.8 collective-permute-start.53
  225.3 4.7 %collective-permute-done.54 = bf16[80,512]{1,0:T(8,128)(2,1)S(1)} collective-permute-done((bf16[80,512]{1,0:T(8,128)(2,1)S(1)}, bf16[80,512]{1,0:T(8,128)(2,1)S(1)}, u32[]{:S(2)}, u32[]{:S(2)}) %collective-permute-start.54) | collective-permute-done | bytes 81952 | tf_op jit(solution)/shard_map/ppermute | solution.py:64
  231.6 6.3 %collective-permute-start.70 = (bf16[320,512]{1,0:T(8,128)(2,1)S(1)}, bf16[320,512]{1,0:T(8,128)(2,1)S(1)}, u32[]{:S(2)}, u32[]{:S(2)}) collective-permute-start(bf16[320,512]{1,0:T(8,128)(2,1)S(1)} %bitcast.184), channel_id=1, source_target_pairs={{0,2},{2,0},{4,6},{6,4},{8,10},{10,8},{12,14},{14,12},{16,18},{18,... | collective-permute-start | bytes 983048 | tf_op jit(solution)/shard_map/ppermute | solution.py:58
  240.4 4.1 %collective-permute-done.29 = bf16[352,384]{1,0:T(8,128)(2,1)S(1)} collective-permute-done((bf16[352,384]{1,0:T(8,128)(2,1)S(1)}, bf16[352,384]{1,0:T(8,128)(2,1)S(1)}, u32[]{:S(2)}, u32[]{:S(2)}) %collective-permute-start.29) | collective-permute-done | bytes 270368 | tf_op jit(solution)/shard_map/ppermute | solution.py:61
  244.7 1.7 collective-permute-start.30
  246.4 2.2 collective-permute-start.32
  252.1 4.8 %collective-permute-start.50 = (bf16[128,640]{1,0:T(8,128)(2,1)S(1)}, bf16[128,640]{1,0:T(8,128)(2,1)S(1)}, u32[]{:S(2)}, u32[]{:S(2)}) collective-permute-start(bf16[128,640]{1,0:T(8,128)(2,1)S(1)} %bitcast.202), channel_id=1, source_target_pairs={{0,2},{2,0},{4,6},{6,4},{8,10},{10,8},{12,14},{14,12},{16,18},{18,... | collective-permute-start | bytes 491528 | tf_op jit(solution)/shard_map/ppermute | solution.py:58
  257.1 2.5 collective-permute-start.35
  264.1 3.6 %collective-permute-start.71 = (bf16[320,512]{1,0:T(8,128)(2,1)S(1)}, bf16[320,512]{1,0:T(8,128)(2,1)S(1)}, u32[]{:S(2)}, u32[]{:S(2)}) collective-permute-start(bf16[320,512]{1,0:T(8,128)(2,1)S(1)} %collective-permute-done.69), channel_id=1, source_target_pairs={{0,2},{2,0},{4,6},{6,4},{8,10},{10,8},{12,14},{14,12},{16,18},{18,... | collective-permute-start | bytes 983048 | tf_op jit(solution)/shard_map/ppermute | solution.py:58
  270.1 2.9 %collective-permute-done.59 = bf16[320,512]{1,0:T(8,128)(2,1)S(1)} collective-permute-done((bf16[320,512]{1,0:T(8,128)(2,1)S(1)}, bf16[320,512]{1,0:T(8,128)(2,1)S(1)}, u32[]{:S(2)}, u32[]{:S(2)}) %collective-permute-start.59) | collective-permute-done | bytes 327712 | tf_op jit(solution)/shard_map/ppermute | solution.py:61
  274.9 4.0 %collective-permute-done.36 = bf16[352,384]{1,0:T(8,128)(2,1)S(1)} collective-permute-done((bf16[352,384]{1,0:T(8,128)(2,1)S(1)}, bf16[352,384]{1,0:T(8,128)(2,1)S(1)}, u32[]{:S(2)}, u32[]{:S(2)}) %collective-permute-start.36) | collective-permute-done | bytes 270368 | tf_op jit(solution)/shard_map/ppermute | solution.py:61
  280.2 1.8 maximum_convert_fusion.1
  282.0 1.8 maximum_convert_fusion
  (261 shorter events, 84.7 us)
Async XLA Ops:
  0.7 25.3 %collective-permute-start.1 = (bf16[256,640]{1,0:T(8,128)(2,1)}, bf16[256,640]{1,0:T(8,128)(2,1)}, u32[]{:S(2)}, u32[]{:S(2)}) collective-permute-start(bf16[256,640]{1,0:T(8,128)(2,1)} %refs_20_.1), channel_id=1, source_target_pairs={{0,1},{1,2},{2,3},{3,4},{4,5},{5,6},{6,7},{7,8},{8,9},{9,10},{10,1... | collective-permute-start | bytes 983048 | tf_op jit(solution)/shard_map/ppermute | solution.py:72
  4.6 21.3 %collective-permute-start = (bf16[256,640]{1,0:T(8,128)(2,1)}, bf16[256,640]{1,0:T(8,128)(2,1)}, u32[]{:S(2)}, u32[]{:S(2)}) collective-permute-start(bf16[256,640]{1,0:T(8,128)(2,1)} %refs_20_.1), channel_id=1, source_target_pairs={{0,2},{1,3},{2,4},{3,5},{4,6},{5,7},{6,8},{7,9},{8,10},{9,11},{10,... | collective-permute-start | bytes 983048 | tf_op jit(solution)/shard_map/ppermute | solution.py:72
  12.8 11.7 %collective-permute-start.2 = (bf16[1536]{0:T(1024)(128)(2,1)S(1)}, bf16[1536]{0:T(1024)(128)(2,1)S(1)}, u32[]{:S(2)}, u32[]{:S(2)}) collective-permute-start(bf16[1536]{0:T(1024)(128)(2,1)S(1)} %concatenate.33), channel_id=1, source_target_pairs={{0,1},{1,0},{2,3},{3,2},{4,5},{5,4},{6,7},{7,6},{8,9},{9,8},{10,11... | collective-permute-start | bytes 9224 | tf_op jit(solution)/shard_map/ppermute | solution.py:67
  24.5 11.5 %collective-permute-start.5 = (bf16[320,384]{1,0:T(8,128)(2,1)}, bf16[320,384]{1,0:T(8,128)(2,1)S(1)}, u32[]{:S(2)}, u32[]{:S(2)}) collective-permute-start(bf16[320,384]{1,0:T(8,128)(2,1)} %collective-permute-done.3.refs_13_.refs_24_), channel_id=1, source_target_pairs={{0,2},{2,0},{4,6},{6,4},{8,10},{10,8},{12,14},{14,12},{16,18},{18,... | collective-permute-start | bytes 737288 | tf_op jit(solution)/shard_map/ppermute | solution.py:58
  26.0 9.3 %collective-permute-start.7 = (bf16[256,640]{1,0:T(8,128)(2,1)S(1)}, bf16[256,640]{1,0:T(8,128)(2,1)S(1)}, u32[]{:S(2)}, u32[]{:S(2)}) collective-permute-start(bf16[256,640]{1,0:T(8,128)(2,1)S(1)} %constant_dynamic-slice_fusion.29), channel_id=1, source_target_pairs={{0,1},{1,0},{2,3},{3,2},{4,5},{5,4},{6,7},{7,6},{8,9},{9,8},{10,11... | collective-permute-start | bytes 983048 | tf_op jit(solution)/shard_map/ppermute | solution.py:67
  32.4 13.3 %collective-permute-start.9 = (bf16[320,512]{1,0:T(8,128)(2,1)S(1)}, bf16[320,512]{1,0:T(8,128)(2,1)S(1)}, u32[]{:S(2)}, u32[]{:S(2)}) collective-permute-start(bf16[320,512]{1,0:T(8,128)(2,1)S(1)} %constant_dynamic-slice_fusion.28), channel_id=1, source_target_pairs={{0,1},{1,0},{2,3},{3,2},{4,5},{5,4},{6,7},{7,6},{8,9},{9,8},{10,11... | collective-permute-start | bytes 983048 | tf_op jit(solution)/shard_map/ppermute | solution.py:67
  35.3 21.3 %collective-permute-start.13 = (bf16[320,1024]{1,0:T(8,128)(2,1)S(1)}, bf16[320,1024]{1,0:T(8,128)(2,1)S(1)}, u32[]{:S(2)}, u32[]{:S(2)}) collective-permute-start(bf16[320,1024]{1,0:T(8,128)(2,1)S(1)} %constant_dynamic-slice_fusion.27), channel_id=1, source_target_pairs={{0,1},{1,0},{2,3},{3,2},{4,5},{5,4},{6,7},{7,6},{8,9},{9,8},{10,11... | collective-permute-start | bytes 1966088 | tf_op jit(solution)/shard_map/ppermute | solution.py:67
  45.7 19.6 %collective-permute-start.10 = (bf16[320,512]{1,0:T(8,128)(2,1)S(1)}, bf16[320,512]{1,0:T(8,128)(2,1)S(1)}, u32[]{:S(2)}, u32[]{:S(2)}) collective-permute-start(bf16[320,512]{1,0:T(8,128)(2,1)S(1)} %collective-permute-done.9.refs_9_.refs_13_), channel_id=1, source_target_pairs={{0,4},{2,6},{4,0},{6,2},{8,12},{10,14},{12,8},{14,10},{16,20},{18,... | collective-permute-start | bytes 983048 | tf_op jit(solution)/shard_map/ppermute | solution.py:61
  46.7 17.0 %collective-permute-start.15 = (bf16[256,640]{1,0:T(8,128)(2,1)S(1)}, bf16[256,640]{1,0:T(8,128)(2,1)}, u32[]{:S(2)}, u32[]{:S(2)}) collective-permute-start(bf16[256,640]{1,0:T(8,128)(2,1)S(1)} %constant_dynamic-slice_fusion.26), channel_id=1, source_target_pairs={{0,1},{1,0},{2,3},{3,2},{4,5},{5,4},{6,7},{7,6},{8,9},{9,8},{10,11... | collective-permute-start | bytes 983048 | tf_op jit(solution)/shard_map/ppermute | solution.py:67
  56.6 17.6 %collective-permute-start.14 = (bf16[320,1024]{1,0:T(8,128)(2,1)S(1)}, bf16[320,1024]{1,0:T(8,128)(2,1)S(1)}, u32[]{:S(2)}, u32[]{:S(2)}) collective-permute-start(bf16[320,1024]{1,0:T(8,128)(2,1)S(1)} %collective-permute-done.13.refs_14_.refs_18_), channel_id=1, source_target_pairs={{0,2},{2,0},{4,6},{6,4},{8,10},{10,8},{12,14},{14,12},{16,18},{18,... | collective-permute-start | bytes 1966088 | tf_op jit(solution)/shard_map/ppermute | solution.py:58
  57.5 9.9 %collective-permute-start.8 = (bf16[256,640]{1,0:T(8,128)(2,1)S(1)}, bf16[256,640]{1,0:T(8,128)(2,1)S(1)}, u32[]{:S(2)}, u32[]{:S(2)}) collective-permute-start(bf16[256,640]{1,0:T(8,128)(2,1)S(1)} %collective-permute-done.7.refs_6_.refs_10_), channel_id=1, source_target_pairs={{0,2},{2,0},{4,6},{6,4},{8,10},{10,8},{12,14},{14,12},{16,18},{18,... | collective-permute-start | bytes 983048 | tf_op jit(solution)/shard_map/ppermute | solution.py:58
  63.7 8.9 %collective-permute-start.16 = (bf16[256,640]{1,0:T(8,128)(2,1)}, bf16[256,640]{1,0:T(8,128)(2,1)}, u32[]{:S(2)}, u32[]{:S(2)}) collective-permute-start(bf16[256,640]{1,0:T(8,128)(2,1)} %collective-permute-done.15.refs_6_), channel_id=1, source_target_pairs={{0,4},{2,6},{4,0},{6,2},{8,12},{10,14},{12,8},{14,10},{16,20},{18,... | collective-permute-start | bytes 983048 | tf_op jit(solution)/shard_map/ppermute | solution.py:61
  64.2 9.9 %collective-permute-start.11 = (bf16[320,512]{1,0:T(8,128)(2,1)S(1)}, bf16[320,512]{1,0:T(8,128)(2,1)S(1)}, u32[]{:S(2)}, u32[]{:S(2)}) collective-permute-start(bf16[320,512]{1,0:T(8,128)(2,1)S(1)} %collective-permute-done.9.refs_9_.refs_13_), channel_id=1, source_target_pairs={{0,2},{2,0},{4,6},{6,4},{8,10},{10,8},{12,14},{14,12},{16,18},{18,... | collective-permute-start | bytes 983048 | tf_op jit(solution)/shard_map/ppermute | solution.py:58
  65.3 8.9 %collective-permute-start.12 = (bf16[320,512]{1,0:T(8,128)(2,1)S(1)}, bf16[320,512]{1,0:T(8,128)(2,1)S(1)}, u32[]{:S(2)}, u32[]{:S(2)}) collective-permute-start(bf16[320,512]{1,0:T(8,128)(2,1)S(1)} %collective-permute-done.10.refs_10_.refs_14_), channel_id=1, source_target_pairs={{0,2},{2,0},{4,6},{6,4},{8,10},{10,8},{12,14},{14,12},{16,18},{18,... | collective-permute-start | bytes 983048 | tf_op jit(solution)/shard_map/ppermute | solution.py:58
  67.3 19.0 %collective-permute-start.17 = (bf16[256,640]{1,0:T(8,128)(2,1)}, bf16[256,640]{1,0:T(8,128)(2,1)S(1)}, u32[]{:S(2)}, u32[]{:S(2)}) collective-permute-start(bf16[256,640]{1,0:T(8,128)(2,1)} %collective-permute-done.15.refs_6_), channel_id=1, source_target_pairs={{0,2},{2,0},{4,6},{6,4},{8,10},{10,8},{12,14},{14,12},{16,18},{18,... | collective-permute-start | bytes 983048 | tf_op jit(solution)/shard_map/ppermute | solution.py:58
  72.6 13.7 %collective-permute-start.18 = (bf16[256,640]{1,0:T(8,128)(2,1)}, bf16[256,640]{1,0:T(8,128)(2,1)S(1)}, u32[]{:S(2)}, u32[]{:S(2)}) collective-permute-start(bf16[256,640]{1,0:T(8,128)(2,1)} %collective-permute-done.16.refs_7_), channel_id=1, source_target_pairs={{0,2},{2,0},{4,6},{6,4},{8,10},{10,8},{12,14},{14,12},{16,18},{18,... | collective-permute-start | bytes 983048 | tf_op jit(solution)/shard_map/ppermute | solution.py:58
  100.3 22.7 %collective-permute-start.22 = (bf16[2,256,640]{2,1,0:T(8,128)(2,1)}, bf16[2,256,640]{2,1,0:T(8,128)(2,1)}, u32[]{:S(2)}, u32[]{:S(2)}) collective-permute-start(bf16[2,256,640]{2,1,0:T(8,128)(2,1)} %fusion), channel_id=1, source_target_pairs={{0,1},{1,0},{2,3},{3,2},{4,5},{5,4},{6,7},{7,6},{8,9},{9,8},{10,11... | collective-permute-start | bytes 1966088 | tf_op jit(solution)/shard_map/ppermute | solution.py:67
  111.5 16.5 %collective-permute-start.20 = (bf16[2,2,320,512]{3,2,1,0:T(8,128)(2,1)}, bf16[2,2,320,512]{3,2,1,0:T(8,128)(2,1)S(1)}, u32[]{:S(2)}, u32[]{:S(2)}) collective-permute-start(bf16[2,2,320,512]{3,2,1,0:T(8,128)(2,1)} %get-tuple-element.106), channel_id=1, source_target_pairs={{0,2},{2,0},{4,6},{6,4},{8,10},{10,8},{12,14},{14,12},{16,18},{18,... | collective-permute-start | bytes 3932168 | tf_op jit(solution)/shard_map/ppermute | solution.py:58
  112.0 17.2 %collective-permute-start.21 = (bf16[2,2,320,512]{3,2,1,0:T(8,128)(2,1)}, bf16[2,2,320,512]{3,2,1,0:T(8,128)(2,1)}, u32[]{:S(2)}, u32[]{:S(2)}) collective-permute-start(bf16[2,2,320,512]{3,2,1,0:T(8,128)(2,1)} %get-tuple-element.107), channel_id=1, source_target_pairs={{0,2},{2,0},{4,6},{6,4},{8,10},{10,8},{12,14},{14,12},{16,18},{18,... | collective-permute-start | bytes 3932168 | tf_op jit(solution)/shard_map/ppermute | solution.py:58
  125.0 18.9 %collective-permute-start.25 = (bf16[256,640]{1,0:T(8,128)(2,1)}, bf16[256,640]{1,0:T(8,128)(2,1)}, u32[]{:S(2)}, u32[]{:S(2)}) collective-permute-start(bf16[256,640]{1,0:T(8,128)(2,1)} %fusion.11), channel_id=1, source_target_pairs={{0,4},{2,6},{4,0},{6,2},{8,12},{10,14},{12,8},{14,10},{16,20},{18,... | collective-permute-start | bytes 983048 | tf_op jit(solution)/shard_map/ppermute | solution.py:61
  129.1 16.2 %collective-permute-start.26 = (bf16[2,320,512]{2,1,0:T(8,128)(2,1)}, bf16[2,320,512]{2,1,0:T(8,128)(2,1)}, u32[]{:S(2)}, u32[]{:S(2)}) collective-permute-start(bf16[2,320,512]{2,1,0:T(8,128)(2,1)} %fusion.1), channel_id=1, source_target_pairs={{0,1},{1,0},{2,3},{3,2},{4,5},{5,4},{6,7},{7,6},{8,9},{9,8},{10,11... | collective-permute-start | bytes 1966088 | tf_op jit(solution)/shard_map/ppermute | solution.py:67
  145.3 16.5 %collective-permute-start.27 = (bf16[2,2,352,384]{3,2,1,0:T(8,128)(2,1)}, bf16[2,2,352,384]{3,2,1,0:T(8,128)(2,1)S(1)}, u32[]{:S(2)}, u32[]{:S(2)}) collective-permute-start(bf16[2,2,352,384]{3,2,1,0:T(8,128)(2,1)} %get-tuple-element.125), channel_id=1, source_target_pairs={{0,2},{2,0},{4,6},{6,4},{8,10},{10,8},{12,14},{14,12},{16,18},{18,... | collective-permute-start | bytes 3244040 | tf_op jit(solution)/shard_map/ppermute | solution.py:58
  147.7 11.3 %collective-permute-start.23 = (bf16[256,640]{1,0:T(8,128)(2,1)S(1)}, bf16[256,640]{1,0:T(8,128)(2,1)S(1)}, u32[]{:S(2)}, u32[]{:S(2)}) collective-permute-start(bf16[256,640]{1,0:T(8,128)(2,1)S(1)} %get-tuple-element.163), channel_id=1, source_target_pairs={{1,0},{2,1},{3,2},{4,3},{5,4},{6,5},{7,6},{8,7},{9,8},{10,9},{11,1... | collective-permute-start | bytes 983048 | tf_op jit(solution)/shard_map/ppermute | solution.py:72
  149.7 10.0 %collective-permute-start.24 = (bf16[256,640]{1,0:T(8,128)(2,1)S(1)}, bf16[256,640]{1,0:T(8,128)(2,1)S(1)}, u32[]{:S(2)}, u32[]{:S(2)}) collective-permute-start(bf16[256,640]{1,0:T(8,128)(2,1)S(1)} %get-tuple-element.164), channel_id=1, source_target_pairs={{2,0},{3,1},{4,2},{5,3},{6,4},{7,5},{8,6},{9,7},{10,8},{11,9},{12,... | collective-permute-start | bytes 983048 | tf_op jit(solution)/shard_map/ppermute | solution.py:72
  152.9 20.1 %collective-permute-start.40 = (bf16[2,320,512]{2,1,0:T(8,128)(2,1)S(1)}, bf16[2,320,512]{2,1,0:T(8,128)(2,1)S(1)}, u32[]{:S(2)}, u32[]{:S(2)}) collective-permute-start(bf16[2,320,512]{2,1,0:T(8,128)(2,1)S(1)} %fusion.2), channel_id=1, source_target_pairs={{0,1},{1,0},{2,3},{3,2},{4,5},{5,4},{6,7},{7,6},{8,9},{9,8},{10,11... | collective-permute-start | bytes 1966088 | tf_op jit(solution)/shard_map/ppermute | solution.py:67
  161.9 13.6 %collective-permute-start.72 = (bf16[64,640]{1,0:T(8,128)(2,1)S(1)}, bf16[64,640]{1,0:T(8,128)(2,1)S(1)}, u32[]{:S(2)}, u32[]{:S(2)}) collective-permute-start(bf16[64,640]{1,0:T(8,128)(2,1)S(1)} %get-tuple-element.177), channel_id=1, source_target_pairs={{0,8},{2,10},{4,12},{6,14},{8,16},{10,18},{12,20},{14,22},{16,24},... | collective-permute-start | bytes 245768 | tf_op jit(solution)/shard_map/ppermute | solution.py:64
  163.2 12.2 %collective-permute-start.74 = (bf16[64,640]{1,0:T(8,128)(2,1)S(1)}, bf16[64,640]{1,0:T(8,128)(2,1)S(1)}, u32[]{:S(2)}, u32[]{:S(2)}) collective-permute-start(bf16[64,640]{1,0:T(8,128)(2,1)S(1)} %get-tuple-element.178), channel_id=1, source_target_pairs={{0,24},{2,26},{4,28},{6,30},{8,0},{10,2},{12,4},{14,6},{16,8},{18,... | collective-permute-start | bytes 245768 | tf_op jit(solution)/shard_map/ppermute | solution.py:64
  165.2 10.3 %collective-permute-start.73 = (bf16[64,640]{1,0:T(8,128)(2,1)S(1)}, bf16[64,640]{1,0:T(8,128)(2,1)S(1)}, u32[]{:S(2)}, u32[]{:S(2)}) collective-permute-start(bf16[64,640]{1,0:T(8,128)(2,1)S(1)} %get-tuple-element.179), channel_id=1, source_target_pairs={{0,16},{2,18},{4,20},{6,22},{8,24},{10,26},{12,28},{14,30},{16,0},... | collective-permute-start | bytes 245768 | tf_op jit(solution)/shard_map/ppermute | solution.py:64
  174.1 17.3 %collective-permute-start.41 = (bf16[2,128,640]{2,1,0:T(8,128)(2,1)S(1)}, bf16[2,128,640]{2,1,0:T(8,128)(2,1)S(1)}, u32[]{:S(2)}, u32[]{:S(2)}) collective-permute-start(bf16[2,128,640]{2,1,0:T(8,128)(2,1)S(1)} %copy-done.12), channel_id=1, source_target_pairs={{0,1},{1,0},{2,3},{3,2},{4,5},{5,4},{6,7},{7,6},{8,9},{9,8},{10,11... | collective-permute-start | bytes 983048 | tf_op jit(solution)/shard_map/ppermute | solution.py:67
  174.6 20.1 %collective-permute-start.52 = (bf16[320,512]{1,0:T(8,128)(2,1)S(1)}, bf16[320,512]{1,0:T(8,128)(2,1)S(1)}, u32[]{:S(2)}, u32[]{:S(2)}) collective-permute-start(bf16[320,512]{1,0:T(8,128)(2,1)S(1)} %fusion.8), channel_id=1, source_target_pairs={{0,4},{2,6},{4,0},{6,2},{8,12},{10,14},{12,8},{14,10},{16,20},{18,... | collective-permute-start | bytes 983048 | tf_op jit(solution)/shard_map/ppermute | solution.py:61
  178.0 9.4 %collective-permute-start.75 = (bf16[64,640]{1,0:T(8,128)(2,1)S(1)}, bf16[64,640]{1,0:T(8,128)(2,1)S(1)}, u32[]{:S(2)}, u32[]{:S(2)}) collective-permute-start(bf16[64,640]{1,0:T(8,128)(2,1)S(1)} %fusion.24), channel_id=1, source_target_pairs={{0,8},{2,10},{4,12},{6,14},{8,16},{10,18},{12,20},{14,22},{16,24},... | collective-permute-start | bytes 245768 | tf_op jit(solution)/shard_map/ppermute | solution.py:64
  179.5 10.7 %collective-permute-start.62 = (bf16[320,512]{1,0:T(8,128)(2,1)S(1)}, bf16[320,512]{1,0:T(8,128)(2,1)S(1)}, u32[]{:S(2)}, u32[]{:S(2)}) collective-permute-start(bf16[320,512]{1,0:T(8,128)(2,1)S(1)} %fusion.5), channel_id=1, source_target_pairs={{0,4},{2,6},{4,0},{6,2},{8,12},{10,14},{12,8},{14,10},{16,20},{18,... | collective-permute-start | bytes 983048 | tf_op jit(solution)/shard_map/ppermute | solution.py:61
  185.6 32.4 %collective-permute-start.28 = (bf16[2,352,384]{2,1,0:T(8,128)(2,1)S(1)}, bf16[2,352,384]{2,1,0:T(8,128)(2,1)S(1)}, u32[]{:S(2)}, u32[]{:S(2)}) collective-permute-start(bf16[2,352,384]{2,1,0:T(8,128)(2,1)S(1)} %fusion.12), channel_id=1, source_target_pairs={{0,1},{1,0},{2,3},{3,2},{4,5},{5,4},{6,7},{7,6},{8,9},{9,8},{10,11... | collective-permute-start | bytes 1622024 | tf_op jit(solution)/shard_map/ppermute | solution.py:67
  187.6 58.9 %collective-permute-start.79 = (bf16[256,640]{1,0:T(8,128)(2,1)S(1)}, bf16[256,640]{1,0:T(8,128)(2,1)S(1)}, u32[]{:S(2)}, u32[]{:S(2)}) collective-permute-start(bf16[256,640]{1,0:T(8,128)(2,1)S(1)} %bitcast.188), channel_id=1, source_target_pairs={{0,2},{2,0},{4,6},{6,4},{8,10},{10,8},{12,14},{14,12},{16,18},{18,... | collective-permute-start | bytes 983048 | tf_op jit(solution)/shard_map/ppermute | solution.py:58
  210.4 21.2 %collective-permute-start.78 = (bf16[256,640]{1,0:T(8,128)(2,1)S(1)}, bf16[256,640]{1,0:T(8,128)(2,1)S(1)}, u32[]{:S(2)}, u32[]{:S(2)}) collective-permute-start(bf16[256,640]{1,0:T(8,128)(2,1)S(1)} %bitcast.189), channel_id=1, source_target_pairs={{0,4},{2,6},{4,0},{6,2},{8,12},{10,14},{12,8},{14,10},{16,20},{18,... | collective-permute-start | bytes 983048 | tf_op jit(solution)/shard_map/ppermute | solution.py:61
  230.0 7.9 %collective-permute-start.58 = (bf16[80,512]{1,0:T(8,128)(2,1)S(1)}, bf16[80,512]{1,0:T(8,128)(2,1)S(1)}, u32[]{:S(2)}, u32[]{:S(2)}) collective-permute-start(bf16[80,512]{1,0:T(8,128)(2,1)S(1)} %fusion.30), channel_id=1, source_target_pairs={{0,24},{2,26},{4,28},{6,30},{8,0},{10,2},{12,4},{14,6},{16,8},{18,... | collective-permute-start | bytes 245768 | tf_op jit(solution)/shard_map/ppermute | solution.py:64
  230.8 8.1 %collective-permute-start.57 = (bf16[80,512]{1,0:T(8,128)(2,1)S(1)}, bf16[80,512]{1,0:T(8,128)(2,1)S(1)}, u32[]{:S(2)}, u32[]{:S(2)}) collective-permute-start(bf16[80,512]{1,0:T(8,128)(2,1)S(1)} %fusion.30), channel_id=1, source_target_pairs={{0,16},{2,18},{4,20},{6,22},{8,24},{10,26},{12,28},{14,30},{16,0},... | collective-permute-start | bytes 245768 | tf_op jit(solution)/shard_map/ppermute | solution.py:64
  230.8 9.3 %collective-permute-start.56 = (bf16[80,512]{1,0:T(8,128)(2,1)S(1)}, bf16[80,512]{1,0:T(8,128)(2,1)S(1)}, u32[]{:S(2)}, u32[]{:S(2)}) collective-permute-start(bf16[80,512]{1,0:T(8,128)(2,1)S(1)} %fusion.30), channel_id=1, source_target_pairs={{0,8},{2,10},{4,12},{6,14},{8,16},{10,18},{12,20},{14,22},{16,24},... | collective-permute-start | bytes 245768 | tf_op jit(solution)/shard_map/ppermute | solution.py:64
  231.6 48.2 %collective-permute-start.70 = (bf16[320,512]{1,0:T(8,128)(2,1)S(1)}, bf16[320,512]{1,0:T(8,128)(2,1)S(1)}, u32[]{:S(2)}, u32[]{:S(2)}) collective-permute-start(bf16[320,512]{1,0:T(8,128)(2,1)S(1)} %bitcast.184), channel_id=1, source_target_pairs={{0,2},{2,0},{4,6},{6,4},{8,10},{10,8},{12,14},{14,12},{16,18},{18,... | collective-permute-start | bytes 983048 | tf_op jit(solution)/shard_map/ppermute | solution.py:58
  237.9 10.8 %collective-permute-start.80 = (bf16[256,640]{1,0:T(8,128)(2,1)S(1)}, bf16[256,640]{1,0:T(8,128)(2,1)S(1)}, u32[]{:S(2)}, u32[]{:S(2)}) collective-permute-start(bf16[256,640]{1,0:T(8,128)(2,1)S(1)} %collective-permute-done.78), channel_id=1, source_target_pairs={{0,2},{2,0},{4,6},{6,4},{8,10},{10,8},{12,14},{14,12},{16,18},{18,... | collective-permute-start | bytes 983048 | tf_op jit(solution)/shard_map/ppermute | solution.py:58
  240.1 10.8 %collective-permute-start.49 = (bf16[128,640]{1,0:T(8,128)(2,1)S(1)}, bf16[128,640]{1,0:T(8,128)(2,1)S(1)}, u32[]{:S(2)}, u32[]{:S(2)}) collective-permute-start(bf16[128,640]{1,0:T(8,128)(2,1)S(1)} %bitcast.201), channel_id=1, source_target_pairs={{0,4},{2,6},{4,0},{6,2},{8,12},{10,14},{12,8},{14,10},{16,20},{18,... | collective-permute-start | bytes 491528 | tf_op jit(solution)/shard_map/ppermute | solution.py:61
  246.4 10.5 %collective-permute-start.32 = (bf16[88,384]{1,0:T(8,128)(2,1)S(1)}, bf16[88,384]{1,0:T(8,128)(2,1)S(1)}, u32[]{:S(2)}, u32[]{:S(2)}) collective-permute-start(bf16[88,384]{1,0:T(8,128)(2,1)S(1)} %get-tuple-element.199), channel_id=1, source_target_pairs={{0,24},{2,26},{4,28},{6,30},{8,0},{10,2},{12,4},{14,6},{16,8},{18,... | collective-permute-start | bytes 202760 | tf_op jit(solution)/shard_map/ppermute | solution.py:64
  248.7 8.3 %collective-permute-start.31 = (bf16[88,384]{1,0:T(8,128)(2,1)S(1)}, bf16[88,384]{1,0:T(8,128)(2,1)S(1)}, u32[]{:S(2)}, u32[]{:S(2)}) collective-permute-start(bf16[88,384]{1,0:T(8,128)(2,1)S(1)} %get-tuple-element.200), channel_id=1, source_target_pairs={{0,16},{2,18},{4,20},{6,22},{8,24},{10,26},{12,28},{14,30},{16,0},... | collective-permute-start | bytes 202760 | tf_op jit(solution)/shard_map/ppermute | solution.py:64
  250.8 11.7 %collective-permute-start.69 = (bf16[320,512]{1,0:T(8,128)(2,1)S(1)}, bf16[320,512]{1,0:T(8,128)(2,1)S(1)}, u32[]{:S(2)}, u32[]{:S(2)}) collective-permute-start(bf16[320,512]{1,0:T(8,128)(2,1)S(1)} %bitcast.185), channel_id=1, source_target_pairs={{0,4},{2,6},{4,0},{6,2},{8,12},{10,14},{12,8},{14,10},{16,20},{18,... | collective-permute-start | bytes 983048 | tf_op jit(solution)/shard_map/ppermute | solution.py:61
  262.5 17.4 %collective-permute-start.60 = (bf16[320,512]{1,0:T(8,128)(2,1)S(1)}, bf16[320,512]{1,0:T(8,128)(2,1)S(1)}, u32[]{:S(2)}, u32[]{:S(2)}) collective-permute-start(bf16[320,512]{1,0:T(8,128)(2,1)S(1)} %bitcast.186), channel_id=1, source_target_pairs={{0,2},{2,0},{4,6},{6,4},{8,10},{10,8},{12,14},{14,12},{16,18},{18,... | collective-permute-start | bytes 983048 | tf_op jit(solution)/shard_map/ppermute | solution.py:58
  263.8 9.3 %collective-permute-start.59 = (bf16[320,512]{1,0:T(8,128)(2,1)S(1)}, bf16[320,512]{1,0:T(8,128)(2,1)S(1)}, u32[]{:S(2)}, u32[]{:S(2)}) collective-permute-start(bf16[320,512]{1,0:T(8,128)(2,1)S(1)} %bitcast.187), channel_id=1, source_target_pairs={{0,4},{2,6},{4,0},{6,2},{8,12},{10,14},{12,8},{14,10},{16,20},{18,... | collective-permute-start | bytes 983048 | tf_op jit(solution)/shard_map/ppermute | solution.py:61
  264.1 15.8 %collective-permute-start.71 = (bf16[320,512]{1,0:T(8,128)(2,1)S(1)}, bf16[320,512]{1,0:T(8,128)(2,1)S(1)}, u32[]{:S(2)}, u32[]{:S(2)}) collective-permute-start(bf16[320,512]{1,0:T(8,128)(2,1)S(1)} %collective-permute-done.69), channel_id=1, source_target_pairs={{0,2},{2,0},{4,6},{6,4},{8,10},{10,8},{12,14},{14,12},{16,18},{18,... | collective-permute-start | bytes 983048 | tf_op jit(solution)/shard_map/ppermute | solution.py:58
  267.9 11.0 %collective-permute-start.36 = (bf16[352,384]{1,0:T(8,128)(2,1)S(1)}, bf16[352,384]{1,0:T(8,128)(2,1)S(1)}, u32[]{:S(2)}, u32[]{:S(2)}) collective-permute-start(bf16[352,384]{1,0:T(8,128)(2,1)S(1)} %bitcast.197), channel_id=1, source_target_pairs={{0,4},{2,6},{4,0},{6,2},{8,12},{10,14},{12,8},{14,10},{16,20},{18,... | collective-permute-start | bytes 811016 | tf_op jit(solution)/shard_map/ppermute | solution.py:61
  (60 other events, 390.9 us)

commit v4 on v3

--- a/solution.py
+++ b/solution.py
@@ -34,6 +34,7 @@
         self.seq = lax.axis_size("seq")
         self.fsdp = lax.axis_size("fsdp")
         self.outer = self.seq // 4
+        self.bits = self.outer.bit_length() - 1
         index = lax.axis_index("seq").astype(jnp.int32)
         fsdp_at = lax.axis_index("fsdp").astype(jnp.int32)
         outer_at = lax.shift_right_logical(index, 2)
@@ -44,15 +45,15 @@
                 mid_at,
                 fsdp_at,
                 core_at * 2 + mid_at,
-                tuple(wrapped(outer_at + by, self.outer) for by in range(self.outer)),
-                tuple(wrapped(outer_at - by + self.outer, self.outer) for by in range(self.outer)),
+                tuple(lax.shift_right_logical(outer_at, bit) & 1 for bit in range(self.bits)),
+                tuple(1 - (lax.shift_right_logical(outer_at, bit) & 1) for bit in range(self.bits)),
                 tuple(wrapped(fsdp_at + by, self.fsdp) for by in range(self.fsdp)),
                 tuple(wrapped(fsdp_at - by + self.fsdp, self.fsdp) for by in range(self.fsdp)),
                 jnp.stack([core_at, mid_at, fsdp_at]),
             )
         )
         self.core_at, self.mid_at, self.fsdp_at, self.quarter_at = scalars[:4]
-        self.outer_ahead, self.outer_behind, self.fsdp_ahead, self.fsdp_behind, self.vector = scalars[4:]
+        self.bit_at, self.bit_off, self.fsdp_ahead, self.fsdp_behind, self.vector = scalars[4:]
 
     def core_swap(self, array):
         return lax.ppermute(array, "seq", [(i, i ^ 1) for i in range(self.seq)])
@@ -60,8 +61,8 @@
     def mid_swap(self, array):
         return lax.ppermute(array, "seq", [(i, i ^ 2) for i in range(self.seq)])
 
-    def outer_shift(self, array, by):
-        return lax.ppermute(array, "seq", [(i, (i + 4 * by) % self.seq) for i in range(self.seq)])
+    def outer_swap(self, array, bit):
+        return lax.ppermute(array, "seq", [(i, i ^ (4 << bit)) for i in range(self.seq)])
 
     def fsdp_shift(self, array, by):
         return lax.ppermute(array, "fsdp", [(i, (i + by) % self.fsdp) for i in range(self.fsdp)])
@@ -89,8 +90,15 @@
     place = here.quarter_at if ways == 4 else here.core_at
     if len(shards) == 1:
         return lax.dynamic_slice_in_dim(shards[0], place * size, size, axis, allow_negative_indices=False)
-    joined = jnp.concatenate(shards, axis)
-    parts = [lax.slice_in_dim(joined, i * size, (i + 1) * size, axis=axis) for i in range(ways)]
+    parts = []
+    for i in range(ways):
+        pieces, start = [], 0
+        for shard in shards:
+            low, high = max(i * size - start, 0), min((i + 1) * size - start, shard.shape[axis])
+            if low < high:
+                pieces.append(lax.slice_in_dim(shard, low, high, axis=axis))
+            start += shard.shape[axis]
+        parts.append(jnp.concatenate(pieces, axis))
     return functools.reduce(lambda rest, i: jnp.where(place == i, parts[i], rest), range(1, ways), parts[0])
 
 
@@ -259,7 +267,7 @@
     groups = (
         place_copies(out_w[:1], out_w[1:], out_full, out_sems, at, 0, 2),
         place_copies(gate_w[:1], gate_w[1:], gate_full, gate_sems, at, 1, 4),
-        place_copies(up_w[:1], up_w[1:], up_full, up_sems, at, 1, 2),
+        place_copies(up_w[:1], up_w[1:], up_full, up_sems, at, 1, 4),
     )
     for group in groups:
         for copy in group:
@@ -303,12 +311,21 @@
                 yield c, f, x, core, row, mid
 
 
+def column_blocks(at, fsdp, left_t, right, keep, send):
+    tall, wide = left_t.shape[0] // fsdp, keep.shape[3]
+    for c, f, x, core, row, mid in relative_blocks(at, fsdp):
+        cut = pl.ds(multiple((core * 2 + mid) * wide, 128), wide)
+        left = left_t[pl.ds(multiple(row * tall, 16), tall), :]
+        target = keep if c == 0 else send
+        target[f, x, :tall, :] = dot(left, right[:, cut]).astype(BF16)
+
+
 def down_kernel(n_down, fsdp, *refs):
     at, mixed, residual, cotangent, gain_out = refs[:5]
     down_w = refs[5 : 5 + n_down]
     layer_out, d_down, grad_gain, keep, send = refs[5 + n_down : 10 + n_down]
     down_full, mixed_t, sems = refs[10 + n_down :]
-    copies = place_copies(down_w[:1], down_w[1:], down_full, sems, at, 0, 4)
+    copies = place_copies(down_w[:1], down_w[1:], down_full, sems, at, 0, 2)
     for copy in copies:
         copy.start()
     mixed_t[...] = mixed[...].T
@@ -331,9 +348,9 @@
 def gate_back_kernel(n_down, fsdp, *refs):
     at, d_down, gelu_out, gate_slope, ffn_in = refs[:5]
     down_w = refs[5 : 5 + n_down]
-    d_gate, d_up, gate_keep, gate_send, up_keep, up_send = refs[5 + n_down : 11 + n_down]
-    down_full, ffn_t, sems = refs[11 + n_down :]
-    copies = place_copies(down_w[:1], down_w[1:], down_full, sems, at, 0, 4)
+    d_gate, d_up, ffn_t, keep, send = refs[5 + n_down : 10 + n_down]
+    down_full, sems = refs[10 + n_down :]
+    copies = place_copies(down_w[:1], down_w[1:], down_full, sems, at, 0, 2)
     for copy in copies:
         copy.start()
     ffn_t[...] = ffn_in[...].T
@@ -349,12 +366,11 @@
         return 0
 
     lax.fori_loop(0, d_gate.shape[1] // width, step, 0)
-    tall, wide = gate_keep.shape[2:]
-    for source, targets in ((d_gate, (gate_keep, gate_send)), (d_up, (up_keep, up_send))):
-        for c, f, x, core, row, mid in relative_blocks(at, fsdp):
-            cut = pl.ds(multiple((core * 2 + mid) * wide, 128), wide)
-            left = ffn_t[pl.ds(multiple(row * tall, 16), tall), :]
-            targets[c][f, x] = dot(left, source[:, cut]).astype(BF16)
+    column_blocks(at, fsdp, ffn_t, d_gate, keep, send)
+
+
+def up_back_kernel(fsdp, at, ffn_t, d_up, keep, send):
+    column_blocks(at, fsdp, ffn_t, d_up, keep, send)
 
 
 def middle_kernel(n_out, n_gate, n_up, fsdp, heads, *refs):
@@ -370,7 +386,7 @@
     out_full, gate_full, up_full, att_t, out_sems, gate_sems, up_sems = refs[6:]
     groups = (
         place_copies(gate_w[:1], gate_w[1:], gate_full, gate_sems, at, 1, 4),
-        place_copies(up_w[:1], up_w[1:], up_full, up_sems, at, 1, 2),
+        place_copies(up_w[:1], up_w[1:], up_full, up_sems, at, 1, 4),
         place_copies(out_w[:1], out_w[1:], out_full, out_sems, at, 0, 2),
     )
     for group in groups:
@@ -405,27 +421,11 @@
         target[f, x] = dot(att_t[pl.ds(start, block), :], d_proj).astype(BF16)
 
 
-def last_kernel(n_qkv, n_tok, fsdp, heads, *refs):
-    (
-        at, d_residual, d_att,
-        q_raw, k_raw, q_st, keys, values, probs, cosine, sine, gain_q, gain_k, gain_in, normed, g_ffn, g_attn, g_out,
-    ) = refs[:18]
-    toks = refs[18 : 18 + n_tok]
-    refs = refs[18 + n_tok :]
-    qkv_w, refs = refs[:n_qkv], refs[n_qkv:]
-    grad_tokens, d_halo, keep, send = refs[:4]
-    w_full, normed_t, d_scores, d_q, d_k, d_v, d_qkv, gain_rows, qkv_sems = refs[4:]
-    copies = place_copies(qkv_w[:3], qkv_w[3:], w_full, qkv_sems, at, 1, 4)
-    for copy in copies:
-        copy.start()
-    normed_t[...] = normed[...].T
-    rows = toks[0].shape[0]
-    halo = (n_tok - 1) * rows
+def attend_back_kernel(halo, heads, d_att, q_st, keys, values, probs, d_q, d_k, d_v, d_scores):
+    rows = d_q.shape[0]
     dim = keys.shape[1]
-    half = dim // 2
     blocks = rows // QBLOCK
     span = WINDOW + QBLOCK
-    tall, wide = normed_t.shape[0] // fsdp, keep.shape[3]
     scale = dim ** (-0.5)
     d_k[...] = jnp.zeros(d_k.shape, F32)
     d_v[...] = jnp.zeros(d_v.shape, F32)
@@ -445,6 +445,26 @@
         d_k[here, :] += dot_tn(d_scores[...], q_st[stack, :])
         d_v[here, :] += dot_tn(probs[stack, :], d_att[stack, :])
 
+
+def last_kernel(n_qkv, n_tok, fsdp, heads, *refs):
+    (
+        at, d_residual, d_q, d_k, d_v,
+        q_raw, k_raw, cosine, sine, gain_q, gain_k, gain_in, normed, g_ffn, g_attn, g_out,
+    ) = refs[:16]
+    toks = refs[16 : 16 + n_tok]
+    refs = refs[16 + n_tok :]
+    qkv_w, refs = refs[:n_qkv], refs[n_qkv:]
+    grad_tokens, d_halo, keep, send = refs[:4]
+    w_full, normed_t, d_qkv, gain_rows, qkv_sems = refs[4:]
+    copies = place_copies(qkv_w[:3], qkv_w[3:], w_full, qkv_sems, at, 1, 4)
+    for copy in copies:
+        copy.start()
+    normed_t[...] = normed[...].T
+    rows = toks[0].shape[0]
+    halo = (n_tok - 1) * rows
+    dim = k_raw.shape[1]
+    half = dim // 2
+    tall, wide = normed_t.shape[0] // fsdp, keep.shape[3]
     def turned_back(u, g, dz, cos, sin):
         first, second = dz[:, :half], dz[:, half:]
         dz = jnp.concatenate([first * cos + second * sin, second * cos - first * sin], axis=1)
@@ -465,11 +485,7 @@
         total_k += dg
         d_qkv[here, heads * dim : (heads + 1) * dim] = du.astype(BF16)
         d_qkv[here, (heads + 1) * dim :] = d_v[here, :].astype(BF16)
-    for c, f, x, core, row, mid in relative_blocks(at, fsdp):
-        cut = pl.ds(multiple((core * 2 + mid) * wide, 128), wide)
-        left = normed_t[pl.ds(multiple(row * tall, 16), tall), :]
-        target = keep if c == 0 else send
-        target[f, x, :tall, :] = dot(left, d_qkv[:, cut]).astype(BF16)
+    column_blocks(at, fsdp, normed_t, d_qkv, keep, send)
     for copy in copies:
         copy.wait()
     total_in = jnp.zeros(gain_in.shape, F32)
@@ -509,6 +525,7 @@
     def __init__(self, here, keep, send):
         self.here, self.keep = here, keep
         self.other = here.core_swap(send)
+        self.sums = []
 
     def over_fsdp(self, *earlier):
         here = self.here
@@ -516,20 +533,34 @@
         self.arrived = [here.fsdp_shift(after(part, *earlier), by + 1) for by, part in enumerate(parts)]
 
     def over_mid(self, *earlier):
+        self.arrived = [after(a, *earlier) for a in self.arrived]
         terms = [self.keep[0, 1], self.other[0, 1]] + [a[1] for a in self.arrived]
-        self.across = self.here.mid_swap(after(add(*terms).astype(BF16), *earlier))
-
-    def finish(self, *earlier):
+        self.across = self.here.mid_swap(add(*terms).astype(BF16))
+
+    def gather_sums(self, bit, *earlier):
         here = self.here
-        n, w = self.across.shape
-        terms = [self.keep[0, 0], self.other[0, 0]] + [a[0] for a in self.arrived] + [self.across]
-        mine = after(add(*terms).astype(BF16), *earlier).reshape(here.outer, n // here.outer, w)
-        terms = [pick(mine, here.outer_ahead[0])]
-        for by in range(1, here.outer):
-            terms.append(here.outer_shift(pick(mine, here.outer_ahead[by]), by))
-        own = add(*terms).astype(BF16)
-        block = ordered([own] + [here.outer_shift(own, by) for by in range(1, here.outer)], here.outer_behind)
-        block = block.reshape(n, w)
+        if bit == 0:
+            self.across = after(self.across, *earlier)
+            terms = [self.keep[0, 0], self.other[0, 0]] + [a[0] for a in self.arrived] + [self.across]
+        else:
+            terms = [after(self.sums[-1], *earlier)]
+        n, w = terms[0].shape
+        halves = [term.reshape(2, n // 2, w) for term in terms]
+        off = add(*[pick(half, here.bit_off[bit]) for half in halves]).astype(BF16)
+        came = here.outer_swap(off, bit)
+        self.sums.append(add(*[pick(half, here.bit_at[bit]) for half in halves], came).astype(BF16))
+
+    def finish(self, *earlier, last=()):
+        here = self.here
+        for bit in range(len(self.sums), here.bits):
+            self.gather_sums(bit, *earlier)
+        block = self.sums[-1]
+        for bit in reversed(range(here.bits)):
+            n, w = block.shape
+            both = [block, here.outer_swap(block, bit)]
+            low, high = jnp.concatenate(both), jnp.concatenate(both[::-1])
+            block = jnp.where(here.bit_at[bit] == 0, low, high)
+        block = after(block, *last)
         across = here.mid_swap(block)
         return [[block, across], [here.core_swap(block), here.core_swap(across)]]
 
@@ -570,15 +601,14 @@
     gain_in, gain_q, gain_k, gain_attn, gain_ffn, gain_out = (
         gain_rows[:, cuts[i] : cuts[i + 1]].reshape(1, -1) for i in range(6)
     )
-    toks = [linear_shift(tokens, by) for by in range(hops, 0, -1)] + [tokens]
     qkv_w = [w_query, w_key, w_value]
-    qkv_w += on_chips(here, over_links(here, own_part(here, qkv_w, 1, 4)), 4)
-    out_part = after(own_part(here, [w_out], 0, 2), *toks[:-1])
-    out_arrived = over_links(here, out_part)
-    gate_part = after(own_part(here, [w_gate], 1, 4), qkv_w[3])
-    gate_arrived = over_links(here, gate_part)
-    up_part = after(own_part(here, [w_up], 1, 2), out_arrived[0])
-    up_arrived = over_links(here, up_part)
+    qkv_part = own_part(here, qkv_w, 1, 4)
+    tokens_out = after(tokens, qkv_part)
+    toks = [linear_shift(tokens_out, by) for by in range(hops, 0, -1)] + [tokens]
+    qkv_w += on_chips(here, over_links(here, qkv_part), 4)
+    out_arrived = over_links(here, after(own_part(here, [w_out], 0, 2), *toks[:-1]))
+    gate_arrived = over_links(here, after(own_part(here, [w_gate], 1, 4), qkv_w[3]))
+    up_arrived = over_links(here, after(own_part(here, [w_up], 1, 4), out_arrived[0]))
 
     all_positions = jnp.concatenate([positions[0] - halo + jnp.arange(halo, dtype=jnp.int32), positions])
     frequency = ROPE_BASE ** (-(jnp.arange(dim // 2, dtype=F32) * 2.0 / dim))
@@ -610,11 +640,10 @@
         name="attend",
     )(at, *toks, positions[:, None], cosine, sine, gain_in, gain_q, gain_k, *qkv_w)
 
-    down_part = after(own_part(here, [w_down], 0, 4), attended)
+    down_arrived = over_links(here, after(own_part(here, [w_down], 0, 2), attended))
     out_w = [w_out] + on_chips(here, [after(a, attended) for a in out_arrived], 2)
     gate_w = [w_gate] + on_chips(here, [after(a, attended) for a in gate_arrived], 4)
-    up_w = [w_up] + on_chips(here, [after(a, attended) for a in up_arrived], 2)
-    down_w = [w_down] + on_chips(here, over_links(here, down_part), 4)
+    up_w = [w_up] + on_chips(here, [after(a, attended) for a in up_arrived], 4)
     projected, residual, ffn_in, mixed, gelu_out, gate_slope = pl.pallas_call(
         functools.partial(gate_kernel, len(out_w), len(gate_w), len(up_w)),
         out_shape=(
@@ -640,6 +669,7 @@
         name="gate",
     )(at, attended, tokens, gain_attn, gain_ffn, *out_w, *gate_w, *up_w)
 
+    down_w = [w_down] + on_chips(here, [after(a, mixed) for a in down_arrived], 2)
     down_block = w_down.shape[0] // 4
     down_shape = shape((fsdp, 2, down_block, width), BF16)
     layer_out, d_down, g_ffn_out, down_keep, down_send = pl.pallas_call(
@@ -664,37 +694,44 @@
     )(at, mixed, residual, cotangent, gain_out, *down_w)
 
     down_sum = Chunk(here, down_keep, down_send)
-    d_down = after(d_down, down_sum.other)
     gate_shape = shape((fsdp, 2, w_gate.shape[0], hidden // 4), BF16)
-    d_gate, d_up, gate_keep, gate_send, up_keep, up_send = pl.pallas_call(
+    d_gate, d_up, ffn_t, gate_keep, gate_send = pl.pallas_call(
         functools.partial(gate_back_kernel, len(down_w), fsdp),
         out_shape=(
             shape((rows, hidden), BF16),
             shape((rows, hidden), BF16),
-            gate_shape,
-            gate_shape,
+            shape((width, rows), BF16),
             gate_shape,
             gate_shape,
         ),
         in_specs=[SMEM] + [VMEM] * 4 + [ANY] * len(down_w),
-        out_specs=(VMEM,) * 6,
+        out_specs=(VMEM,) * 5,
         scratch_shapes=[
             pltpu.VMEM((hidden, width), BF16),
-            pltpu.VMEM((width, rows), BF16),
             pltpu.SemaphoreType.DMA((len(down_w),)),
         ],
         compiler_params=params(),
         cost_estimate=cost(6e9, 3 * weight_bytes),
         name="gate_back",
     )(at, d_down, gelu_out, gate_slope, ffn_in, *down_w)
+    gate_sum = Chunk(here, gate_keep, gate_send)
+    up_keep, up_send = pl.pallas_call(
+        functools.partial(up_back_kernel, fsdp),
+        out_shape=(gate_shape, gate_shape),
+        in_specs=[SMEM] + [VMEM] * 2,
+        out_specs=(VMEM,) * 2,
+        compiler_params=params(),
+        cost_estimate=cost(6e9, 3 * weight_bytes),
+        name="up_back",
+    )(at, ffn_t, after(d_up, down_sum.other))
+    up_sum = Chunk(here, up_keep, up_send)
+    down_sum.over_fsdp(d_gate)
+    d_gate = after(d_gate, gate_sum.other, up_keep)
 
     qkv_cols = query_cols + 2 * dim
     last_wide = qkv_cols // 4
     shard_rows = w_query.shape[0]
     last_shape = shape((fsdp, 2, shard_rows + GAIN_ROWS, last_wide), BF16)
-    gate_sum = Chunk(here, gate_keep, gate_send)
-    up_sum = Chunk(here, up_keep, up_send)
-    down_sum.over_fsdp()
     out_shape = shape((fsdp, 2, w_out.shape[0] // 4, width), BF16)
     d_residual, g_ffn, g_attn, d_att, out_keep, out_send = pl.pallas_call(
         functools.partial(middle_kernel, len(out_w), len(gate_w), len(up_w), fsdp, heads),
@@ -722,10 +759,24 @@
         name="middle",
     )(at, d_gate, d_up, residual, projected, cotangent, gain_ffn, gain_attn, attended, *out_w, *gate_w, *up_w)
 
-    gate_sum.over_fsdp()
     out_sum = Chunk(here, out_keep, out_send)
-    d_att = after(d_att, gate_sum.other, up_sum.other, *down_sum.arrived)
-    down_sum.over_mid()
+    gate_sum.over_fsdp(up_keep)
+    d_q, d_k, d_v = pl.pallas_call(
+        functools.partial(attend_back_kernel, halo, heads),
+        out_shape=(shape((rows, query_cols), F32), shape((every, dim), F32), shape((every, dim), F32)),
+        in_specs=[VMEM] * 5,
+        out_specs=(VMEM,) * 3,
+        scratch_shapes=[pltpu.VMEM((heads * QBLOCK, span), BF16)],
+        compiler_params=params(),
+        cost_estimate=cost(6e9, 3 * weight_bytes),
+        name="attend_back",
+    )(after(d_att, up_sum.other, *down_sum.arrived), q_st, keys, values, probs)
+    down_sum.over_mid(g_ffn)
+    up_sum.over_fsdp(g_ffn)
+    d_k_token = d_k
+    d_q = after(d_q, out_sum.other, down_sum.across, *gate_sum.arrived)
+    gate_sum.over_mid(d_k_token)
+    out_sum.over_fsdp(d_k_token)
     grad_tokens, d_halo, last_keep, last_send = pl.pallas_call(
         functools.partial(last_kernel, len(qkv_w), n_tok, fsdp, heads),
         out_shape=(
@@ -734,15 +785,11 @@
             last_shape,
             last_shape,
         ),
-        in_specs=[SMEM] + [VMEM] * (17 + n_tok) + [ANY] * len(qkv_w),
+        in_specs=[SMEM] + [VMEM] * (15 + n_tok) + [ANY] * len(qkv_w),
         out_specs=(VMEM,) * 4,
         scratch_shapes=[
             pltpu.VMEM((width, qkv_cols), BF16),
             pltpu.VMEM((width, every), BF16),
-            pltpu.VMEM((heads * QBLOCK, span), BF16),
-            pltpu.VMEM((rows, query_cols), F32),
-            pltpu.VMEM((every, dim), F32),
-            pltpu.VMEM((every, dim), F32),
             pltpu.VMEM((every, qkv_cols), BF16),
             pltpu.VMEM((GAIN_ROWS, last_wide), F32),
             pltpu.SemaphoreType.DMA((len(qkv_w),)),
@@ -751,30 +798,28 @@
         cost_estimate=cost(15e9, 4 * weight_bytes),
         name="last",
     )(
-        at, d_residual, d_att,
-        q_raw, k_raw, q_st, keys, values, probs, cosine, sine, gain_q, gain_k, gain_in, normed,
-        g_ffn, g_attn, g_ffn_out, *toks, *qkv_w,
+        at, d_residual, d_q, d_k, d_v,
+        q_raw, k_raw, cosine, sine, gain_q, gain_k, gain_in, normed, g_ffn, g_attn, g_ffn_out, *toks, *qkv_w,
     )
 
-    last_sum = Chunk(here, last_keep, after(last_send, down_sum.across, *gate_sum.arrived))
-    up_sum.over_fsdp()
-    gate_sum.over_mid(last_sum.other)
+    last_sum = Chunk(here, last_keep, last_send)
     last_sum.over_fsdp()
-    out_sum.over_fsdp(last_sum.other, *up_sum.arrived)
-    down_blocks = by_place(here, down_sum.finish(last_sum.other))
-    up_sum.over_mid(last_sum.other)
+    arrived = last_sum.other
+    down_blocks = by_place(here, down_sum.finish(arrived))
+    gate_blocks = by_place(here, gate_sum.finish(arrived, last=last_sum.arrived))
+    up_sum.over_mid(arrived)
+    out_sum.over_mid(arrived)
+    up_blocks = by_place(here, up_sum.finish())
+    out_blocks = by_place(here, out_sum.finish())
     last_sum.over_mid()
-    gate_blocks = by_place(here, gate_sum.finish(*last_sum.arrived))
-    out_sum.over_mid()
-    up_blocks = by_place(here, up_sum.finish(*out_sum.arrived))
     last_blocks = last_sum.finish()
     total_gains = last_blocks[0][0][shard_rows:, :LANES].astype(F32)
     last_blocks = by_place(here, last_blocks)
-    out_blocks = by_place(here, out_sum.finish())
 
     for by in range(1, hops + 1):
         start = halo - by * rows
-        grad_tokens = grad_tokens + linear_shift(d_halo[start : start + rows], -by).astype(F32)
+        came = linear_shift(after(d_halo[start : start + rows], arrived), -by)
+        grad_tokens = grad_tokens + after(came, *last_sum.arrived).astype(F32)
 
     total_down = jnp.concatenate(down_blocks, axis=0).astype(F32)
     total_gate = jnp.concatenate(gate_blocks, axis=1).astype(F32)

time: 289 us -> 306 us (1.059)
  waiting for transfers between devices: 75.1 us -> 97.9 us
  other arithmetic: 29.7 us -> 21 us
  Pallas kernels: 61.2 us -> 68.3 us
    ppermute x30 -> x20, waiting for transfers between devices: 22.9 us -> 47 us  [outer_swap(): lax.ppermute(array, 'seq', [(i, i ^ 4 << bit) for i in range(self.seq)])]
    pallas_call x0 -> x2, Pallas kernels: none -> 10.8 us  [the longest x1 6.9 us: on_device(): pl.pallas_call(functools.partial(attend_back_kernel, halo, heads), out_sh...]
    ppermute x23, starting transfers between devices: 30.2 us -> 39.3 us  [core_swap(): return lax.ppermute(array, 'seq', [(i, i ^ 1) for i in range(self.seq)])]
    ppermute x11, waiting for transfers between devices: 25.8 us -> 34.6 us  [fsdp_shift(): lax.ppermute(array, 'fsdp', [(i, (i + by) % self.fsdp) for i in range(sel...]
    ppermute x30 -> x20, starting transfers between devices: 31.7 us -> 24.3 us  [outer_swap(): lax.ppermute(array, 'seq', [(i, i ^ 4 << bit) for i in range(self.seq)])]
    ppermute x13, starting transfers between devices: 14.3 us -> 7.65 us  [mid_swap(): return lax.ppermute(array, 'seq', [(i, i ^ 2) for i in range(self.seq)])]
    convert_element_type x15, other arithmetic: 8.68 us -> 3.05 us  [the longest x5 2.46 us: over_mid(): self.across = self.here.mid_swap(add(*terms).astype(BF16))]
    slice x1 -> x18, local copies, waits for them, and re-layouts: 1.13 us -> 6.35 us  [the longest x5 3.21 us: gather_sums(): self.other[0, 0]]
  transfers between devices with their start and end apart: 81 -> 71, of which waited for: 28 -> 27; matrix products, arithmetic and copies ran while one was open for 14% -> 10% of each run, Pallas kernels for 19% -> 16%
where the time goes in v4:
time: 306 us; the launch traced here: 305 us
  waiting for transfers between devices  97.9 us (32%)
  starting transfers between devices  95.5 us (31%)
  Pallas kernels  68.3 us (22%)
  other arithmetic  21 us (7%)
  local copies, waits for them, and re-layouts  20 us (7%)
    ppermute x20, waiting for transfers between devices, outer_swap(): lax.ppermute(array, 'seq', [(i, i ^ 4 << bit) for i in range(self.seq)])  47 us
    ppermute x23, starting transfers between devices, core_swap(): return lax.ppermute(array, 'seq', [(i, i ^ 1) for i in range(self.seq)])  39.3 us
    ppermute x11, waiting for transfers between devices, fsdp_shift(): lax.ppermute(array, 'fsdp', [(i, (i + by) % self.fsdp) for i in range(sel...  34.6 us
    ppermute x20, starting transfers between devices, outer_swap(): lax.ppermute(array, 'seq', [(i, i ^ 4 << bit) for i in range(self.seq)])  24.3 us
    ppermute x13, waiting for transfers between devices, mid_swap(): return lax.ppermute(array, 'seq', [(i, i ^ 2) for i in range(self.seq)])  15.2 us
    ppermute x4, starting transfers between devices, linear_shift(): lax.ppermute(array, ('seq', 'fsdp'), [(i, i + by) for i in range(count) i...  15.1 us
    pallas_call x1, Pallas kernels, on_device(): pl.pallas_call(functools.partial(last_kernel, len(qkv_w), n_tok, fsdp, he...  11.8 us
    pallas_call x1, Pallas kernels, on_device(): pl.pallas_call(functools.partial(middle_kernel, len(out_w), len(gate_w),...  10.6 us
  transfers between devices with their start and end apart: 71, of which 27 were waited for; matrix products, arithmetic and copies ran while one was open for 10% of the time, Pallas kernels for 16%

profile of v4, /device:TPU:1, one launch (start us, length us, event | category | flops | bytes accessed | tf_op | source)
XLA Modules:
  0.0 305.2 jit_solution(6276850853117834108)
XLA Ops:
  4.5 4.6 %collective-permute-start = (bf16[256,640]{1,0:T(8,128)(2,1)S(1)}, bf16[256,640]{1,0:T(8,128)(2,1)S(1)}, u32[]{:S(2)}, u32[]{:S(2)}) collective-permute-start(bf16[256,640]{1,0:T(8,128)(2,1)S(1)} %copy-done.32), channel_id=1, source_target_pairs={{0,2},{1,3},{2,4},{3,5},{4,6},{5,7},{6,8},{7,9},{8,10},{9,11},{10,... | collective-permute-start | bytes 983048 | tf_op jit(solution)/shard_map/ppermute | solution.py:73
  9.2 3.1 %collective-permute-start.1 = (bf16[256,640]{1,0:T(8,128)(2,1)S(1)}, bf16[256,640]{1,0:T(8,128)(2,1)S(1)}, u32[]{:S(2)}, u32[]{:S(2)}) collective-permute-start(bf16[256,640]{1,0:T(8,128)(2,1)S(1)} %copy-done.32), channel_id=1, source_target_pairs={{0,1},{1,2},{2,3},{3,4},{4,5},{5,6},{6,7},{7,8},{8,9},{9,10},{10,1... | collective-permute-start | bytes 983048 | tf_op jit(solution)/shard_map/ppermute | solution.py:73
  17.2 2.5 multiply_sine_fusion
  19.7 4.6 %collective-permute-done.3.refs_13_.refs_22_ = bf16[320,384]{1,0:T(8,128)(2,1)S(1)} collective-permute-done((bf16[320,384]{1,0:T(8,128)(2,1)S(1)}, bf16[320,384]{1,0:T(8,128)(2,1)S(1)}, u32[]{:S(2)}, u32[]{:S(2)}) %collective-permute-start.3) | collective-permute-done | bytes 245792 | tf_op jit(solution)/shard_map/ppermute | solution.py:68
  26.6 3.0 collective-permute-start.5
  29.7 3.1 %collective-permute-start.6 = (bf16[320,384]{1,0:T(8,128)(2,1)S(1)}, bf16[320,384]{1,0:T(8,128)(2,1)S(1)}, u32[]{:S(2)}, u32[]{:S(2)}) collective-permute-start(bf16[320,384]{1,0:T(8,128)(2,1)S(1)} %collective-permute-done.4.refs_14_.refs_23_), channel_id=1, source_target_pairs={{0,2},{2,0},{4,6},{6,4},{8,10},{10,8},{12,14},{14,12},{16,18},{18,... | collective-permute-start | bytes 737288 | tf_op jit(solution)/shard_map/ppermute | solution.py:59
  36.6 2.4 collective-permute-done.7.refs_6_.refs_10_
  40.0 9.0 %attend.1 = (bf16[768,640]{1,0:T(8,128)(2,1)}, f32[256,1024]{1,0:T(8,128)}, f32[768,256]{1,0:T(8,128)}, bf16[1024,256]{1,0:T(8,128)(2,1)}, bf16[768,256]{1,0:T(8...) custom-call(s32[3]{0:T(128)} %pad_add_fusion.refs_0_.at, ...), custom_call_target="tpu_custom_call" | custom-call | flops 80000000000 | bytes 200000000 | tf_op jit(solution)/shard_map/attend/pallas_call | solution.py:620
  49.1 4.0 %collective-permute-done.13.refs_14_.refs_18_ = bf16[320,512]{1,0:T(8,128)(2,1)} collective-permute-done((bf16[320,512]{1,0:T(8,128)(2,1)S(1)}, bf16[320,512]{1,0:T(8,128)(2,1)}, u32[]{:S(2)}, u32[]{:S(2)}) %collective-permute-start.13) | collective-permute-done | bytes 327712 | tf_op jit(solution)/shard_map/ppermute | solution.py:68
  54.6 2.7 collective-permute-done.10.refs_10_.refs_14_
  57.3 3.6 %collective-permute-start.12 = (bf16[320,512]{1,0:T(8,128)(2,1)S(1)}, bf16[320,512]{1,0:T(8,128)(2,1)}, u32[]{:S(2)}, u32[]{:S(2)}) collective-permute-start(bf16[320,512]{1,0:T(8,128)(2,1)S(1)} %collective-permute-done.10.refs_10_.refs_14_), channel_id=1, source_target_pairs={{0,2},{2,0},{4,6},{6,4},{8,10},{10,8},{12,14},{14,12},{16,18},{18,... | collective-permute-start | bytes 983048 | tf_op jit(solution)/shard_map/ppermute | solution.py:59
  60.8 3.4 %collective-permute-done.14.refs_15_.refs_19_ = bf16[320,512]{1,0:T(8,128)(2,1)S(1)} collective-permute-done((bf16[320,512]{1,0:T(8,128)(2,1)}, bf16[320,512]{1,0:T(8,128)(2,1)S(1)}, u32[]{:S(2)}, u32[]{:S(2)}) %collective-permute-start.14) | collective-permute-done | bytes 327712 | tf_op jit(solution)/shard_map/ppermute | solution.py:62
  64.3 2.0 collective-permute-start.16
  69.0 10.6 %gate.1 = (f32[256,640]{1,0:T(8,128)}, f32[256,640]{1,0:T(8,128)}, bf16[256,640]{1,0:T(8,128)(2,1)}, bf16[256,2048]{1,0:T(8,128)(2,1)}, bf16[256,2048]{1,0:T(8,128)(2,1)}, /*index=5*/bf16[256,2048]{1,0:T(8,128)(2,1)}) custom-call(s32[3]{0:T(128)} %pad_add_fusion.refs_0_.at, bf16[256,1024]{1,0:T(8,128)(2,1)} %get-tuple-element.98.refs_1_.refs_8_, ...), custom_call_target="tpu_custom_call" | custom-call | flops 80000000000 | bytes 104857600 | tf_op jit(solution)/shard_map/gate/pallas_call | solution.py:647
  79.6 4.4 %collective-permute-done.17.refs_6_ = bf16[512,640]{1,0:T(8,128)(2,1)S(1)} collective-permute-done((bf16[512,640]{1,0:T(8,128)(2,1)S(1)}, bf16[512,640]{1,0:T(8,128)(2,1)S(1)}, u32[]{:S(2)}, u32[]{:S(2)}) %collective-permute-start.17) | collective-permute-done | bytes 655392 | tf_op jit(solution)/shard_map/ppermute | solution.py:68
  87.4 6.6 %down.1 = (bf16[256,640]{1,0:T(8,128)(2,1)}, bf16[256,640]{1,0:T(8,128)(2,1)}, f32[1,640]{1,0:T(1,128)}, bf16[2,2,256,640]{3,2,1,0:T(8,128)(2,1)}, bf16[2,2,256,640]{3,2,1,0:T(8,128)(2,1)}) custom-call(s32[3]{0:T(128)} %pad_add_fusion.refs_0_.at, bf16[256,2048]{1,0:T(8,128)(2,1)} %get-tuple-element.106.refs_1_, ...), custom_call_target="tpu_custom_call" | custom-call | flops 80000000000 | bytes 104857600 | tf_op jit(solution)/shard_map/down/pallas_call | solution.py:675
  94.5 8.8 %gate_back.1 = (bf16[256,2048]{1,0:T(8,128)(2,1)}, bf16[256,2048]{1,0:T(8,128)(2,1)}, bf16[640,256]{1,0:T(8,128)(2,1)}, bf16[2,2,320,512]{3,2,1,0:T(8,128)(2,1)}, bf16[2,2,320,512]{3,2,1,0:T(8,128)(2,1)}) custom-call(s32[3]{0:T(128)} %pad_add_fusion.refs_0_.at, bf16[256,640]{1,0:T(8,128)(2,1)} %get-tuple-element.111.refs_1_, ...), custom_call_target="tpu_custom_call" | custom-call | flops 120000004096 | bytes 157286400 | tf_op jit(solution)/shard_map/gate_back/pallas_call | solution.py:698
  103.5 3.9 %up_back.1 = (bf16[2,2,320,512]{3,2,1,0:T(8,128)(2,1)}, bf16[2,2,320,512]{3,2,1,0:T(8,128)(2,1)}) custom-call(s32[3]{0:T(128)} %pad_add_fusion.refs_0_.at, bf16[640,256]{1,0:T(8,128)(2,1)} %get-tuple-element.117.ffn_t, bf16[256,2048]{1,0:T(8,128)(2,1)} %get-tuple-element.120.d_up.refs_2_), custom_call_target="tpu_custom_call" | custom-call | flops 120000004096 | bytes 157286400 | tf_op jit(solution)/shard_map/up_back/pallas_call | solution.py:718
  110.0 10.6 %middle.1 = (f32[256,640]{1,0:T(8,128)}, f32[1,640]{1,0:T(1,128)}, f32[1,640]{1,0:T(1,128)}, bf16[1024,256]{1,0:T(8,128)(2,1)}, bf16[2,2,128,640]{3,2,1,0:T(8,128)(2,1)}, /*index=5*/bf16[2,2,128,640]{3,2,1,0:T(8,128)(2,1)}) custom-call(s32[3]{0:T(128)} %pad_add_fusion.refs_0_.at, bf16[256,2048]{1,0:T(8,128)(2,1)} %get-tuple-element.122.refs_1_, ...), custom_call_target="tpu_custom_call" | custom-call | flops 120000004096 | bytes 209715200 | tf_op jit(solution)/shard_map/middle/pallas_call | solution.py:736
  122.5 2.5 collective-permute-done.22
  125.3 6.9 %attend_back.1 = (f32[256,1024]{1,0:T(8,128)}, f32[768,256]{1,0:T(8,128)}, f32[768,256]{1,0:T(8,128)}) custom-call(bf16[1024,256]{1,0:T(8,128)(2,1)} %get-tuple-element.129.d_att, bf16[1024,256]{1,0:T(8,128)(2,1)} %get-tuple-element.130.q_st, bf16[768,256]{1,0:T(8,128)(2,1)} %get-tuple-element.131.keys, bf16[768,256]{1,0:T(8,128)(2,1)} %get-tuple-element.132.values, ...), custom_call_target="tpu_custom_call" | custom-call | flops 120000004096 | bytes 157286400 | tf_op jit(solution)/shard_map/attend_back/pallas_call | solution.py:764
  132.2 7.1 %collective-permute-done.25 = bf16[2,320,512]{2,1,0:T(8,128)(2,1)S(1)} collective-permute-done((bf16[2,320,512]{2,1,0:T(8,128)(2,1)}, bf16[2,320,512]{2,1,0:T(8,128)(2,1)S(1)}, u32[]{:S(2)}, u32[]{:S(2)}) %collective-permute-start.25) | collective-permute-done | bytes 655392 | tf_op jit(solution)/shard_map/ppermute | solution.py:68
  139.4 11.8 %last.1 = (f32[256,640]{1,0:T(8,128)}, bf16[512,640]{1,0:T(8,128)(2,1)}, bf16[2,2,352,384]{3,2,1,0:T(8,128)(2,1)}, bf16[2,2,352,384]{3,2,1,0:T(8,128)(2,1)}) custom-call(s32[3]{0:T(128)} %pad_add_fusion.refs_0_.at, f32[256,640]{1,0:T(8,128)} %get-tuple-element.124.refs_1_, f32[256,1024]{1,0:T(8,128)} %get-tuple-element.140.refs_2_, ...), custom_call_target="tpu_custom_call" | custom-call | flops 299999985664 | bytes 209715200 | tf_op jit(solution)/shard_map/last/pallas_call | solution.py:780
  159.9 3.1 %collective-permute-start.29 = (bf16[256,640]{1,0:T(8,128)(2,1)S(1)}, bf16[256,640]{1,0:T(8,128)(2,1)S(1)}, u32[]{:S(2)}, u32[]{:S(2)}) collective-permute-start(bf16[256,640]{1,0:T(8,128)(2,1)S(1)} %get-tuple-element.154), channel_id=1, source_target_pairs={{2,0},{3,1},{4,2},{5,3},{6,4},{7,5},{8,6},{9,7},{10,8},{11,9},{12,... | collective-permute-start | bytes 983048 | tf_op jit(solution)/shard_map/ppermute | solution.py:73
  165.6 4.1 %collective-permute-start.27 = (bf16[256,640]{1,0:T(8,128)(2,1)S(1)}, bf16[256,640]{1,0:T(8,128)(2,1)S(1)}, u32[]{:S(2)}, u32[]{:S(2)}) collective-permute-start(bf16[256,640]{1,0:T(8,128)(2,1)S(1)} %get-tuple-element.151), channel_id=1, source_target_pairs={{1,0},{2,1},{3,2},{4,3},{5,4},{6,5},{7,6},{8,7},{9,8},{10,9},{11,1... | collective-permute-start | bytes 983048 | tf_op jit(solution)/shard_map/ppermute | solution.py:73
  171.8 9.5 %collective-permute-done.55 = bf16[2,320,512]{2,1,0:T(8,128)(2,1)S(1)} collective-permute-done((bf16[2,320,512]{2,1,0:T(8,128)(2,1)S(1)}, bf16[2,320,512]{2,1,0:T(8,128)(2,1)S(1)}, u32[]{:S(2)}, u32[]{:S(2)}) %collective-permute-start.55) | collective-permute-done | bytes 655392 | tf_op jit(solution)/shard_map/ppermute | solution.py:68
  183.8 1.9 collective-permute-done.48
  187.4 2.7 collective-permute-done.64
  191.6 2.8 collective-permute-done.40
  194.4 2.3 collective-permute-start.49
  196.8 1.9 collective-permute-done.49
  198.7 2.7 collective-permute-start.41
  202.8 2.4 collective-permute-start.65
  205.2 2.7 collective-permute-done.65
  209.4 2.6 collective-permute-done.42
  213.1 5.4 %collective-permute-done.50 = bf16[80,512]{1,0:T(8,128)(2,1)S(1)} collective-permute-done((bf16[80,512]{1,0:T(8,128)(2,1)S(1)}, bf16[80,512]{1,0:T(8,128)(2,1)S(1)}, u32[]{:S(2)}, u32[]{:S(2)}) %collective-permute-start.50) | collective-permute-done | bytes 81952 | tf_op jit(solution)/shard_map/ppermute | solution.py:65
  220.3 3.2 %collective-permute-done.66 = bf16[64,640]{1,0:T(8,128)(2,1)S(1)} collective-permute-done((bf16[64,640]{1,0:T(8,128)(2,1)S(1)}, bf16[64,640]{1,0:T(8,128)(2,1)S(1)}, u32[]{:S(2)}, u32[]{:S(2)}) %collective-permute-start.66) | collective-permute-done | bytes 81952 | tf_op jit(solution)/shard_map/ppermute | solution.py:65
  225.1 2.6 collective-permute-done.57
  229.0 3.1 %collective-permute-done.67 = bf16[128,640]{1,0:T(8,128)(2,1)S(1)} collective-permute-done((bf16[128,640]{1,0:T(8,128)(2,1)S(1)}, bf16[128,640]{1,0:T(8,128)(2,1)S(1)}, u32[]{:S(2)}, u32[]{:S(2)}) %collective-permute-start.67) | collective-permute-done | bytes 163872 | tf_op jit(solution)/shard_map/ppermute | solution.py:65
  232.3 14.4 %collective-permute-start.45 = (bf16[128,640]{1,0:T(8,128)(2,1)S(1)}, bf16[128,640]{1,0:T(8,128)(2,1)S(1)}, u32[]{:S(2)}, u32[]{:S(2)}) collective-permute-start(bf16[128,640]{1,0:T(8,128)(2,1)S(1)} %maximum_select_fusion.6), channel_id=1, source_target_pairs={{0,2},{2,0},{4,6},{6,4},{8,10},{10,8},{12,14},{14,12},{16,18},{18,... | collective-permute-start | bytes 491528 | tf_op jit(solution)/shard_map/ppermute | solution.py:59
  249.9 3.5 %collective-permute-done.58 = bf16[80,512]{1,0:T(8,128)(2,1)S(1)} collective-permute-done((bf16[80,512]{1,0:T(8,128)(2,1)S(1)}, bf16[80,512]{1,0:T(8,128)(2,1)S(1)}, u32[]{:S(2)}, u32[]{:S(2)}) %collective-permute-start.58) | collective-permute-done | bytes 81952 | tf_op jit(solution)/shard_map/ppermute | solution.py:65
  255.0 4.7 %collective-permute-done.59 = bf16[80,512]{1,0:T(8,128)(2,1)S(1)} collective-permute-done((bf16[80,512]{1,0:T(8,128)(2,1)S(1)}, bf16[80,512]{1,0:T(8,128)(2,1)S(1)}, u32[]{:S(2)}, u32[]{:S(2)}) %collective-permute-start.59) | collective-permute-done | bytes 81952 | tf_op jit(solution)/shard_map/ppermute | solution.py:65
  260.2 3.7 %collective-permute-done.30 = bf16[352,384]{1,0:T(8,128)(2,1)S(1)} collective-permute-done((bf16[352,384]{1,0:T(8,128)(2,1)S(1)}, bf16[352,384]{1,0:T(8,128)(2,1)S(1)}, u32[]{:S(2)}, u32[]{:S(2)}) %collective-permute-start.30) | collective-permute-done | bytes 270368 | tf_op jit(solution)/shard_map/ppermute | solution.py:62
  266.7 5.8 %collective-permute-done.31 = bf16[176,384]{1,0:T(8,128)(2,1)S(1)} collective-permute-done((bf16[176,384]{1,0:T(8,128)(2,1)S(1)}, bf16[176,384]{1,0:T(8,128)(2,1)S(1)}, u32[]{:S(2)}, u32[]{:S(2)}) %collective-permute-start.31) | collective-permute-done | bytes 135200 | tf_op jit(solution)/shard_map/ppermute | solution.py:65
  275.3 2.6 collective-permute-start.70
  279.7 2.7 collective-permute-done.33
  282.5 2.7 collective-permute-start.53
  294.6 5.3 %collective-permute-done.35 = bf16[352,384]{1,0:T(8,128)(2,1)S(1)} collective-permute-done((bf16[352,384]{1,0:T(8,128)(2,1)S(1)}, bf16[352,384]{1,0:T(8,128)(2,1)S(1)}, u32[]{:S(2)}, u32[]{:S(2)}) %collective-permute-start.35) | collective-permute-done | bytes 270368 | tf_op jit(solution)/shard_map/ppermute | solution.py:62
  (293 shorter events, 82.8 us)
Async XLA Ops:
  4.5 25.1 %collective-permute-start = (bf16[256,640]{1,0:T(8,128)(2,1)S(1)}, bf16[256,640]{1,0:T(8,128)(2,1)S(1)}, u32[]{:S(2)}, u32[]{:S(2)}) collective-permute-start(bf16[256,640]{1,0:T(8,128)(2,1)S(1)} %copy-done.32), channel_id=1, source_target_pairs={{0,2},{1,3},{2,4},{3,5},{4,6},{5,7},{6,8},{7,9},{8,10},{9,11},{10,... | collective-permute-start | bytes 983048 | tf_op jit(solution)/shard_map/ppermute | solution.py:73
  9.2 20.4 %collective-permute-start.1 = (bf16[256,640]{1,0:T(8,128)(2,1)S(1)}, bf16[256,640]{1,0:T(8,128)(2,1)S(1)}, u32[]{:S(2)}, u32[]{:S(2)}) collective-permute-start(bf16[256,640]{1,0:T(8,128)(2,1)S(1)} %copy-done.32), channel_id=1, source_target_pairs={{0,1},{1,2},{2,3},{3,4},{4,5},{5,6},{6,7},{7,8},{8,9},{9,10},{10,1... | collective-permute-start | bytes 983048 | tf_op jit(solution)/shard_map/ppermute | solution.py:73
  12.3 12.0 %collective-permute-start.3 = (bf16[320,384]{1,0:T(8,128)(2,1)S(1)}, bf16[320,384]{1,0:T(8,128)(2,1)S(1)}, u32[]{:S(2)}, u32[]{:S(2)}) collective-permute-start(bf16[320,384]{1,0:T(8,128)(2,1)S(1)} %maximum_select_fusion.4), channel_id=1, source_target_pairs={{0,1},{1,0},{2,3},{3,2},{4,5},{5,4},{6,7},{7,6},{8,9},{9,8},{10,11... | collective-permute-start | bytes 737288 | tf_op jit(solution)/shard_map/ppermute | solution.py:68
  12.6 14.0 %collective-permute-start.2 = (bf16[1536]{0:T(1024)(128)(2,1)S(1)}, bf16[1536]{0:T(1024)(128)(2,1)S(1)}, u32[]{:S(2)}, u32[]{:S(2)}) collective-permute-start(bf16[1536]{0:T(1024)(128)(2,1)S(1)} %concatenate.94), channel_id=1, source_target_pairs={{0,1},{1,0},{2,3},{3,2},{4,5},{5,4},{6,7},{7,6},{8,9},{9,8},{10,11... | collective-permute-start | bytes 9224 | tf_op jit(solution)/shard_map/ppermute | solution.py:68
  26.6 12.6 %collective-permute-start.5 = (bf16[320,384]{1,0:T(8,128)(2,1)S(1)}, bf16[320,384]{1,0:T(8,128)(2,1)S(1)}, u32[]{:S(2)}, u32[]{:S(2)}) collective-permute-start(bf16[320,384]{1,0:T(8,128)(2,1)S(1)} %collective-permute-done.3.refs_13_.refs_22_), channel_id=1, source_target_pairs={{0,2},{2,0},{4,6},{6,4},{8,10},{10,8},{12,14},{14,12},{16,18},{18,... | collective-permute-start | bytes 737288 | tf_op jit(solution)/shard_map/ppermute | solution.py:59
  29.6 9.4 %collective-permute-start.7 = (bf16[256,640]{1,0:T(8,128)(2,1)S(1)}, bf16[256,640]{1,0:T(8,128)(2,1)S(1)}, u32[]{:S(2)}, u32[]{:S(2)}) collective-permute-start(bf16[256,640]{1,0:T(8,128)(2,1)S(1)} %constant_dynamic-slice_fusion.9), channel_id=1, source_target_pairs={{0,1},{1,0},{2,3},{3,2},{4,5},{5,4},{6,7},{7,6},{8,9},{9,8},{10,11... | collective-permute-start | bytes 983048 | tf_op jit(solution)/shard_map/ppermute | solution.py:68
  29.7 9.5 %collective-permute-start.6 = (bf16[320,384]{1,0:T(8,128)(2,1)S(1)}, bf16[320,384]{1,0:T(8,128)(2,1)S(1)}, u32[]{:S(2)}, u32[]{:S(2)}) collective-permute-start(bf16[320,384]{1,0:T(8,128)(2,1)S(1)} %collective-permute-done.4.refs_14_.refs_23_), channel_id=1, source_target_pairs={{0,2},{2,0},{4,6},{6,4},{8,10},{10,8},{12,14},{14,12},{16,18},{18,... | collective-permute-start | bytes 737288 | tf_op jit(solution)/shard_map/ppermute | solution.py:59
  34.8 14.3 %collective-permute-start.9 = (bf16[320,512]{1,0:T(8,128)(2,1)S(1)}, bf16[320,512]{1,0:T(8,128)(2,1)S(1)}, u32[]{:S(2)}, u32[]{:S(2)}) collective-permute-start(bf16[320,512]{1,0:T(8,128)(2,1)S(1)} %constant_dynamic-slice_fusion.8), channel_id=1, source_target_pairs={{0,1},{1,0},{2,3},{3,2},{4,5},{5,4},{6,7},{7,6},{8,9},{9,8},{10,11... | collective-permute-start | bytes 983048 | tf_op jit(solution)/shard_map/ppermute | solution.py:68
  39.0 14.1 %collective-permute-start.13 = (bf16[320,512]{1,0:T(8,128)(2,1)S(1)}, bf16[320,512]{1,0:T(8,128)(2,1)}, u32[]{:S(2)}, u32[]{:S(2)}) collective-permute-start(bf16[320,512]{1,0:T(8,128)(2,1)S(1)} %constant_dynamic-slice_fusion.7), channel_id=1, source_target_pairs={{0,1},{1,0},{2,3},{3,2},{4,5},{5,4},{6,7},{7,6},{8,9},{9,8},{10,11... | collective-permute-start | bytes 983048 | tf_op jit(solution)/shard_map/ppermute | solution.py:68
  49.1 8.2 %collective-permute-start.10 = (bf16[320,512]{1,0:T(8,128)(2,1)S(1)}, bf16[320,512]{1,0:T(8,128)(2,1)S(1)}, u32[]{:S(2)}, u32[]{:S(2)}) collective-permute-start(bf16[320,512]{1,0:T(8,128)(2,1)S(1)} %collective-permute-done.9.refs_9_.refs_13_), channel_id=1, source_target_pairs={{0,4},{2,6},{4,0},{6,2},{8,12},{10,14},{12,8},{14,10},{16,20},{18,... | collective-permute-start | bytes 983048 | tf_op jit(solution)/shard_map/ppermute | solution.py:62
  53.1 11.1 %collective-permute-start.14 = (bf16[320,512]{1,0:T(8,128)(2,1)}, bf16[320,512]{1,0:T(8,128)(2,1)S(1)}, u32[]{:S(2)}, u32[]{:S(2)}) collective-permute-start(bf16[320,512]{1,0:T(8,128)(2,1)} %collective-permute-done.13.refs_14_.refs_18_), channel_id=1, source_target_pairs={{0,4},{2,6},{4,0},{6,2},{8,12},{10,14},{12,8},{14,10},{16,20},{18,... | collective-permute-start | bytes 983048 | tf_op jit(solution)/shard_map/ppermute | solution.py:62
  53.1 14.5 %collective-permute-start.8 = (bf16[256,640]{1,0:T(8,128)(2,1)S(1)}, bf16[256,640]{1,0:T(8,128)(2,1)}, u32[]{:S(2)}, u32[]{:S(2)}) collective-permute-start(bf16[256,640]{1,0:T(8,128)(2,1)S(1)} %collective-permute-done.7.refs_6_.refs_10_), channel_id=1, source_target_pairs={{0,2},{2,0},{4,6},{6,4},{8,10},{10,8},{12,14},{14,12},{16,18},{18,... | collective-permute-start | bytes 983048 | tf_op jit(solution)/shard_map/ppermute | solution.py:59
  54.0 14.9 %collective-permute-start.11 = (bf16[320,512]{1,0:T(8,128)(2,1)S(1)}, bf16[320,512]{1,0:T(8,128)(2,1)}, u32[]{:S(2)}, u32[]{:S(2)}) collective-permute-start(bf16[320,512]{1,0:T(8,128)(2,1)S(1)} %collective-permute-done.9.refs_9_.refs_13_), channel_id=1, source_target_pairs={{0,2},{2,0},{4,6},{6,4},{8,10},{10,8},{12,14},{14,12},{16,18},{18,... | collective-permute-start | bytes 983048 | tf_op jit(solution)/shard_map/ppermute | solution.py:59
  54.0 14.9 %collective-permute-start.15 = (bf16[320,512]{1,0:T(8,128)(2,1)}, bf16[320,512]{1,0:T(8,128)(2,1)}, u32[]{:S(2)}, u32[]{:S(2)}) collective-permute-start(bf16[320,512]{1,0:T(8,128)(2,1)} %collective-permute-done.13.refs_14_.refs_18_), channel_id=1, source_target_pairs={{0,2},{2,0},{4,6},{6,4},{8,10},{10,8},{12,14},{14,12},{16,18},{18,... | collective-permute-start | bytes 983048 | tf_op jit(solution)/shard_map/ppermute | solution.py:59
  57.3 11.7 %collective-permute-start.12 = (bf16[320,512]{1,0:T(8,128)(2,1)S(1)}, bf16[320,512]{1,0:T(8,128)(2,1)}, u32[]{:S(2)}, u32[]{:S(2)}) collective-permute-start(bf16[320,512]{1,0:T(8,128)(2,1)S(1)} %collective-permute-done.10.refs_10_.refs_14_), channel_id=1, source_target_pairs={{0,2},{2,0},{4,6},{6,4},{8,10},{10,8},{12,14},{14,12},{16,18},{18,... | collective-permute-start | bytes 983048 | tf_op jit(solution)/shard_map/ppermute | solution.py:59
  67.7 16.4 %collective-permute-start.17 = (bf16[512,640]{1,0:T(8,128)(2,1)S(1)}, bf16[512,640]{1,0:T(8,128)(2,1)S(1)}, u32[]{:S(2)}, u32[]{:S(2)}) collective-permute-start(bf16[512,640]{1,0:T(8,128)(2,1)S(1)} %constant_dynamic-slice_fusion.6), channel_id=1, source_target_pairs={{0,1},{1,0},{2,3},{3,2},{4,5},{5,4},{6,7},{7,6},{8,9},{9,8},{10,11... | collective-permute-start | bytes 1966088 | tf_op jit(solution)/shard_map/ppermute | solution.py:68
  94.0 9.5 %collective-permute-start.20 = (bf16[2,2,256,640]{3,2,1,0:T(8,128)(2,1)}, bf16[2,2,256,640]{3,2,1,0:T(8,128)(2,1)S(1)}, u32[]{:S(2)}, u32[]{:S(2)}) collective-permute-start(bf16[2,2,256,640]{3,2,1,0:T(8,128)(2,1)} %get-tuple-element.119), channel_id=1, source_target_pairs={{0,2},{2,0},{4,6},{6,4},{8,10},{10,8},{12,14},{14,12},{16,18},{18,... | collective-permute-start | bytes 3932168 | tf_op jit(solution)/shard_map/ppermute | solution.py:59
  107.4 17.8 %collective-permute-start.21 = (bf16[2,2,320,512]{3,2,1,0:T(8,128)(2,1)}, bf16[2,2,320,512]{3,2,1,0:T(8,128)(2,1)S(1)}, u32[]{:S(2)}, u32[]{:S(2)}) collective-permute-start(bf16[2,2,320,512]{3,2,1,0:T(8,128)(2,1)} %get-tuple-element.126), channel_id=1, source_target_pairs={{0,2},{2,0},{4,6},{6,4},{8,10},{10,8},{12,14},{14,12},{16,18},{18,... | collective-permute-start | bytes 3932168 | tf_op jit(solution)/shard_map/ppermute | solution.py:59
  108.8 16.3 %collective-permute-start.22 = (bf16[2,256,640]{2,1,0:T(8,128)(2,1)}, bf16[2,256,640]{2,1,0:T(8,128)(2,1)S(1)}, u32[]{:S(2)}, u32[]{:S(2)}) collective-permute-start(bf16[2,256,640]{2,1,0:T(8,128)(2,1)} %fusion), channel_id=1, source_target_pairs={{0,1},{1,0},{2,3},{3,2},{4,5},{5,4},{6,7},{7,6},{8,9},{9,8},{10,11... | collective-permute-start | bytes 1966088 | tf_op jit(solution)/shard_map/ppermute | solution.py:68
  120.7 11.5 %collective-permute-start.23 = (bf16[2,2,128,640]{3,2,1,0:T(8,128)(2,1)}, bf16[2,2,128,640]{3,2,1,0:T(8,128)(2,1)S(1)}, u32[]{:S(2)}, u32[]{:S(2)}) collective-permute-start(bf16[2,2,128,640]{3,2,1,0:T(8,128)(2,1)} %get-tuple-element.135), channel_id=1, source_target_pairs={{0,2},{2,0},{4,6},{6,4},{8,10},{10,8},{12,14},{14,12},{16,18},{18,... | collective-permute-start | bytes 1966088 | tf_op jit(solution)/shard_map/ppermute | solution.py:59
  122.3 17.0 %collective-permute-start.25 = (bf16[2,320,512]{2,1,0:T(8,128)(2,1)}, bf16[2,320,512]{2,1,0:T(8,128)(2,1)S(1)}, u32[]{:S(2)}, u32[]{:S(2)}) collective-permute-start(bf16[2,320,512]{2,1,0:T(8,128)(2,1)} %fusion.1), channel_id=1, source_target_pairs={{0,1},{1,0},{2,3},{3,2},{4,5},{5,4},{6,7},{7,6},{8,9},{9,8},{10,11... | collective-permute-start | bytes 1966088 | tf_op jit(solution)/shard_map/ppermute | solution.py:68
  125.2 14.2 %collective-permute-start.24 = (bf16[256,640]{1,0:T(8,128)(2,1)S(1)}, bf16[256,640]{1,0:T(8,128)(2,1)S(1)}, u32[]{:S(2)}, u32[]{:S(2)}) collective-permute-start(bf16[256,640]{1,0:T(8,128)(2,1)S(1)} %fusion.5), channel_id=1, source_target_pairs={{0,4},{2,6},{4,0},{6,2},{8,12},{10,14},{12,8},{14,10},{16,20},{18,... | collective-permute-start | bytes 983048 | tf_op jit(solution)/shard_map/ppermute | solution.py:62
  151.2 8.7 %collective-permute-start.26 = (bf16[2,2,352,384]{3,2,1,0:T(8,128)(2,1)}, bf16[2,2,352,384]{3,2,1,0:T(8,128)(2,1)}, u32[]{:S(2)}, u32[]{:S(2)}) collective-permute-start(bf16[2,2,352,384]{3,2,1,0:T(8,128)(2,1)} %get-tuple-element.150), channel_id=1, source_target_pairs={{0,2},{2,0},{4,6},{6,4},{8,10},{10,8},{12,14},{14,12},{16,18},{18,... | collective-permute-start | bytes 3244040 | tf_op jit(solution)/shard_map/ppermute | solution.py:59
  155.7 9.9 %collective-permute-start.38 = (bf16[2,128,640]{2,1,0:T(8,128)(2,1)S(1)}, bf16[2,128,640]{2,1,0:T(8,128)(2,1)S(1)}, u32[]{:S(2)}, u32[]{:S(2)}) collective-permute-start(bf16[2,128,640]{2,1,0:T(8,128)(2,1)S(1)} %fusion.8), channel_id=1, source_target_pairs={{0,1},{1,0},{2,3},{3,2},{4,5},{5,4},{6,7},{7,6},{8,9},{9,8},{10,11... | collective-permute-start | bytes 983048 | tf_op jit(solution)/shard_map/ppermute | solution.py:68
  157.2 24.1 %collective-permute-start.55 = (bf16[2,320,512]{2,1,0:T(8,128)(2,1)S(1)}, bf16[2,320,512]{2,1,0:T(8,128)(2,1)S(1)}, u32[]{:S(2)}, u32[]{:S(2)}) collective-permute-start(bf16[2,320,512]{2,1,0:T(8,128)(2,1)S(1)} %fusion.2), channel_id=1, source_target_pairs={{0,1},{1,0},{2,3},{3,2},{4,5},{5,4},{6,7},{7,6},{8,9},{9,8},{10,11... | collective-permute-start | bytes 1966088 | tf_op jit(solution)/shard_map/ppermute | solution.py:68
  159.8 10.0 %collective-permute-start.47 = (bf16[320,512]{1,0:T(8,128)(2,1)S(1)}, bf16[320,512]{1,0:T(8,128)(2,1)S(1)}, u32[]{:S(2)}, u32[]{:S(2)}) collective-permute-start(bf16[320,512]{1,0:T(8,128)(2,1)S(1)} %fusion.4), channel_id=1, source_target_pairs={{0,4},{2,6},{4,0},{6,2},{8,12},{10,14},{12,8},{14,10},{16,20},{18,... | collective-permute-start | bytes 983048 | tf_op jit(solution)/shard_map/ppermute | solution.py:62
  159.9 88.0 %collective-permute-start.29 = (bf16[256,640]{1,0:T(8,128)(2,1)S(1)}, bf16[256,640]{1,0:T(8,128)(2,1)S(1)}, u32[]{:S(2)}, u32[]{:S(2)}) collective-permute-start(bf16[256,640]{1,0:T(8,128)(2,1)S(1)} %get-tuple-element.154), channel_id=1, source_target_pairs={{2,0},{3,1},{4,2},{5,3},{6,4},{7,5},{8,6},{9,7},{10,8},{11,9},{12,... | collective-permute-start | bytes 983048 | tf_op jit(solution)/shard_map/ppermute | solution.py:73
  164.2 82.6 %collective-permute-start.28 = (bf16[2,352,384]{2,1,0:T(8,128)(2,1)S(1)}, bf16[2,352,384]{2,1,0:T(8,128)(2,1)S(1)}, u32[]{:S(2)}, u32[]{:S(2)}) collective-permute-start(bf16[2,352,384]{2,1,0:T(8,128)(2,1)S(1)} %fusion.6), channel_id=1, source_target_pairs={{0,1},{1,0},{2,3},{3,2},{4,5},{5,4},{6,7},{7,6},{8,9},{9,8},{10,11... | collective-permute-start | bytes 1622024 | tf_op jit(solution)/shard_map/ppermute | solution.py:68
  165.6 84.2 %collective-permute-start.27 = (bf16[256,640]{1,0:T(8,128)(2,1)S(1)}, bf16[256,640]{1,0:T(8,128)(2,1)S(1)}, u32[]{:S(2)}, u32[]{:S(2)}) collective-permute-start(bf16[256,640]{1,0:T(8,128)(2,1)S(1)} %get-tuple-element.151), channel_id=1, source_target_pairs={{1,0},{2,1},{3,2},{4,3},{5,4},{6,5},{7,6},{8,7},{9,8},{10,9},{11,1... | collective-permute-start | bytes 983048 | tf_op jit(solution)/shard_map/ppermute | solution.py:73
  169.8 17.3 %collective-permute-start.39 = (bf16[128,640]{1,0:T(8,128)(2,1)S(1)}, bf16[128,640]{1,0:T(8,128)(2,1)S(1)}, u32[]{:S(2)}, u32[]{:S(2)}) collective-permute-start(bf16[128,640]{1,0:T(8,128)(2,1)S(1)} %fusion.9), channel_id=1, source_target_pairs={{0,4},{2,6},{4,0},{6,2},{8,12},{10,14},{12,8},{14,10},{16,20},{18,... | collective-permute-start | bytes 491528 | tf_op jit(solution)/shard_map/ppermute | solution.py:62
  187.1 31.4 %collective-permute-start.56 = (bf16[320,512]{1,0:T(8,128)(2,1)S(1)}, bf16[320,512]{1,0:T(8,128)(2,1)S(1)}, u32[]{:S(2)}, u32[]{:S(2)}) collective-permute-start(bf16[320,512]{1,0:T(8,128)(2,1)S(1)} %fusion.3), channel_id=1, source_target_pairs={{0,4},{2,6},{4,0},{6,2},{8,12},{10,14},{12,8},{14,10},{16,20},{18,... | collective-permute-start | bytes 983048 | tf_op jit(solution)/shard_map/ppermute | solution.py:62
  223.6 8.7 %collective-permute-start.51 = (bf16[160,512]{1,0:T(8,128)(2,1)S(1)}, bf16[160,512]{1,0:T(8,128)(2,1)S(1)}, u32[]{:S(2)}, u32[]{:S(2)}) collective-permute-start(bf16[160,512]{1,0:T(8,128)(2,1)S(1)} %maximum_select_fusion.7), channel_id=1, source_target_pairs={{0,8},{2,10},{4,12},{6,14},{8,0},{10,2},{12,4},{14,6},{16,24},{18,... | collective-permute-start | bytes 491528 | tf_op jit(solution)/shard_map/ppermute | solution.py:65
  232.1 22.4 %collective-permute-start.44 = (bf16[128,640]{1,0:T(8,128)(2,1)S(1)}, bf16[128,640]{1,0:T(8,128)(2,1)S(1)}, u32[]{:S(2)}, u32[]{:S(2)}) collective-permute-start(bf16[128,640]{1,0:T(8,128)(2,1)S(1)} %maximum_select_fusion.6), channel_id=1, source_target_pairs={{0,4},{2,6},{4,0},{6,2},{8,12},{10,14},{12,8},{14,10},{16,20},{18,... | collective-permute-start | bytes 491528 | tf_op jit(solution)/shard_map/ppermute | solution.py:62
  232.3 32.4 %collective-permute-start.45 = (bf16[128,640]{1,0:T(8,128)(2,1)S(1)}, bf16[128,640]{1,0:T(8,128)(2,1)S(1)}, u32[]{:S(2)}, u32[]{:S(2)}) collective-permute-start(bf16[128,640]{1,0:T(8,128)(2,1)S(1)} %maximum_select_fusion.6), channel_id=1, source_target_pairs={{0,2},{2,0},{4,6},{6,4},{8,10},{10,8},{12,14},{14,12},{16,18},{18,... | collective-permute-start | bytes 491528 | tf_op jit(solution)/shard_map/ppermute | solution.py:59
  246.8 6.6 %collective-permute-start.58 = (bf16[80,512]{1,0:T(8,128)(2,1)S(1)}, bf16[80,512]{1,0:T(8,128)(2,1)S(1)}, u32[]{:S(2)}, u32[]{:S(2)}) collective-permute-start(bf16[80,512]{1,0:T(8,128)(2,1)S(1)} %dynamic-slice_bitcast_fusion.1), channel_id=1, source_target_pairs={{0,16},{2,18},{4,20},{6,22},{8,24},{10,26},{12,28},{14,30},{16,0},... | collective-permute-start | bytes 245768 | tf_op jit(solution)/shard_map/ppermute | solution.py:65
  248.0 27.3 %collective-permute-start.68 = (bf16[256,640]{1,0:T(8,128)(2,1)S(1)}, bf16[256,640]{1,0:T(8,128)(2,1)S(1)}, u32[]{:S(2)}, u32[]{:S(2)}) collective-permute-start(bf16[256,640]{1,0:T(8,128)(2,1)S(1)} %maximum_select_fusion.2), channel_id=1, source_target_pairs={{0,4},{2,6},{4,0},{6,2},{8,12},{10,14},{12,8},{14,10},{16,20},{18,... | collective-permute-start | bytes 983048 | tf_op jit(solution)/shard_map/ppermute | solution.py:62
  249.8 14.1 %collective-permute-start.30 = (bf16[352,384]{1,0:T(8,128)(2,1)S(1)}, bf16[352,384]{1,0:T(8,128)(2,1)S(1)}, u32[]{:S(2)}, u32[]{:S(2)}) collective-permute-start(bf16[352,384]{1,0:T(8,128)(2,1)S(1)} %fusion.7), channel_id=1, source_target_pairs={{0,4},{2,6},{4,0},{6,2},{8,12},{10,14},{12,8},{14,10},{16,20},{18,... | collective-permute-start | bytes 811016 | tf_op jit(solution)/shard_map/ppermute | solution.py:62
  254.5 30.8 %collective-permute-start.69 = (bf16[256,640]{1,0:T(8,128)(2,1)S(1)}, bf16[256,640]{1,0:T(8,128)(2,1)S(1)}, u32[]{:S(2)}, u32[]{:S(2)}) collective-permute-start(bf16[256,640]{1,0:T(8,128)(2,1)S(1)} %maximum_select_fusion.2), channel_id=1, source_target_pairs={{0,2},{2,0},{4,6},{6,4},{8,10},{10,8},{12,14},{14,12},{16,18},{18,... | collective-permute-start | bytes 983048 | tf_op jit(solution)/shard_map/ppermute | solution.py:59
  259.6 6.8 %collective-permute-start.46 = (bf16[128,640]{1,0:T(8,128)(2,1)S(1)}, bf16[128,640]{1,0:T(8,128)(2,1)S(1)}, u32[]{:S(2)}, u32[]{:S(2)}) collective-permute-start(bf16[128,640]{1,0:T(8,128)(2,1)S(1)} %collective-permute-done.44), channel_id=1, source_target_pairs={{0,2},{2,0},{4,6},{6,4},{8,10},{10,8},{12,14},{14,12},{16,18},{18,... | collective-permute-start | bytes 491528 | tf_op jit(solution)/shard_map/ppermute | solution.py:59
  263.9 21.4 %collective-permute-start.52 = (bf16[320,512]{1,0:T(8,128)(2,1)S(1)}, bf16[320,512]{1,0:T(8,128)(2,1)S(1)}, u32[]{:S(2)}, u32[]{:S(2)}) collective-permute-start(bf16[320,512]{1,0:T(8,128)(2,1)S(1)} %maximum_select_fusion), channel_id=1, source_target_pairs={{0,4},{2,6},{4,0},{6,2},{8,12},{10,14},{12,8},{14,10},{16,20},{18,... | collective-permute-start | bytes 983048 | tf_op jit(solution)/shard_map/ppermute | solution.py:62
  264.7 9.8 %collective-permute-start.60 = (bf16[160,512]{1,0:T(8,128)(2,1)S(1)}, bf16[160,512]{1,0:T(8,128)(2,1)S(1)}, u32[]{:S(2)}, u32[]{:S(2)}) collective-permute-start(bf16[160,512]{1,0:T(8,128)(2,1)S(1)} %maximum_select_fusion.8), channel_id=1, source_target_pairs={{0,8},{2,10},{4,12},{6,14},{8,0},{10,2},{12,4},{14,6},{16,24},{18,... | collective-permute-start | bytes 491528 | tf_op jit(solution)/shard_map/ppermute | solution.py:65
  274.5 11.3 %collective-permute-start.61 = (bf16[320,512]{1,0:T(8,128)(2,1)S(1)}, bf16[320,512]{1,0:T(8,128)(2,1)S(1)}, u32[]{:S(2)}, u32[]{:S(2)}) collective-permute-start(bf16[320,512]{1,0:T(8,128)(2,1)S(1)} %maximum_select_fusion.1), channel_id=1, source_target_pairs={{0,4},{2,6},{4,0},{6,2},{8,12},{10,14},{12,8},{14,10},{16,20},{18,... | collective-permute-start | bytes 983048 | tf_op jit(solution)/shard_map/ppermute | solution.py:62
  275.3 12.0 %collective-permute-start.70 = (bf16[256,640]{1,0:T(8,128)(2,1)S(1)}, bf16[256,640]{1,0:T(8,128)(2,1)S(1)}, u32[]{:S(2)}, u32[]{:S(2)}) collective-permute-start(bf16[256,640]{1,0:T(8,128)(2,1)S(1)} %collective-permute-done.68), channel_id=1, source_target_pairs={{0,2},{2,0},{4,6},{6,4},{8,10},{10,8},{12,14},{14,12},{16,18},{18,... | collective-permute-start | bytes 983048 | tf_op jit(solution)/shard_map/ppermute | solution.py:59
  282.5 7.0 %collective-permute-start.53 = (bf16[320,512]{1,0:T(8,128)(2,1)S(1)}, bf16[320,512]{1,0:T(8,128)(2,1)S(1)}, u32[]{:S(2)}, u32[]{:S(2)}) collective-permute-start(bf16[320,512]{1,0:T(8,128)(2,1)S(1)} %maximum_select_fusion), channel_id=1, source_target_pairs={{0,2},{2,0},{4,6},{6,4},{8,10},{10,8},{12,14},{14,12},{16,18},{18,... | collective-permute-start | bytes 983048 | tf_op jit(solution)/shard_map/ppermute | solution.py:59
  285.2 9.3 %collective-permute-start.62 = (bf16[320,512]{1,0:T(8,128)(2,1)S(1)}, bf16[320,512]{1,0:T(8,128)(2,1)S(1)}, u32[]{:S(2)}, u32[]{:S(2)}) collective-permute-start(bf16[320,512]{1,0:T(8,128)(2,1)S(1)} %maximum_select_fusion.1), channel_id=1, source_target_pairs={{0,2},{2,0},{4,6},{6,4},{8,10},{10,8},{12,14},{14,12},{16,18},{18,... | collective-permute-start | bytes 983048 | tf_op jit(solution)/shard_map/ppermute | solution.py:59
  287.3 7.2 %collective-permute-start.63 = (bf16[320,512]{1,0:T(8,128)(2,1)S(1)}, bf16[320,512]{1,0:T(8,128)(2,1)S(1)}, u32[]{:S(2)}, u32[]{:S(2)}) collective-permute-start(bf16[320,512]{1,0:T(8,128)(2,1)S(1)} %collective-permute-done.61), channel_id=1, source_target_pairs={{0,2},{2,0},{4,6},{6,4},{8,10},{10,8},{12,14},{14,12},{16,18},{18,... | collective-permute-start | bytes 983048 | tf_op jit(solution)/shard_map/ppermute | solution.py:59
  291.5 11.2 %collective-permute-start.36 = (bf16[352,384]{1,0:T(8,128)(2,1)S(1)}, bf16[352,384]{1,0:T(8,128)(2,1)S(1)}, u32[]{:S(2)}, u32[]{:S(2)}) collective-permute-start(bf16[352,384]{1,0:T(8,128)(2,1)S(1)} %maximum_select_fusion.3), channel_id=1, source_target_pairs={{0,2},{2,0},{4,6},{6,4},{8,10},{10,8},{12,14},{14,12},{16,18},{18,... | collective-permute-start | bytes 811016 | tf_op jit(solution)/shard_map/ppermute | solution.py:59
  292.0 7.9 %collective-permute-start.35 = (bf16[352,384]{1,0:T(8,128)(2,1)S(1)}, bf16[352,384]{1,0:T(8,128)(2,1)S(1)}, u32[]{:S(2)}, u32[]{:S(2)}) collective-permute-start(bf16[352,384]{1,0:T(8,128)(2,1)S(1)} %maximum_select_fusion.3), channel_id=1, source_target_pairs={{0,4},{2,6},{4,0},{6,2},{8,12},{10,14},{12,8},{14,10},{16,20},{18,... | collective-permute-start | bytes 811016 | tf_op jit(solution)/shard_map/ppermute | solution.py:62
  (66 other events, 522.1 us)

commit v5 on v4

--- a/solution.py
+++ b/solution.py
@@ -34,7 +34,6 @@
         self.seq = lax.axis_size("seq")
         self.fsdp = lax.axis_size("fsdp")
         self.outer = self.seq // 4
-        self.bits = self.outer.bit_length() - 1
         index = lax.axis_index("seq").astype(jnp.int32)
         fsdp_at = lax.axis_index("fsdp").astype(jnp.int32)
         outer_at = lax.shift_right_logical(index, 2)
@@ -45,15 +44,15 @@
                 mid_at,
                 fsdp_at,
                 core_at * 2 + mid_at,
-                tuple(lax.shift_right_logical(outer_at, bit) & 1 for bit in range(self.bits)),
-                tuple(1 - (lax.shift_right_logical(outer_at, bit) & 1) for bit in range(self.bits)),
+                tuple(wrapped(outer_at + by, self.outer) for by in range(self.outer)),
+                tuple(wrapped(outer_at - by + self.outer, self.outer) for by in range(self.outer)),
                 tuple(wrapped(fsdp_at + by, self.fsdp) for by in range(self.fsdp)),
                 tuple(wrapped(fsdp_at - by + self.fsdp, self.fsdp) for by in range(self.fsdp)),
                 jnp.stack([core_at, mid_at, fsdp_at]),
             )
         )
         self.core_at, self.mid_at, self.fsdp_at, self.quarter_at = scalars[:4]
-        self.bit_at, self.bit_off, self.fsdp_ahead, self.fsdp_behind, self.vector = scalars[4:]
+        self.outer_ahead, self.outer_behind, self.fsdp_ahead, self.fsdp_behind, self.vector = scalars[4:]
 
     def core_swap(self, array):
         return lax.ppermute(array, "seq", [(i, i ^ 1) for i in range(self.seq)])
@@ -61,8 +60,8 @@
     def mid_swap(self, array):
         return lax.ppermute(array, "seq", [(i, i ^ 2) for i in range(self.seq)])
 
-    def outer_swap(self, array, bit):
-        return lax.ppermute(array, "seq", [(i, i ^ (4 << bit)) for i in range(self.seq)])
+    def outer_shift(self, array, by):
+        return lax.ppermute(array, "seq", [(i, (i + 4 * by) % self.seq) for i in range(self.seq)])
 
     def fsdp_shift(self, array, by):
         return lax.ppermute(array, "fsdp", [(i, (i + by) % self.fsdp) for i in range(self.fsdp)])
@@ -104,6 +103,10 @@
 
 def after(value, *earlier):
     return lax.optimization_barrier((value, *earlier))[0]
+
+
+def together(*groups):
+    return lax.optimization_barrier(tuple(tuple(group) for group in groups))
 
 
 def over_links(here, part):
@@ -191,17 +194,18 @@
 def attend_kernel(n_tok, n_qkv, heads, *refs):
     at = refs[0]
     toks = refs[1 : 1 + n_tok]
-    pos, cosine, sine, gain_in, gain_q, gain_k = refs[1 + n_tok : 7 + n_tok]
-    qkv = refs[7 + n_tok : 7 + n_tok + n_qkv]
-    normed, q_raw, k_raw, q_st, keys, values, probs, attended, w_full, sems = refs[7 + n_tok + n_qkv :]
-    copies = place_copies(qkv[:3], qkv[3:], w_full, sems, at, 1, 4)
+    pos, cosine, sine, gain_table = refs[1 + n_tok : 5 + n_tok]
+    qkv = refs[5 + n_tok : 5 + n_tok + n_qkv]
+    normed, q_raw, k_raw, q_st, keys, values, probs, attended, w_full, sems = refs[5 + n_tok + n_qkv :]
+    copies = place_copies(qkv[:3], qkv[3:], w_full, sems, at, 1, 2)
     for copy in copies:
         copy.start()
     rows = toks[0].shape[0]
     dim = keys.shape[1]
     half = dim // 2
     halo = (n_tok - 1) * rows
-    gain = gain_in[...]
+    gain = gain_table[0:1, :]
+    gain_q, gain_k = gain_table[1:2, :dim], gain_table[2:3, :dim]
     for i, tok in enumerate(toks):
         u = tok[...].astype(F32)
         normed[i * rows : (i + 1) * rows, :] = (u * inverse_rms(u) * gain).astype(BF16)
@@ -218,14 +222,14 @@
         kv = dot(normed[here, :], w_full[:, heads * dim :])
         k_raw[here, :] = kv[:, :dim]
         values[here, :] = kv[:, dim:].astype(BF16)
-        first, second = turned(kv[:, :dim], gain_k[...], cosine[here, :], sine[here, :])
+        first, second = turned(kv[:, :dim], gain_k, cosine[here, :], sine[here, :])
         keys[here, :half] = first
         keys[here, half:] = second
     blocks = rows // QBLOCK
     for h in range(heads):
         u = dot(normed[halo:, :], w_full[:, h * dim : (h + 1) * dim])
         q_raw[:, h * dim : (h + 1) * dim] = u
-        first, second = turned(u, gain_q[...], cosine[halo:, :], sine[halo:, :])
+        first, second = turned(u, gain_q, cosine[halo:, :], sine[halo:, :])
         for b in range(blocks):
             start = (b * heads + h) * QBLOCK
             q_st[start : start + QBLOCK, :half] = first[b * QBLOCK : (b + 1) * QBLOCK, :]
@@ -254,8 +258,8 @@
 
 
 def gate_kernel(n_out, n_gate, n_up, *refs):
-    at, attended, tokens, gain_attn, gain_ffn = refs[:5]
-    refs = refs[5:]
+    at, attended, tokens, gain_table = refs[:4]
+    refs = refs[4:]
     out_w, gate_w, up_w, refs = (
         refs[:n_out],
         refs[n_out : n_out + n_gate],
@@ -267,7 +271,7 @@
     groups = (
         place_copies(out_w[:1], out_w[1:], out_full, out_sems, at, 0, 2),
         place_copies(gate_w[:1], gate_w[1:], gate_full, gate_sems, at, 1, 4),
-        place_copies(up_w[:1], up_w[1:], up_full, up_sems, at, 1, 4),
+        place_copies(up_w[:1], up_w[1:], up_full, up_sems, at, 1, 2),
     )
     for group in groups:
         for copy in group:
@@ -276,9 +280,9 @@
         copy.wait()
     projected = dot(attended[...], out_full[...])
     projected_ref[...] = projected
-    residual = tokens[...].astype(F32) + projected * inverse_rms(projected) * gain_attn[...]
+    residual = tokens[...].astype(F32) + projected * inverse_rms(projected) * gain_table[3:4, :]
     residual_ref[...] = residual
-    ffn_in_ref[...] = (residual * inverse_rms(residual) * gain_ffn[...]).astype(BF16)
+    ffn_in_ref[...] = (residual * inverse_rms(residual) * gain_table[4:5, :]).astype(BF16)
     for group in groups[1:]:
         for copy in group:
             copy.wait()
@@ -321,7 +325,7 @@
 
 
 def down_kernel(n_down, fsdp, *refs):
-    at, mixed, residual, cotangent, gain_out = refs[:5]
+    at, mixed, residual, cotangent, gain_table = refs[:5]
     down_w = refs[5 : 5 + n_down]
     layer_out, d_down, grad_gain, keep, send = refs[5 + n_down : 10 + n_down]
     down_full, mixed_t, sems = refs[10 + n_down :]
@@ -333,7 +337,7 @@
         copy.wait()
     down = dot(mixed[...], down_full[...])
     r = inverse_rms(down)
-    gain = gain_out[...]
+    gain = gain_table[5:6, :]
     layer_out[...] = (residual[...] + down * r * gain).astype(BF16)
     du, dg = norm_back(down, gain, cotangent[...].astype(F32))
     grad_gain[...] = dg
@@ -348,8 +352,8 @@
 def gate_back_kernel(n_down, fsdp, *refs):
     at, d_down, gelu_out, gate_slope, ffn_in = refs[:5]
     down_w = refs[5 : 5 + n_down]
-    d_gate, d_up, ffn_t, keep, send = refs[5 + n_down : 10 + n_down]
-    down_full, sems = refs[10 + n_down :]
+    d_gate, d_up, keep, send, up_keep, up_send = refs[5 + n_down : 11 + n_down]
+    down_full, ffn_t, sems = refs[11 + n_down :]
     copies = place_copies(down_w[:1], down_w[1:], down_full, sems, at, 0, 2)
     for copy in copies:
         copy.start()
@@ -367,15 +371,12 @@
 
     lax.fori_loop(0, d_gate.shape[1] // width, step, 0)
     column_blocks(at, fsdp, ffn_t, d_gate, keep, send)
-
-
-def up_back_kernel(fsdp, at, ffn_t, d_up, keep, send):
-    column_blocks(at, fsdp, ffn_t, d_up, keep, send)
+    column_blocks(at, fsdp, ffn_t, d_up, up_keep, up_send)
 
 
 def middle_kernel(n_out, n_gate, n_up, fsdp, heads, *refs):
-    at, d_gate, d_up, residual, projected, cotangent, gain_ffn, gain_attn, attended = refs[:9]
-    refs = refs[9:]
+    at, d_gate, d_up, residual, projected, cotangent, gain_table, attended = refs[:8]
+    refs = refs[8:]
     out_w, gate_w, up_w, refs = (
         refs[:n_out],
         refs[n_out : n_out + n_gate],
@@ -386,7 +387,7 @@
     out_full, gate_full, up_full, att_t, out_sems, gate_sems, up_sems = refs[6:]
     groups = (
         place_copies(gate_w[:1], gate_w[1:], gate_full, gate_sems, at, 1, 4),
-        place_copies(up_w[:1], up_w[1:], up_full, up_sems, at, 1, 4),
+        place_copies(up_w[:1], up_w[1:], up_full, up_sems, at, 1, 2),
         place_copies(out_w[:1], out_w[1:], out_full, out_sems, at, 0, 2),
     )
     for group in groups:
@@ -399,11 +400,11 @@
     for copy in groups[1]:
         copy.wait()
     d_ffn_in = d_ffn_in + dot_nt(d_up[...], up_full[...])
-    du, dg = norm_back(residual[...], gain_ffn[...], d_ffn_in)
+    du, dg = norm_back(residual[...], gain_table[4:5, :], d_ffn_in)
     g_ffn[...] = dg
     d_residual = cotangent[...].astype(F32) + du
     d_residual_ref[...] = d_residual
-    du, dg = norm_back(projected[...], gain_attn[...], d_residual)
+    du, dg = norm_back(projected[...], gain_table[3:4, :], d_residual)
     g_attn[...] = dg
     d_proj = du.astype(BF16)
     rows, dim = d_proj.shape[0], d_att.shape[1]
@@ -414,11 +415,17 @@
         for b in range(rows // QBLOCK):
             start = (b * heads + h) * QBLOCK
             d_att[start : start + QBLOCK, :] = part[b * QBLOCK : (b + 1) * QBLOCK, :]
-    block = keep.shape[2]
+    block = att_t.shape[0] // (4 * fsdp)
+    wide = keep.shape[3]
+    parts = wide // LANES
+    deep = block // parts
     for c, f, x, core, row, mid in relative_blocks(at, fsdp):
         start = multiple(((row * 2 + core) * 2 + mid) * block, 16)
+        part = dot(att_t[pl.ds(start, block), :], d_proj).astype(BF16)
         target = keep if c == 0 else send
-        target[f, x] = dot(att_t[pl.ds(start, block), :], d_proj).astype(BF16)
+        target[f, x, :block, :] = part[:, :wide]
+        for i in range(parts):
+            target[f, x, block:, i * LANES : (i + 1) * LANES] = part[i * deep : (i + 1) * deep, wide:]
 
 
 def attend_back_kernel(halo, heads, d_att, q_st, keys, values, probs, d_q, d_k, d_v, d_scores):
@@ -449,20 +456,21 @@
 def last_kernel(n_qkv, n_tok, fsdp, heads, *refs):
     (
         at, d_residual, d_q, d_k, d_v,
-        q_raw, k_raw, cosine, sine, gain_q, gain_k, gain_in, normed, g_ffn, g_attn, g_out,
-    ) = refs[:16]
-    toks = refs[16 : 16 + n_tok]
-    refs = refs[16 + n_tok :]
+        q_raw, k_raw, cosine, sine, gain_table, normed, g_ffn, g_attn, g_out,
+    ) = refs[:14]
+    toks = refs[14 : 14 + n_tok]
+    refs = refs[14 + n_tok :]
     qkv_w, refs = refs[:n_qkv], refs[n_qkv:]
     grad_tokens, d_halo, keep, send = refs[:4]
     w_full, normed_t, d_qkv, gain_rows, qkv_sems = refs[4:]
-    copies = place_copies(qkv_w[:3], qkv_w[3:], w_full, qkv_sems, at, 1, 4)
+    copies = place_copies(qkv_w[:3], qkv_w[3:], w_full, qkv_sems, at, 1, 2)
     for copy in copies:
         copy.start()
     normed_t[...] = normed[...].T
     rows = toks[0].shape[0]
     halo = (n_tok - 1) * rows
     dim = k_raw.shape[1]
+    gain_in, gain_q, gain_k = gain_table[0:1, :], gain_table[1:2, :dim], gain_table[2:3, :dim]
     half = dim // 2
     tall, wide = normed_t.shape[0] // fsdp, keep.shape[3]
     def turned_back(u, g, dz, cos, sin):
@@ -475,13 +483,13 @@
         d_qkv[:halo, : heads * dim] = jnp.zeros((halo, heads * dim), BF16)
     for h in range(heads):
         cut = slice(h * dim, (h + 1) * dim)
-        du, dg = turned_back(q_raw[:, cut], gain_q[...], d_q[:, cut], cosine[halo:, :], sine[halo:, :])
+        du, dg = turned_back(q_raw[:, cut], gain_q, d_q[:, cut], cosine[halo:, :], sine[halo:, :])
         total_q += dg
         d_qkv[halo:, cut] = du.astype(BF16)
     total_k = jnp.zeros((1, dim), F32)
     for i in range(n_tok):
         here = slice(i * rows, (i + 1) * rows)
-        du, dg = turned_back(k_raw[here, :], gain_k[...], d_k[here, :], cosine[here, :], sine[here, :])
+        du, dg = turned_back(k_raw[here, :], gain_k, d_k[here, :], cosine[here, :], sine[here, :])
         total_k += dg
         d_qkv[here, heads * dim : (heads + 1) * dim] = du.astype(BF16)
         d_qkv[here, (heads + 1) * dim :] = d_v[here, :].astype(BF16)
@@ -495,7 +503,7 @@
             d_normed = dot_nt(d_qkv[here, heads * dim :], w_full[:, heads * dim :])
         else:
             d_normed = dot_nt(d_qkv[here, :], w_full[...])
-        du, dg = norm_back(toks[i][...].astype(F32), gain_in[...], d_normed)
+        du, dg = norm_back(toks[i][...].astype(F32), gain_in, d_normed)
         total_in += dg
         if i < n_tok - 1:
             d_halo[here, :] = du.astype(BF16)
@@ -525,7 +533,6 @@
     def __init__(self, here, keep, send):
         self.here, self.keep = here, keep
         self.other = here.core_swap(send)
-        self.sums = []
 
     def over_fsdp(self, *earlier):
         here = self.here
@@ -536,33 +543,45 @@
         self.arrived = [after(a, *earlier) for a in self.arrived]
         terms = [self.keep[0, 1], self.other[0, 1]] + [a[1] for a in self.arrived]
         self.across = self.here.mid_swap(add(*terms).astype(BF16))
-
-    def gather_sums(self, bit, *earlier):
+        self.mine = [self.keep[0, 0], self.other[0, 0]] + [a[0] for a in self.arrived]
+        return self.arrived[0] if self.arrived else self.other
+
+    def join(self, below, *earlier):
+        for chunk in (self, below):
+            chunk.arrived = [after(a, *earlier) for a in chunk.arrived]
+        pairs = [
+            [[c.keep[0, x], c.other[0, x]] + [a[x] for a in c.arrived] for c in (self, below)] for x in range(2)
+        ]
+        self.across_sent = jnp.concatenate([add(*terms).astype(BF16) for terms in pairs[1]])
+        self.across = self.here.mid_swap(self.across_sent)
+        self.mine = [jnp.concatenate([add(*terms).astype(BF16) for terms in pairs[0]])]
+
+    def outer_sums(self, *earlier):
         here = self.here
-        if bit == 0:
-            self.across = after(self.across, *earlier)
-            terms = [self.keep[0, 0], self.other[0, 0]] + [a[0] for a in self.arrived] + [self.across]
-        else:
-            terms = [after(self.sums[-1], *earlier)]
-        n, w = terms[0].shape
-        halves = [term.reshape(2, n // 2, w) for term in terms]
-        off = add(*[pick(half, here.bit_off[bit]) for half in halves]).astype(BF16)
-        came = here.outer_swap(off, bit)
-        self.sums.append(add(*[pick(half, here.bit_at[bit]) for half in halves], came).astype(BF16))
-
-    def finish(self, *earlier, last=()):
+        self.across = after(self.across, *earlier)
+        mine = add(*self.mine, self.across).astype(BF16)
+        n, w = mine.shape
+        mine = mine.reshape(here.outer, n // here.outer, w)
+        self.shares = [pick(mine, here.outer_ahead[0])]
+        for by in range(1, here.outer):
+            self.shares.append(here.outer_shift(pick(mine, here.outer_ahead[by]), by))
+        return self.across
+
+    def outer_gather(self, *earlier):
         here = self.here
-        for bit in range(len(self.sums), here.bits):
-            self.gather_sums(bit, *earlier)
-        block = self.sums[-1]
-        for bit in reversed(range(here.bits)):
-            n, w = block.shape
-            both = [block, here.outer_swap(block, bit)]
-            low, high = jnp.concatenate(both), jnp.concatenate(both[::-1])
-            block = jnp.where(here.bit_at[bit] == 0, low, high)
-        block = after(block, *last)
+        self.shares = list(after(tuple(self.shares), *earlier))
+        own = add(*self.shares).astype(BF16)
+        self.gathered = [own] + [here.outer_shift(own, by) for by in range(1, here.outer)]
+        return self.shares[-1]
+
+    def mid_gather(self, *earlier):
+        here = self.here
+        self.gathered = list(after(tuple(self.gathered), *earlier))
+        block = ordered(self.gathered, here.outer_behind)
+        block = block.reshape(-1, block.shape[-1])
         across = here.mid_swap(block)
-        return [[block, across], [here.core_swap(block), here.core_swap(across)]]
+        self.blocks = [[block, across], [here.core_swap(block), here.core_swap(across)]]
+        return self.gathered[-1]
 
 
 def by_place(here, blocks):
@@ -598,17 +617,22 @@
     gain_row = jnp.concatenate(gains)
     gain_rows = ordered([gain_row] + [here.fsdp_shift(gain_row, by) for by in range(1, fsdp)], here.fsdp_behind)
     gain_rows = gain_rows.astype(F32)
-    gain_in, gain_q, gain_k, gain_attn, gain_ffn, gain_out = (
-        gain_rows[:, cuts[i] : cuts[i + 1]].reshape(1, -1) for i in range(6)
+    gain_table = jnp.concatenate(
+        [
+            jnp.pad(gain_rows[:, cuts[i] : cuts[i + 1]].reshape(1, -1), ((0, 0), (0, width - fsdp * gains[i].shape[0])))
+            for i in range(6)
+        ]
+        + [jnp.zeros((2, width), F32)],
+        axis=0,
     )
     qkv_w = [w_query, w_key, w_value]
-    qkv_part = own_part(here, qkv_w, 1, 4)
+    qkv_part = own_part(here, qkv_w, 1, 2)
     tokens_out = after(tokens, qkv_part)
     toks = [linear_shift(tokens_out, by) for by in range(hops, 0, -1)] + [tokens]
-    qkv_w += on_chips(here, over_links(here, qkv_part), 4)
+    qkv_w += on_chips(here, over_links(here, qkv_part), 2)
     out_arrived = over_links(here, after(own_part(here, [w_out], 0, 2), *toks[:-1]))
     gate_arrived = over_links(here, after(own_part(here, [w_gate], 1, 4), qkv_w[3]))
-    up_arrived = over_links(here, after(own_part(here, [w_up], 1, 4), out_arrived[0]))
+    up_arrived = over_links(here, after(own_part(here, [w_up], 1, 2), out_arrived[0]))
 
     all_positions = jnp.concatenate([positions[0] - halo + jnp.arange(halo, dtype=jnp.int32), positions])
     frequency = ROPE_BASE ** (-(jnp.arange(dim // 2, dtype=F32) * 2.0 / dim))
@@ -629,7 +653,7 @@
             shape((heads * rows, span), BF16),
             shape((rows, query_cols), BF16),
         ),
-        in_specs=[SMEM] + [VMEM] * (n_tok + 6) + [ANY] * len(qkv_w),
+        in_specs=[SMEM] + [VMEM] * (n_tok + 4) + [ANY] * len(qkv_w),
         out_specs=(VMEM,) * 8,
         scratch_shapes=[
             pltpu.VMEM((width, query_cols + 2 * dim), BF16),
@@ -638,12 +662,12 @@
         compiler_params=params(),
         cost_estimate=cost(4e9, 1e7),
         name="attend",
-    )(at, *toks, positions[:, None], cosine, sine, gain_in, gain_q, gain_k, *qkv_w)
+    )(at, *toks, positions[:, None], cosine, sine, gain_table, *qkv_w)
 
     down_arrived = over_links(here, after(own_part(here, [w_down], 0, 2), attended))
     out_w = [w_out] + on_chips(here, [after(a, attended) for a in out_arrived], 2)
     gate_w = [w_gate] + on_chips(here, [after(a, attended) for a in gate_arrived], 4)
-    up_w = [w_up] + on_chips(here, [after(a, attended) for a in up_arrived], 4)
+    up_w = [w_up] + on_chips(here, [after(a, attended) for a in up_arrived], 2)
     projected, residual, ffn_in, mixed, gelu_out, gate_slope = pl.pallas_call(
         functools.partial(gate_kernel, len(out_w), len(gate_w), len(up_w)),
         out_shape=(
@@ -654,7 +678,7 @@
             shape((rows, hidden), BF16),
             shape((rows, hidden), BF16),
         ),
-        in_specs=[SMEM] + [VMEM] * 4 + [ANY] * (len(out_w) + len(gate_w) + len(up_w)),
+        in_specs=[SMEM] + [VMEM] * 3 + [ANY] * (len(out_w) + len(gate_w) + len(up_w)),
         out_specs=(VMEM,) * 6,
         scratch_shapes=[
             pltpu.VMEM((query_cols, width), BF16),
@@ -667,7 +691,7 @@
         compiler_params=params(),
         cost_estimate=cost(4e9, 2 * weight_bytes),
         name="gate",
-    )(at, attended, tokens, gain_attn, gain_ffn, *out_w, *gate_w, *up_w)
+    )(at, attended, tokens, gain_table, *out_w, *gate_w, *up_w)
 
     down_w = [w_down] + on_chips(here, [after(a, mixed) for a in down_arrived], 2)
     down_block = w_down.shape[0] // 4
@@ -691,23 +715,25 @@
         compiler_params=params(),
         cost_estimate=cost(4e9, 2 * weight_bytes),
         name="down",
-    )(at, mixed, residual, cotangent, gain_out, *down_w)
+    )(at, mixed, residual, cotangent, gain_table, *down_w)
 
     down_sum = Chunk(here, down_keep, down_send)
     gate_shape = shape((fsdp, 2, w_gate.shape[0], hidden // 4), BF16)
-    d_gate, d_up, ffn_t, gate_keep, gate_send = pl.pallas_call(
+    d_gate, d_up, gate_keep, gate_send, up_keep, up_send = pl.pallas_call(
         functools.partial(gate_back_kernel, len(down_w), fsdp),
         out_shape=(
             shape((rows, hidden), BF16),
             shape((rows, hidden), BF16),
-            shape((width, rows), BF16),
+            gate_shape,
+            gate_shape,
             gate_shape,
             gate_shape,
         ),
         in_specs=[SMEM] + [VMEM] * 4 + [ANY] * len(down_w),
-        out_specs=(VMEM,) * 5,
+        out_specs=(VMEM,) * 6,
         scratch_shapes=[
             pltpu.VMEM((hidden, width), BF16),
+            pltpu.VMEM((width, rows), BF16),
             pltpu.SemaphoreType.DMA((len(down_w),)),
         ],
         compiler_params=params(),
@@ -715,24 +741,15 @@
         name="gate_back",
     )(at, d_down, gelu_out, gate_slope, ffn_in, *down_w)
     gate_sum = Chunk(here, gate_keep, gate_send)
-    up_keep, up_send = pl.pallas_call(
-        functools.partial(up_back_kernel, fsdp),
-        out_shape=(gate_shape, gate_shape),
-        in_specs=[SMEM] + [VMEM] * 2,
-        out_specs=(VMEM,) * 2,
-        compiler_params=params(),
-        cost_estimate=cost(6e9, 3 * weight_bytes),
-        name="up_back",
-    )(at, ffn_t, after(d_up, down_sum.other))
     up_sum = Chunk(here, up_keep, up_send)
     down_sum.over_fsdp(d_gate)
-    d_gate = after(d_gate, gate_sum.other, up_keep)
-
+    d_gate = after(d_gate, down_sum.other)
     qkv_cols = query_cols + 2 * dim
     last_wide = qkv_cols // 4
     shard_rows = w_query.shape[0]
     last_shape = shape((fsdp, 2, shard_rows + GAIN_ROWS, last_wide), BF16)
-    out_shape = shape((fsdp, 2, w_out.shape[0] // 4, width), BF16)
+    out_block = w_out.shape[0] // 4
+    out_shape = shape((fsdp, 2, out_block * width // (hidden // 4), hidden // 4), BF16)
     d_residual, g_ffn, g_attn, d_att, out_keep, out_send = pl.pallas_call(
         functools.partial(middle_kernel, len(out_w), len(gate_w), len(up_w), fsdp, heads),
         out_shape=(
@@ -743,7 +760,7 @@
             out_shape,
             out_shape,
         ),
-        in_specs=[SMEM] + [VMEM] * 8 + [ANY] * (len(out_w) + len(gate_w) + len(up_w)),
+        in_specs=[SMEM] + [VMEM] * 7 + [ANY] * (len(out_w) + len(gate_w) + len(up_w)),
         out_specs=(VMEM,) * 6,
         scratch_shapes=[
             pltpu.VMEM((query_cols, width), BF16),
@@ -757,10 +774,12 @@
         compiler_params=params(),
         cost_estimate=cost(6e9, 4 * weight_bytes),
         name="middle",
-    )(at, d_gate, d_up, residual, projected, cotangent, gain_ffn, gain_attn, attended, *out_w, *gate_w, *up_w)
+    )(at, d_gate, d_up, residual, projected, cotangent, gain_table, attended, *out_w, *gate_w, *up_w)
 
     out_sum = Chunk(here, out_keep, out_send)
-    gate_sum.over_fsdp(up_keep)
+    gate_sum.over_fsdp(g_ffn)
+    up_sum.over_fsdp(g_ffn)
+    down_sum.over_mid(g_ffn)
     d_q, d_k, d_v = pl.pallas_call(
         functools.partial(attend_back_kernel, halo, heads),
         out_shape=(shape((rows, query_cols), F32), shape((every, dim), F32), shape((every, dim), F32)),
@@ -770,13 +789,10 @@
         compiler_params=params(),
         cost_estimate=cost(6e9, 3 * weight_bytes),
         name="attend_back",
-    )(after(d_att, up_sum.other, *down_sum.arrived), q_st, keys, values, probs)
-    down_sum.over_mid(g_ffn)
-    up_sum.over_fsdp(g_ffn)
-    d_k_token = d_k
-    d_q = after(d_q, out_sum.other, down_sum.across, *gate_sum.arrived)
-    gate_sum.over_mid(d_k_token)
-    out_sum.over_fsdp(d_k_token)
+    )(after(d_att, gate_sum.other, up_sum.other, *down_sum.arrived), q_st, keys, values, probs)
+    out_sum.over_fsdp(d_k)
+    down_sum.outer_sums(d_k)
+    d_q = after(d_q, out_sum.other, down_sum.across)
     grad_tokens, d_halo, last_keep, last_send = pl.pallas_call(
         functools.partial(last_kernel, len(qkv_w), n_tok, fsdp, heads),
         out_shape=(
@@ -785,7 +801,7 @@
             last_shape,
             last_shape,
         ),
-        in_specs=[SMEM] + [VMEM] * (15 + n_tok) + [ANY] * len(qkv_w),
+        in_specs=[SMEM] + [VMEM] * (13 + n_tok) + [ANY] * len(qkv_w),
         out_specs=(VMEM,) * 4,
         scratch_shapes=[
             pltpu.VMEM((width, qkv_cols), BF16),
@@ -799,33 +815,60 @@
         name="last",
     )(
         at, d_residual, d_q, d_k, d_v,
-        q_raw, k_raw, cosine, sine, gain_q, gain_k, gain_in, normed, g_ffn, g_attn, g_ffn_out, *toks, *qkv_w,
+        q_raw, k_raw, cosine, sine, gain_table, normed, g_ffn, g_attn, g_ffn_out, *toks, *qkv_w,
     )
 
     last_sum = Chunk(here, last_keep, last_send)
+    gate_sum.over_mid(last_keep)
+    down_sum.outer_sums(last_keep)
+    (last_sum.other,), (gate_sum.across,), down_sum.shares, up_sum.arrived, out_sum.arrived = together(
+        (last_sum.other,), (gate_sum.across,), down_sum.shares, up_sum.arrived, out_sum.arrived
+    )
     last_sum.over_fsdp()
-    arrived = last_sum.other
-    down_blocks = by_place(here, down_sum.finish(arrived))
-    gate_blocks = by_place(here, gate_sum.finish(arrived, last=last_sum.arrived))
-    up_sum.over_mid(arrived)
-    out_sum.over_mid(arrived)
-    up_blocks = by_place(here, up_sum.finish())
-    out_blocks = by_place(here, out_sum.finish())
+    up_sum.join(out_sum)
+    gate_sum.outer_sums()
+    down_sum.outer_gather()
+    last_sum.arrived, (up_sum.across,), gate_sum.shares, down_sum.gathered = together(
+        last_sum.arrived, (up_sum.across,), gate_sum.shares, down_sum.gathered
+    )
     last_sum.over_mid()
-    last_blocks = last_sum.finish()
-    total_gains = last_blocks[0][0][shard_rows:, :LANES].astype(F32)
-    last_blocks = by_place(here, last_blocks)
-
-    for by in range(1, hops + 1):
-        start = halo - by * rows
-        came = linear_shift(after(d_halo[start : start + rows], arrived), -by)
-        grad_tokens = grad_tokens + after(came, *last_sum.arrived).astype(F32)
+    up_sum.outer_sums()
+    gate_sum.outer_gather()
+    down_sum.mid_gather()
+    (last_sum.across,), up_sum.shares, gate_sum.gathered, down_last = together(
+        (last_sum.across,), up_sum.shares, gate_sum.gathered, down_sum.blocks[0]
+    )
+    down_sum.blocks[0] = list(down_last)
+    last_sum.outer_sums()
+    up_sum.outer_gather()
+    gate_sum.mid_gather()
+    halos = [linear_shift(after(d_halo, last_sum.across)[halo - by * rows :][:rows], -by) for by in range(1, hops + 1)]
+    last_sum.shares, up_sum.gathered, gate_last, halos = together(
+        last_sum.shares, up_sum.gathered, gate_sum.blocks[0], halos
+    )
+    gate_sum.blocks[0] = list(gate_last)
+    last_sum.outer_gather()
+    up_sum.mid_gather()
+    last_sum.mid_gather()
+    down_blocks, gate_blocks = by_place(here, down_sum.blocks), by_place(here, gate_sum.blocks)
+    both_blocks, last_blocks = by_place(here, up_sum.blocks), by_place(here, last_sum.blocks)
+    total_gains = last_sum.blocks[0][0][shard_rows:, :LANES].astype(F32)
+
+    for came in halos:
+        grad_tokens = grad_tokens + came.astype(F32)
 
     total_down = jnp.concatenate(down_blocks, axis=0).astype(F32)
     total_gate = jnp.concatenate(gate_blocks, axis=1).astype(F32)
-    total_up = jnp.concatenate(up_blocks, axis=1).astype(F32)
+    total_up = jnp.concatenate([b[:shard_rows] for b in both_blocks], axis=1).astype(F32)
     total_qkv = jnp.concatenate([b[:shard_rows] for b in last_blocks], axis=1).astype(F32)
-    total_out = jnp.concatenate(out_blocks, axis=0).astype(F32)
+    wide = hidden // 4
+    parts = wide // LANES
+    total_out = []
+    for block in both_blocks:
+        below = block[shard_rows + out_block :].reshape(out_block // parts, parts, LANES)
+        below = below.transpose(1, 0, 2).reshape(out_block, LANES)
+        total_out.append(jnp.concatenate([block[shard_rows : shard_rows + out_block], below], axis=1))
+    total_out = jnp.concatenate(total_out, axis=0).astype(F32)
     g, at_row = [], 0
     for gain in gains:
         deep = fsdp * gain.shape[0] // total_gains.shape[1]

time: 306 us -> 275 us (0.90)
  waiting for transfers between devices: 97.9 us -> 79.7 us
  local copies, waits for them, and re-layouts: 20 us -> 12.8 us
  starting transfers between devices: 95.5 us -> 89.6 us
  Pallas kernels: 68.3 us -> 64.8 us
  other arithmetic: 21 us -> 24.3 us
    ppermute x23 -> x19, starting transfers between devices: 39.3 us -> 17.2 us  [core_swap(): return lax.ppermute(array, 'seq', [(i, i ^ 1) for i in range(self.seq)])]
    ppermute x20 -> x24, waiting for transfers between devices: 47 us -> 29.4 us  [outer_shift(): lax.ppermute(array, 'seq', [(i, (i + 4 * by) % self.seq) for i in range(s...]
    ppermute x20 -> x24, starting transfers between devices: 24.3 us -> 33.7 us  [outer_shift(): lax.ppermute(array, 'seq', [(i, (i + 4 * by) % self.seq) for i in range(s...]
    ppermute x13 -> x9, waiting for transfers between devices: 15.2 us -> 10.4 us  [mid_swap(): return lax.ppermute(array, 'seq', [(i, i ^ 2) for i in range(self.seq)])]
    slice x16 -> x12, local copies, waits for them, and re-layouts: 4.48 us -> 0.21 us  [the longest x4 0.09 us: on_device(): b[:shard_rows]]
    pallas_call x1 -> x0, Pallas kernels: 3.9 us -> none  [on_device(): pl.pallas_call(functools.partial(up_back_kernel, fsdp), out_shape=(gate_s...]
    convert_element_type x13, other arithmetic: 3.55 us -> 7.11 us  [the longest x4 2.64 us: outer_sums(): mine = add(*self.mine, self.across).astype(BF16)]
    ppermute x11, starting transfers between devices: 9.26 us -> 12.8 us  [fsdp_shift(): lax.ppermute(array, 'fsdp', [(i, (i + by) % self.fsdp) for i in range(sel...]
  transfers between devices with their start and end apart: 71 -> 67, of which waited for: 27 -> 28; matrix products, arithmetic and copies ran while one was open for 10% -> 9% of each run, Pallas kernels for 16% -> 21%
where the time goes in v5:
time: 275 us; the launch traced here: 274 us
  starting transfers between devices  89.6 us (33%)
  waiting for transfers between devices  79.7 us (29%)
  Pallas kernels  64.8 us (24%)
  other arithmetic  24.3 us (9%)
  local copies, waits for them, and re-layouts  12.8 us (5%)
    ppermute x11, waiting for transfers between devices, fsdp_shift(): lax.ppermute(array, 'fsdp', [(i, (i + by) % self.fsdp) for i in range(sel...  36.9 us
    ppermute x24, starting transfers between devices, outer_shift(): lax.ppermute(array, 'seq', [(i, (i + 4 * by) % self.seq) for i in range(s...  33.7 us
    ppermute x24, waiting for transfers between devices, outer_shift(): lax.ppermute(array, 'seq', [(i, (i + 4 * by) % self.seq) for i in range(s...  29.4 us
    ppermute x4, starting transfers between devices, linear_shift(): lax.ppermute(array, ('seq', 'fsdp'), [(i, i + by) for i in range(count) i...  17.2 us
    ppermute x19, starting transfers between devices, core_swap(): return lax.ppermute(array, 'seq', [(i, i ^ 1) for i in range(self.seq)])  17.2 us
    ppermute x11, starting transfers between devices, fsdp_shift(): lax.ppermute(array, 'fsdp', [(i, (i + by) % self.fsdp) for i in range(sel...  12.8 us
    pallas_call x1, Pallas kernels, on_device(): pl.pallas_call(functools.partial(last_kernel, len(qkv_w), n_tok, fsdp, he...  11.2 us
    pallas_call x1, Pallas kernels, on_device(): pl.pallas_call(functools.partial(middle_kernel, len(out_w), len(gate_w),...  10.7 us
  transfers between devices with their start and end apart: 67, of which 28 were waited for; matrix products, arithmetic and copies ran while one was open for 9% of the time, Pallas kernels for 21%

profile of v5, /device:TPU:1, one launch (start us, length us, event | category | flops | bytes accessed | tf_op | source)
XLA Modules:
  0.0 273.5 jit_solution(790645031008915634)
XLA Ops:
  3.6 2.1 collective-permute-start.3
  5.7 4.0 %collective-permute-start = (bf16[256,640]{1,0:T(8,128)(2,1)}, bf16[256,640]{1,0:T(8,128)(2,1)}, u32[]{:S(2)}, u32[]{:S(2)}) collective-permute-start(bf16[256,640]{1,0:T(8,128)(2,1)} %refs_16_.3), channel_id=1, source_target_pairs={{0,2},{1,3},{2,4},{3,5},{4,6},{5,7},{6,8},{7,9},{8,10},{9,11},{10,... | collective-permute-start | bytes 983048 | tf_op jit(solution)/shard_map/ppermute | solution.py:72
  9.7 2.1 collective-permute-start.1
  14.3 2.5 multiply_sine_fusion
  18.6 4.1 %collective-permute-done.2 = bf16[1536]{0:T(1024)(128)(2,1)S(1)} collective-permute-done((bf16[1536]{0:T(1024)(128)(2,1)S(1)}, bf16[1536]{0:T(1024)(128)(2,1)S(1)}, u32[]{:S(2)}, u32[]{:S(2)}) %collective-permute-start.2) | collective-permute-done | bytes 3104 | tf_op jit(solution)/shard_map/ppermute | solution.py:67
  22.8 1.7 collective-permute-start.4
  24.5 2.3 collective-permute-start.5
  27.9 7.0 %collective-permute-done.5.refs_5_.refs_9_ = bf16[256,640]{1,0:T(8,128)(2,1)} collective-permute-done((bf16[256,640]{1,0:T(8,128)(2,1)S(1)}, bf16[256,640]{1,0:T(8,128)(2,1)}, u32[]{:S(2)}, u32[]{:S(2)}) %collective-permute-start.5) | collective-permute-done | bytes 327712 | tf_op jit(solution)/shard_map/ppermute | solution.py:67
  37.0 9.0 %attend.1 = (bf16[768,640]{1,0:T(8,128)(2,1)}, f32[256,1024]{1,0:T(8,128)}, f32[768,256]{1,0:T(8,128)}, bf16[1024,256]{1,0:T(8,128)(2,1)}, bf16[768,256]{1,0:T(8...) custom-call(s32[3]{0:T(128)} %pad_add_fusion.refs_0_, ...), custom_call_target="tpu_custom_call" | custom-call | flops 80000000000 | bytes 200000000 | tf_op jit(solution)/shard_map/attend/pallas_call | solution.py:644
  47.2 8.7 %collective-permute-done.11.refs_13_.refs_17_ = bf16[320,1024]{1,0:T(8,128)(2,1)S(1)} collective-permute-done((bf16[320,1024]{1,0:T(8,128)(2,1)S(1)}, bf16[320,1024]{1,0:T(8,128)(2,1)S(1)}, u32[]{:S(2)}, u32[]{:S(2)}) %collective-permute-start.11) | collective-permute-done | bytes 655392 | tf_op jit(solution)/shard_map/ppermute | solution.py:67
  60.9 10.4 %gate.1 = (f32[256,640]{1,0:T(8,128)}, f32[256,640]{1,0:T(8,128)}, bf16[256,640]{1,0:T(8,128)(2,1)}, bf16[256,2048]{1,0:T(8,128)(2,1)}, bf16[256,2048]{1,0:T(8,128)(2,1)}, /*index=5*/bf16[256,2048]{1,0:T(8,128)(2,1)}) custom-call(s32[3]{0:T(128)} %pad_add_fusion.refs_0_, bf16[256,1024]{1,0:T(8,128)(2,1)} %get-tuple-element.165.refs_1_.refs_7_, ...), custom_call_target="tpu_custom_call" | custom-call | flops 80000000000 | bytes 104857600 | tf_op jit(solution)/shard_map/gate/pallas_call | solution.py:671
  71.3 1.8 collective-permute-done.13.refs_6_
  74.4 1.7 collective-permute-done.14.refs_7_
  77.0 6.6 %down.1 = (bf16[256,640]{1,0:T(8,128)(2,1)}, bf16[256,640]{1,0:T(8,128)(2,1)}, f32[1,640]{1,0:T(1,128)}, bf16[2,2,256,640]{3,2,1,0:T(8,128)(2,1)}, bf16[2,2,256,640]{3,2,1,0:T(8,128)(2,1)}) custom-call(s32[3]{0:T(128)} %pad_add_fusion.refs_0_, bf16[256,2048]{1,0:T(8,128)(2,1)} %get-tuple-element.173.refs_1_, f32[256,640]{1,0:T(8,128)} %get-tuple-element.174.refs_2_.refs_3_, ...), custom_call_target="tpu_custom_call" | custom-call | flops 80000000000 | bytes 104857600 | tf_op jit(solution)/shard_map/down/pallas_call | solution.py:699
  84.0 10.4 %gate_back.1 = (bf16[256,2048]{1,0:T(8,128)(2,1)}, bf16[256,2048]{1,0:T(8,128)(2,1)}, bf16[2,2,320,512]{3,2,1,0:T(8,128)(2,1)}, bf16[2,2,320,512]{3,2,1,0:T(8,12...) custom-call(s32[3]{0:T(128)} %pad_add_fusion.refs_0_, ...), custom_call_target="tpu_custom_call" | custom-call | flops 120000004096 | bytes 157286400 | tf_op jit(solution)/shard_map/gate_back/pallas_call | solution.py:722
  97.6 10.7 %middle.1 = (f32[256,640]{1,0:T(8,128)}, f32[1,640]{1,0:T(1,128)}, f32[1,640]{1,0:T(1,128)}, bf16[1024,256]{1,0:T(8,128)(2,1)}, bf16[2,2,160,512]{3,2,1,0:T(8,128)(2,1)}, /*index=5*/bf16[2,2,160,512]{3,2,1,0:T(8,128)(2,1)}) custom-call(s32[3]{0:T(128)} %pad_add_fusion.refs_0_, bf16[256,2048]{1,0:T(8,128)(2,1)} %get-tuple-element.184.refs_1_, ...), custom_call_target="tpu_custom_call" | custom-call | flops 120000004096 | bytes 209715200 | tf_op jit(solution)/shard_map/middle/pallas_call | solution.py:753
  110.0 2.5 collective-permute-done.18
  114.2 6.5 %attend_back.1 = (f32[256,1024]{1,0:T(8,128)}, f32[768,256]{1,0:T(8,128)}, f32[768,256]{1,0:T(8,128)}) custom-call(bf16[1024,256]{1,0:T(8,128)(2,1)} %get-tuple-element.195.d_att, bf16[1024,256]{1,0:T(8,128)(2,1)} %get-tuple-element.196.q_st, bf16[768,256]{1,0:T(8,128)(2,1)} %get-tuple-element.197.keys, bf16[768,256]{1,0:T(8,128)(2,1)} %get-tuple-element.198.values, ...), custom_call_target="tpu_custom_call" | custom-call | flops 120000004096 | bytes 157286400 | tf_op jit(solution)/shard_map/attend_back/pallas_call | solution.py:783
  121.8 11.2 %last.1 = (f32[256,640]{1,0:T(8,128)}, bf16[512,640]{1,0:T(8,128)(2,1)}, bf16[2,2,352,384]{3,2,1,0:T(8,128)(2,1)}, bf16[2,2,352,384]{3,2,1,0:T(8,128)(2,1)}) custom-call(s32[3]{0:T(128)} %pad_add_fusion.refs_0_, f32[256,640]{1,0:T(8,128)} %get-tuple-element.187.refs_1_, f32[256,1024]{1,0:T(8,128)} %get-tuple-element.204.refs_2_, ...), custom_call_target="tpu_custom_call" | custom-call | flops 299999985664 | bytes 209715200 | tf_op jit(solution)/shard_map/last/pallas_call | solution.py:796
  133.0 1.9 collective-permute-start.21
  139.2 1.5 collective-permute-start.23
  143.3 8.2 %collective-permute-done.27 = bf16[2,320,512]{2,1,0:T(8,128)(2,1)S(1)} collective-permute-done((bf16[2,320,512]{2,1,0:T(8,128)(2,1)S(1)}, bf16[2,320,512]{2,1,0:T(8,128)(2,1)S(1)}, u32[]{:S(2)}, u32[]{:S(2)}) %collective-permute-start.27) | collective-permute-done | bytes 655392 | tf_op jit(solution)/shard_map/ppermute | solution.py:67
  151.5 2.4 collective-permute-start.25
  154.0 4.6 %collective-permute-done.28 = bf16[2,160,512]{2,1,0:T(8,128)(2,1)S(1)} collective-permute-done((bf16[2,160,512]{2,1,0:T(8,128)(2,1)S(1)}, bf16[2,160,512]{2,1,0:T(8,128)(2,1)S(1)}, u32[]{:S(2)}, u32[]{:S(2)}) %collective-permute-start.28) | collective-permute-done | bytes 327712 | tf_op jit(solution)/shard_map/ppermute | solution.py:67
  158.6 3.4 %collective-permute-start.26 = (bf16[64,640]{1,0:T(8,128)(2,1)S(1)}, bf16[64,640]{1,0:T(8,128)(2,1)S(1)}, u32[]{:S(2)}, u32[]{:S(2)}) collective-permute-start(bf16[64,640]{1,0:T(8,128)(2,1)S(1)} %get-tuple-element.355), channel_id=1, source_target_pairs={{0,24},{2,26},{4,28},{6,30},{8,0},{10,2},{12,4},{14,6},{16,8},{18,... | collective-permute-start | bytes 245768 | tf_op jit(solution)/shard_map/ppermute | solution.py:64
  167.9 3.9 %collective-permute-start.35 = (bf16[64,640]{1,0:T(8,128)(2,1)S(1)}, bf16[64,640]{1,0:T(8,128)(2,1)S(1)}, u32[]{:S(2)}, u32[]{:S(2)}) collective-permute-start(bf16[64,640]{1,0:T(8,128)(2,1)S(1)} %add_convert_fusion.8), channel_id=1, source_target_pairs={{0,16},{2,18},{4,20},{6,22},{8,24},{10,26},{12,28},{14,30},{16,0},... | collective-permute-start | bytes 245768 | tf_op jit(solution)/shard_map/ppermute | solution.py:64
  179.0 2.9 %collective-permute-done.32 = bf16[80,512]{1,0:T(8,128)(2,1)S(1)} collective-permute-done((bf16[80,512]{1,0:T(8,128)(2,1)S(1)}, bf16[80,512]{1,0:T(8,128)(2,1)S(1)}, u32[]{:S(2)}, u32[]{:S(2)}) %collective-permute-start.32) | collective-permute-done | bytes 81952 | tf_op jit(solution)/shard_map/ppermute | solution.py:64
  190.9 1.8 collective-permute-start.40
  192.7 2.4 collective-permute-done.38
  195.1 4.5 %collective-permute-done.39 = bf16[120,512]{1,0:T(8,128)(2,1)S(1)} collective-permute-done((bf16[120,512]{1,0:T(8,128)(2,1)S(1)}, bf16[120,512]{1,0:T(8,128)(2,1)S(1)}, u32[]{:S(2)}, u32[]{:S(2)}) %collective-permute-start.39) | collective-permute-done | bytes 122912 | tf_op jit(solution)/shard_map/ppermute | solution.py:64
  199.9 9.2 %collective-permute-start.52 = (bf16[256,640]{1,0:T(8,128)(2,1)S(1)}, bf16[256,640]{1,0:T(8,128)(2,1)S(1)}, u32[]{:S(2)}, u32[]{:S(2)}) collective-permute-start(bf16[256,640]{1,0:T(8,128)(2,1)S(1)} %get-tuple-element.326), channel_id=1, source_target_pairs={{1,0},{2,1},{3,2},{4,3},{5,4},{6,5},{7,6},{8,7},{9,8},{10,9},{11,1... | collective-permute-start | bytes 983048 | tf_op jit(solution)/shard_map/ppermute | solution.py:72
  209.1 1.9 collective-permute-start.53
  213.2 2.0 collective-permute-start.46
  215.2 2.5 collective-permute-done.45
  217.8 1.6 collective-permute-done.46
  219.4 1.7 collective-permute-start.47
  221.1 3.4 %collective-permute-done.47 = bf16[88,384]{1,0:T(8,128)(2,1)S(1)} collective-permute-done((bf16[88,384]{1,0:T(8,128)(2,1)S(1)}, bf16[88,384]{1,0:T(8,128)(2,1)S(1)}, u32[]{:S(2)}, u32[]{:S(2)}) %collective-permute-start.47) | collective-permute-done | bytes 67616 | tf_op jit(solution)/shard_map/ppermute | solution.py:64
  225.8 2.1 collective-permute-start.50
  227.9 4.6 %collective-permute-done.49 = bf16[120,512]{1,0:T(8,128)(2,1)S(1)} collective-permute-done((bf16[120,512]{1,0:T(8,128)(2,1)S(1)}, bf16[120,512]{1,0:T(8,128)(2,1)S(1)}, u32[]{:S(2)}, u32[]{:S(2)}) %collective-permute-start.49) | collective-permute-done | bytes 122912 | tf_op jit(solution)/shard_map/ppermute | solution.py:64
  232.5 3.6 %collective-permute-start.65 = (bf16[256,640]{1,0:T(8,128)(2,1)S(1)}, bf16[256,640]{1,0:T(8,128)(2,1)S(1)}, u32[]{:S(2)}, u32[]{:S(2)}) collective-permute-start(bf16[256,640]{1,0:T(8,128)(2,1)S(1)} %bitcast.166), channel_id=1, source_target_pairs={{0,2},{2,0},{4,6},{6,4},{8,10},{10,8},{12,14},{14,12},{16,18},{18,... | collective-permute-start | bytes 983048 | tf_op jit(solution)/shard_map/ppermute | solution.py:58
  236.0 2.1 collective-permute-start.63
  239.1 2.0 collective-permute-start.54
  241.2 2.8 %collective-permute-start.55 = (bf16[88,384]{1,0:T(8,128)(2,1)S(1)}, bf16[88,384]{1,0:T(8,128)(2,1)S(1)}, u32[]{:S(2)}, u32[]{:S(2)}) collective-permute-start(bf16[88,384]{1,0:T(8,128)(2,1)S(1)} %add_convert_fusion.9), channel_id=1, source_target_pairs={{0,16},{2,18},{4,20},{6,22},{8,24},{10,26},{12,28},{14,30},{16,0},... | collective-permute-start | bytes 202760 | tf_op jit(solution)/shard_map/ppermute | solution.py:64
  246.3 1.7 maximum_convert_fusion.2
  253.8 10.0 %collective-permute-done.57 = bf16[352,384]{1,0:T(8,128)(2,1)S(1)} collective-permute-done((bf16[352,384]{1,0:T(8,128)(2,1)S(1)}, bf16[352,384]{1,0:T(8,128)(2,1)S(1)}, u32[]{:S(2)}, u32[]{:S(2)}) %collective-permute-start.57) | collective-permute-done | bytes 270368 | tf_op jit(solution)/shard_map/ppermute | solution.py:61
  263.8 1.8 collective-permute-start.59
  265.5 1.8 maximum_convert_fusion
  270.6 1.8 maximum_convert_fusion.1
  (276 shorter events, 71.9 us)
Async XLA Ops:
  3.6 19.2 %collective-permute-start.3 = (bf16[320,768]{1,0:T(8,128)(2,1)S(1)}, bf16[320,768]{1,0:T(8,128)(2,1)S(1)}, u32[]{:S(2)}, u32[]{:S(2)}) collective-permute-start(bf16[320,768]{1,0:T(8,128)(2,1)S(1)} %maximum_select_fusion), channel_id=1, source_target_pairs={{0,1},{1,0},{2,3},{3,2},{4,5},{5,4},{6,7},{7,6},{8,9},{9,8},{10,11... | collective-permute-start | bytes 1474568 | tf_op jit(solution)/shard_map/ppermute | solution.py:67
  5.7 18.7 %collective-permute-start = (bf16[256,640]{1,0:T(8,128)(2,1)}, bf16[256,640]{1,0:T(8,128)(2,1)}, u32[]{:S(2)}, u32[]{:S(2)}) collective-permute-start(bf16[256,640]{1,0:T(8,128)(2,1)} %refs_16_.3), channel_id=1, source_target_pairs={{0,2},{1,3},{2,4},{3,5},{4,6},{5,7},{6,8},{7,9},{8,10},{9,11},{10,... | collective-permute-start | bytes 983048 | tf_op jit(solution)/shard_map/ppermute | solution.py:72
  9.7 14.8 %collective-permute-start.1 = (bf16[256,640]{1,0:T(8,128)(2,1)}, bf16[256,640]{1,0:T(8,128)(2,1)}, u32[]{:S(2)}, u32[]{:S(2)}) collective-permute-start(bf16[256,640]{1,0:T(8,128)(2,1)} %refs_16_.3), channel_id=1, source_target_pairs={{0,1},{1,2},{2,3},{3,4},{4,5},{5,6},{6,7},{7,8},{8,9},{9,10},{10,1... | collective-permute-start | bytes 983048 | tf_op jit(solution)/shard_map/ppermute | solution.py:72
  12.0 10.8 %collective-permute-start.2 = (bf16[1536]{0:T(1024)(128)(2,1)S(1)}, bf16[1536]{0:T(1024)(128)(2,1)S(1)}, u32[]{:S(2)}, u32[]{:S(2)}) collective-permute-start(bf16[1536]{0:T(1024)(128)(2,1)S(1)} %concatenate.51), channel_id=1, source_target_pairs={{0,1},{1,0},{2,3},{3,2},{4,5},{5,4},{6,7},{7,6},{8,9},{9,8},{10,11... | collective-permute-start | bytes 9224 | tf_op jit(solution)/shard_map/ppermute | solution.py:67
  22.8 13.4 %collective-permute-start.4 = (bf16[320,768]{1,0:T(8,128)(2,1)S(1)}, bf16[320,768]{1,0:T(8,128)(2,1)S(1)}, u32[]{:S(2)}, u32[]{:S(2)}) collective-permute-start(bf16[320,768]{1,0:T(8,128)(2,1)S(1)} %collective-permute-done.3.refs_11_.refs_20_), channel_id=1, source_target_pairs={{0,2},{2,0},{4,6},{6,4},{8,10},{10,8},{12,14},{14,12},{16,18},{18,... | collective-permute-start | bytes 1474568 | tf_op jit(solution)/shard_map/ppermute | solution.py:58
  24.5 10.4 %collective-permute-start.5 = (bf16[256,640]{1,0:T(8,128)(2,1)S(1)}, bf16[256,640]{1,0:T(8,128)(2,1)}, u32[]{:S(2)}, u32[]{:S(2)}) collective-permute-start(bf16[256,640]{1,0:T(8,128)(2,1)S(1)} %constant_dynamic-slice_fusion.25), channel_id=1, source_target_pairs={{0,1},{1,0},{2,3},{3,2},{4,5},{5,4},{6,7},{7,6},{8,9},{9,8},{10,11... | collective-permute-start | bytes 983048 | tf_op jit(solution)/shard_map/ppermute | solution.py:67
  27.9 18.0 %collective-permute-start.7 = (bf16[320,512]{1,0:T(8,128)(2,1)S(1)}, bf16[320,512]{1,0:T(8,128)(2,1)}, u32[]{:S(2)}, u32[]{:S(2)}) collective-permute-start(bf16[320,512]{1,0:T(8,128)(2,1)S(1)} %constant_dynamic-slice_fusion.24), channel_id=1, source_target_pairs={{0,1},{1,0},{2,3},{3,2},{4,5},{5,4},{6,7},{7,6},{8,9},{9,8},{10,11... | collective-permute-start | bytes 983048 | tf_op jit(solution)/shard_map/ppermute | solution.py:67
  34.9 21.0 %collective-permute-start.11 = (bf16[320,1024]{1,0:T(8,128)(2,1)S(1)}, bf16[320,1024]{1,0:T(8,128)(2,1)S(1)}, u32[]{:S(2)}, u32[]{:S(2)}) collective-permute-start(bf16[320,1024]{1,0:T(8,128)(2,1)S(1)} %constant_dynamic-slice_fusion.23), channel_id=1, source_target_pairs={{0,1},{1,0},{2,3},{3,2},{4,5},{5,4},{6,7},{7,6},{8,9},{9,8},{10,11... | collective-permute-start | bytes 1966088 | tf_op jit(solution)/shard_map/ppermute | solution.py:67
  45.9 11.1 %collective-permute-start.8 = (bf16[320,512]{1,0:T(8,128)(2,1)}, bf16[320,512]{1,0:T(8,128)(2,1)S(1)}, u32[]{:S(2)}, u32[]{:S(2)}) collective-permute-start(bf16[320,512]{1,0:T(8,128)(2,1)} %collective-permute-done.7.refs_8_.refs_12_), channel_id=1, source_target_pairs={{0,4},{2,6},{4,0},{6,2},{8,12},{10,14},{12,8},{14,10},{16,20},{18,... | collective-permute-start | bytes 983048 | tf_op jit(solution)/shard_map/ppermute | solution.py:61
  57.1 15.9 %collective-permute-start.13 = (bf16[512,640]{1,0:T(8,128)(2,1)S(1)}, bf16[512,640]{1,0:T(8,128)(2,1)S(1)}, u32[]{:S(2)}, u32[]{:S(2)}) collective-permute-start(bf16[512,640]{1,0:T(8,128)(2,1)S(1)} %constant_dynamic-slice_fusion.22), channel_id=1, source_target_pairs={{0,1},{1,0},{2,3},{3,2},{4,5},{5,4},{6,7},{7,6},{8,9},{9,8},{10,11... | collective-permute-start | bytes 1966088 | tf_op jit(solution)/shard_map/ppermute | solution.py:67
  83.6 11.4 %collective-permute-start.15 = (bf16[2,2,256,640]{3,2,1,0:T(8,128)(2,1)}, bf16[2,2,256,640]{3,2,1,0:T(8,128)(2,1)S(1)}, u32[]{:S(2)}, u32[]{:S(2)}) collective-permute-start(bf16[2,2,256,640]{3,2,1,0:T(8,128)(2,1)} %get-tuple-element.183), channel_id=1, source_target_pairs={{0,2},{2,0},{4,6},{6,4},{8,10},{10,8},{12,14},{14,12},{16,18},{18,... | collective-permute-start | bytes 3932168 | tf_op jit(solution)/shard_map/ppermute | solution.py:58
  94.4 14.4 %collective-permute-start.16 = (bf16[2,2,320,512]{3,2,1,0:T(8,128)(2,1)}, bf16[2,2,320,512]{3,2,1,0:T(8,128)(2,1)S(1)}, u32[]{:S(2)}, u32[]{:S(2)}) collective-permute-start(bf16[2,2,320,512]{3,2,1,0:T(8,128)(2,1)} %get-tuple-element.189), channel_id=1, source_target_pairs={{0,2},{2,0},{4,6},{6,4},{8,10},{10,8},{12,14},{14,12},{16,18},{18,... | collective-permute-start | bytes 3932168 | tf_op jit(solution)/shard_map/ppermute | solution.py:58
  94.6 17.9 %collective-permute-start.17 = (bf16[2,2,320,512]{3,2,1,0:T(8,128)(2,1)}, bf16[2,2,320,512]{3,2,1,0:T(8,128)(2,1)S(1)}, u32[]{:S(2)}, u32[]{:S(2)}) collective-permute-start(bf16[2,2,320,512]{3,2,1,0:T(8,128)(2,1)} %get-tuple-element.190), channel_id=1, source_target_pairs={{0,2},{2,0},{4,6},{6,4},{8,10},{10,8},{12,14},{14,12},{16,18},{18,... | collective-permute-start | bytes 3932168 | tf_op jit(solution)/shard_map/ppermute | solution.py:58
  96.2 16.4 %collective-permute-start.18 = (bf16[2,256,640]{2,1,0:T(8,128)(2,1)}, bf16[2,256,640]{2,1,0:T(8,128)(2,1)S(1)}, u32[]{:S(2)}, u32[]{:S(2)}) collective-permute-start(bf16[2,256,640]{2,1,0:T(8,128)(2,1)} %fusion), channel_id=1, source_target_pairs={{0,1},{1,0},{2,3},{3,2},{4,5},{5,4},{6,7},{7,6},{8,9},{9,8},{10,11... | collective-permute-start | bytes 1966088 | tf_op jit(solution)/shard_map/ppermute | solution.py:67
  108.3 12.7 %collective-permute-start.19 = (bf16[2,2,160,512]{3,2,1,0:T(8,128)(2,1)}, bf16[2,2,160,512]{3,2,1,0:T(8,128)(2,1)S(1)}, u32[]{:S(2)}, u32[]{:S(2)}) collective-permute-start(bf16[2,2,160,512]{3,2,1,0:T(8,128)(2,1)} %get-tuple-element.201), channel_id=1, source_target_pairs={{0,2},{2,0},{4,6},{6,4},{8,10},{10,8},{12,14},{14,12},{16,18},{18,... | collective-permute-start | bytes 1966088 | tf_op jit(solution)/shard_map/ppermute | solution.py:58
  110.0 28.0 %collective-permute-start.22 = (bf16[2,320,512]{2,1,0:T(8,128)(2,1)}, bf16[2,320,512]{2,1,0:T(8,128)(2,1)}, u32[]{:S(2)}, u32[]{:S(2)}) collective-permute-start(bf16[2,320,512]{2,1,0:T(8,128)(2,1)} %fusion.1), channel_id=1, source_target_pairs={{0,1},{1,0},{2,3},{3,2},{4,5},{5,4},{6,7},{7,6},{8,9},{9,8},{10,11... | collective-permute-start | bytes 1966088 | tf_op jit(solution)/shard_map/ppermute | solution.py:67
  112.7 8.3 %collective-permute-start.20 = (bf16[256,640]{1,0:T(8,128)(2,1)S(1)}, bf16[256,640]{1,0:T(8,128)(2,1)S(1)}, u32[]{:S(2)}, u32[]{:S(2)}) collective-permute-start(bf16[256,640]{1,0:T(8,128)(2,1)S(1)} %fusion.10), channel_id=1, source_target_pairs={{0,4},{2,6},{4,0},{6,2},{8,12},{10,14},{12,8},{14,10},{16,20},{18,... | collective-permute-start | bytes 983048 | tf_op jit(solution)/shard_map/ppermute | solution.py:61
  133.0 30.5 %collective-permute-start.21 = (bf16[2,2,352,384]{3,2,1,0:T(8,128)(2,1)}, bf16[2,2,352,384]{3,2,1,0:T(8,128)(2,1)S(1)}, u32[]{:S(2)}, u32[]{:S(2)}) collective-permute-start(bf16[2,2,352,384]{3,2,1,0:T(8,128)(2,1)} %get-tuple-element.213), channel_id=1, source_target_pairs={{0,2},{2,0},{4,6},{6,4},{8,10},{10,8},{12,14},{14,12},{16,18},{18,... | collective-permute-start | bytes 3244040 | tf_op jit(solution)/shard_map/ppermute | solution.py:58
  135.1 16.4 %collective-permute-start.27 = (bf16[2,320,512]{2,1,0:T(8,128)(2,1)S(1)}, bf16[2,320,512]{2,1,0:T(8,128)(2,1)S(1)}, u32[]{:S(2)}, u32[]{:S(2)}) collective-permute-start(bf16[2,320,512]{2,1,0:T(8,128)(2,1)S(1)} %fusion.2), channel_id=1, source_target_pairs={{0,1},{1,0},{2,3},{3,2},{4,5},{5,4},{6,7},{7,6},{8,9},{9,8},{10,11... | collective-permute-start | bytes 1966088 | tf_op jit(solution)/shard_map/ppermute | solution.py:67
  137.8 20.7 %collective-permute-start.28 = (bf16[2,160,512]{2,1,0:T(8,128)(2,1)S(1)}, bf16[2,160,512]{2,1,0:T(8,128)(2,1)S(1)}, u32[]{:S(2)}, u32[]{:S(2)}) collective-permute-start(bf16[2,160,512]{2,1,0:T(8,128)(2,1)S(1)} %fusion.15), channel_id=1, source_target_pairs={{0,1},{1,0},{2,3},{3,2},{4,5},{5,4},{6,7},{7,6},{8,9},{9,8},{10,11... | collective-permute-start | bytes 983048 | tf_op jit(solution)/shard_map/ppermute | solution.py:67
  139.2 24.3 %collective-permute-start.23 = (bf16[320,512]{1,0:T(8,128)(2,1)S(1)}, bf16[320,512]{1,0:T(8,128)(2,1)S(1)}, u32[]{:S(2)}, u32[]{:S(2)}) collective-permute-start(bf16[320,512]{1,0:T(8,128)(2,1)S(1)} %fusion.9), channel_id=1, source_target_pairs={{0,4},{2,6},{4,0},{6,2},{8,12},{10,14},{12,8},{14,10},{16,20},{18,... | collective-permute-start | bytes 983048 | tf_op jit(solution)/shard_map/ppermute | solution.py:61
  142.0 20.0 %collective-permute-start.24 = (bf16[64,640]{1,0:T(8,128)(2,1)S(1)}, bf16[64,640]{1,0:T(8,128)(2,1)S(1)}, u32[]{:S(2)}, u32[]{:S(2)}) collective-permute-start(bf16[64,640]{1,0:T(8,128)(2,1)S(1)} %get-tuple-element.357), channel_id=1, source_target_pairs={{0,8},{2,10},{4,12},{6,14},{8,16},{10,18},{12,20},{14,22},{16,24},... | collective-permute-start | bytes 245768 | tf_op jit(solution)/shard_map/ppermute | solution.py:64
  151.5 10.5 %collective-permute-start.25 = (bf16[64,640]{1,0:T(8,128)(2,1)S(1)}, bf16[64,640]{1,0:T(8,128)(2,1)S(1)}, u32[]{:S(2)}, u32[]{:S(2)}) collective-permute-start(bf16[64,640]{1,0:T(8,128)(2,1)S(1)} %get-tuple-element.356), channel_id=1, source_target_pairs={{0,16},{2,18},{4,20},{6,22},{8,24},{10,26},{12,28},{14,30},{16,0},... | collective-permute-start | bytes 245768 | tf_op jit(solution)/shard_map/ppermute | solution.py:64
  164.9 18.2 %collective-permute-start.30 = (bf16[480,512]{1,0:T(8,128)(2,1)S(1)}, bf16[480,512]{1,0:T(8,128)(2,1)S(1)}, u32[]{:S(2)}, u32[]{:S(2)}) collective-permute-start(bf16[480,512]{1,0:T(8,128)(2,1)S(1)} %pad_maximum_fusion), channel_id=1, source_target_pairs={{0,4},{2,6},{4,0},{6,2},{8,12},{10,14},{12,8},{14,10},{16,20},{18,... | collective-permute-start | bytes 1474568 | tf_op jit(solution)/shard_map/ppermute | solution.py:61
  166.4 16.7 %collective-permute-start.29 = (bf16[2,352,384]{2,1,0:T(8,128)(2,1)S(1)}, bf16[2,352,384]{2,1,0:T(8,128)(2,1)S(1)}, u32[]{:S(2)}, u32[]{:S(2)}) collective-permute-start(bf16[2,352,384]{2,1,0:T(8,128)(2,1)S(1)} %fusion.11), channel_id=1, source_target_pairs={{0,1},{1,0},{2,3},{3,2},{4,5},{5,4},{6,7},{7,6},{8,9},{9,8},{10,11... | collective-permute-start | bytes 1622024 | tf_op jit(solution)/shard_map/ppermute | solution.py:67
  167.9 7.3 %collective-permute-start.35 = (bf16[64,640]{1,0:T(8,128)(2,1)S(1)}, bf16[64,640]{1,0:T(8,128)(2,1)S(1)}, u32[]{:S(2)}, u32[]{:S(2)}) collective-permute-start(bf16[64,640]{1,0:T(8,128)(2,1)S(1)} %add_convert_fusion.8), channel_id=1, source_target_pairs={{0,16},{2,18},{4,20},{6,22},{8,24},{10,26},{12,28},{14,30},{16,0},... | collective-permute-start | bytes 245768 | tf_op jit(solution)/shard_map/ppermute | solution.py:64
  175.2 6.7 %collective-permute-start.32 = (bf16[80,512]{1,0:T(8,128)(2,1)S(1)}, bf16[80,512]{1,0:T(8,128)(2,1)S(1)}, u32[]{:S(2)}, u32[]{:S(2)}) collective-permute-start(bf16[80,512]{1,0:T(8,128)(2,1)S(1)} %get-tuple-element.352), channel_id=1, source_target_pairs={{0,16},{2,18},{4,20},{6,22},{8,24},{10,26},{12,28},{14,30},{16,0},... | collective-permute-start | bytes 245768 | tf_op jit(solution)/shard_map/ppermute | solution.py:64
  184.2 6.4 %collective-permute-start.42 = (bf16[80,512]{1,0:T(8,128)(2,1)S(1)}, bf16[80,512]{1,0:T(8,128)(2,1)S(1)}, u32[]{:S(2)}, u32[]{:S(2)}) collective-permute-start(bf16[80,512]{1,0:T(8,128)(2,1)S(1)} %add_convert_fusion.7), channel_id=1, source_target_pairs={{0,16},{2,18},{4,20},{6,22},{8,24},{10,26},{12,28},{14,30},{16,0},... | collective-permute-start | bytes 245768 | tf_op jit(solution)/shard_map/ppermute | solution.py:64
  186.7 13.0 %collective-permute-start.44 = (bf16[256,640]{1,0:T(8,128)(2,1)S(1)}, bf16[256,640]{1,0:T(8,128)(2,1)S(1)}, u32[]{:S(2)}, u32[]{:S(2)}) collective-permute-start(bf16[256,640]{1,0:T(8,128)(2,1)S(1)} %bitcast.165), channel_id=1, source_target_pairs={{0,4},{2,6},{4,0},{6,2},{8,12},{10,14},{12,8},{14,10},{16,20},{18,... | collective-permute-start | bytes 983048 | tf_op jit(solution)/shard_map/ppermute | solution.py:61
  187.8 11.8 %collective-permute-start.37 = (bf16[352,384]{1,0:T(8,128)(2,1)S(1)}, bf16[352,384]{1,0:T(8,128)(2,1)S(1)}, u32[]{:S(2)}, u32[]{:S(2)}) collective-permute-start(bf16[352,384]{1,0:T(8,128)(2,1)S(1)} %fusion.12), channel_id=1, source_target_pairs={{0,4},{2,6},{4,0},{6,2},{8,12},{10,14},{12,8},{14,10},{16,20},{18,... | collective-permute-start | bytes 811016 | tf_op jit(solution)/shard_map/ppermute | solution.py:61
  188.6 6.6 %collective-permute-start.38 = (bf16[120,512]{1,0:T(8,128)(2,1)S(1)}, bf16[120,512]{1,0:T(8,128)(2,1)S(1)}, u32[]{:S(2)}, u32[]{:S(2)}) collective-permute-start(bf16[120,512]{1,0:T(8,128)(2,1)S(1)} %get-tuple-element.341), channel_id=1, source_target_pairs={{0,8},{2,10},{4,12},{6,14},{8,16},{10,18},{12,20},{14,22},{16,24},... | collective-permute-start | bytes 368648 | tf_op jit(solution)/shard_map/ppermute | solution.py:64
  190.6 9.1 %collective-permute-start.39 = (bf16[120,512]{1,0:T(8,128)(2,1)S(1)}, bf16[120,512]{1,0:T(8,128)(2,1)S(1)}, u32[]{:S(2)}, u32[]{:S(2)}) collective-permute-start(bf16[120,512]{1,0:T(8,128)(2,1)S(1)} %get-tuple-element.340), channel_id=1, source_target_pairs={{0,16},{2,18},{4,20},{6,22},{8,24},{10,26},{12,28},{14,30},{16,0},... | collective-permute-start | bytes 368648 | tf_op jit(solution)/shard_map/ppermute | solution.py:64
  190.9 8.7 %collective-permute-start.40 = (bf16[120,512]{1,0:T(8,128)(2,1)S(1)}, bf16[120,512]{1,0:T(8,128)(2,1)S(1)}, u32[]{:S(2)}, u32[]{:S(2)}) collective-permute-start(bf16[120,512]{1,0:T(8,128)(2,1)S(1)} %get-tuple-element.339), channel_id=1, source_target_pairs={{0,24},{2,26},{4,28},{6,30},{8,0},{10,2},{12,4},{14,6},{16,8},{18,... | collective-permute-start | bytes 368648 | tf_op jit(solution)/shard_map/ppermute | solution.py:64
  199.9 38.3 %collective-permute-start.52 = (bf16[256,640]{1,0:T(8,128)(2,1)S(1)}, bf16[256,640]{1,0:T(8,128)(2,1)S(1)}, u32[]{:S(2)}, u32[]{:S(2)}) collective-permute-start(bf16[256,640]{1,0:T(8,128)(2,1)S(1)} %get-tuple-element.326), channel_id=1, source_target_pairs={{1,0},{2,1},{3,2},{4,3},{5,4},{6,5},{7,6},{8,7},{9,8},{10,9},{11,1... | collective-permute-start | bytes 983048 | tf_op jit(solution)/shard_map/ppermute | solution.py:72
  209.1 29.0 %collective-permute-start.53 = (bf16[256,640]{1,0:T(8,128)(2,1)S(1)}, bf16[256,640]{1,0:T(8,128)(2,1)S(1)}, u32[]{:S(2)}, u32[]{:S(2)}) collective-permute-start(bf16[256,640]{1,0:T(8,128)(2,1)S(1)} %get-tuple-element.325), channel_id=1, source_target_pairs={{2,0},{3,1},{4,2},{5,3},{6,4},{7,5},{8,6},{9,7},{10,8},{11,9},{12,... | collective-permute-start | bytes 983048 | tf_op jit(solution)/shard_map/ppermute | solution.py:72
  211.2 27.0 %collective-permute-start.51 = (bf16[320,512]{1,0:T(8,128)(2,1)S(1)}, bf16[320,512]{1,0:T(8,128)(2,1)S(1)}, u32[]{:S(2)}, u32[]{:S(2)}) collective-permute-start(bf16[320,512]{1,0:T(8,128)(2,1)S(1)} %bitcast.162), channel_id=1, source_target_pairs={{0,4},{2,6},{4,0},{6,2},{8,12},{10,14},{12,8},{14,10},{16,20},{18,... | collective-permute-start | bytes 983048 | tf_op jit(solution)/shard_map/ppermute | solution.py:61
  217.8 8.0 %collective-permute-start.48 = (bf16[120,512]{1,0:T(8,128)(2,1)S(1)}, bf16[120,512]{1,0:T(8,128)(2,1)S(1)}, u32[]{:S(2)}, u32[]{:S(2)}) collective-permute-start(bf16[120,512]{1,0:T(8,128)(2,1)S(1)} %add_convert_fusion.6), channel_id=1, source_target_pairs={{0,8},{2,10},{4,12},{6,14},{8,16},{10,18},{12,20},{14,22},{16,24},... | collective-permute-start | bytes 368648 | tf_op jit(solution)/shard_map/ppermute | solution.py:64
  224.5 8.0 %collective-permute-start.49 = (bf16[120,512]{1,0:T(8,128)(2,1)S(1)}, bf16[120,512]{1,0:T(8,128)(2,1)S(1)}, u32[]{:S(2)}, u32[]{:S(2)}) collective-permute-start(bf16[120,512]{1,0:T(8,128)(2,1)S(1)} %add_convert_fusion.6), channel_id=1, source_target_pairs={{0,16},{2,18},{4,20},{6,22},{8,24},{10,26},{12,28},{14,30},{16,0},... | collective-permute-start | bytes 368648 | tf_op jit(solution)/shard_map/ppermute | solution.py:64
  225.8 10.2 %collective-permute-start.50 = (bf16[120,512]{1,0:T(8,128)(2,1)S(1)}, bf16[120,512]{1,0:T(8,128)(2,1)}, u32[]{:S(2)}, u32[]{:S(2)}) collective-permute-start(bf16[120,512]{1,0:T(8,128)(2,1)S(1)} %add_convert_fusion.6), channel_id=1, source_target_pairs={{0,24},{2,26},{4,28},{6,30},{8,0},{10,2},{12,4},{14,6},{16,8},{18,... | collective-permute-start | bytes 368648 | tf_op jit(solution)/shard_map/ppermute | solution.py:64
  232.5 13.6 %collective-permute-start.65 = (bf16[256,640]{1,0:T(8,128)(2,1)S(1)}, bf16[256,640]{1,0:T(8,128)(2,1)S(1)}, u32[]{:S(2)}, u32[]{:S(2)}) collective-permute-start(bf16[256,640]{1,0:T(8,128)(2,1)S(1)} %bitcast.166), channel_id=1, source_target_pairs={{0,2},{2,0},{4,6},{6,4},{8,10},{10,8},{12,14},{14,12},{16,18},{18,... | collective-permute-start | bytes 983048 | tf_op jit(solution)/shard_map/ppermute | solution.py:58
  236.0 16.9 %collective-permute-start.63 = (bf16[320,512]{1,0:T(8,128)(2,1)S(1)}, bf16[320,512]{1,0:T(8,128)(2,1)S(1)}, u32[]{:S(2)}, u32[]{:S(2)}) collective-permute-start(bf16[320,512]{1,0:T(8,128)(2,1)S(1)} %bitcast.163), channel_id=1, source_target_pairs={{0,2},{2,0},{4,6},{6,4},{8,10},{10,8},{12,14},{14,12},{16,18},{18,... | collective-permute-start | bytes 983048 | tf_op jit(solution)/shard_map/ppermute | solution.py:58
  238.2 7.9 %collective-permute-start.66 = (bf16[256,640]{1,0:T(8,128)(2,1)S(1)}, bf16[256,640]{1,0:T(8,128)(2,1)S(1)}, u32[]{:S(2)}, u32[]{:S(2)}) collective-permute-start(bf16[256,640]{1,0:T(8,128)(2,1)S(1)} %collective-permute-done.44), channel_id=1, source_target_pairs={{0,2},{2,0},{4,6},{6,4},{8,10},{10,8},{12,14},{14,12},{16,18},{18,... | collective-permute-start | bytes 983048 | tf_op jit(solution)/shard_map/ppermute | solution.py:58
  239.1 8.8 %collective-permute-start.54 = (bf16[88,384]{1,0:T(8,128)(2,1)S(1)}, bf16[88,384]{1,0:T(8,128)(2,1)S(1)}, u32[]{:S(2)}, u32[]{:S(2)}) collective-permute-start(bf16[88,384]{1,0:T(8,128)(2,1)S(1)} %add_convert_fusion.9), channel_id=1, source_target_pairs={{0,8},{2,10},{4,12},{6,14},{8,16},{10,18},{12,20},{14,22},{16,24},... | collective-permute-start | bytes 202760 | tf_op jit(solution)/shard_map/ppermute | solution.py:64
  241.2 8.0 %collective-permute-start.55 = (bf16[88,384]{1,0:T(8,128)(2,1)S(1)}, bf16[88,384]{1,0:T(8,128)(2,1)S(1)}, u32[]{:S(2)}, u32[]{:S(2)}) collective-permute-start(bf16[88,384]{1,0:T(8,128)(2,1)S(1)} %add_convert_fusion.9), channel_id=1, source_target_pairs={{0,16},{2,18},{4,20},{6,22},{8,24},{10,26},{12,28},{14,30},{16,0},... | collective-permute-start | bytes 202760 | tf_op jit(solution)/shard_map/ppermute | solution.py:64
  246.1 21.4 %collective-permute-start.60 = (bf16[480,512]{1,0:T(8,128)(2,1)S(1)}, bf16[480,512]{1,0:T(8,128)(2,1)S(1)}, u32[]{:S(2)}, u32[]{:S(2)}) collective-permute-start(bf16[480,512]{1,0:T(8,128)(2,1)S(1)} %bitcast.159), channel_id=1, source_target_pairs={{0,4},{2,6},{4,0},{6,2},{8,12},{10,14},{12,8},{14,10},{16,20},{18,... | collective-permute-start | bytes 1474568 | tf_op jit(solution)/shard_map/ppermute | solution.py:61
  248.0 22.0 %collective-permute-start.61 = (bf16[480,512]{1,0:T(8,128)(2,1)S(1)}, bf16[480,512]{1,0:T(8,128)(2,1)S(1)}, u32[]{:S(2)}, u32[]{:S(2)}) collective-permute-start(bf16[480,512]{1,0:T(8,128)(2,1)S(1)} %bitcast.160), channel_id=1, source_target_pairs={{0,2},{2,0},{4,6},{6,4},{8,10},{10,8},{12,14},{14,12},{16,18},{18,... | collective-permute-start | bytes 1474568 | tf_op jit(solution)/shard_map/ppermute | solution.py:58
  250.2 13.5 %collective-permute-start.57 = (bf16[352,384]{1,0:T(8,128)(2,1)S(1)}, bf16[352,384]{1,0:T(8,128)(2,1)S(1)}, u32[]{:S(2)}, u32[]{:S(2)}) collective-permute-start(bf16[352,384]{1,0:T(8,128)(2,1)S(1)} %bitcast.171), channel_id=1, source_target_pairs={{0,4},{2,6},{4,0},{6,2},{8,12},{10,14},{12,8},{14,10},{16,20},{18,... | collective-permute-start | bytes 811016 | tf_op jit(solution)/shard_map/ppermute | solution.py:61
  252.9 14.6 %collective-permute-start.58 = (bf16[352,384]{1,0:T(8,128)(2,1)S(1)}, bf16[352,384]{1,0:T(8,128)(2,1)S(1)}, u32[]{:S(2)}, u32[]{:S(2)}) collective-permute-start(bf16[352,384]{1,0:T(8,128)(2,1)S(1)} %bitcast.172), channel_id=1, source_target_pairs={{0,2},{2,0},{4,6},{6,4},{8,10},{10,8},{12,14},{14,12},{16,18},{18,... | collective-permute-start | bytes 811016 | tf_op jit(solution)/shard_map/ppermute | solution.py:58
  (58 other events, 390.2 us)

commit v6 on v5

--- a/solution.py
+++ b/solution.py
@@ -197,7 +197,7 @@
     pos, cosine, sine, gain_table = refs[1 + n_tok : 5 + n_tok]
     qkv = refs[5 + n_tok : 5 + n_tok + n_qkv]
     normed, q_raw, k_raw, q_st, keys, values, probs, attended, w_full, sems = refs[5 + n_tok + n_qkv :]
-    copies = place_copies(qkv[:3], qkv[3:], w_full, sems, at, 1, 2)
+    copies = place_copies(qkv[:3], qkv[3:], w_full, sems, at, 1, 4)
     for copy in copies:
         copy.start()
     rows = toks[0].shape[0]
@@ -463,7 +463,7 @@
     qkv_w, refs = refs[:n_qkv], refs[n_qkv:]
     grad_tokens, d_halo, keep, send = refs[:4]
     w_full, normed_t, d_qkv, gain_rows, qkv_sems = refs[4:]
-    copies = place_copies(qkv_w[:3], qkv_w[3:], w_full, qkv_sems, at, 1, 2)
+    copies = place_copies(qkv_w[:3], qkv_w[3:], w_full, qkv_sems, at, 1, 4)
     for copy in copies:
         copy.start()
     normed_t[...] = normed[...].T
@@ -626,13 +626,12 @@
         axis=0,
     )
     qkv_w = [w_query, w_key, w_value]
-    qkv_part = own_part(here, qkv_w, 1, 2)
+    qkv_part = own_part(here, qkv_w, 1, 4)
     tokens_out = after(tokens, qkv_part)
     toks = [linear_shift(tokens_out, by) for by in range(hops, 0, -1)] + [tokens]
-    qkv_w += on_chips(here, over_links(here, qkv_part), 2)
+    qkv_w += on_chips(here, over_links(here, qkv_part), 4)
     out_arrived = over_links(here, after(own_part(here, [w_out], 0, 2), *toks[:-1]))
     gate_arrived = over_links(here, after(own_part(here, [w_gate], 1, 4), qkv_w[3]))
-    up_arrived = over_links(here, after(own_part(here, [w_up], 1, 2), out_arrived[0]))
 
     all_positions = jnp.concatenate([positions[0] - halo + jnp.arange(halo, dtype=jnp.int32), positions])
     frequency = ROPE_BASE ** (-(jnp.arange(dim // 2, dtype=F32) * 2.0 / dim))
@@ -664,10 +663,12 @@
         name="attend",
     )(at, *toks, positions[:, None], cosine, sine, gain_table, *qkv_w)
 
+    up_part = after(own_part(here, [w_up], 1, 2), attended, *gate_arrived, *out_arrived)
+    up_arrived = over_links(here, up_part)
     down_arrived = over_links(here, after(own_part(here, [w_down], 0, 2), attended))
     out_w = [w_out] + on_chips(here, [after(a, attended) for a in out_arrived], 2)
     gate_w = [w_gate] + on_chips(here, [after(a, attended) for a in gate_arrived], 4)
-    up_w = [w_up] + on_chips(here, [after(a, attended) for a in up_arrived], 2)
+    up_w = [w_up] + on_chips(here, up_arrived, 2)
     projected, residual, ffn_in, mixed, gelu_out, gate_slope = pl.pallas_call(
         functools.partial(gate_kernel, len(out_w), len(gate_w), len(up_w)),
         out_shape=(
@@ -819,10 +820,10 @@
     )
 
     last_sum = Chunk(here, last_keep, last_send)
-    gate_sum.over_mid(last_keep)
     down_sum.outer_sums(last_keep)
-    (last_sum.other,), (gate_sum.across,), down_sum.shares, up_sum.arrived, out_sum.arrived = together(
-        (last_sum.other,), (gate_sum.across,), down_sum.shares, up_sum.arrived, out_sum.arrived
+    gate_sum.over_mid(last_keep, *up_sum.arrived)
+    (last_sum.other,), (gate_sum.across,), down_sum.shares, out_sum.arrived = together(
+        (last_sum.other,), (gate_sum.across,), down_sum.shares, out_sum.arrived
     )
     last_sum.over_fsdp()
     up_sum.join(out_sum)
@@ -842,13 +843,12 @@
     last_sum.outer_sums()
     up_sum.outer_gather()
     gate_sum.mid_gather()
-    halos = [linear_shift(after(d_halo, last_sum.across)[halo - by * rows :][:rows], -by) for by in range(1, hops + 1)]
-    last_sum.shares, up_sum.gathered, gate_last, halos = together(
-        last_sum.shares, up_sum.gathered, gate_sum.blocks[0], halos
-    )
+    last_sum.shares, up_sum.gathered, gate_last = together(last_sum.shares, up_sum.gathered, gate_sum.blocks[0])
     gate_sum.blocks[0] = list(gate_last)
     last_sum.outer_gather()
     up_sum.mid_gather()
+    d_halo = after(d_halo, *last_sum.shares)
+    halos = [linear_shift(d_halo[halo - by * rows :][:rows], -by) for by in range(1, hops + 1)]
     last_sum.mid_gather()
     down_blocks, gate_blocks = by_place(here, down_sum.blocks), by_place(here, gate_sum.blocks)
     both_blocks, last_blocks = by_place(here, up_sum.blocks), by_place(here, last_sum.blocks)

time: 275 us -> 258 us (0.938)
  waiting for transfers between devices: 79.7 us -> 59.8 us
    ppermute x11, waiting for transfers between devices: 36.9 us -> 25.8 us  [fsdp_shift(): lax.ppermute(array, 'fsdp', [(i, (i + by) % self.fsdp) for i in range(sel...]
    ppermute x19 -> x20, starting transfers between devices: 17.2 us -> 26.2 us  [core_swap(): return lax.ppermute(array, 'seq', [(i, i ^ 1) for i in range(self.seq)])]
    ppermute x24, waiting for transfers between devices: 29.4 us -> 21.5 us  [outer_shift(): lax.ppermute(array, 'seq', [(i, (i + 4 * by) % self.seq) for i in range(s...]
    ppermute x4, starting transfers between devices: 17.2 us -> 11.8 us  [linear_shift(): lax.ppermute(array, ('seq', 'fsdp'), [(i, i + by) for i in range(count) i...]
    ppermute x11, starting transfers between devices: 12.8 us -> 8.77 us  [fsdp_shift(): lax.ppermute(array, 'fsdp', [(i, (i + by) % self.fsdp) for i in range(sel...]
    ppermute x9 -> x10, waiting for transfers between devices: 10.4 us -> 8.6 us  [mid_swap(): return lax.ppermute(array, 'seq', [(i, i ^ 2) for i in range(self.seq)])]
    ppermute x9 -> x10, starting transfers between devices: 8.66 us -> 9.91 us  [mid_swap(): return lax.ppermute(array, 'seq', [(i, i ^ 2) for i in range(self.seq)])]
  transfers between devices with their start and end apart: 67 -> 69, of which waited for: 28 -> 24; matrix products, arithmetic and copies ran while one was open for 9% -> 11% of each run, Pallas kernels for 21% -> 23%
where the time goes in v6:
time: 258 us; the launch traced here: 257 us
  starting transfers between devices  89.5 us (35%)
  Pallas kernels  65.3 us (25%)
  waiting for transfers between devices  59.8 us (23%)
  other arithmetic  26.5 us (10%)
  local copies, waits for them, and re-layouts  13.7 us (5%)
    ppermute x24, starting transfers between devices, outer_shift(): lax.ppermute(array, 'seq', [(i, (i + 4 * by) % self.seq) for i in range(s...  32.9 us
    ppermute x20, starting transfers between devices, core_swap(): return lax.ppermute(array, 'seq', [(i, i ^ 1) for i in range(self.seq)])  26.2 us
    ppermute x11, waiting for transfers between devices, fsdp_shift(): lax.ppermute(array, 'fsdp', [(i, (i + by) % self.fsdp) for i in range(sel...  25.8 us
    ppermute x24, waiting for transfers between devices, outer_shift(): lax.ppermute(array, 'seq', [(i, (i + 4 * by) % self.seq) for i in range(s...  21.5 us
    ppermute x4, starting transfers between devices, linear_shift(): lax.ppermute(array, ('seq', 'fsdp'), [(i, i + by) for i in range(count) i...  11.8 us
    pallas_call x1, Pallas kernels, on_device(): pl.pallas_call(functools.partial(last_kernel, len(qkv_w), n_tok, fsdp, he...  11.7 us
    pallas_call x1, Pallas kernels, on_device(): pl.pallas_call(functools.partial(middle_kernel, len(out_w), len(gate_w),...  10.7 us
    pallas_call x1, Pallas kernels, on_device(): pl.pallas_call(functools.partial(gate_kernel, len(out_w), len(gate_w), le...  10.5 us
  transfers between devices with their start and end apart: 69, of which 24 were waited for; matrix products, arithmetic and copies ran while one was open for 11% of the time, Pallas kernels for 23%

profile of v6, /device:TPU:1, one launch (start us, length us, event | category | flops | bytes accessed | tf_op | source)
XLA Modules:
  0.0 257.0 jit_solution(872170102191618261)
XLA Ops:
  4.6 2.1 collective-permute-start.3
  6.8 3.9 %collective-permute-start = (bf16[256,640]{1,0:T(8,128)(2,1)S(1)}, bf16[256,640]{1,0:T(8,128)(2,1)S(1)}, u32[]{:S(2)}, u32[]{:S(2)}) collective-permute-start(bf16[256,640]{1,0:T(8,128)(2,1)S(1)} %copy-done.34), channel_id=1, source_target_pairs={{0,2},{1,3},{2,4},{3,5},{4,6},{5,7},{6,8},{7,9},{8,10},{9,11},{10,... | collective-permute-start | bytes 983048 | tf_op jit(solution)/shard_map/ppermute | solution.py:72
  10.7 2.1 collective-permute-start.1
  15.3 2.5 multiply_sine_fusion
  22.3 2.1 collective-permute-done.4.refs_12_.refs_21_
  24.4 1.9 collective-permute-start.6
  29.7 9.0 %attend.1 = (bf16[768,640]{1,0:T(8,128)(2,1)}, f32[256,1024]{1,0:T(8,128)}, f32[768,256]{1,0:T(8,128)}, bf16[1024,256]{1,0:T(8,128)(2,1)}, bf16[768,256]{1,0:T(8...) custom-call(s32[3]{0:T(128)} %pad_add_fusion.refs_0_, ...), custom_call_target="tpu_custom_call" | custom-call | flops 80000000000 | bytes 200000000 | tf_op jit(solution)/shard_map/attend/pallas_call | solution.py:643
  38.8 5.0 %collective-permute-done.7.refs_5_.refs_9_ = bf16[256,640]{1,0:T(8,128)(2,1)S(1)} collective-permute-done((bf16[256,640]{1,0:T(8,128)(2,1)S(1)}, bf16[256,640]{1,0:T(8,128)(2,1)S(1)}, u32[]{:S(2)}, u32[]{:S(2)}) %collective-permute-start.7) | collective-permute-done | bytes 327712 | tf_op jit(solution)/shard_map/ppermute | solution.py:67
  45.5 13.7 %collective-permute-done.13.refs_13_.refs_17_ = bf16[320,1024]{1,0:T(8,128)(2,1)S(1)} collective-permute-done((bf16[320,1024]{1,0:T(8,128)(2,1)S(1)}, bf16[320,1024]{1,0:T(8,128)(2,1)S(1)}, u32[]{:S(2)}, u32[]{:S(2)}) %collective-permute-start.13) | collective-permute-done | bytes 655392 | tf_op jit(solution)/shard_map/ppermute | solution.py:67
  59.2 1.7 collective-permute-start.14
  62.1 1.7 collective-permute-done.11.refs_10_.refs_14_
  65.0 10.5 %gate.1 = (f32[256,640]{1,0:T(8,128)}, f32[256,640]{1,0:T(8,128)}, bf16[256,640]{1,0:T(8,128)(2,1)}, bf16[256,2048]{1,0:T(8,128)(2,1)}, bf16[256,2048]{1,0:T(8,128)(2,1)}, /*index=5*/bf16[256,2048]{1,0:T(8,128)(2,1)}) custom-call(s32[3]{0:T(128)} %pad_add_fusion.refs_0_, bf16[256,1024]{1,0:T(8,128)(2,1)} %get-tuple-element.161.refs_1_.refs_7_, ...), custom_call_target="tpu_custom_call" | custom-call | flops 80000000000 | bytes 104857600 | tf_op jit(solution)/shard_map/gate/pallas_call | solution.py:672
  75.5 2.0 collective-permute-done.15.refs_6_
  78.8 1.7 collective-permute-done.16.refs_7_
  81.4 6.6 %down.1 = (bf16[256,640]{1,0:T(8,128)(2,1)}, bf16[256,640]{1,0:T(8,128)(2,1)}, f32[1,640]{1,0:T(1,128)}, bf16[2,2,256,640]{3,2,1,0:T(8,128)(2,1)}, bf16[2,2,256,640]{3,2,1,0:T(8,128)(2,1)}) custom-call(s32[3]{0:T(128)} %pad_add_fusion.refs_0_, bf16[256,2048]{1,0:T(8,128)(2,1)} %get-tuple-element.168.refs_1_, f32[256,640]{1,0:T(8,128)} %get-tuple-element.169.refs_2_.refs_3_, ...), custom_call_target="tpu_custom_call" | custom-call | flops 80000000000 | bytes 104857600 | tf_op jit(solution)/shard_map/down/pallas_call | solution.py:700
  88.4 10.4 %gate_back.1 = (bf16[256,2048]{1,0:T(8,128)(2,1)}, bf16[256,2048]{1,0:T(8,128)(2,1)}, bf16[2,2,320,512]{3,2,1,0:T(8,128)(2,1)}, bf16[2,2,320,512]{3,2,1,0:T(8,12...) custom-call(s32[3]{0:T(128)} %pad_add_fusion.refs_0_, ...), custom_call_target="tpu_custom_call" | custom-call | flops 120000004096 | bytes 157286400 | tf_op jit(solution)/shard_map/gate_back/pallas_call | solution.py:723
  101.1 10.7 %middle.1 = (f32[256,640]{1,0:T(8,128)}, f32[1,640]{1,0:T(1,128)}, f32[1,640]{1,0:T(1,128)}, bf16[1024,256]{1,0:T(8,128)(2,1)}, bf16[2,2,160,512]{3,2,1,0:T(8,128)(2,1)}, /*index=5*/bf16[2,2,160,512]{3,2,1,0:T(8,128)(2,1)}) custom-call(s32[3]{0:T(128)} %pad_add_fusion.refs_0_, bf16[256,2048]{1,0:T(8,128)(2,1)} %get-tuple-element.179.refs_1_, ...), custom_call_target="tpu_custom_call" | custom-call | flops 120000004096 | bytes 209715200 | tf_op jit(solution)/shard_map/middle/pallas_call | solution.py:754
  118.5 6.4 %attend_back.1 = (f32[256,1024]{1,0:T(8,128)}, f32[768,256]{1,0:T(8,128)}, f32[768,256]{1,0:T(8,128)}) custom-call(bf16[1024,256]{1,0:T(8,128)(2,1)} %get-tuple-element.190.d_att, bf16[1024,256]{1,0:T(8,128)(2,1)} %get-tuple-element.191.q_st, bf16[768,256]{1,0:T(8,128)(2,1)} %get-tuple-element.192.keys, bf16[768,256]{1,0:T(8,128)(2,1)} %get-tuple-element.193.values, ...), custom_call_target="tpu_custom_call" | custom-call | flops 120000004096 | bytes 157286400 | tf_op jit(solution)/shard_map/attend_back/pallas_call | solution.py:784
  125.7 11.7 %last.1 = (f32[256,640]{1,0:T(8,128)}, bf16[512,640]{1,0:T(8,128)(2,1)}, bf16[2,2,352,384]{3,2,1,0:T(8,128)(2,1)}, bf16[2,2,352,384]{3,2,1,0:T(8,128)(2,1)}) custom-call(s32[3]{0:T(128)} %pad_add_fusion.refs_0_, f32[256,640]{1,0:T(8,128)} %get-tuple-element.182.refs_1_, f32[256,1024]{1,0:T(8,128)} %get-tuple-element.199.refs_2_, ...), custom_call_target="tpu_custom_call" | custom-call | flops 299999985664 | bytes 209715200 | tf_op jit(solution)/shard_map/last/pallas_call | solution.py:797
  137.4 2.4 collective-permute-start.23
  141.5 3.7 %collective-permute-done.24 = bf16[2,320,512]{2,1,0:T(8,128)(2,1)} collective-permute-done((bf16[2,320,512]{2,1,0:T(8,128)(2,1)}, bf16[2,320,512]{2,1,0:T(8,128)(2,1)}, u32[]{:S(2)}, u32[]{:S(2)}) %collective-permute-start.24) | collective-permute-done | bytes 655392 | tf_op jit(solution)/shard_map/ppermute | solution.py:67
  152.1 3.3 %collective-permute-start.29 = (bf16[64,640]{1,0:T(8,128)(2,1)S(1)}, bf16[64,640]{1,0:T(8,128)(2,1)S(1)}, u32[]{:S(2)}, u32[]{:S(2)}) collective-permute-start(bf16[64,640]{1,0:T(8,128)(2,1)S(1)} %get-tuple-element.347), channel_id=1, source_target_pairs={{0,24},{2,26},{4,28},{6,30},{8,0},{10,2},{12,4},{14,6},{16,8},{18,... | collective-permute-start | bytes 245768 | tf_op jit(solution)/shard_map/ppermute | solution.py:64
  159.4 2.1 collective-permute-start.36
  161.6 1.5 collective-permute-start.37
  168.4 1.6 collective-permute-start.35
  170.6 2.5 collective-permute-done.34
  173.7 1.9 collective-permute-start.43
  175.6 1.5 collective-permute-start.44
  181.8 2.0 collective-permute-start.42
  183.9 2.1 collective-permute-done.40
  186.0 5.0 %collective-permute-done.41 = bf16[120,512]{1,0:T(8,128)(2,1)S(1)} collective-permute-done((bf16[120,512]{1,0:T(8,128)(2,1)S(1)}, bf16[120,512]{1,0:T(8,128)(2,1)S(1)}, u32[]{:S(2)}, u32[]{:S(2)}) %collective-permute-start.41) | collective-permute-done | bytes 122912 | tf_op jit(solution)/shard_map/ppermute | solution.py:64
  192.5 3.6 %collective-permute-start.47 = (bf16[88,384]{1,0:T(8,128)(2,1)S(1)}, bf16[88,384]{1,0:T(8,128)(2,1)S(1)}, u32[]{:S(2)}, u32[]{:S(2)}) collective-permute-start(bf16[88,384]{1,0:T(8,128)(2,1)S(1)} %get-tuple-element.357), channel_id=1, source_target_pairs={{0,8},{2,10},{4,12},{6,14},{8,16},{10,18},{12,20},{14,22},{16,24},... | collective-permute-start | bytes 202760 | tf_op jit(solution)/shard_map/ppermute | solution.py:64
  196.3 2.3 collective-permute-start.51
  198.7 2.3 collective-permute-start.52
  201.0 2.4 collective-permute-done.48
  203.3 3.9 %collective-permute-done.49 = bf16[88,384]{1,0:T(8,128)(2,1)S(1)} collective-permute-done((bf16[88,384]{1,0:T(8,128)(2,1)S(1)}, bf16[88,384]{1,0:T(8,128)(2,1)S(1)}, u32[]{:S(2)}, u32[]{:S(2)}) %collective-permute-start.49) | collective-permute-done | bytes 67616 | tf_op jit(solution)/shard_map/ppermute | solution.py:64
  207.2 9.9 %collective-permute-start.67 = (bf16[256,640]{1,0:T(8,128)(2,1)S(1)}, bf16[256,640]{1,0:T(8,128)(2,1)S(1)}, u32[]{:S(2)}, u32[]{:S(2)}) collective-permute-start(bf16[256,640]{1,0:T(8,128)(2,1)S(1)} %bitcast.166), channel_id=1, source_target_pairs={{0,2},{2,0},{4,6},{6,4},{8,10},{10,8},{12,14},{14,12},{16,18},{18,... | collective-permute-start | bytes 983048 | tf_op jit(solution)/shard_map/ppermute | solution.py:58
  217.6 1.5 collective-permute-start.56
  219.1 1.8 collective-permute-start.57
  222.7 1.7 maximum_convert_fusion.2
  225.0 1.5 collective-permute-done.57
  226.5 3.3 %collective-permute-start.54 = (bf16[256,640]{1,0:T(8,128)(2,1)S(1)}, bf16[256,640]{1,0:T(8,128)(2,1)}, u32[]{:S(2)}, u32[]{:S(2)}) collective-permute-start(bf16[256,640]{1,0:T(8,128)(2,1)S(1)} %get-tuple-element.317), channel_id=1, source_target_pairs={{1,0},{2,1},{3,2},{4,3},{5,4},{6,5},{7,6},{8,7},{9,8},{10,9},{11,1... | collective-permute-start | bytes 983048 | tf_op jit(solution)/shard_map/ppermute | solution.py:72
  232.1 2.4 collective-permute-start.55
  236.4 1.8 maximum_convert_fusion
  239.2 6.4 %collective-permute-done.59 = bf16[352,384]{1,0:T(8,128)(2,1)S(1)} collective-permute-done((bf16[352,384]{1,0:T(8,128)(2,1)S(1)}, bf16[352,384]{1,0:T(8,128)(2,1)S(1)}, u32[]{:S(2)}, u32[]{:S(2)}) %collective-permute-start.59) | collective-permute-done | bytes 270368 | tf_op jit(solution)/shard_map/ppermute | solution.py:61
  245.6 3.4 %collective-permute-start.61 = (bf16[352,384]{1,0:T(8,128)(2,1)S(1)}, bf16[352,384]{1,0:T(8,128)(2,1)S(1)}, u32[]{:S(2)}, u32[]{:S(2)}) collective-permute-start(bf16[352,384]{1,0:T(8,128)(2,1)S(1)} %collective-permute-done.59), channel_id=1, source_target_pairs={{0,2},{2,0},{4,6},{6,4},{8,10},{10,8},{12,14},{14,12},{16,18},{18,... | collective-permute-start | bytes 811016 | tf_op jit(solution)/shard_map/ppermute | solution.py:58
  248.9 1.9 convert_add_fusion.6
  254.1 1.8 maximum_convert_fusion.1
  (287 shorter events, 67.6 us)
Async XLA Ops:
  4.6 13.2 %collective-permute-start.3 = (bf16[320,384]{1,0:T(8,128)(2,1)S(1)}, bf16[320,384]{1,0:T(8,128)(2,1)S(1)}, u32[]{:S(2)}, u32[]{:S(2)}) collective-permute-start(bf16[320,384]{1,0:T(8,128)(2,1)S(1)} %maximum_select_fusion), channel_id=1, source_target_pairs={{0,1},{1,0},{2,3},{3,2},{4,5},{5,4},{6,7},{7,6},{8,9},{9,8},{10,11... | collective-permute-start | bytes 737288 | tf_op jit(solution)/shard_map/ppermute | solution.py:67
  6.8 21.2 %collective-permute-start = (bf16[256,640]{1,0:T(8,128)(2,1)S(1)}, bf16[256,640]{1,0:T(8,128)(2,1)S(1)}, u32[]{:S(2)}, u32[]{:S(2)}) collective-permute-start(bf16[256,640]{1,0:T(8,128)(2,1)S(1)} %copy-done.34), channel_id=1, source_target_pairs={{0,2},{1,3},{2,4},{3,5},{4,6},{5,7},{6,8},{7,9},{8,10},{9,11},{10,... | collective-permute-start | bytes 983048 | tf_op jit(solution)/shard_map/ppermute | solution.py:72
  10.7 17.2 %collective-permute-start.1 = (bf16[256,640]{1,0:T(8,128)(2,1)S(1)}, bf16[256,640]{1,0:T(8,128)(2,1)}, u32[]{:S(2)}, u32[]{:S(2)}) collective-permute-start(bf16[256,640]{1,0:T(8,128)(2,1)S(1)} %copy-done.34), channel_id=1, source_target_pairs={{0,1},{1,2},{2,3},{3,4},{4,5},{5,6},{6,7},{7,8},{8,9},{9,10},{10,1... | collective-permute-start | bytes 983048 | tf_op jit(solution)/shard_map/ppermute | solution.py:72
  13.0 8.0 %collective-permute-start.2 = (bf16[1536]{0:T(1024)(128)(2,1)S(1)}, bf16[1536]{0:T(1024)(128)(2,1)S(1)}, u32[]{:S(2)}, u32[]{:S(2)}) collective-permute-start(bf16[1536]{0:T(1024)(128)(2,1)S(1)} %concatenate.55), channel_id=1, source_target_pairs={{0,1},{1,0},{2,3},{3,2},{4,5},{5,4},{6,7},{7,6},{8,9},{9,8},{10,11... | collective-permute-start | bytes 9224 | tf_op jit(solution)/shard_map/ppermute | solution.py:67
  17.9 6.5 %collective-permute-start.4 = (bf16[320,384]{1,0:T(8,128)(2,1)S(1)}, bf16[320,384]{1,0:T(8,128)(2,1)S(1)}, u32[]{:S(2)}, u32[]{:S(2)}) collective-permute-start(bf16[320,384]{1,0:T(8,128)(2,1)S(1)} %collective-permute-done.3.refs_11_.refs_20_), channel_id=1, source_target_pairs={{0,4},{2,6},{4,0},{6,2},{8,12},{10,14},{12,8},{14,10},{16,20},{18,... | collective-permute-start | bytes 737288 | tf_op jit(solution)/shard_map/ppermute | solution.py:61
  21.0 7.9 %collective-permute-start.5 = (bf16[320,384]{1,0:T(8,128)(2,1)S(1)}, bf16[320,384]{1,0:T(8,128)(2,1)S(1)}, u32[]{:S(2)}, u32[]{:S(2)}) collective-permute-start(bf16[320,384]{1,0:T(8,128)(2,1)S(1)} %collective-permute-done.3.refs_11_.refs_20_), channel_id=1, source_target_pairs={{0,2},{2,0},{4,6},{6,4},{8,10},{10,8},{12,14},{14,12},{16,18},{18,... | collective-permute-start | bytes 737288 | tf_op jit(solution)/shard_map/ppermute | solution.py:58
  27.4 11.4 %collective-permute-start.9 = (bf16[320,512]{1,0:T(8,128)(2,1)S(1)}, bf16[320,512]{1,0:T(8,128)(2,1)}, u32[]{:S(2)}, u32[]{:S(2)}) collective-permute-start(bf16[320,512]{1,0:T(8,128)(2,1)S(1)} %constant_dynamic-slice_fusion.24), channel_id=1, source_target_pairs={{0,1},{1,0},{2,3},{3,2},{4,5},{5,4},{6,7},{7,6},{8,9},{9,8},{10,11... | collective-permute-start | bytes 983048 | tf_op jit(solution)/shard_map/ppermute | solution.py:67
  27.9 15.9 %collective-permute-start.7 = (bf16[256,640]{1,0:T(8,128)(2,1)S(1)}, bf16[256,640]{1,0:T(8,128)(2,1)S(1)}, u32[]{:S(2)}, u32[]{:S(2)}) collective-permute-start(bf16[256,640]{1,0:T(8,128)(2,1)S(1)} %constant_dynamic-slice_fusion.25), channel_id=1, source_target_pairs={{0,1},{1,0},{2,3},{3,2},{4,5},{5,4},{6,7},{7,6},{8,9},{9,8},{10,11... | collective-permute-start | bytes 983048 | tf_op jit(solution)/shard_map/ppermute | solution.py:67
  43.8 15.5 %collective-permute-start.13 = (bf16[320,1024]{1,0:T(8,128)(2,1)S(1)}, bf16[320,1024]{1,0:T(8,128)(2,1)S(1)}, u32[]{:S(2)}, u32[]{:S(2)}) collective-permute-start(bf16[320,1024]{1,0:T(8,128)(2,1)S(1)} %constant_dynamic-slice_fusion.23), channel_id=1, source_target_pairs={{0,1},{1,0},{2,3},{3,2},{4,5},{5,4},{6,7},{7,6},{8,9},{9,8},{10,11... | collective-permute-start | bytes 1966088 | tf_op jit(solution)/shard_map/ppermute | solution.py:67
  44.3 17.2 %collective-permute-start.10 = (bf16[320,512]{1,0:T(8,128)(2,1)}, bf16[320,512]{1,0:T(8,128)(2,1)S(1)}, u32[]{:S(2)}, u32[]{:S(2)}) collective-permute-start(bf16[320,512]{1,0:T(8,128)(2,1)} %collective-permute-done.9.refs_8_.refs_12_), channel_id=1, source_target_pairs={{0,4},{2,6},{4,0},{6,2},{8,12},{10,14},{12,8},{14,10},{16,20},{18,... | collective-permute-start | bytes 983048 | tf_op jit(solution)/shard_map/ppermute | solution.py:61
  61.6 15.9 %collective-permute-start.15 = (bf16[512,640]{1,0:T(8,128)(2,1)S(1)}, bf16[512,640]{1,0:T(8,128)(2,1)S(1)}, u32[]{:S(2)}, u32[]{:S(2)}) collective-permute-start(bf16[512,640]{1,0:T(8,128)(2,1)S(1)} %constant_dynamic-slice_fusion.22), channel_id=1, source_target_pairs={{0,1},{1,0},{2,3},{3,2},{4,5},{5,4},{6,7},{7,6},{8,9},{9,8},{10,11... | collective-permute-start | bytes 1966088 | tf_op jit(solution)/shard_map/ppermute | solution.py:67
  88.0 11.4 %collective-permute-start.17 = (bf16[2,2,256,640]{3,2,1,0:T(8,128)(2,1)}, bf16[2,2,256,640]{3,2,1,0:T(8,128)(2,1)S(1)}, u32[]{:S(2)}, u32[]{:S(2)}) collective-permute-start(bf16[2,2,256,640]{3,2,1,0:T(8,128)(2,1)} %get-tuple-element.178), channel_id=1, source_target_pairs={{0,2},{2,0},{4,6},{6,4},{8,10},{10,8},{12,14},{14,12},{16,18},{18,... | collective-permute-start | bytes 3932168 | tf_op jit(solution)/shard_map/ppermute | solution.py:58
  98.8 15.6 %collective-permute-start.18 = (bf16[2,2,320,512]{3,2,1,0:T(8,128)(2,1)}, bf16[2,2,320,512]{3,2,1,0:T(8,128)(2,1)S(1)}, u32[]{:S(2)}, u32[]{:S(2)}) collective-permute-start(bf16[2,2,320,512]{3,2,1,0:T(8,128)(2,1)} %get-tuple-element.184), channel_id=1, source_target_pairs={{0,2},{2,0},{4,6},{6,4},{8,10},{10,8},{12,14},{14,12},{16,18},{18,... | collective-permute-start | bytes 3932168 | tf_op jit(solution)/shard_map/ppermute | solution.py:58
  99.0 13.2 %collective-permute-start.19 = (bf16[2,2,320,512]{3,2,1,0:T(8,128)(2,1)}, bf16[2,2,320,512]{3,2,1,0:T(8,128)(2,1)S(1)}, u32[]{:S(2)}, u32[]{:S(2)}) collective-permute-start(bf16[2,2,320,512]{3,2,1,0:T(8,128)(2,1)} %get-tuple-element.185), channel_id=1, source_target_pairs={{0,2},{2,0},{4,6},{6,4},{8,10},{10,8},{12,14},{14,12},{16,18},{18,... | collective-permute-start | bytes 3932168 | tf_op jit(solution)/shard_map/ppermute | solution.py:58
  100.6 16.4 %collective-permute-start.20 = (bf16[2,256,640]{2,1,0:T(8,128)(2,1)}, bf16[2,256,640]{2,1,0:T(8,128)(2,1)S(1)}, u32[]{:S(2)}, u32[]{:S(2)}) collective-permute-start(bf16[2,256,640]{2,1,0:T(8,128)(2,1)} %fusion), channel_id=1, source_target_pairs={{0,1},{1,0},{2,3},{3,2},{4,5},{5,4},{6,7},{7,6},{8,9},{9,8},{10,11... | collective-permute-start | bytes 1966088 | tf_op jit(solution)/shard_map/ppermute | solution.py:67
  111.8 13.3 %collective-permute-start.21 = (bf16[2,2,160,512]{3,2,1,0:T(8,128)(2,1)}, bf16[2,2,160,512]{3,2,1,0:T(8,128)(2,1)S(1)}, u32[]{:S(2)}, u32[]{:S(2)}) collective-permute-start(bf16[2,2,160,512]{3,2,1,0:T(8,128)(2,1)} %get-tuple-element.196), channel_id=1, source_target_pairs={{0,2},{2,0},{4,6},{6,4},{8,10},{10,8},{12,14},{14,12},{16,18},{18,... | collective-permute-start | bytes 1966088 | tf_op jit(solution)/shard_map/ppermute | solution.py:58
  113.5 28.0 %collective-permute-start.25 = (bf16[2,320,512]{2,1,0:T(8,128)(2,1)}, bf16[2,320,512]{2,1,0:T(8,128)(2,1)}, u32[]{:S(2)}, u32[]{:S(2)}) collective-permute-start(bf16[2,320,512]{2,1,0:T(8,128)(2,1)} %fusion.2), channel_id=1, source_target_pairs={{0,1},{1,0},{2,3},{3,2},{4,5},{5,4},{6,7},{7,6},{8,9},{9,8},{10,11... | collective-permute-start | bytes 1966088 | tf_op jit(solution)/shard_map/ppermute | solution.py:67
  115.7 29.5 %collective-permute-start.24 = (bf16[2,320,512]{2,1,0:T(8,128)(2,1)}, bf16[2,320,512]{2,1,0:T(8,128)(2,1)}, u32[]{:S(2)}, u32[]{:S(2)}) collective-permute-start(bf16[2,320,512]{2,1,0:T(8,128)(2,1)} %fusion.1), channel_id=1, source_target_pairs={{0,1},{1,0},{2,3},{3,2},{4,5},{5,4},{6,7},{7,6},{8,9},{9,8},{10,11... | collective-permute-start | bytes 1966088 | tf_op jit(solution)/shard_map/ppermute | solution.py:67
  117.1 7.9 %collective-permute-start.22 = (bf16[256,640]{1,0:T(8,128)(2,1)S(1)}, bf16[256,640]{1,0:T(8,128)(2,1)S(1)}, u32[]{:S(2)}, u32[]{:S(2)}) collective-permute-start(bf16[256,640]{1,0:T(8,128)(2,1)S(1)} %fusion.10), channel_id=1, source_target_pairs={{0,4},{2,6},{4,0},{6,2},{8,12},{10,14},{12,8},{14,10},{16,20},{18,... | collective-permute-start | bytes 983048 | tf_op jit(solution)/shard_map/ppermute | solution.py:61
  137.4 19.8 %collective-permute-start.23 = (bf16[2,2,352,384]{3,2,1,0:T(8,128)(2,1)}, bf16[2,2,352,384]{3,2,1,0:T(8,128)(2,1)S(1)}, u32[]{:S(2)}, u32[]{:S(2)}) collective-permute-start(bf16[2,2,352,384]{3,2,1,0:T(8,128)(2,1)} %get-tuple-element.209), channel_id=1, source_target_pairs={{0,2},{2,0},{4,6},{6,4},{8,10},{10,8},{12,14},{14,12},{16,18},{18,... | collective-permute-start | bytes 3244040 | tf_op jit(solution)/shard_map/ppermute | solution.py:58
  140.9 11.2 %collective-permute-start.30 = (bf16[2,160,512]{2,1,0:T(8,128)(2,1)S(1)}, bf16[2,160,512]{2,1,0:T(8,128)(2,1)S(1)}, u32[]{:S(2)}, u32[]{:S(2)}) collective-permute-start(bf16[2,160,512]{2,1,0:T(8,128)(2,1)S(1)} %fusion.15), channel_id=1, source_target_pairs={{0,1},{1,0},{2,3},{3,2},{4,5},{5,4},{6,7},{7,6},{8,9},{9,8},{10,11... | collective-permute-start | bytes 983048 | tf_op jit(solution)/shard_map/ppermute | solution.py:67
  146.4 10.9 %collective-permute-start.26 = (bf16[320,512]{1,0:T(8,128)(2,1)S(1)}, bf16[320,512]{1,0:T(8,128)(2,1)S(1)}, u32[]{:S(2)}, u32[]{:S(2)}) collective-permute-start(bf16[320,512]{1,0:T(8,128)(2,1)S(1)} %fusion.9), channel_id=1, source_target_pairs={{0,4},{2,6},{4,0},{6,2},{8,12},{10,14},{12,8},{14,10},{16,20},{18,... | collective-permute-start | bytes 983048 | tf_op jit(solution)/shard_map/ppermute | solution.py:61
  149.0 7.7 %collective-permute-start.27 = (bf16[64,640]{1,0:T(8,128)(2,1)S(1)}, bf16[64,640]{1,0:T(8,128)(2,1)S(1)}, u32[]{:S(2)}, u32[]{:S(2)}) collective-permute-start(bf16[64,640]{1,0:T(8,128)(2,1)S(1)} %get-tuple-element.349), channel_id=1, source_target_pairs={{0,8},{2,10},{4,12},{6,14},{8,16},{10,18},{12,20},{14,22},{16,24},... | collective-permute-start | bytes 245768 | tf_op jit(solution)/shard_map/ppermute | solution.py:64
  150.4 6.9 %collective-permute-start.28 = (bf16[64,640]{1,0:T(8,128)(2,1)S(1)}, bf16[64,640]{1,0:T(8,128)(2,1)S(1)}, u32[]{:S(2)}, u32[]{:S(2)}) collective-permute-start(bf16[64,640]{1,0:T(8,128)(2,1)S(1)} %get-tuple-element.348), channel_id=1, source_target_pairs={{0,16},{2,18},{4,20},{6,22},{8,24},{10,26},{12,28},{14,30},{16,0},... | collective-permute-start | bytes 245768 | tf_op jit(solution)/shard_map/ppermute | solution.py:64
  157.5 16.2 %collective-permute-start.32 = (bf16[480,512]{1,0:T(8,128)(2,1)S(1)}, bf16[480,512]{1,0:T(8,128)(2,1)S(1)}, u32[]{:S(2)}, u32[]{:S(2)}) collective-permute-start(bf16[480,512]{1,0:T(8,128)(2,1)S(1)} %pad_maximum_fusion), channel_id=1, source_target_pairs={{0,4},{2,6},{4,0},{6,2},{8,12},{10,14},{12,8},{14,10},{16,20},{18,... | collective-permute-start | bytes 1474568 | tf_op jit(solution)/shard_map/ppermute | solution.py:61
  158.8 14.8 %collective-permute-start.31 = (bf16[2,352,384]{2,1,0:T(8,128)(2,1)S(1)}, bf16[2,352,384]{2,1,0:T(8,128)(2,1)S(1)}, u32[]{:S(2)}, u32[]{:S(2)}) collective-permute-start(bf16[2,352,384]{2,1,0:T(8,128)(2,1)S(1)} %fusion.11), channel_id=1, source_target_pairs={{0,1},{1,0},{2,3},{3,2},{4,5},{5,4},{6,7},{7,6},{8,9},{9,8},{10,11... | collective-permute-start | bytes 1622024 | tf_op jit(solution)/shard_map/ppermute | solution.py:67
  166.5 6.5 %collective-permute-start.34 = (bf16[80,512]{1,0:T(8,128)(2,1)S(1)}, bf16[80,512]{1,0:T(8,128)(2,1)S(1)}, u32[]{:S(2)}, u32[]{:S(2)}) collective-permute-start(bf16[80,512]{1,0:T(8,128)(2,1)S(1)} %get-tuple-element.344), channel_id=1, source_target_pairs={{0,16},{2,18},{4,20},{6,22},{8,24},{10,26},{12,28},{14,30},{16,0},... | collective-permute-start | bytes 245768 | tf_op jit(solution)/shard_map/ppermute | solution.py:64
  177.9 13.1 %collective-permute-start.46 = (bf16[256,640]{1,0:T(8,128)(2,1)S(1)}, bf16[256,640]{1,0:T(8,128)(2,1)S(1)}, u32[]{:S(2)}, u32[]{:S(2)}) collective-permute-start(bf16[256,640]{1,0:T(8,128)(2,1)S(1)} %bitcast.165), channel_id=1, source_target_pairs={{0,4},{2,6},{4,0},{6,2},{8,12},{10,14},{12,8},{14,10},{16,20},{18,... | collective-permute-start | bytes 983048 | tf_op jit(solution)/shard_map/ppermute | solution.py:61
  179.2 11.8 %collective-permute-start.39 = (bf16[352,384]{1,0:T(8,128)(2,1)S(1)}, bf16[352,384]{1,0:T(8,128)(2,1)S(1)}, u32[]{:S(2)}, u32[]{:S(2)}) collective-permute-start(bf16[352,384]{1,0:T(8,128)(2,1)S(1)} %fusion.12), channel_id=1, source_target_pairs={{0,4},{2,6},{4,0},{6,2},{8,12},{10,14},{12,8},{14,10},{16,20},{18,... | collective-permute-start | bytes 811016 | tf_op jit(solution)/shard_map/ppermute | solution.py:61
  179.8 6.2 %collective-permute-start.40 = (bf16[120,512]{1,0:T(8,128)(2,1)S(1)}, bf16[120,512]{1,0:T(8,128)(2,1)S(1)}, u32[]{:S(2)}, u32[]{:S(2)}) collective-permute-start(bf16[120,512]{1,0:T(8,128)(2,1)S(1)} %get-tuple-element.333), channel_id=1, source_target_pairs={{0,8},{2,10},{4,12},{6,14},{8,16},{10,18},{12,20},{14,22},{16,24},... | collective-permute-start | bytes 368648 | tf_op jit(solution)/shard_map/ppermute | solution.py:64
  181.5 9.5 %collective-permute-start.41 = (bf16[120,512]{1,0:T(8,128)(2,1)S(1)}, bf16[120,512]{1,0:T(8,128)(2,1)S(1)}, u32[]{:S(2)}, u32[]{:S(2)}) collective-permute-start(bf16[120,512]{1,0:T(8,128)(2,1)S(1)} %get-tuple-element.332), channel_id=1, source_target_pairs={{0,16},{2,18},{4,20},{6,22},{8,24},{10,26},{12,28},{14,30},{16,0},... | collective-permute-start | bytes 368648 | tf_op jit(solution)/shard_map/ppermute | solution.py:64
  181.8 9.2 %collective-permute-start.42 = (bf16[120,512]{1,0:T(8,128)(2,1)S(1)}, bf16[120,512]{1,0:T(8,128)(2,1)S(1)}, u32[]{:S(2)}, u32[]{:S(2)}) collective-permute-start(bf16[120,512]{1,0:T(8,128)(2,1)S(1)} %get-tuple-element.331), channel_id=1, source_target_pairs={{0,24},{2,26},{4,28},{6,30},{8,0},{10,2},{12,4},{14,6},{16,8},{18,... | collective-permute-start | bytes 368648 | tf_op jit(solution)/shard_map/ppermute | solution.py:64
  191.2 26.4 %collective-permute-start.53 = (bf16[320,512]{1,0:T(8,128)(2,1)S(1)}, bf16[320,512]{1,0:T(8,128)(2,1)S(1)}, u32[]{:S(2)}, u32[]{:S(2)}) collective-permute-start(bf16[320,512]{1,0:T(8,128)(2,1)S(1)} %bitcast.162), channel_id=1, source_target_pairs={{0,4},{2,6},{4,0},{6,2},{8,12},{10,14},{12,8},{14,10},{16,20},{18,... | collective-permute-start | bytes 983048 | tf_op jit(solution)/shard_map/ppermute | solution.py:61
  196.1 7.2 %collective-permute-start.48 = (bf16[88,384]{1,0:T(8,128)(2,1)S(1)}, bf16[88,384]{1,0:T(8,128)(2,1)S(1)}, u32[]{:S(2)}, u32[]{:S(2)}) collective-permute-start(bf16[88,384]{1,0:T(8,128)(2,1)S(1)} %get-tuple-element.356), channel_id=1, source_target_pairs={{0,16},{2,18},{4,20},{6,22},{8,24},{10,26},{12,28},{14,30},{16,0},... | collective-permute-start | bytes 202760 | tf_op jit(solution)/shard_map/ppermute | solution.py:64
  196.2 20.9 %collective-permute-start.50 = (bf16[120,512]{1,0:T(8,128)(2,1)S(1)}, bf16[120,512]{1,0:T(8,128)(2,1)S(1)}, u32[]{:S(2)}, u32[]{:S(2)}) collective-permute-start(bf16[120,512]{1,0:T(8,128)(2,1)S(1)} %add_convert_fusion.6), channel_id=1, source_target_pairs={{0,8},{2,10},{4,12},{6,14},{8,16},{10,18},{12,20},{14,22},{16,24},... | collective-permute-start | bytes 368648 | tf_op jit(solution)/shard_map/ppermute | solution.py:64
  196.3 20.8 %collective-permute-start.51 = (bf16[120,512]{1,0:T(8,128)(2,1)S(1)}, bf16[120,512]{1,0:T(8,128)(2,1)S(1)}, u32[]{:S(2)}, u32[]{:S(2)}) collective-permute-start(bf16[120,512]{1,0:T(8,128)(2,1)S(1)} %add_convert_fusion.6), channel_id=1, source_target_pairs={{0,16},{2,18},{4,20},{6,22},{8,24},{10,26},{12,28},{14,30},{16,0},... | collective-permute-start | bytes 368648 | tf_op jit(solution)/shard_map/ppermute | solution.py:64
  198.7 18.9 %collective-permute-start.52 = (bf16[120,512]{1,0:T(8,128)(2,1)S(1)}, bf16[120,512]{1,0:T(8,128)(2,1)S(1)}, u32[]{:S(2)}, u32[]{:S(2)}) collective-permute-start(bf16[120,512]{1,0:T(8,128)(2,1)S(1)} %add_convert_fusion.6), channel_id=1, source_target_pairs={{0,24},{2,26},{4,28},{6,30},{8,0},{10,2},{12,4},{14,6},{16,8},{18,... | collective-permute-start | bytes 368648 | tf_op jit(solution)/shard_map/ppermute | solution.py:64
  207.2 14.9 %collective-permute-start.67 = (bf16[256,640]{1,0:T(8,128)(2,1)S(1)}, bf16[256,640]{1,0:T(8,128)(2,1)S(1)}, u32[]{:S(2)}, u32[]{:S(2)}) collective-permute-start(bf16[256,640]{1,0:T(8,128)(2,1)S(1)} %bitcast.166), channel_id=1, source_target_pairs={{0,2},{2,0},{4,6},{6,4},{8,10},{10,8},{12,14},{14,12},{16,18},{18,... | collective-permute-start | bytes 983048 | tf_op jit(solution)/shard_map/ppermute | solution.py:58
  217.1 15.1 %collective-permute-start.65 = (bf16[320,512]{1,0:T(8,128)(2,1)S(1)}, bf16[320,512]{1,0:T(8,128)(2,1)S(1)}, u32[]{:S(2)}, u32[]{:S(2)}) collective-permute-start(bf16[320,512]{1,0:T(8,128)(2,1)S(1)} %bitcast.163), channel_id=1, source_target_pairs={{0,2},{2,0},{4,6},{6,4},{8,10},{10,8},{12,14},{14,12},{16,18},{18,... | collective-permute-start | bytes 983048 | tf_op jit(solution)/shard_map/ppermute | solution.py:58
  217.6 6.7 %collective-permute-start.56 = (bf16[88,384]{1,0:T(8,128)(2,1)S(1)}, bf16[88,384]{1,0:T(8,128)(2,1)S(1)}, u32[]{:S(2)}, u32[]{:S(2)}) collective-permute-start(bf16[88,384]{1,0:T(8,128)(2,1)S(1)} %add_convert_fusion.9), channel_id=1, source_target_pairs={{0,8},{2,10},{4,12},{6,14},{8,16},{10,18},{12,20},{14,22},{16,24},... | collective-permute-start | bytes 202760 | tf_op jit(solution)/shard_map/ppermute | solution.py:64
  219.1 7.4 %collective-permute-start.57 = (bf16[88,384]{1,0:T(8,128)(2,1)S(1)}, bf16[88,384]{1,0:T(8,128)(2,1)S(1)}, u32[]{:S(2)}, u32[]{:S(2)}) collective-permute-start(bf16[88,384]{1,0:T(8,128)(2,1)S(1)} %add_convert_fusion.9), channel_id=1, source_target_pairs={{0,16},{2,18},{4,20},{6,22},{8,24},{10,26},{12,28},{14,30},{16,0},... | collective-permute-start | bytes 202760 | tf_op jit(solution)/shard_map/ppermute | solution.py:64
  222.1 7.8 %collective-permute-start.58 = (bf16[88,384]{1,0:T(8,128)(2,1)S(1)}, bf16[88,384]{1,0:T(8,128)(2,1)S(1)}, u32[]{:S(2)}, u32[]{:S(2)}) collective-permute-start(bf16[88,384]{1,0:T(8,128)(2,1)S(1)} %add_convert_fusion.9), channel_id=1, source_target_pairs={{0,24},{2,26},{4,28},{6,30},{8,0},{10,2},{12,4},{14,6},{16,8},{18,... | collective-permute-start | bytes 202760 | tf_op jit(solution)/shard_map/ppermute | solution.py:64
  222.5 28.5 %collective-permute-start.62 = (bf16[480,512]{1,0:T(8,128)(2,1)S(1)}, bf16[480,512]{1,0:T(8,128)(2,1)S(1)}, u32[]{:S(2)}, u32[]{:S(2)}) collective-permute-start(bf16[480,512]{1,0:T(8,128)(2,1)S(1)} %bitcast.159), channel_id=1, source_target_pairs={{0,4},{2,6},{4,0},{6,2},{8,12},{10,14},{12,8},{14,10},{16,20},{18,... | collective-permute-start | bytes 1474568 | tf_op jit(solution)/shard_map/ppermute | solution.py:61
  224.3 29.2 %collective-permute-start.63 = (bf16[480,512]{1,0:T(8,128)(2,1)S(1)}, bf16[480,512]{1,0:T(8,128)(2,1)S(1)}, u32[]{:S(2)}, u32[]{:S(2)}) collective-permute-start(bf16[480,512]{1,0:T(8,128)(2,1)S(1)} %bitcast.160), channel_id=1, source_target_pairs={{0,2},{2,0},{4,6},{6,4},{8,10},{10,8},{12,14},{14,12},{16,18},{18,... | collective-permute-start | bytes 1474568 | tf_op jit(solution)/shard_map/ppermute | solution.py:58
  226.5 11.7 %collective-permute-start.54 = (bf16[256,640]{1,0:T(8,128)(2,1)S(1)}, bf16[256,640]{1,0:T(8,128)(2,1)}, u32[]{:S(2)}, u32[]{:S(2)}) collective-permute-start(bf16[256,640]{1,0:T(8,128)(2,1)S(1)} %get-tuple-element.317), channel_id=1, source_target_pairs={{1,0},{2,1},{3,2},{4,3},{5,4},{6,5},{7,6},{8,7},{9,8},{10,9},{11,1... | collective-permute-start | bytes 983048 | tf_op jit(solution)/shard_map/ppermute | solution.py:72
  232.1 16.8 %collective-permute-start.55 = (bf16[256,640]{1,0:T(8,128)(2,1)S(1)}, bf16[256,640]{1,0:T(8,128)(2,1)S(1)}, u32[]{:S(2)}, u32[]{:S(2)}) collective-permute-start(bf16[256,640]{1,0:T(8,128)(2,1)S(1)} %get-tuple-element.318), channel_id=1, source_target_pairs={{2,0},{3,1},{4,2},{5,3},{6,4},{7,5},{8,6},{9,7},{10,8},{11,9},{12,... | collective-permute-start | bytes 983048 | tf_op jit(solution)/shard_map/ppermute | solution.py:72
  234.5 11.0 %collective-permute-start.59 = (bf16[352,384]{1,0:T(8,128)(2,1)S(1)}, bf16[352,384]{1,0:T(8,128)(2,1)S(1)}, u32[]{:S(2)}, u32[]{:S(2)}) collective-permute-start(bf16[352,384]{1,0:T(8,128)(2,1)S(1)} %bitcast.171), channel_id=1, source_target_pairs={{0,4},{2,6},{4,0},{6,2},{8,12},{10,14},{12,8},{14,10},{16,20},{18,... | collective-permute-start | bytes 811016 | tf_op jit(solution)/shard_map/ppermute | solution.py:61
  238.2 12.9 %collective-permute-start.60 = (bf16[352,384]{1,0:T(8,128)(2,1)S(1)}, bf16[352,384]{1,0:T(8,128)(2,1)S(1)}, u32[]{:S(2)}, u32[]{:S(2)}) collective-permute-start(bf16[352,384]{1,0:T(8,128)(2,1)S(1)} %bitcast.172), channel_id=1, source_target_pairs={{0,2},{2,0},{4,6},{6,4},{8,10},{10,8},{12,14},{14,12},{16,18},{18,... | collective-permute-start | bytes 811016 | tf_op jit(solution)/shard_map/ppermute | solution.py:58
  (63 other events, 486.9 us)

commit v7 on v6

--- a/solution.py
+++ b/solution.py
@@ -632,6 +632,7 @@
     qkv_w += on_chips(here, over_links(here, qkv_part), 4)
     out_arrived = over_links(here, after(own_part(here, [w_out], 0, 2), *toks[:-1]))
     gate_arrived = over_links(here, after(own_part(here, [w_gate], 1, 4), qkv_w[3]))
+    up_arrived = over_links(here, after(own_part(here, [w_up], 1, 2), *gate_arrived))
 
     all_positions = jnp.concatenate([positions[0] - halo + jnp.arange(halo, dtype=jnp.int32), positions])
     frequency = ROPE_BASE ** (-(jnp.arange(dim // 2, dtype=F32) * 2.0 / dim))
@@ -661,14 +662,12 @@
         compiler_params=params(),
         cost_estimate=cost(4e9, 1e7),
         name="attend",
-    )(at, *toks, positions[:, None], cosine, sine, gain_table, *qkv_w)
-
-    up_part = after(own_part(here, [w_up], 1, 2), attended, *gate_arrived, *out_arrived)
-    up_arrived = over_links(here, up_part)
+    )(at, *toks, after(positions[:, None], *gate_arrived), cosine, sine, gain_table, *qkv_w)
+
     down_arrived = over_links(here, after(own_part(here, [w_down], 0, 2), attended))
     out_w = [w_out] + on_chips(here, [after(a, attended) for a in out_arrived], 2)
-    gate_w = [w_gate] + on_chips(here, [after(a, attended) for a in gate_arrived], 4)
-    up_w = [w_up] + on_chips(here, up_arrived, 2)
+    gate_w = [w_gate] + on_chips(here, gate_arrived, 4)
+    up_w = [w_up] + on_chips(here, [after(a, attended) for a in up_arrived], 2)
     projected, residual, ffn_in, mixed, gelu_out, gate_slope = pl.pallas_call(
         functools.partial(gate_kernel, len(out_w), len(gate_w), len(up_w)),
         out_shape=(
@@ -847,9 +846,9 @@
     gate_sum.blocks[0] = list(gate_last)
     last_sum.outer_gather()
     up_sum.mid_gather()
-    d_halo = after(d_halo, *last_sum.shares)
+    last_sum.mid_gather(up_sum.blocks[0][1])
+    d_halo = after(d_halo, up_sum.blocks[0][1])
     halos = [linear_shift(d_halo[halo - by * rows :][:rows], -by) for by in range(1, hops + 1)]
-    last_sum.mid_gather()
     down_blocks, gate_blocks = by_place(here, down_sum.blocks), by_place(here, gate_sum.blocks)
     both_blocks, last_blocks = by_place(here, up_sum.blocks), by_place(here, last_sum.blocks)
     total_gains = last_sum.blocks[0][0][shard_rows:, :LANES].astype(F32)

time: 258 us -> 247 us (0.957)
  waiting for transfers between devices: 59.8 us -> 50.9 us
  starting transfers between devices: 89.5 us -> 86.9 us
    ppermute x11, waiting for transfers between devices: 25.8 us -> 16.5 us  [fsdp_shift(): lax.ppermute(array, 'fsdp', [(i, (i + by) % self.fsdp) for i in range(sel...]
    ppermute x20, starting transfers between devices: 26.2 us -> 22.2 us  [core_swap(): return lax.ppermute(array, 'seq', [(i, i ^ 1) for i in range(self.seq)])]
    ppermute x4, waiting for transfers between devices: 0.01 us -> 3.88 us  [linear_shift(): lax.ppermute(array, ('seq', 'fsdp'), [(i, i + by) for i in range(count) i...]
    ppermute x10, waiting for transfers between devices: 8.6 us -> 5.97 us  [mid_swap(): return lax.ppermute(array, 'seq', [(i, i ^ 2) for i in range(self.seq)])]
  transfers between devices with their start and end apart: 69 -> 69, of which waited for: 24 -> 27; matrix products, arithmetic and copies ran while one was open for 11% -> 12% of each run, Pallas kernels for 23% -> 24%
where the time goes in v7:
time: 247 us; the launch traced here: 246 us
  starting transfers between devices  86.9 us (35%)
  Pallas kernels  65.3 us (26%)
  waiting for transfers between devices  50.9 us (21%)
  other arithmetic  26.6 us (11%)
  local copies, waits for them, and re-layouts  14 us (6%)
    ppermute x24, starting transfers between devices, outer_shift(): lax.ppermute(array, 'seq', [(i, (i + 4 * by) % self.seq) for i in range(s...  34.1 us
    ppermute x20, starting transfers between devices, core_swap(): return lax.ppermute(array, 'seq', [(i, i ^ 1) for i in range(self.seq)])  22.2 us
    ppermute x24, waiting for transfers between devices, outer_shift(): lax.ppermute(array, 'seq', [(i, (i + 4 * by) % self.seq) for i in range(s...  20.4 us
    ppermute x11, waiting for transfers between devices, fsdp_shift(): lax.ppermute(array, 'fsdp', [(i, (i + by) % self.fsdp) for i in range(sel...  16.5 us
    pallas_call x1, Pallas kernels, on_device(): pl.pallas_call(functools.partial(last_kernel, len(qkv_w), n_tok, fsdp, he...  11.7 us
    ppermute x11, starting transfers between devices, fsdp_shift(): lax.ppermute(array, 'fsdp', [(i, (i + by) % self.fsdp) for i in range(sel...  11.2 us
    ppermute x4, starting transfers between devices, linear_shift(): lax.ppermute(array, ('seq', 'fsdp'), [(i, i + by) for i in range(count) i...  11.1 us
    pallas_call x1, Pallas kernels, on_device(): pl.pallas_call(functools.partial(middle_kernel, len(out_w), len(gate_w),...  10.7 us
  transfers between devices with their start and end apart: 69, of which 27 were waited for; matrix products, arithmetic and copies ran while one was open for 12% of the time, Pallas kernels for 24%

profile of v7, /device:TPU:1, one launch (start us, length us, event | category | flops | bytes accessed | tf_op | source)
XLA Modules:
  0.0 245.9 jit_solution(5985007814032462975)
XLA Ops:
  4.5 2.1 collective-permute-start.2
  6.7 3.9 %collective-permute-start = (bf16[256,640]{1,0:T(8,128)(2,1)S(1)}, bf16[256,640]{1,0:T(8,128)(2,1)}, u32[]{:S(2)}, u32[]{:S(2)}) collective-permute-start(bf16[256,640]{1,0:T(8,128)(2,1)S(1)} %copy-done.35), channel_id=1, source_target_pairs={{0,2},{1,3},{2,4},{3,5},{4,6},{5,7},{6,8},{7,9},{8,10},{9,11},{10,... | collective-permute-start | bytes 983048 | tf_op jit(solution)/shard_map/ppermute | solution.py:72
  10.6 2.1 collective-permute-start.1
  16.2 2.5 %multiply_sine_fusion = (f32[768,128]{1,0:T(8,128)}, f32[768,128]{1,0:T(8,128)}) fusion(f32[128]{0:T(128)S(1)} %negate_power_fusion, f32[768]{0:T(1024)S(1)} %add_convert_fusion.10), kind=kLoop, calls=%fused_computation.29 | loop fusion | flops 98304 | bytes 790016 | tf_op jit(solution)/shard_map/sin | solution.py:640
  20.1 1.7 collective-permute-start.3
  22.3 3.3 %collective-permute-done.5.refs_12_.refs_21_ = bf16[320,384]{1,0:T(8,128)(2,1)S(1)} collective-permute-done((bf16[320,384]{1,0:T(8,128)(2,1)}, bf16[320,384]{1,0:T(8,128)(2,1)S(1)}, u32[]{:S(2)}, u32[]{:S(2)}) %collective-permute-start.5) | collective-permute-done | bytes 245792 | tf_op jit(solution)/shard_map/ppermute | solution.py:61
  25.6 1.8 collective-permute-start.7
  29.8 2.2 collective-permute-start.13
  32.8 9.0 %attend.1 = (bf16[768,640]{1,0:T(8,128)(2,1)}, f32[256,1024]{1,0:T(8,128)}, f32[768,256]{1,0:T(8,128)}, bf16[1024,256]{1,0:T(8,128)(2,1)}, bf16[768,256]{1,0:T(8...) custom-call(s32[3]{0:T(128)} %pad_add_fusion.refs_0_, ...), custom_call_target="tpu_custom_call" | custom-call | flops 80000000000 | bytes 200000000 | tf_op jit(solution)/shard_map/attend/pallas_call | solution.py:644
  41.9 10.0 %collective-permute-done.13.refs_13_.refs_17_ = bf16[320,1024]{1,0:T(8,128)(2,1)S(1)} collective-permute-done((bf16[320,1024]{1,0:T(8,128)(2,1)S(1)}, bf16[320,1024]{1,0:T(8,128)(2,1)S(1)}, u32[]{:S(2)}, u32[]{:S(2)}) %collective-permute-start.13) | collective-permute-done | bytes 655392 | tf_op jit(solution)/shard_map/ppermute | solution.py:67
  53.9 1.6 collective-permute-done.11.refs_10_.refs_14_
  57.3 10.5 %gate.1 = (f32[256,640]{1,0:T(8,128)}, f32[256,640]{1,0:T(8,128)}, bf16[256,640]{1,0:T(8,128)(2,1)}, bf16[256,2048]{1,0:T(8,128)(2,1)}, bf16[256,2048]{1,0:T(8,128)(2,1)}, /*index=5*/bf16[256,2048]{1,0:T(8,128)(2,1)}) custom-call(s32[3]{0:T(128)} %pad_add_fusion.refs_0_, bf16[256,1024]{1,0:T(8,128)(2,1)} %get-tuple-element.164.refs_1_.refs_7_, ...), custom_call_target="tpu_custom_call" | custom-call | flops 80000000000 | bytes 104857600 | tf_op jit(solution)/shard_map/gate/pallas_call | solution.py:671
  67.9 1.4 collective-permute-done.15.refs_6_
  70.5 1.7 collective-permute-done.16.refs_7_
  73.1 6.6 %down.1 = (bf16[256,640]{1,0:T(8,128)(2,1)}, bf16[256,640]{1,0:T(8,128)(2,1)}, f32[1,640]{1,0:T(1,128)}, bf16[2,2,256,640]{3,2,1,0:T(8,128)(2,1)}, bf16[2,2,256,640]{3,2,1,0:T(8,128)(2,1)}) custom-call(s32[3]{0:T(128)} %pad_add_fusion.refs_0_, bf16[256,2048]{1,0:T(8,128)(2,1)} %get-tuple-element.170.refs_1_, f32[256,640]{1,0:T(8,128)} %get-tuple-element.171.refs_2_.refs_3_, ...), custom_call_target="tpu_custom_call" | custom-call | flops 80000000000 | bytes 104857600 | tf_op jit(solution)/shard_map/down/pallas_call | solution.py:699
  80.2 10.4 %gate_back.1 = (bf16[256,2048]{1,0:T(8,128)(2,1)}, bf16[256,2048]{1,0:T(8,128)(2,1)}, bf16[2,2,320,512]{3,2,1,0:T(8,128)(2,1)}, bf16[2,2,320,512]{3,2,1,0:T(8,12...) custom-call(s32[3]{0:T(128)} %pad_add_fusion.refs_0_, ...), custom_call_target="tpu_custom_call" | custom-call | flops 120000004096 | bytes 157286400 | tf_op jit(solution)/shard_map/gate_back/pallas_call | solution.py:722
  92.9 10.7 %middle.1 = (f32[256,640]{1,0:T(8,128)}, f32[1,640]{1,0:T(1,128)}, f32[1,640]{1,0:T(1,128)}, bf16[1024,256]{1,0:T(8,128)(2,1)}, bf16[2,2,160,512]{3,2,1,0:T(8,128)(2,1)}, /*index=5*/bf16[2,2,160,512]{3,2,1,0:T(8,128)(2,1)}) custom-call(s32[3]{0:T(128)} %pad_add_fusion.refs_0_, bf16[256,2048]{1,0:T(8,128)(2,1)} %get-tuple-element.181.refs_1_, ...), custom_call_target="tpu_custom_call" | custom-call | flops 120000004096 | bytes 209715200 | tf_op jit(solution)/shard_map/middle/pallas_call | solution.py:753
  110.3 6.4 %attend_back.1 = (f32[256,1024]{1,0:T(8,128)}, f32[768,256]{1,0:T(8,128)}, f32[768,256]{1,0:T(8,128)}) custom-call(bf16[1024,256]{1,0:T(8,128)(2,1)} %get-tuple-element.192.d_att, bf16[1024,256]{1,0:T(8,128)(2,1)} %get-tuple-element.193.q_st, bf16[768,256]{1,0:T(8,128)(2,1)} %get-tuple-element.194.keys, bf16[768,256]{1,0:T(8,128)(2,1)} %get-tuple-element.195.values, ...), custom_call_target="tpu_custom_call" | custom-call | flops 120000004096 | bytes 157286400 | tf_op jit(solution)/shard_map/attend_back/pallas_call | solution.py:783
  117.5 11.7 %last.1 = (f32[256,640]{1,0:T(8,128)}, bf16[512,640]{1,0:T(8,128)(2,1)}, bf16[2,2,352,384]{3,2,1,0:T(8,128)(2,1)}, bf16[2,2,352,384]{3,2,1,0:T(8,128)(2,1)}) custom-call(s32[3]{0:T(128)} %pad_add_fusion.refs_0_, f32[256,640]{1,0:T(8,128)} %get-tuple-element.184.refs_1_, f32[256,1024]{1,0:T(8,128)} %get-tuple-element.201.refs_2_, ...), custom_call_target="tpu_custom_call" | custom-call | flops 299999985664 | bytes 209715200 | tf_op jit(solution)/shard_map/last/pallas_call | solution.py:796
  129.2 2.4 collective-permute-start.23
  133.3 3.7 %collective-permute-done.24 = bf16[2,320,512]{2,1,0:T(8,128)(2,1)} collective-permute-done((bf16[2,320,512]{2,1,0:T(8,128)(2,1)}, bf16[2,320,512]{2,1,0:T(8,128)(2,1)}, u32[]{:S(2)}, u32[]{:S(2)}) %collective-permute-start.24) | collective-permute-done | bytes 655392 | tf_op jit(solution)/shard_map/ppermute | solution.py:67
  143.9 3.3 %collective-permute-start.29 = (bf16[64,640]{1,0:T(8,128)(2,1)S(1)}, bf16[64,640]{1,0:T(8,128)(2,1)S(1)}, u32[]{:S(2)}, u32[]{:S(2)}) collective-permute-start(bf16[64,640]{1,0:T(8,128)(2,1)S(1)} %get-tuple-element.349), channel_id=1, source_target_pairs={{0,24},{2,26},{4,28},{6,30},{8,0},{10,2},{12,4},{14,6},{16,8},{18,... | collective-permute-start | bytes 245768 | tf_op jit(solution)/shard_map/ppermute | solution.py:64
  151.2 2.1 collective-permute-start.36
  153.4 1.6 collective-permute-start.37
  160.2 1.6 collective-permute-start.35
  162.4 2.5 %collective-permute-done.34 = bf16[80,512]{1,0:T(8,128)(2,1)S(1)} collective-permute-done((bf16[80,512]{1,0:T(8,128)(2,1)S(1)}, bf16[80,512]{1,0:T(8,128)(2,1)S(1)}, u32[]{:S(2)}, u32[]{:S(2)}) %collective-permute-start.34) | collective-permute-done | bytes 81952 | tf_op jit(solution)/shard_map/ppermute | solution.py:64
  165.5 1.9 collective-permute-start.43
  167.4 1.5 collective-permute-start.44
  173.7 2.0 collective-permute-start.42
  175.7 2.1 collective-permute-done.40
  177.8 5.0 %collective-permute-done.41 = bf16[120,512]{1,0:T(8,128)(2,1)S(1)} collective-permute-done((bf16[120,512]{1,0:T(8,128)(2,1)S(1)}, bf16[120,512]{1,0:T(8,128)(2,1)S(1)}, u32[]{:S(2)}, u32[]{:S(2)}) %collective-permute-start.41) | collective-permute-done | bytes 122912 | tf_op jit(solution)/shard_map/ppermute | solution.py:64
  184.3 3.6 %collective-permute-start.47 = (bf16[88,384]{1,0:T(8,128)(2,1)S(1)}, bf16[88,384]{1,0:T(8,128)(2,1)S(1)}, u32[]{:S(2)}, u32[]{:S(2)}) collective-permute-start(bf16[88,384]{1,0:T(8,128)(2,1)S(1)} %get-tuple-element.359), channel_id=1, source_target_pairs={{0,8},{2,10},{4,12},{6,14},{8,16},{10,18},{12,20},{14,22},{16,24},... | collective-permute-start | bytes 202760 | tf_op jit(solution)/shard_map/ppermute | solution.py:64
  188.1 2.3 collective-permute-start.51
  190.5 2.3 collective-permute-start.52
  192.8 2.4 collective-permute-done.48
  195.2 3.9 %collective-permute-done.49 = bf16[88,384]{1,0:T(8,128)(2,1)S(1)} collective-permute-done((bf16[88,384]{1,0:T(8,128)(2,1)S(1)}, bf16[88,384]{1,0:T(8,128)(2,1)S(1)}, u32[]{:S(2)}, u32[]{:S(2)}) %collective-permute-start.49) | collective-permute-done | bytes 67616 | tf_op jit(solution)/shard_map/ppermute | solution.py:64
  199.0 9.8 %collective-permute-start.67 = (bf16[256,640]{1,0:T(8,128)(2,1)S(1)}, bf16[256,640]{1,0:T(8,128)(2,1)S(1)}, u32[]{:S(2)}, u32[]{:S(2)}) collective-permute-start(bf16[256,640]{1,0:T(8,128)(2,1)S(1)} %bitcast.163), channel_id=1, source_target_pairs={{0,2},{2,0},{4,6},{6,4},{8,10},{10,8},{12,14},{14,12},{16,18},{18,... | collective-permute-start | bytes 983048 | tf_op jit(solution)/shard_map/ppermute | solution.py:58
  210.1 1.4 collective-permute-start.57
  212.4 1.7 maximum_convert_fusion.2
  214.0 1.8 collective-permute-start.58
  215.8 1.4 collective-permute-start.59
  217.4 1.8 maximum_convert_fusion
  219.8 2.6 %collective-permute-done.54 = bf16[480,512]{1,0:T(8,128)(2,1)S(1)} collective-permute-done((bf16[480,512]{1,0:T(8,128)(2,1)S(1)}, bf16[480,512]{1,0:T(8,128)(2,1)S(1)}, u32[]{:S(2)}, u32[]{:S(2)}) %collective-permute-start.54) | collective-permute-done | bytes 491552 | tf_op jit(solution)/shard_map/ppermute | solution.py:61
  224.2 3.1 %collective-permute-start.55 = (bf16[256,640]{1,0:T(8,128)(2,1)S(1)}, bf16[256,640]{1,0:T(8,128)(2,1)S(1)}, u32[]{:S(2)}, u32[]{:S(2)}) collective-permute-start(bf16[256,640]{1,0:T(8,128)(2,1)S(1)} %get-tuple-element.319), channel_id=1, source_target_pairs={{1,0},{2,1},{3,2},{4,3},{5,4},{6,5},{7,6},{8,7},{9,8},{10,9},{11,1... | collective-permute-start | bytes 983048 | tf_op jit(solution)/shard_map/ppermute | solution.py:72
  227.3 1.9 collective-permute-start.56
  233.3 2.1 collective-permute-done.55
  236.2 1.7 collective-permute-done.56
  241.6 1.8 maximum_convert_fusion.1
  (285 shorter events, 68.5 us)
Async XLA Ops:
  4.5 14.2 %collective-permute-start.2 = (bf16[320,384]{1,0:T(8,128)(2,1)S(1)}, bf16[320,384]{1,0:T(8,128)(2,1)}, u32[]{:S(2)}, u32[]{:S(2)}) collective-permute-start(bf16[320,384]{1,0:T(8,128)(2,1)S(1)} %maximum_select_fusion), channel_id=1, source_target_pairs={{0,1},{1,0},{2,3},{3,2},{4,5},{5,4},{6,7},{7,6},{8,9},{9,8},{10,11... | collective-permute-start | bytes 737288 | tf_op jit(solution)/shard_map/ppermute | solution.py:67
  6.7 21.8 %collective-permute-start = (bf16[256,640]{1,0:T(8,128)(2,1)S(1)}, bf16[256,640]{1,0:T(8,128)(2,1)}, u32[]{:S(2)}, u32[]{:S(2)}) collective-permute-start(bf16[256,640]{1,0:T(8,128)(2,1)S(1)} %copy-done.35), channel_id=1, source_target_pairs={{0,2},{1,3},{2,4},{3,5},{4,6},{5,7},{6,8},{7,9},{8,10},{9,11},{10,... | collective-permute-start | bytes 983048 | tf_op jit(solution)/shard_map/ppermute | solution.py:72
  10.6 17.9 %collective-permute-start.1 = (bf16[256,640]{1,0:T(8,128)(2,1)S(1)}, bf16[256,640]{1,0:T(8,128)(2,1)}, u32[]{:S(2)}, u32[]{:S(2)}) collective-permute-start(bf16[256,640]{1,0:T(8,128)(2,1)S(1)} %copy-done.35), channel_id=1, source_target_pairs={{0,1},{1,2},{2,3},{3,4},{4,5},{5,6},{6,7},{7,8},{8,9},{9,10},{10,1... | collective-permute-start | bytes 983048 | tf_op jit(solution)/shard_map/ppermute | solution.py:72
  12.9 7.2 %collective-permute-start.4 = (bf16[1536]{0:T(1024)(128)(2,1)S(1)}, bf16[1536]{0:T(1024)(128)(2,1)S(1)}, u32[]{:S(2)}, u32[]{:S(2)}) collective-permute-start(bf16[1536]{0:T(1024)(128)(2,1)S(1)} %concatenate.55), channel_id=1, source_target_pairs={{0,1},{1,0},{2,3},{3,2},{4,5},{5,4},{6,7},{7,6},{8,9},{9,8},{10,11... | collective-permute-start | bytes 9224 | tf_op jit(solution)/shard_map/ppermute | solution.py:67
  18.7 6.8 %collective-permute-start.5 = (bf16[320,384]{1,0:T(8,128)(2,1)}, bf16[320,384]{1,0:T(8,128)(2,1)S(1)}, u32[]{:S(2)}, u32[]{:S(2)}) collective-permute-start(bf16[320,384]{1,0:T(8,128)(2,1)} %collective-permute-done.2.refs_11_.refs_20_), channel_id=1, source_target_pairs={{0,4},{2,6},{4,0},{6,2},{8,12},{10,14},{12,8},{14,10},{16,20},{18,... | collective-permute-start | bytes 737288 | tf_op jit(solution)/shard_map/ppermute | solution.py:61
  20.1 8.9 %collective-permute-start.3 = (bf16[320,512]{1,0:T(8,128)(2,1)S(1)}, bf16[320,512]{1,0:T(8,128)(2,1)}, u32[]{:S(2)}, u32[]{:S(2)}) collective-permute-start(bf16[320,512]{1,0:T(8,128)(2,1)S(1)} %constant_dynamic-slice_fusion.25), channel_id=1, source_target_pairs={{0,1},{1,0},{2,3},{3,2},{4,5},{5,4},{6,7},{7,6},{8,9},{9,8},{10,11... | collective-permute-start | bytes 983048 | tf_op jit(solution)/shard_map/ppermute | solution.py:67
  21.9 10.2 %collective-permute-start.6 = (bf16[320,384]{1,0:T(8,128)(2,1)}, bf16[320,384]{1,0:T(8,128)(2,1)S(1)}, u32[]{:S(2)}, u32[]{:S(2)}) collective-permute-start(bf16[320,384]{1,0:T(8,128)(2,1)} %collective-permute-done.2.refs_11_.refs_20_), channel_id=1, source_target_pairs={{0,2},{2,0},{4,6},{6,4},{8,10},{10,8},{12,14},{14,12},{16,18},{18,... | collective-permute-start | bytes 737288 | tf_op jit(solution)/shard_map/ppermute | solution.py:58
  25.6 6.5 %collective-permute-start.7 = (bf16[320,384]{1,0:T(8,128)(2,1)S(1)}, bf16[320,384]{1,0:T(8,128)(2,1)S(1)}, u32[]{:S(2)}, u32[]{:S(2)}) collective-permute-start(bf16[320,384]{1,0:T(8,128)(2,1)S(1)} %collective-permute-done.5.refs_12_.refs_21_), channel_id=1, source_target_pairs={{0,2},{2,0},{4,6},{6,4},{8,10},{10,8},{12,14},{14,12},{16,18},{18,... | collective-permute-start | bytes 737288 | tf_op jit(solution)/shard_map/ppermute | solution.py:58
  28.5 24.2 %collective-permute-start.8 = (bf16[256,640]{1,0:T(8,128)(2,1)S(1)}, bf16[256,640]{1,0:T(8,128)(2,1)S(1)}, u32[]{:S(2)}, u32[]{:S(2)}) collective-permute-start(bf16[256,640]{1,0:T(8,128)(2,1)S(1)} %constant_dynamic-slice_fusion.24), channel_id=1, source_target_pairs={{0,1},{1,0},{2,3},{3,2},{4,5},{5,4},{6,7},{7,6},{8,9},{9,8},{10,11... | collective-permute-start | bytes 983048 | tf_op jit(solution)/shard_map/ppermute | solution.py:67
  29.8 22.1 %collective-permute-start.13 = (bf16[320,1024]{1,0:T(8,128)(2,1)S(1)}, bf16[320,1024]{1,0:T(8,128)(2,1)S(1)}, u32[]{:S(2)}, u32[]{:S(2)}) collective-permute-start(bf16[320,1024]{1,0:T(8,128)(2,1)S(1)} %constant_dynamic-slice_fusion.23), channel_id=1, source_target_pairs={{0,1},{1,0},{2,3},{3,2},{4,5},{5,4},{6,7},{7,6},{8,9},{9,8},{10,11... | collective-permute-start | bytes 1966088 | tf_op jit(solution)/shard_map/ppermute | solution.py:67
  31.9 21.2 %collective-permute-start.10 = (bf16[320,512]{1,0:T(8,128)(2,1)}, bf16[320,512]{1,0:T(8,128)(2,1)}, u32[]{:S(2)}, u32[]{:S(2)}) collective-permute-start(bf16[320,512]{1,0:T(8,128)(2,1)} %collective-permute-done.3.refs_8_.refs_12_), channel_id=1, source_target_pairs={{0,4},{2,6},{4,0},{6,2},{8,12},{10,14},{12,8},{14,10},{16,20},{18,... | collective-permute-start | bytes 983048 | tf_op jit(solution)/shard_map/ppermute | solution.py:61
  53.3 15.9 %collective-permute-start.15 = (bf16[512,640]{1,0:T(8,128)(2,1)S(1)}, bf16[512,640]{1,0:T(8,128)(2,1)S(1)}, u32[]{:S(2)}, u32[]{:S(2)}) collective-permute-start(bf16[512,640]{1,0:T(8,128)(2,1)S(1)} %constant_dynamic-slice_fusion.22), channel_id=1, source_target_pairs={{0,1},{1,0},{2,3},{3,2},{4,5},{5,4},{6,7},{7,6},{8,9},{9,8},{10,11... | collective-permute-start | bytes 1966088 | tf_op jit(solution)/shard_map/ppermute | solution.py:67
  79.7 11.4 %collective-permute-start.17 = (bf16[2,2,256,640]{3,2,1,0:T(8,128)(2,1)}, bf16[2,2,256,640]{3,2,1,0:T(8,128)(2,1)S(1)}, u32[]{:S(2)}, u32[]{:S(2)}) collective-permute-start(bf16[2,2,256,640]{3,2,1,0:T(8,128)(2,1)} %get-tuple-element.180), channel_id=1, source_target_pairs={{0,2},{2,0},{4,6},{6,4},{8,10},{10,8},{12,14},{14,12},{16,18},{18,... | collective-permute-start | bytes 3932168 | tf_op jit(solution)/shard_map/ppermute | solution.py:58
  90.6 15.7 %collective-permute-start.18 = (bf16[2,2,320,512]{3,2,1,0:T(8,128)(2,1)}, bf16[2,2,320,512]{3,2,1,0:T(8,128)(2,1)S(1)}, u32[]{:S(2)}, u32[]{:S(2)}) collective-permute-start(bf16[2,2,320,512]{3,2,1,0:T(8,128)(2,1)} %get-tuple-element.186), channel_id=1, source_target_pairs={{0,2},{2,0},{4,6},{6,4},{8,10},{10,8},{12,14},{14,12},{16,18},{18,... | collective-permute-start | bytes 3932168 | tf_op jit(solution)/shard_map/ppermute | solution.py:58
  90.8 13.3 %collective-permute-start.19 = (bf16[2,2,320,512]{3,2,1,0:T(8,128)(2,1)}, bf16[2,2,320,512]{3,2,1,0:T(8,128)(2,1)S(1)}, u32[]{:S(2)}, u32[]{:S(2)}) collective-permute-start(bf16[2,2,320,512]{3,2,1,0:T(8,128)(2,1)} %get-tuple-element.187), channel_id=1, source_target_pairs={{0,2},{2,0},{4,6},{6,4},{8,10},{10,8},{12,14},{14,12},{16,18},{18,... | collective-permute-start | bytes 3932168 | tf_op jit(solution)/shard_map/ppermute | solution.py:58
  92.4 16.4 %collective-permute-start.20 = (bf16[2,256,640]{2,1,0:T(8,128)(2,1)}, bf16[2,256,640]{2,1,0:T(8,128)(2,1)S(1)}, u32[]{:S(2)}, u32[]{:S(2)}) collective-permute-start(bf16[2,256,640]{2,1,0:T(8,128)(2,1)} %fusion), channel_id=1, source_target_pairs={{0,1},{1,0},{2,3},{3,2},{4,5},{5,4},{6,7},{7,6},{8,9},{9,8},{10,11... | collective-permute-start | bytes 1966088 | tf_op jit(solution)/shard_map/ppermute | solution.py:67
  103.6 13.2 %collective-permute-start.21 = (bf16[2,2,160,512]{3,2,1,0:T(8,128)(2,1)}, bf16[2,2,160,512]{3,2,1,0:T(8,128)(2,1)S(1)}, u32[]{:S(2)}, u32[]{:S(2)}) collective-permute-start(bf16[2,2,160,512]{3,2,1,0:T(8,128)(2,1)} %get-tuple-element.198), channel_id=1, source_target_pairs={{0,2},{2,0},{4,6},{6,4},{8,10},{10,8},{12,14},{14,12},{16,18},{18,... | collective-permute-start | bytes 1966088 | tf_op jit(solution)/shard_map/ppermute | solution.py:58
  105.3 27.9 %collective-permute-start.25 = (bf16[2,320,512]{2,1,0:T(8,128)(2,1)}, bf16[2,320,512]{2,1,0:T(8,128)(2,1)}, u32[]{:S(2)}, u32[]{:S(2)}) collective-permute-start(bf16[2,320,512]{2,1,0:T(8,128)(2,1)} %fusion.2), channel_id=1, source_target_pairs={{0,1},{1,0},{2,3},{3,2},{4,5},{5,4},{6,7},{7,6},{8,9},{9,8},{10,11... | collective-permute-start | bytes 1966088 | tf_op jit(solution)/shard_map/ppermute | solution.py:67
  107.5 29.5 %collective-permute-start.24 = (bf16[2,320,512]{2,1,0:T(8,128)(2,1)}, bf16[2,320,512]{2,1,0:T(8,128)(2,1)}, u32[]{:S(2)}, u32[]{:S(2)}) collective-permute-start(bf16[2,320,512]{2,1,0:T(8,128)(2,1)} %fusion.1), channel_id=1, source_target_pairs={{0,1},{1,0},{2,3},{3,2},{4,5},{5,4},{6,7},{7,6},{8,9},{9,8},{10,11... | collective-permute-start | bytes 1966088 | tf_op jit(solution)/shard_map/ppermute | solution.py:67
  108.9 7.9 %collective-permute-start.22 = (bf16[256,640]{1,0:T(8,128)(2,1)S(1)}, bf16[256,640]{1,0:T(8,128)(2,1)S(1)}, u32[]{:S(2)}, u32[]{:S(2)}) collective-permute-start(bf16[256,640]{1,0:T(8,128)(2,1)S(1)} %fusion.10), channel_id=1, source_target_pairs={{0,4},{2,6},{4,0},{6,2},{8,12},{10,14},{12,8},{14,10},{16,20},{18,... | collective-permute-start | bytes 983048 | tf_op jit(solution)/shard_map/ppermute | solution.py:61
  129.2 19.9 %collective-permute-start.23 = (bf16[2,2,352,384]{3,2,1,0:T(8,128)(2,1)}, bf16[2,2,352,384]{3,2,1,0:T(8,128)(2,1)S(1)}, u32[]{:S(2)}, u32[]{:S(2)}) collective-permute-start(bf16[2,2,352,384]{3,2,1,0:T(8,128)(2,1)} %get-tuple-element.211), channel_id=1, source_target_pairs={{0,2},{2,0},{4,6},{6,4},{8,10},{10,8},{12,14},{14,12},{16,18},{18,... | collective-permute-start | bytes 3244040 | tf_op jit(solution)/shard_map/ppermute | solution.py:58
  132.7 11.2 %collective-permute-start.30 = (bf16[2,160,512]{2,1,0:T(8,128)(2,1)S(1)}, bf16[2,160,512]{2,1,0:T(8,128)(2,1)S(1)}, u32[]{:S(2)}, u32[]{:S(2)}) collective-permute-start(bf16[2,160,512]{2,1,0:T(8,128)(2,1)S(1)} %fusion.15), channel_id=1, source_target_pairs={{0,1},{1,0},{2,3},{3,2},{4,5},{5,4},{6,7},{7,6},{8,9},{9,8},{10,11... | collective-permute-start | bytes 983048 | tf_op jit(solution)/shard_map/ppermute | solution.py:67
  138.2 10.9 %collective-permute-start.26 = (bf16[320,512]{1,0:T(8,128)(2,1)S(1)}, bf16[320,512]{1,0:T(8,128)(2,1)S(1)}, u32[]{:S(2)}, u32[]{:S(2)}) collective-permute-start(bf16[320,512]{1,0:T(8,128)(2,1)S(1)} %fusion.9), channel_id=1, source_target_pairs={{0,4},{2,6},{4,0},{6,2},{8,12},{10,14},{12,8},{14,10},{16,20},{18,... | collective-permute-start | bytes 983048 | tf_op jit(solution)/shard_map/ppermute | solution.py:61
  140.8 7.8 %collective-permute-start.27 = (bf16[64,640]{1,0:T(8,128)(2,1)S(1)}, bf16[64,640]{1,0:T(8,128)(2,1)S(1)}, u32[]{:S(2)}, u32[]{:S(2)}) collective-permute-start(bf16[64,640]{1,0:T(8,128)(2,1)S(1)} %get-tuple-element.351), channel_id=1, source_target_pairs={{0,8},{2,10},{4,12},{6,14},{8,16},{10,18},{12,20},{14,22},{16,24},... | collective-permute-start | bytes 245768 | tf_op jit(solution)/shard_map/ppermute | solution.py:64
  142.2 6.9 %collective-permute-start.28 = (bf16[64,640]{1,0:T(8,128)(2,1)S(1)}, bf16[64,640]{1,0:T(8,128)(2,1)S(1)}, u32[]{:S(2)}, u32[]{:S(2)}) collective-permute-start(bf16[64,640]{1,0:T(8,128)(2,1)S(1)} %get-tuple-element.350), channel_id=1, source_target_pairs={{0,16},{2,18},{4,20},{6,22},{8,24},{10,26},{12,28},{14,30},{16,0},... | collective-permute-start | bytes 245768 | tf_op jit(solution)/shard_map/ppermute | solution.py:64
  149.3 16.2 %collective-permute-start.32 = (bf16[480,512]{1,0:T(8,128)(2,1)S(1)}, bf16[480,512]{1,0:T(8,128)(2,1)S(1)}, u32[]{:S(2)}, u32[]{:S(2)}) collective-permute-start(bf16[480,512]{1,0:T(8,128)(2,1)S(1)} %pad_maximum_fusion), channel_id=1, source_target_pairs={{0,4},{2,6},{4,0},{6,2},{8,12},{10,14},{12,8},{14,10},{16,20},{18,... | collective-permute-start | bytes 1474568 | tf_op jit(solution)/shard_map/ppermute | solution.py:61
  150.6 14.8 %collective-permute-start.31 = (bf16[2,352,384]{2,1,0:T(8,128)(2,1)S(1)}, bf16[2,352,384]{2,1,0:T(8,128)(2,1)S(1)}, u32[]{:S(2)}, u32[]{:S(2)}) collective-permute-start(bf16[2,352,384]{2,1,0:T(8,128)(2,1)S(1)} %fusion.11), channel_id=1, source_target_pairs={{0,1},{1,0},{2,3},{3,2},{4,5},{5,4},{6,7},{7,6},{8,9},{9,8},{10,11... | collective-permute-start | bytes 1622024 | tf_op jit(solution)/shard_map/ppermute | solution.py:67
  158.3 6.5 %collective-permute-start.34 = (bf16[80,512]{1,0:T(8,128)(2,1)S(1)}, bf16[80,512]{1,0:T(8,128)(2,1)S(1)}, u32[]{:S(2)}, u32[]{:S(2)}) collective-permute-start(bf16[80,512]{1,0:T(8,128)(2,1)S(1)} %get-tuple-element.346), channel_id=1, source_target_pairs={{0,16},{2,18},{4,20},{6,22},{8,24},{10,26},{12,28},{14,30},{16,0},... | collective-permute-start | bytes 245768 | tf_op jit(solution)/shard_map/ppermute | solution.py:64
  169.7 13.1 %collective-permute-start.46 = (bf16[256,640]{1,0:T(8,128)(2,1)S(1)}, bf16[256,640]{1,0:T(8,128)(2,1)S(1)}, u32[]{:S(2)}, u32[]{:S(2)}) collective-permute-start(bf16[256,640]{1,0:T(8,128)(2,1)S(1)} %bitcast.162), channel_id=1, source_target_pairs={{0,4},{2,6},{4,0},{6,2},{8,12},{10,14},{12,8},{14,10},{16,20},{18,... | collective-permute-start | bytes 983048 | tf_op jit(solution)/shard_map/ppermute | solution.py:61
  171.0 11.8 %collective-permute-start.39 = (bf16[352,384]{1,0:T(8,128)(2,1)S(1)}, bf16[352,384]{1,0:T(8,128)(2,1)S(1)}, u32[]{:S(2)}, u32[]{:S(2)}) collective-permute-start(bf16[352,384]{1,0:T(8,128)(2,1)S(1)} %fusion.12), channel_id=1, source_target_pairs={{0,4},{2,6},{4,0},{6,2},{8,12},{10,14},{12,8},{14,10},{16,20},{18,... | collective-permute-start | bytes 811016 | tf_op jit(solution)/shard_map/ppermute | solution.py:61
  171.6 6.2 %collective-permute-start.40 = (bf16[120,512]{1,0:T(8,128)(2,1)S(1)}, bf16[120,512]{1,0:T(8,128)(2,1)S(1)}, u32[]{:S(2)}, u32[]{:S(2)}) collective-permute-start(bf16[120,512]{1,0:T(8,128)(2,1)S(1)} %get-tuple-element.335), channel_id=1, source_target_pairs={{0,8},{2,10},{4,12},{6,14},{8,16},{10,18},{12,20},{14,22},{16,24},... | collective-permute-start | bytes 368648 | tf_op jit(solution)/shard_map/ppermute | solution.py:64
  173.3 9.5 %collective-permute-start.41 = (bf16[120,512]{1,0:T(8,128)(2,1)S(1)}, bf16[120,512]{1,0:T(8,128)(2,1)S(1)}, u32[]{:S(2)}, u32[]{:S(2)}) collective-permute-start(bf16[120,512]{1,0:T(8,128)(2,1)S(1)} %get-tuple-element.334), channel_id=1, source_target_pairs={{0,16},{2,18},{4,20},{6,22},{8,24},{10,26},{12,28},{14,30},{16,0},... | collective-permute-start | bytes 368648 | tf_op jit(solution)/shard_map/ppermute | solution.py:64
  173.7 9.1 %collective-permute-start.42 = (bf16[120,512]{1,0:T(8,128)(2,1)S(1)}, bf16[120,512]{1,0:T(8,128)(2,1)S(1)}, u32[]{:S(2)}, u32[]{:S(2)}) collective-permute-start(bf16[120,512]{1,0:T(8,128)(2,1)S(1)} %get-tuple-element.333), channel_id=1, source_target_pairs={{0,24},{2,26},{4,28},{6,30},{8,0},{10,2},{12,4},{14,6},{16,8},{18,... | collective-permute-start | bytes 368648 | tf_op jit(solution)/shard_map/ppermute | solution.py:64
  183.0 26.4 %collective-permute-start.53 = (bf16[320,512]{1,0:T(8,128)(2,1)S(1)}, bf16[320,512]{1,0:T(8,128)(2,1)S(1)}, u32[]{:S(2)}, u32[]{:S(2)}) collective-permute-start(bf16[320,512]{1,0:T(8,128)(2,1)S(1)} %bitcast.165), channel_id=1, source_target_pairs={{0,4},{2,6},{4,0},{6,2},{8,12},{10,14},{12,8},{14,10},{16,20},{18,... | collective-permute-start | bytes 983048 | tf_op jit(solution)/shard_map/ppermute | solution.py:61
  187.9 7.3 %collective-permute-start.48 = (bf16[88,384]{1,0:T(8,128)(2,1)S(1)}, bf16[88,384]{1,0:T(8,128)(2,1)S(1)}, u32[]{:S(2)}, u32[]{:S(2)}) collective-permute-start(bf16[88,384]{1,0:T(8,128)(2,1)S(1)} %get-tuple-element.358), channel_id=1, source_target_pairs={{0,16},{2,18},{4,20},{6,22},{8,24},{10,26},{12,28},{14,30},{16,0},... | collective-permute-start | bytes 202760 | tf_op jit(solution)/shard_map/ppermute | solution.py:64
  188.0 20.9 %collective-permute-start.50 = (bf16[120,512]{1,0:T(8,128)(2,1)S(1)}, bf16[120,512]{1,0:T(8,128)(2,1)S(1)}, u32[]{:S(2)}, u32[]{:S(2)}) collective-permute-start(bf16[120,512]{1,0:T(8,128)(2,1)S(1)} %add_convert_fusion.6), channel_id=1, source_target_pairs={{0,8},{2,10},{4,12},{6,14},{8,16},{10,18},{12,20},{14,22},{16,24},... | collective-permute-start | bytes 368648 | tf_op jit(solution)/shard_map/ppermute | solution.py:64
  188.1 20.8 %collective-permute-start.51 = (bf16[120,512]{1,0:T(8,128)(2,1)S(1)}, bf16[120,512]{1,0:T(8,128)(2,1)S(1)}, u32[]{:S(2)}, u32[]{:S(2)}) collective-permute-start(bf16[120,512]{1,0:T(8,128)(2,1)S(1)} %add_convert_fusion.6), channel_id=1, source_target_pairs={{0,16},{2,18},{4,20},{6,22},{8,24},{10,26},{12,28},{14,30},{16,0},... | collective-permute-start | bytes 368648 | tf_op jit(solution)/shard_map/ppermute | solution.py:64
  190.5 18.9 %collective-permute-start.52 = (bf16[120,512]{1,0:T(8,128)(2,1)S(1)}, bf16[120,512]{1,0:T(8,128)(2,1)S(1)}, u32[]{:S(2)}, u32[]{:S(2)}) collective-permute-start(bf16[120,512]{1,0:T(8,128)(2,1)S(1)} %add_convert_fusion.6), channel_id=1, source_target_pairs={{0,24},{2,26},{4,28},{6,30},{8,0},{10,2},{12,4},{14,6},{16,8},{18,... | collective-permute-start | bytes 368648 | tf_op jit(solution)/shard_map/ppermute | solution.py:64
  199.0 11.1 %collective-permute-start.67 = (bf16[256,640]{1,0:T(8,128)(2,1)S(1)}, bf16[256,640]{1,0:T(8,128)(2,1)S(1)}, u32[]{:S(2)}, u32[]{:S(2)}) collective-permute-start(bf16[256,640]{1,0:T(8,128)(2,1)S(1)} %bitcast.163), channel_id=1, source_target_pairs={{0,2},{2,0},{4,6},{6,4},{8,10},{10,8},{12,14},{14,12},{16,18},{18,... | collective-permute-start | bytes 983048 | tf_op jit(solution)/shard_map/ppermute | solution.py:58
  209.6 12.8 %collective-permute-start.54 = (bf16[480,512]{1,0:T(8,128)(2,1)S(1)}, bf16[480,512]{1,0:T(8,128)(2,1)S(1)}, u32[]{:S(2)}, u32[]{:S(2)}) collective-permute-start(bf16[480,512]{1,0:T(8,128)(2,1)S(1)} %bitcast.159), channel_id=1, source_target_pairs={{0,4},{2,6},{4,0},{6,2},{8,12},{10,14},{12,8},{14,10},{16,20},{18,... | collective-permute-start | bytes 1474568 | tf_op jit(solution)/shard_map/ppermute | solution.py:61
  209.7 29.2 %collective-permute-start.63 = (bf16[480,512]{1,0:T(8,128)(2,1)S(1)}, bf16[480,512]{1,0:T(8,128)(2,1)}, u32[]{:S(2)}, u32[]{:S(2)}) collective-permute-start(bf16[480,512]{1,0:T(8,128)(2,1)S(1)} %bitcast.160), channel_id=1, source_target_pairs={{0,2},{2,0},{4,6},{6,4},{8,10},{10,8},{12,14},{14,12},{16,18},{18,... | collective-permute-start | bytes 1474568 | tf_op jit(solution)/shard_map/ppermute | solution.py:58
  210.1 9.1 %collective-permute-start.57 = (bf16[88,384]{1,0:T(8,128)(2,1)S(1)}, bf16[88,384]{1,0:T(8,128)(2,1)S(1)}, u32[]{:S(2)}, u32[]{:S(2)}) collective-permute-start(bf16[88,384]{1,0:T(8,128)(2,1)S(1)} %add_convert_fusion.9), channel_id=1, source_target_pairs={{0,8},{2,10},{4,12},{6,14},{8,16},{10,18},{12,20},{14,22},{16,24},... | collective-permute-start | bytes 202760 | tf_op jit(solution)/shard_map/ppermute | solution.py:64
  222.6 8.3 %collective-permute-start.60 = (bf16[352,384]{1,0:T(8,128)(2,1)S(1)}, bf16[352,384]{1,0:T(8,128)(2,1)S(1)}, u32[]{:S(2)}, u32[]{:S(2)}) collective-permute-start(bf16[352,384]{1,0:T(8,128)(2,1)S(1)} %bitcast.171), channel_id=1, source_target_pairs={{0,4},{2,6},{4,0},{6,2},{8,12},{10,14},{12,8},{14,10},{16,20},{18,... | collective-permute-start | bytes 811016 | tf_op jit(solution)/shard_map/ppermute | solution.py:61
  222.9 20.5 %collective-permute-start.61 = (bf16[352,384]{1,0:T(8,128)(2,1)S(1)}, bf16[352,384]{1,0:T(8,128)(2,1)S(1)}, u32[]{:S(2)}, u32[]{:S(2)}) collective-permute-start(bf16[352,384]{1,0:T(8,128)(2,1)S(1)} %bitcast.172), channel_id=1, source_target_pairs={{0,2},{2,0},{4,6},{6,4},{8,10},{10,8},{12,14},{14,12},{16,18},{18,... | collective-permute-start | bytes 811016 | tf_op jit(solution)/shard_map/ppermute | solution.py:58
  224.2 11.2 %collective-permute-start.55 = (bf16[256,640]{1,0:T(8,128)(2,1)S(1)}, bf16[256,640]{1,0:T(8,128)(2,1)S(1)}, u32[]{:S(2)}, u32[]{:S(2)}) collective-permute-start(bf16[256,640]{1,0:T(8,128)(2,1)S(1)} %get-tuple-element.319), channel_id=1, source_target_pairs={{1,0},{2,1},{3,2},{4,3},{5,4},{6,5},{7,6},{8,7},{9,8},{10,9},{11,1... | collective-permute-start | bytes 983048 | tf_op jit(solution)/shard_map/ppermute | solution.py:72
  227.3 10.7 %collective-permute-start.56 = (bf16[256,640]{1,0:T(8,128)(2,1)S(1)}, bf16[256,640]{1,0:T(8,128)(2,1)S(1)}, u32[]{:S(2)}, u32[]{:S(2)}) collective-permute-start(bf16[256,640]{1,0:T(8,128)(2,1)S(1)} %get-tuple-element.320), channel_id=1, source_target_pairs={{2,0},{3,1},{4,2},{5,3},{6,4},{7,5},{8,6},{9,7},{10,8},{11,9},{12,... | collective-permute-start | bytes 983048 | tf_op jit(solution)/shard_map/ppermute | solution.py:72
  231.6 7.3 %collective-permute-start.64 = (bf16[480,512]{1,0:T(8,128)(2,1)S(1)}, bf16[480,512]{1,0:T(8,128)(2,1)S(1)}, u32[]{:S(2)}, u32[]{:S(2)}) collective-permute-start(bf16[480,512]{1,0:T(8,128)(2,1)S(1)} %collective-permute-done.54), channel_id=1, source_target_pairs={{0,2},{2,0},{4,6},{6,4},{8,10},{10,8},{12,14},{14,12},{16,18},{18,... | collective-permute-start | bytes 1474568 | tf_op jit(solution)/shard_map/ppermute | solution.py:58
  235.4 8.0 %collective-permute-start.62 = (bf16[352,384]{1,0:T(8,128)(2,1)}, bf16[352,384]{1,0:T(8,128)(2,1)S(1)}, u32[]{:S(2)}, u32[]{:S(2)}) collective-permute-start(bf16[352,384]{1,0:T(8,128)(2,1)} %copy-done.22), channel_id=1, source_target_pairs={{0,2},{2,0},{4,6},{6,4},{8,10},{10,8},{12,14},{14,12},{16,18},{18,... | collective-permute-start | bytes 811016 | tf_op jit(solution)/shard_map/ppermute | solution.py:58
  (62 other events, 440.7 us)

commit v8 on v7

--- a/solution.py
+++ b/solution.py
@@ -179,6 +179,20 @@
     return du, jnp.sum(dz * ur, axis=0, keepdims=True)
 
 
+class Writer:
+    def __init__(self, sems):
+        self.sems, self.copies = sems, []
+
+    def put(self, source, target):
+        copy = pltpu.make_async_copy(source, target, self.sems.at[len(self.copies)])
+        copy.start()
+        self.copies.append(copy)
+
+    def wait(self):
+        for copy in self.copies:
+            copy.wait()
+
+
 def params(megabytes=56):
     return pltpu.CompilerParams(vmem_limit_bytes=megabytes * 1024 * 1024)
 
@@ -266,8 +280,12 @@
         refs[n_out + n_gate : n_out + n_gate + n_up],
         refs[n_out + n_gate + n_up :],
     )
-    projected_ref, residual_ref, ffn_in_ref, mixed, gelu_out, gate_slope = refs[:6]
-    out_full, gate_full, up_full, out_sems, gate_sems, up_sems = refs[6:]
+    projected_out, residual_out, ffn_in_ref, mixed_out, gelu_out_out, gate_slope_out = refs[:6]
+    (
+        projected_ref, residual_ref, mixed, gelu_out, gate_slope,
+        out_full, gate_full, up_full, out_sems, gate_sems, up_sems, write_sems,
+    ) = refs[6:]
+    writer = Writer(write_sems)
     groups = (
         place_copies(out_w[:1], out_w[1:], out_full, out_sems, at, 0, 2),
         place_copies(gate_w[:1], gate_w[1:], gate_full, gate_sems, at, 1, 4),
@@ -283,13 +301,18 @@
     residual = tokens[...].astype(F32) + projected * inverse_rms(projected) * gain_table[3:4, :]
     residual_ref[...] = residual
     ffn_in_ref[...] = (residual * inverse_rms(residual) * gain_table[4:5, :]).astype(BF16)
-    for group in groups[1:]:
-        for copy in group:
+    writer.put(projected_ref, projected_out)
+    writer.put(residual_ref, residual_out)
+    width = gate_full.shape[1] // 4
+    for k in range(4):
+        waits = groups[1][1 + k :: 4] + (groups[2][1 + k // 2 :: 2] if k % 2 == 0 else [])
+        if k == 0:
+            waits = groups[1][:1] + groups[2][:1] + waits
+        for copy in waits:
             copy.wait()
-    width = 256
-
-    def step(i, _):
-        cut = pl.ds(multiple(i * width, width), width)
+        core = at[0] if k < 2 else 1 - at[0]
+        mid = at[1] if k % 2 == 0 else 1 - at[1]
+        cut = pl.ds(multiple((core * 2 + mid) * width, width), width)
         gate = dot(ffn_in_ref[...], gate_full[:, cut])
         up = dot(ffn_in_ref[...], up_full[:, cut])
         square = gate * gate
@@ -300,9 +323,10 @@
         mixed[:, cut] = (act * up).astype(BF16)
         gelu_out[:, cut] = act.astype(BF16)
         gate_slope[:, cut] = (up * slope).astype(BF16)
-        return 0
-
-    lax.fori_loop(0, gate_full.shape[1] // width, step, 0)
+        writer.put(mixed.at[:, cut], mixed_out.at[:, cut])
+        writer.put(gelu_out.at[:, cut], gelu_out_out.at[:, cut])
+        writer.put(gate_slope.at[:, cut], gate_slope_out.at[:, cut])
+    writer.wait()
 
 
 def relative_blocks(at, fsdp):
@@ -574,12 +598,12 @@
         self.gathered = [own] + [here.outer_shift(own, by) for by in range(1, here.outer)]
         return self.shares[-1]
 
-    def mid_gather(self, *earlier):
+    def mid_gather(self, *earlier, hold=()):
         here = self.here
         self.gathered = list(after(tuple(self.gathered), *earlier))
         block = ordered(self.gathered, here.outer_behind)
         block = block.reshape(-1, block.shape[-1])
-        across = here.mid_swap(block)
+        across = after(here.mid_swap(block), *hold)
         self.blocks = [[block, across], [here.core_swap(block), here.core_swap(across)]]
         return self.gathered[-1]
 
@@ -679,14 +703,20 @@
             shape((rows, hidden), BF16),
         ),
         in_specs=[SMEM] + [VMEM] * 3 + [ANY] * (len(out_w) + len(gate_w) + len(up_w)),
-        out_specs=(VMEM,) * 6,
+        out_specs=(ANY, ANY, VMEM, ANY, ANY, ANY),
         scratch_shapes=[
+            pltpu.VMEM((rows, width), F32),
+            pltpu.VMEM((rows, width), F32),
+            pltpu.VMEM((rows, hidden), BF16),
+            pltpu.VMEM((rows, hidden), BF16),
+            pltpu.VMEM((rows, hidden), BF16),
             pltpu.VMEM((query_cols, width), BF16),
             pltpu.VMEM((width, hidden), BF16),
             pltpu.VMEM((width, hidden), BF16),
             pltpu.SemaphoreType.DMA((len(out_w),)),
             pltpu.SemaphoreType.DMA((len(gate_w),)),
             pltpu.SemaphoreType.DMA((len(up_w),)),
+            pltpu.SemaphoreType.DMA((14,)),
         ],
         compiler_params=params(),
         cost_estimate=cost(4e9, 2 * weight_bytes),
@@ -821,13 +851,13 @@
     last_sum = Chunk(here, last_keep, last_send)
     down_sum.outer_sums(last_keep)
     gate_sum.over_mid(last_keep, *up_sum.arrived)
-    (last_sum.other,), (gate_sum.across,), down_sum.shares, out_sum.arrived = together(
-        (last_sum.other,), (gate_sum.across,), down_sum.shares, out_sum.arrived
+    down_sum.outer_gather()
+    (last_sum.other,), (gate_sum.across,), down_sum.gathered, out_sum.arrived = together(
+        (last_sum.other,), (gate_sum.across,), down_sum.gathered, out_sum.arrived
     )
     last_sum.over_fsdp()
     up_sum.join(out_sum)
     gate_sum.outer_sums()
-    down_sum.outer_gather()
     last_sum.arrived, (up_sum.across,), gate_sum.shares, down_sum.gathered = together(
         last_sum.arrived, (up_sum.across,), gate_sum.shares, down_sum.gathered
     )
@@ -846,20 +876,11 @@
     gate_sum.blocks[0] = list(gate_last)
     last_sum.outer_gather()
     up_sum.mid_gather()
-    last_sum.mid_gather(up_sum.blocks[0][1])
-    d_halo = after(d_halo, up_sum.blocks[0][1])
-    halos = [linear_shift(d_halo[halo - by * rows :][:rows], -by) for by in range(1, hops + 1)]
     down_blocks, gate_blocks = by_place(here, down_sum.blocks), by_place(here, gate_sum.blocks)
-    both_blocks, last_blocks = by_place(here, up_sum.blocks), by_place(here, last_sum.blocks)
-    total_gains = last_sum.blocks[0][0][shard_rows:, :LANES].astype(F32)
-
-    for came in halos:
-        grad_tokens = grad_tokens + came.astype(F32)
-
+    both_blocks = by_place(here, up_sum.blocks)
     total_down = jnp.concatenate(down_blocks, axis=0).astype(F32)
     total_gate = jnp.concatenate(gate_blocks, axis=1).astype(F32)
     total_up = jnp.concatenate([b[:shard_rows] for b in both_blocks], axis=1).astype(F32)
-    total_qkv = jnp.concatenate([b[:shard_rows] for b in last_blocks], axis=1).astype(F32)
     wide = hidden // 4
     parts = wide // LANES
     total_out = []
@@ -868,6 +889,14 @@
         below = below.transpose(1, 0, 2).reshape(out_block, LANES)
         total_out.append(jnp.concatenate([block[shard_rows : shard_rows + out_block], below], axis=1))
     total_out = jnp.concatenate(total_out, axis=0).astype(F32)
+    last_sum.mid_gather(up_sum.blocks[0][1], hold=(total_up, total_out))
+    d_halo = after(d_halo, last_sum.blocks[0][1])
+    for by in range(1, hops + 1):
+        came = linear_shift(d_halo[halo - by * rows :][:rows], -by)
+        grad_tokens = grad_tokens + after(came, last_sum.blocks[1][1]).astype(F32)
+    total_gains = last_sum.blocks[0][0][shard_rows:, :LANES].astype(F32)
+    last_blocks = by_place(here, last_sum.blocks)
+    total_qkv = jnp.concatenate([b[:shard_rows] for b in last_blocks], axis=1).astype(F32)
     g, at_row = [], 0
     for gain in gains:
         deep = fsdp * gain.shape[0] // total_gains.shape[1]

time: 247 us -> 258 us (1.045)
  waiting for transfers between devices: 50.9 us -> 75.7 us
  starting transfers between devices: 86.9 us -> 76.4 us
    ppermute x24, waiting for transfers between devices: 20.4 us -> 33.9 us  [outer_shift(): lax.ppermute(array, 'seq', [(i, (i + 4 * by) % self.seq) for i in range(s...]
    ppermute x10, waiting for transfers between devices: 5.97 us -> 14.5 us  [mid_swap(): return lax.ppermute(array, 'seq', [(i, i ^ 2) for i in range(self.seq)])]
    ppermute x20, starting transfers between devices: 22.2 us -> 15.1 us  [core_swap(): return lax.ppermute(array, 'seq', [(i, i ^ 1) for i in range(self.seq)])]
    ppermute x24, starting transfers between devices: 34.1 us -> 29.3 us  [outer_shift(): lax.ppermute(array, 'seq', [(i, (i + 4 * by) % self.seq) for i in range(s...]
  transfers between devices with their start and end apart: 69 -> 69, of which waited for: 27 -> 22; matrix products, arithmetic and copies ran while one was open for 12% -> 12% of each run, Pallas kernels for 24% -> 22%
where the time goes in v8:
time: 258 us; the launch traced here: 257 us
  starting transfers between devices  76.4 us (30%)
  waiting for transfers between devices  75.7 us (29%)
  Pallas kernels  64.4 us (25%)
  other arithmetic  25.7 us (10%)
  local copies, waits for them, and re-layouts  12.6 us (5%)
    ppermute x24, waiting for transfers between devices, outer_shift(): lax.ppermute(array, 'seq', [(i, (i + 4 * by) % self.seq) for i in range(s...  33.9 us
    ppermute x24, starting transfers between devices, outer_shift(): lax.ppermute(array, 'seq', [(i, (i + 4 * by) % self.seq) for i in range(s...  29.3 us
    ppermute x11, waiting for transfers between devices, fsdp_shift(): lax.ppermute(array, 'fsdp', [(i, (i + by) % self.fsdp) for i in range(sel...  18.1 us
    ppermute x20, starting transfers between devices, core_swap(): return lax.ppermute(array, 'seq', [(i, i ^ 1) for i in range(self.seq)])  15.1 us
    ppermute x10, waiting for transfers between devices, mid_swap(): return lax.ppermute(array, 'seq', [(i, i ^ 2) for i in range(self.seq)])  14.5 us
    pallas_call x1, Pallas kernels, on_device(): pl.pallas_call(functools.partial(last_kernel, len(qkv_w), n_tok, fsdp, he...  11.9 us
    ppermute x11, starting transfers between devices, fsdp_shift(): lax.ppermute(array, 'fsdp', [(i, (i + by) % self.fsdp) for i in range(sel...  11.1 us
    ppermute x4, starting transfers between devices, linear_shift(): lax.ppermute(array, ('seq', 'fsdp'), [(i, i + by) for i in range(count) i...  10.8 us
  transfers between devices with their start and end apart: 69, of which 22 were waited for; matrix products, arithmetic and copies ran while one was open for 12% of the time, Pallas kernels for 22%

profile of v8, /device:TPU:1, one launch (start us, length us, event | category | flops | bytes accessed | tf_op | source)
XLA Modules:
  0.0 257.0 jit_solution(744273580567515684)
XLA Ops:
  4.5 2.1 collective-permute-start.2
  6.7 3.9 %collective-permute-start = (bf16[256,640]{1,0:T(8,128)(2,1)S(1)}, bf16[256,640]{1,0:T(8,128)(2,1)}, u32[]{:S(2)}, u32[]{:S(2)}) collective-permute-start(bf16[256,640]{1,0:T(8,128)(2,1)S(1)} %copy-done.34), channel_id=1, source_target_pairs={{0,2},{1,3},{2,4},{3,5},{4,6},{5,7},{6,8},{7,9},{8,10},{9,11},{10,... | collective-permute-start | bytes 983048 | tf_op jit(solution)/shard_map/ppermute | solution.py:72
  10.6 2.1 collective-permute-start.1
  16.2 2.5 multiply_sine_fusion
  20.1 1.7 collective-permute-start.3
  22.3 3.2 %collective-permute-done.5.refs_12_.refs_21_ = bf16[320,384]{1,0:T(8,128)(2,1)S(1)} collective-permute-done((bf16[320,384]{1,0:T(8,128)(2,1)}, bf16[320,384]{1,0:T(8,128)(2,1)S(1)}, u32[]{:S(2)}, u32[]{:S(2)}) %collective-permute-start.5) | collective-permute-done | bytes 245792 | tf_op jit(solution)/shard_map/ppermute | solution.py:61
  25.6 1.8 collective-permute-start.7
  29.8 2.1 collective-permute-start.13
  32.8 9.0 %attend.1 = (bf16[768,640]{1,0:T(8,128)(2,1)}, f32[256,1024]{1,0:T(8,128)}, f32[768,256]{1,0:T(8,128)}, bf16[1024,256]{1,0:T(8,128)(2,1)}, bf16[768,256]{1,0:T(8...) custom-call(s32[3]{0:T(128)} %pad_add_fusion.refs_0_, ...), custom_call_target="tpu_custom_call" | custom-call | flops 80000000000 | bytes 200000000 | tf_op jit(solution)/shard_map/attend/pallas_call | solution.py:668
  41.8 10.0 %collective-permute-done.13.refs_13_.refs_17_ = bf16[320,1024]{1,0:T(8,128)(2,1)S(1)} collective-permute-done((bf16[320,1024]{1,0:T(8,128)(2,1)S(1)}, bf16[320,1024]{1,0:T(8,128)(2,1)S(1)}, u32[]{:S(2)}, u32[]{:S(2)}) %collective-permute-start.13) | collective-permute-done | bytes 655392 | tf_op jit(solution)/shard_map/ppermute | solution.py:67
  53.9 1.6 collective-permute-done.11.refs_10_.refs_14_
  57.4 9.4 %gate.1 = (f32[256,640]{1,0:T(8,128)}, f32[256,640]{1,0:T(8,128)}, bf16[256,640]{1,0:T(8,128)(2,1)}, bf16[256,2048]{1,0:T(8,128)(2,1)}, bf16[256,2048]{1,0:T(8,128)(2,1)}, /*index=5*/bf16[256,2048]{1,0:T(8,128)(2,1)}) custom-call(s32[3]{0:T(128)} %pad_add_fusion.refs_0_, bf16[256,1024]{1,0:T(8,128)(2,1)} %get-tuple-element.167.refs_1_.refs_7_, ...), custom_call_target="tpu_custom_call" | custom-call | flops 80000000000 | bytes 104857600 | tf_op jit(solution)/shard_map/gate/pallas_call | solution.py:695
  66.7 2.5 collective-permute-done.15.refs_6_
  70.5 1.7 collective-permute-done.16.refs_7_
  73.1 6.6 %down.1 = (bf16[256,640]{1,0:T(8,128)(2,1)}, bf16[256,640]{1,0:T(8,128)(2,1)}, f32[1,640]{1,0:T(1,128)}, bf16[2,2,256,640]{3,2,1,0:T(8,128)(2,1)}, bf16[2,2,256,640]{3,2,1,0:T(8,128)(2,1)}) custom-call(s32[3]{0:T(128)} %pad_add_fusion.refs_0_, bf16[256,2048]{1,0:T(8,128)(2,1)} %get-tuple-element.173.refs_1_, f32[256,640]{1,0:T(8,128)} %get-tuple-element.174.refs_2_.refs_3_, ...), custom_call_target="tpu_custom_call" | custom-call | flops 80000000000 | bytes 104857600 | tf_op jit(solution)/shard_map/down/pallas_call | solution.py:729
  80.2 10.3 %gate_back.1 = (bf16[256,2048]{1,0:T(8,128)(2,1)}, bf16[256,2048]{1,0:T(8,128)(2,1)}, bf16[2,2,320,512]{3,2,1,0:T(8,128)(2,1)}, bf16[2,2,320,512]{3,2,1,0:T(8,12...) custom-call(s32[3]{0:T(128)} %pad_add_fusion.refs_0_, ...), custom_call_target="tpu_custom_call" | custom-call | flops 120000004096 | bytes 157286400 | tf_op jit(solution)/shard_map/gate_back/pallas_call | solution.py:752
  92.8 10.7 %middle.1 = (f32[256,640]{1,0:T(8,128)}, f32[1,640]{1,0:T(1,128)}, f32[1,640]{1,0:T(1,128)}, bf16[1024,256]{1,0:T(8,128)(2,1)}, bf16[2,2,160,512]{3,2,1,0:T(8,128)(2,1)}, /*index=5*/bf16[2,2,160,512]{3,2,1,0:T(8,128)(2,1)}) custom-call(s32[3]{0:T(128)} %pad_add_fusion.refs_0_, bf16[256,2048]{1,0:T(8,128)(2,1)} %get-tuple-element.184.refs_1_, ...), custom_call_target="tpu_custom_call" | custom-call | flops 120000004096 | bytes 209715200 | tf_op jit(solution)/shard_map/middle/pallas_call | solution.py:783
  110.2 6.5 %attend_back.1 = (f32[256,1024]{1,0:T(8,128)}, f32[768,256]{1,0:T(8,128)}, f32[768,256]{1,0:T(8,128)}) custom-call(bf16[1024,256]{1,0:T(8,128)(2,1)} %get-tuple-element.195.d_att, bf16[1024,256]{1,0:T(8,128)(2,1)} %get-tuple-element.196.q_st, bf16[768,256]{1,0:T(8,128)(2,1)} %get-tuple-element.197.keys, bf16[768,256]{1,0:T(8,128)(2,1)} %get-tuple-element.198.values, ...), custom_call_target="tpu_custom_call" | custom-call | flops 120000004096 | bytes 157286400 | tf_op jit(solution)/shard_map/attend_back/pallas_call | solution.py:813
  118.1 4.6 %collective-permute-done.25 = bf16[2,320,512]{2,1,0:T(8,128)(2,1)S(1)} collective-permute-done((bf16[2,320,512]{2,1,0:T(8,128)(2,1)}, bf16[2,320,512]{2,1,0:T(8,128)(2,1)S(1)}, u32[]{:S(2)}, u32[]{:S(2)}) %collective-permute-start.25) | collective-permute-done | bytes 655392 | tf_op jit(solution)/shard_map/ppermute | solution.py:67
  122.8 11.9 %last.1 = (f32[256,640]{1,0:T(8,128)}, bf16[512,640]{1,0:T(8,128)(2,1)}, bf16[2,2,352,384]{3,2,1,0:T(8,128)(2,1)}, bf16[2,2,352,384]{3,2,1,0:T(8,128)(2,1)}) custom-call(s32[3]{0:T(128)} %pad_add_fusion.refs_0_, f32[256,640]{1,0:T(8,128)} %get-tuple-element.187.refs_1_, f32[256,1024]{1,0:T(8,128)} %get-tuple-element.204.refs_2_, ...), custom_call_target="tpu_custom_call" | custom-call | flops 299999985664 | bytes 209715200 | tf_op jit(solution)/shard_map/last/pallas_call | solution.py:826
  134.7 1.6 collective-permute-start.23
  136.3 1.4 fusion.8
  137.8 1.4 collective-permute-start.27
  139.2 2.3 collective-permute-start.28
  145.1 2.5 collective-permute-done.28
  147.7 2.1 collective-permute-start.30
  153.4 4.2 %collective-permute-done.31 = bf16[64,640]{1,0:T(8,128)(2,1)S(1)} collective-permute-done((bf16[64,640]{1,0:T(8,128)(2,1)S(1)}, bf16[64,640]{1,0:T(8,128)(2,1)S(1)}, u32[]{:S(2)}, u32[]{:S(2)}) %collective-permute-start.31) | collective-permute-done | bytes 81952 | tf_op jit(solution)/shard_map/ppermute | solution.py:64
  162.0 2.1 collective-permute-start.36
  164.0 2.2 collective-permute-start.38
  167.2 4.3 %collective-permute-done.37 = bf16[80,512]{1,0:T(8,128)(2,1)S(1)} collective-permute-done((bf16[80,512]{1,0:T(8,128)(2,1)S(1)}, bf16[80,512]{1,0:T(8,128)(2,1)S(1)}, u32[]{:S(2)}, u32[]{:S(2)}) %collective-permute-start.37) | collective-permute-done | bytes 81952 | tf_op jit(solution)/shard_map/ppermute | solution.py:64
  171.5 2.1 collective-permute-start.43
  178.2 2.9 %collective-permute-done.44 = bf16[80,512]{1,0:T(8,128)(2,1)S(1)} collective-permute-done((bf16[80,512]{1,0:T(8,128)(2,1)S(1)}, bf16[80,512]{1,0:T(8,128)(2,1)S(1)}, u32[]{:S(2)}, u32[]{:S(2)}) %collective-permute-start.44) | collective-permute-done | bytes 81952 | tf_op jit(solution)/shard_map/ppermute | solution.py:64
  183.3 7.6 %collective-permute-done.45 = bf16[80,512]{1,0:T(8,128)(2,1)S(1)} collective-permute-done((bf16[80,512]{1,0:T(8,128)(2,1)S(1)}, bf16[80,512]{1,0:T(8,128)(2,1)S(1)}, u32[]{:S(2)}, u32[]{:S(2)}) %collective-permute-start.45) | collective-permute-done | bytes 81952 | tf_op jit(solution)/shard_map/ppermute | solution.py:64
  191.1 2.5 collective-permute-start.53
  195.3 2.3 collective-permute-start.51
  201.1 11.0 %collective-permute-done.48 = bf16[88,384]{1,0:T(8,128)(2,1)S(1)} collective-permute-done((bf16[88,384]{1,0:T(8,128)(2,1)S(1)}, bf16[88,384]{1,0:T(8,128)(2,1)S(1)}, u32[]{:S(2)}, u32[]{:S(2)}) %collective-permute-start.48) | collective-permute-done | bytes 67616 | tf_op jit(solution)/shard_map/ppermute | solution.py:64
  212.1 2.3 collective-permute-start.67
  217.0 1.6 collective-permute-start.56
  218.9 1.7 maximum_convert_fusion.2
  222.3 1.8 maximum_convert_fusion.1
  224.1 8.1 %collective-permute-done.57 = bf16[480,512]{1,0:T(8,128)(2,1)S(1)} collective-permute-done((bf16[480,512]{1,0:T(8,128)(2,1)S(1)}, bf16[480,512]{1,0:T(8,128)(2,1)S(1)}, u32[]{:S(2)}, u32[]{:S(2)}) %collective-permute-start.57) | collective-permute-done | bytes 491552 | tf_op jit(solution)/shard_map/ppermute | solution.py:61
  232.3 1.9 collective-permute-start.60
  238.9 1.8 maximum_convert_fusion
  240.7 1.9 collective-permute-done.58
  243.4 2.8 %collective-permute-start.61 = (bf16[256,640]{1,0:T(8,128)(2,1)S(1)}, bf16[256,640]{1,0:T(8,128)(2,1)S(1)}, u32[]{:S(2)}, u32[]{:S(2)}) collective-permute-start(bf16[256,640]{1,0:T(8,128)(2,1)S(1)} %get-tuple-element.325), channel_id=1, source_target_pairs={{1,0},{2,1},{3,2},{4,3},{5,4},{6,5},{7,6},{8,7},{9,8},{10,9},{11,1... | collective-permute-start | bytes 983048 | tf_op jit(solution)/shard_map/ppermute | solution.py:72
  246.2 1.9 collective-permute-start.63
  250.7 4.0 %collective-permute-done.61 = bf16[256,640]{1,0:T(8,128)(2,1)S(1)} collective-permute-done((bf16[256,640]{1,0:T(8,128)(2,1)S(1)}, bf16[256,640]{1,0:T(8,128)(2,1)S(1)}, u32[]{:S(2)}, u32[]{:S(2)}) %collective-permute-start.61) | collective-permute-done | bytes 327712 | tf_op jit(solution)/shard_map/ppermute | solution.py:72
  254.6 1.4 collective-permute-done.63
  (283 shorter events, 66.6 us)
Async XLA Ops:
  4.5 14.2 %collective-permute-start.2 = (bf16[320,384]{1,0:T(8,128)(2,1)S(1)}, bf16[320,384]{1,0:T(8,128)(2,1)}, u32[]{:S(2)}, u32[]{:S(2)}) collective-permute-start(bf16[320,384]{1,0:T(8,128)(2,1)S(1)} %maximum_select_fusion), channel_id=1, source_target_pairs={{0,1},{1,0},{2,3},{3,2},{4,5},{5,4},{6,7},{7,6},{8,9},{9,8},{10,11... | collective-permute-start | bytes 737288 | tf_op jit(solution)/shard_map/ppermute | solution.py:67
  6.7 21.8 %collective-permute-start = (bf16[256,640]{1,0:T(8,128)(2,1)S(1)}, bf16[256,640]{1,0:T(8,128)(2,1)}, u32[]{:S(2)}, u32[]{:S(2)}) collective-permute-start(bf16[256,640]{1,0:T(8,128)(2,1)S(1)} %copy-done.34), channel_id=1, source_target_pairs={{0,2},{1,3},{2,4},{3,5},{4,6},{5,7},{6,8},{7,9},{8,10},{9,11},{10,... | collective-permute-start | bytes 983048 | tf_op jit(solution)/shard_map/ppermute | solution.py:72
  10.6 17.9 %collective-permute-start.1 = (bf16[256,640]{1,0:T(8,128)(2,1)S(1)}, bf16[256,640]{1,0:T(8,128)(2,1)}, u32[]{:S(2)}, u32[]{:S(2)}) collective-permute-start(bf16[256,640]{1,0:T(8,128)(2,1)S(1)} %copy-done.34), channel_id=1, source_target_pairs={{0,1},{1,2},{2,3},{3,4},{4,5},{5,6},{6,7},{7,8},{8,9},{9,10},{10,1... | collective-permute-start | bytes 983048 | tf_op jit(solution)/shard_map/ppermute | solution.py:72
  20.1 8.9 %collective-permute-start.3 = (bf16[320,512]{1,0:T(8,128)(2,1)S(1)}, bf16[320,512]{1,0:T(8,128)(2,1)}, u32[]{:S(2)}, u32[]{:S(2)}) collective-permute-start(bf16[320,512]{1,0:T(8,128)(2,1)S(1)} %constant_dynamic-slice_fusion.25), channel_id=1, source_target_pairs={{0,1},{1,0},{2,3},{3,2},{4,5},{5,4},{6,7},{7,6},{8,9},{9,8},{10,11... | collective-permute-start | bytes 983048 | tf_op jit(solution)/shard_map/ppermute | solution.py:67
  21.9 10.2 %collective-permute-start.6 = (bf16[320,384]{1,0:T(8,128)(2,1)}, bf16[320,384]{1,0:T(8,128)(2,1)S(1)}, u32[]{:S(2)}, u32[]{:S(2)}) collective-permute-start(bf16[320,384]{1,0:T(8,128)(2,1)} %collective-permute-done.2.refs_11_.refs_20_), channel_id=1, source_target_pairs={{0,2},{2,0},{4,6},{6,4},{8,10},{10,8},{12,14},{14,12},{16,18},{18,... | collective-permute-start | bytes 737288 | tf_op jit(solution)/shard_map/ppermute | solution.py:58
  28.5 24.2 %collective-permute-start.8 = (bf16[256,640]{1,0:T(8,128)(2,1)S(1)}, bf16[256,640]{1,0:T(8,128)(2,1)S(1)}, u32[]{:S(2)}, u32[]{:S(2)}) collective-permute-start(bf16[256,640]{1,0:T(8,128)(2,1)S(1)} %constant_dynamic-slice_fusion.24), channel_id=1, source_target_pairs={{0,1},{1,0},{2,3},{3,2},{4,5},{5,4},{6,7},{7,6},{8,9},{9,8},{10,11... | collective-permute-start | bytes 983048 | tf_op jit(solution)/shard_map/ppermute | solution.py:67
  29.8 22.1 %collective-permute-start.13 = (bf16[320,1024]{1,0:T(8,128)(2,1)S(1)}, bf16[320,1024]{1,0:T(8,128)(2,1)S(1)}, u32[]{:S(2)}, u32[]{:S(2)}) collective-permute-start(bf16[320,1024]{1,0:T(8,128)(2,1)S(1)} %constant_dynamic-slice_fusion.23), channel_id=1, source_target_pairs={{0,1},{1,0},{2,3},{3,2},{4,5},{5,4},{6,7},{7,6},{8,9},{9,8},{10,11... | collective-permute-start | bytes 1966088 | tf_op jit(solution)/shard_map/ppermute | solution.py:67
  31.9 21.2 %collective-permute-start.10 = (bf16[320,512]{1,0:T(8,128)(2,1)}, bf16[320,512]{1,0:T(8,128)(2,1)}, u32[]{:S(2)}, u32[]{:S(2)}) collective-permute-start(bf16[320,512]{1,0:T(8,128)(2,1)} %collective-permute-done.3.refs_8_.refs_12_), channel_id=1, source_target_pairs={{0,4},{2,6},{4,0},{6,2},{8,12},{10,14},{12,8},{14,10},{16,20},{18,... | collective-permute-start | bytes 983048 | tf_op jit(solution)/shard_map/ppermute | solution.py:61
  53.3 15.9 %collective-permute-start.15 = (bf16[512,640]{1,0:T(8,128)(2,1)S(1)}, bf16[512,640]{1,0:T(8,128)(2,1)S(1)}, u32[]{:S(2)}, u32[]{:S(2)}) collective-permute-start(bf16[512,640]{1,0:T(8,128)(2,1)S(1)} %constant_dynamic-slice_fusion.22), channel_id=1, source_target_pairs={{0,1},{1,0},{2,3},{3,2},{4,5},{5,4},{6,7},{7,6},{8,9},{9,8},{10,11... | collective-permute-start | bytes 1966088 | tf_op jit(solution)/shard_map/ppermute | solution.py:67
  79.7 11.4 %collective-permute-start.17 = (bf16[2,2,256,640]{3,2,1,0:T(8,128)(2,1)}, bf16[2,2,256,640]{3,2,1,0:T(8,128)(2,1)S(1)}, u32[]{:S(2)}, u32[]{:S(2)}) collective-permute-start(bf16[2,2,256,640]{3,2,1,0:T(8,128)(2,1)} %get-tuple-element.183), channel_id=1, source_target_pairs={{0,2},{2,0},{4,6},{6,4},{8,10},{10,8},{12,14},{14,12},{16,18},{18,... | collective-permute-start | bytes 3932168 | tf_op jit(solution)/shard_map/ppermute | solution.py:58
  90.5 15.6 %collective-permute-start.18 = (bf16[2,2,320,512]{3,2,1,0:T(8,128)(2,1)}, bf16[2,2,320,512]{3,2,1,0:T(8,128)(2,1)S(1)}, u32[]{:S(2)}, u32[]{:S(2)}) collective-permute-start(bf16[2,2,320,512]{3,2,1,0:T(8,128)(2,1)} %get-tuple-element.189), channel_id=1, source_target_pairs={{0,2},{2,0},{4,6},{6,4},{8,10},{10,8},{12,14},{14,12},{16,18},{18,... | collective-permute-start | bytes 3932168 | tf_op jit(solution)/shard_map/ppermute | solution.py:58
  90.7 13.3 %collective-permute-start.19 = (bf16[2,2,320,512]{3,2,1,0:T(8,128)(2,1)}, bf16[2,2,320,512]{3,2,1,0:T(8,128)(2,1)S(1)}, u32[]{:S(2)}, u32[]{:S(2)}) collective-permute-start(bf16[2,2,320,512]{3,2,1,0:T(8,128)(2,1)} %get-tuple-element.190), channel_id=1, source_target_pairs={{0,2},{2,0},{4,6},{6,4},{8,10},{10,8},{12,14},{14,12},{16,18},{18,... | collective-permute-start | bytes 3932168 | tf_op jit(solution)/shard_map/ppermute | solution.py:58
  92.3 16.4 %collective-permute-start.20 = (bf16[2,256,640]{2,1,0:T(8,128)(2,1)}, bf16[2,256,640]{2,1,0:T(8,128)(2,1)S(1)}, u32[]{:S(2)}, u32[]{:S(2)}) collective-permute-start(bf16[2,256,640]{2,1,0:T(8,128)(2,1)} %fusion), channel_id=1, source_target_pairs={{0,1},{1,0},{2,3},{3,2},{4,5},{5,4},{6,7},{7,6},{8,9},{9,8},{10,11... | collective-permute-start | bytes 1966088 | tf_op jit(solution)/shard_map/ppermute | solution.py:67
  103.5 13.2 %collective-permute-start.21 = (bf16[2,2,160,512]{3,2,1,0:T(8,128)(2,1)}, bf16[2,2,160,512]{3,2,1,0:T(8,128)(2,1)S(1)}, u32[]{:S(2)}, u32[]{:S(2)}) collective-permute-start(bf16[2,2,160,512]{3,2,1,0:T(8,128)(2,1)} %get-tuple-element.201), channel_id=1, source_target_pairs={{0,2},{2,0},{4,6},{6,4},{8,10},{10,8},{12,14},{14,12},{16,18},{18,... | collective-permute-start | bytes 1966088 | tf_op jit(solution)/shard_map/ppermute | solution.py:58
  105.2 17.6 %collective-permute-start.25 = (bf16[2,320,512]{2,1,0:T(8,128)(2,1)}, bf16[2,320,512]{2,1,0:T(8,128)(2,1)S(1)}, u32[]{:S(2)}, u32[]{:S(2)}) collective-permute-start(bf16[2,320,512]{2,1,0:T(8,128)(2,1)} %fusion.2), channel_id=1, source_target_pairs={{0,1},{1,0},{2,3},{3,2},{4,5},{5,4},{6,7},{7,6},{8,9},{9,8},{10,11... | collective-permute-start | bytes 1966088 | tf_op jit(solution)/shard_map/ppermute | solution.py:67
  107.3 34.2 %collective-permute-start.24 = (bf16[2,320,512]{2,1,0:T(8,128)(2,1)}, bf16[2,320,512]{2,1,0:T(8,128)(2,1)}, u32[]{:S(2)}, u32[]{:S(2)}) collective-permute-start(bf16[2,320,512]{2,1,0:T(8,128)(2,1)} %fusion.1), channel_id=1, source_target_pairs={{0,1},{1,0},{2,3},{3,2},{4,5},{5,4},{6,7},{7,6},{8,9},{9,8},{10,11... | collective-permute-start | bytes 1966088 | tf_op jit(solution)/shard_map/ppermute | solution.py:67
  108.8 13.9 %collective-permute-start.22 = (bf16[256,640]{1,0:T(8,128)(2,1)S(1)}, bf16[256,640]{1,0:T(8,128)(2,1)S(1)}, u32[]{:S(2)}, u32[]{:S(2)}) collective-permute-start(bf16[256,640]{1,0:T(8,128)(2,1)S(1)} %fusion.10), channel_id=1, source_target_pairs={{0,4},{2,6},{4,0},{6,2},{8,12},{10,14},{12,8},{14,10},{16,20},{18,... | collective-permute-start | bytes 983048 | tf_op jit(solution)/shard_map/ppermute | solution.py:61
  117.6 33.2 %collective-permute-start.33 = (bf16[2,160,512]{2,1,0:T(8,128)(2,1)}, bf16[2,160,512]{2,1,0:T(8,128)(2,1)}, u32[]{:S(2)}, u32[]{:S(2)}) collective-permute-start(bf16[2,160,512]{2,1,0:T(8,128)(2,1)} %fusion.15), channel_id=1, source_target_pairs={{0,1},{1,0},{2,3},{3,2},{4,5},{5,4},{6,7},{7,6},{8,9},{9,8},{10,11... | collective-permute-start | bytes 983048 | tf_op jit(solution)/shard_map/ppermute | solution.py:67
  134.7 22.8 %collective-permute-start.23 = (bf16[2,2,352,384]{3,2,1,0:T(8,128)(2,1)}, bf16[2,2,352,384]{3,2,1,0:T(8,128)(2,1)S(1)}, u32[]{:S(2)}, u32[]{:S(2)}) collective-permute-start(bf16[2,2,352,384]{3,2,1,0:T(8,128)(2,1)} %get-tuple-element.214), channel_id=1, source_target_pairs={{0,2},{2,0},{4,6},{6,4},{8,10},{10,8},{12,14},{14,12},{16,18},{18,... | collective-permute-start | bytes 3244040 | tf_op jit(solution)/shard_map/ppermute | solution.py:58
  139.2 8.5 %collective-permute-start.28 = (bf16[64,640]{1,0:T(8,128)(2,1)S(1)}, bf16[64,640]{1,0:T(8,128)(2,1)S(1)}, u32[]{:S(2)}, u32[]{:S(2)}) collective-permute-start(bf16[64,640]{1,0:T(8,128)(2,1)S(1)} %get-tuple-element.356), channel_id=1, source_target_pairs={{0,16},{2,18},{4,20},{6,22},{8,24},{10,26},{12,28},{14,30},{16,0},... | collective-permute-start | bytes 245768 | tf_op jit(solution)/shard_map/ppermute | solution.py:64
  143.8 13.7 %collective-permute-start.26 = (bf16[320,512]{1,0:T(8,128)(2,1)S(1)}, bf16[320,512]{1,0:T(8,128)(2,1)S(1)}, u32[]{:S(2)}, u32[]{:S(2)}) collective-permute-start(bf16[320,512]{1,0:T(8,128)(2,1)S(1)} %fusion.9), channel_id=1, source_target_pairs={{0,4},{2,6},{4,0},{6,2},{8,12},{10,14},{12,8},{14,10},{16,20},{18,... | collective-permute-start | bytes 983048 | tf_op jit(solution)/shard_map/ppermute | solution.py:61
  149.8 7.7 %collective-permute-start.31 = (bf16[64,640]{1,0:T(8,128)(2,1)S(1)}, bf16[64,640]{1,0:T(8,128)(2,1)S(1)}, u32[]{:S(2)}, u32[]{:S(2)}) collective-permute-start(bf16[64,640]{1,0:T(8,128)(2,1)S(1)} %add_convert_fusion.8), channel_id=1, source_target_pairs={{0,16},{2,18},{4,20},{6,22},{8,24},{10,26},{12,28},{14,30},{16,0},... | collective-permute-start | bytes 245768 | tf_op jit(solution)/shard_map/ppermute | solution.py:64
  157.7 13.8 %collective-permute-start.34 = (bf16[2,352,384]{2,1,0:T(8,128)(2,1)S(1)}, bf16[2,352,384]{2,1,0:T(8,128)(2,1)S(1)}, u32[]{:S(2)}, u32[]{:S(2)}) collective-permute-start(bf16[2,352,384]{2,1,0:T(8,128)(2,1)S(1)} %fusion.11), channel_id=1, source_target_pairs={{0,1},{1,0},{2,3},{3,2},{4,5},{5,4},{6,7},{7,6},{8,9},{9,8},{10,11... | collective-permute-start | bytes 1622024 | tf_op jit(solution)/shard_map/ppermute | solution.py:67
  159.4 12.1 %collective-permute-start.35 = (bf16[480,512]{1,0:T(8,128)(2,1)S(1)}, bf16[480,512]{1,0:T(8,128)(2,1)S(1)}, u32[]{:S(2)}, u32[]{:S(2)}) collective-permute-start(bf16[480,512]{1,0:T(8,128)(2,1)S(1)} %pad_maximum_fusion), channel_id=1, source_target_pairs={{0,4},{2,6},{4,0},{6,2},{8,12},{10,14},{12,8},{14,10},{16,20},{18,... | collective-permute-start | bytes 1474568 | tf_op jit(solution)/shard_map/ppermute | solution.py:61
  164.0 7.5 %collective-permute-start.37 = (bf16[80,512]{1,0:T(8,128)(2,1)S(1)}, bf16[80,512]{1,0:T(8,128)(2,1)S(1)}, u32[]{:S(2)}, u32[]{:S(2)}) collective-permute-start(bf16[80,512]{1,0:T(8,128)(2,1)S(1)} %get-tuple-element.352), channel_id=1, source_target_pairs={{0,16},{2,18},{4,20},{6,22},{8,24},{10,26},{12,28},{14,30},{16,0},... | collective-permute-start | bytes 245768 | tf_op jit(solution)/shard_map/ppermute | solution.py:64
  164.0 7.5 %collective-permute-start.38 = (bf16[80,512]{1,0:T(8,128)(2,1)S(1)}, bf16[80,512]{1,0:T(8,128)(2,1)S(1)}, u32[]{:S(2)}, u32[]{:S(2)}) collective-permute-start(bf16[80,512]{1,0:T(8,128)(2,1)S(1)} %get-tuple-element.351), channel_id=1, source_target_pairs={{0,24},{2,26},{4,28},{6,30},{8,0},{10,2},{12,4},{14,6},{16,8},{18,... | collective-permute-start | bytes 245768 | tf_op jit(solution)/shard_map/ppermute | solution.py:64
  173.6 7.5 %collective-permute-start.44 = (bf16[80,512]{1,0:T(8,128)(2,1)S(1)}, bf16[80,512]{1,0:T(8,128)(2,1)S(1)}, u32[]{:S(2)}, u32[]{:S(2)}) collective-permute-start(bf16[80,512]{1,0:T(8,128)(2,1)S(1)} %add_convert_fusion.7), channel_id=1, source_target_pairs={{0,16},{2,18},{4,20},{6,22},{8,24},{10,26},{12,28},{14,30},{16,0},... | collective-permute-start | bytes 245768 | tf_op jit(solution)/shard_map/ppermute | solution.py:64
  174.7 7.6 %collective-permute-start.46 = (bf16[256,640]{1,0:T(8,128)(2,1)S(1)}, bf16[256,640]{1,0:T(8,128)(2,1)S(1)}, u32[]{:S(2)}, u32[]{:S(2)}) collective-permute-start(bf16[256,640]{1,0:T(8,128)(2,1)S(1)} %bitcast.162), channel_id=1, source_target_pairs={{0,4},{2,6},{4,0},{6,2},{8,12},{10,14},{12,8},{14,10},{16,20},{18,... | collective-permute-start | bytes 983048 | tf_op jit(solution)/shard_map/ppermute | solution.py:61
  175.2 15.8 %collective-permute-start.39 = (bf16[352,384]{1,0:T(8,128)(2,1)S(1)}, bf16[352,384]{1,0:T(8,128)(2,1)S(1)}, u32[]{:S(2)}, u32[]{:S(2)}) collective-permute-start(bf16[352,384]{1,0:T(8,128)(2,1)S(1)} %fusion.12), channel_id=1, source_target_pairs={{0,4},{2,6},{4,0},{6,2},{8,12},{10,14},{12,8},{14,10},{16,20},{18,... | collective-permute-start | bytes 811016 | tf_op jit(solution)/shard_map/ppermute | solution.py:61
  176.6 14.3 %collective-permute-start.40 = (bf16[120,512]{1,0:T(8,128)(2,1)S(1)}, bf16[120,512]{1,0:T(8,128)(2,1)S(1)}, u32[]{:S(2)}, u32[]{:S(2)}) collective-permute-start(bf16[120,512]{1,0:T(8,128)(2,1)S(1)} %get-tuple-element.341), channel_id=1, source_target_pairs={{0,8},{2,10},{4,12},{6,14},{8,16},{10,18},{12,20},{14,22},{16,24},... | collective-permute-start | bytes 368648 | tf_op jit(solution)/shard_map/ppermute | solution.py:64
  177.3 13.7 %collective-permute-start.41 = (bf16[120,512]{1,0:T(8,128)(2,1)S(1)}, bf16[120,512]{1,0:T(8,128)(2,1)S(1)}, u32[]{:S(2)}, u32[]{:S(2)}) collective-permute-start(bf16[120,512]{1,0:T(8,128)(2,1)S(1)} %get-tuple-element.340), channel_id=1, source_target_pairs={{0,16},{2,18},{4,20},{6,22},{8,24},{10,26},{12,28},{14,30},{16,0},... | collective-permute-start | bytes 368648 | tf_op jit(solution)/shard_map/ppermute | solution.py:64
  181.1 9.9 %collective-permute-start.42 = (bf16[120,512]{1,0:T(8,128)(2,1)S(1)}, bf16[120,512]{1,0:T(8,128)(2,1)S(1)}, u32[]{:S(2)}, u32[]{:S(2)}) collective-permute-start(bf16[120,512]{1,0:T(8,128)(2,1)S(1)} %get-tuple-element.339), channel_id=1, source_target_pairs={{0,24},{2,26},{4,28},{6,30},{8,0},{10,2},{12,4},{14,6},{16,8},{18,... | collective-permute-start | bytes 368648 | tf_op jit(solution)/shard_map/ppermute | solution.py:64
  182.3 8.7 %collective-permute-start.45 = (bf16[80,512]{1,0:T(8,128)(2,1)S(1)}, bf16[80,512]{1,0:T(8,128)(2,1)S(1)}, u32[]{:S(2)}, u32[]{:S(2)}) collective-permute-start(bf16[80,512]{1,0:T(8,128)(2,1)S(1)} %add_convert_fusion.7), channel_id=1, source_target_pairs={{0,24},{2,26},{4,28},{6,30},{8,0},{10,2},{12,4},{14,6},{16,8},{18,... | collective-permute-start | bytes 245768 | tf_op jit(solution)/shard_map/ppermute | solution.py:64
  191.1 8.9 %collective-permute-start.53 = (bf16[320,512]{1,0:T(8,128)(2,1)S(1)}, bf16[320,512]{1,0:T(8,128)(2,1)S(1)}, u32[]{:S(2)}, u32[]{:S(2)}) collective-permute-start(bf16[320,512]{1,0:T(8,128)(2,1)S(1)} %bitcast.165), channel_id=1, source_target_pairs={{0,4},{2,6},{4,0},{6,2},{8,12},{10,14},{12,8},{14,10},{16,20},{18,... | collective-permute-start | bytes 983048 | tf_op jit(solution)/shard_map/ppermute | solution.py:61
  195.3 19.2 %collective-permute-start.50 = (bf16[120,512]{1,0:T(8,128)(2,1)S(1)}, bf16[120,512]{1,0:T(8,128)(2,1)S(1)}, u32[]{:S(2)}, u32[]{:S(2)}) collective-permute-start(bf16[120,512]{1,0:T(8,128)(2,1)S(1)} %add_convert_fusion.6), channel_id=1, source_target_pairs={{0,8},{2,10},{4,12},{6,14},{8,16},{10,18},{12,20},{14,22},{16,24},... | collective-permute-start | bytes 368648 | tf_op jit(solution)/shard_map/ppermute | solution.py:64
  195.3 19.6 %collective-permute-start.51 = (bf16[120,512]{1,0:T(8,128)(2,1)S(1)}, bf16[120,512]{1,0:T(8,128)(2,1)S(1)}, u32[]{:S(2)}, u32[]{:S(2)}) collective-permute-start(bf16[120,512]{1,0:T(8,128)(2,1)S(1)} %add_convert_fusion.6), channel_id=1, source_target_pairs={{0,16},{2,18},{4,20},{6,22},{8,24},{10,26},{12,28},{14,30},{16,0},... | collective-permute-start | bytes 368648 | tf_op jit(solution)/shard_map/ppermute | solution.py:64
  197.6 17.4 %collective-permute-start.52 = (bf16[120,512]{1,0:T(8,128)(2,1)S(1)}, bf16[120,512]{1,0:T(8,128)(2,1)S(1)}, u32[]{:S(2)}, u32[]{:S(2)}) collective-permute-start(bf16[120,512]{1,0:T(8,128)(2,1)S(1)} %add_convert_fusion.6), channel_id=1, source_target_pairs={{0,24},{2,26},{4,28},{6,30},{8,0},{10,2},{12,4},{14,6},{16,8},{18,... | collective-permute-start | bytes 368648 | tf_op jit(solution)/shard_map/ppermute | solution.py:64
  198.9 13.3 %collective-permute-start.48 = (bf16[88,384]{1,0:T(8,128)(2,1)S(1)}, bf16[88,384]{1,0:T(8,128)(2,1)S(1)}, u32[]{:S(2)}, u32[]{:S(2)}) collective-permute-start(bf16[88,384]{1,0:T(8,128)(2,1)S(1)} %get-tuple-element.364), channel_id=1, source_target_pairs={{0,16},{2,18},{4,20},{6,22},{8,24},{10,26},{12,28},{14,30},{16,0},... | collective-permute-start | bytes 202760 | tf_op jit(solution)/shard_map/ppermute | solution.py:64
  200.1 14.4 %collective-permute-start.49 = (bf16[88,384]{1,0:T(8,128)(2,1)S(1)}, bf16[88,384]{1,0:T(8,128)(2,1)S(1)}, u32[]{:S(2)}, u32[]{:S(2)}) collective-permute-start(bf16[88,384]{1,0:T(8,128)(2,1)S(1)} %get-tuple-element.363), channel_id=1, source_target_pairs={{0,24},{2,26},{4,28},{6,30},{8,0},{10,2},{12,4},{14,6},{16,8},{18,... | collective-permute-start | bytes 202760 | tf_op jit(solution)/shard_map/ppermute | solution.py:64
  215.1 19.2 %collective-permute-start.54 = (bf16[88,384]{1,0:T(8,128)(2,1)S(1)}, bf16[88,384]{1,0:T(8,128)(2,1)S(1)}, u32[]{:S(2)}, u32[]{:S(2)}) collective-permute-start(bf16[88,384]{1,0:T(8,128)(2,1)S(1)} %add_convert_fusion.9), channel_id=1, source_target_pairs={{0,8},{2,10},{4,12},{6,14},{8,16},{10,18},{12,20},{14,22},{16,24},... | collective-permute-start | bytes 202760 | tf_op jit(solution)/shard_map/ppermute | solution.py:64
  216.1 18.1 %collective-permute-start.55 = (bf16[88,384]{1,0:T(8,128)(2,1)S(1)}, bf16[88,384]{1,0:T(8,128)(2,1)S(1)}, u32[]{:S(2)}, u32[]{:S(2)}) collective-permute-start(bf16[88,384]{1,0:T(8,128)(2,1)S(1)} %add_convert_fusion.9), channel_id=1, source_target_pairs={{0,16},{2,18},{4,20},{6,22},{8,24},{10,26},{12,28},{14,30},{16,0},... | collective-permute-start | bytes 202760 | tf_op jit(solution)/shard_map/ppermute | solution.py:64
  217.0 17.2 %collective-permute-start.56 = (bf16[88,384]{1,0:T(8,128)(2,1)S(1)}, bf16[88,384]{1,0:T(8,128)(2,1)S(1)}, u32[]{:S(2)}, u32[]{:S(2)}) collective-permute-start(bf16[88,384]{1,0:T(8,128)(2,1)S(1)} %add_convert_fusion.9), channel_id=1, source_target_pairs={{0,24},{2,26},{4,28},{6,30},{8,0},{10,2},{12,4},{14,6},{16,8},{18,... | collective-permute-start | bytes 202760 | tf_op jit(solution)/shard_map/ppermute | solution.py:64
  220.6 11.7 %collective-permute-start.57 = (bf16[480,512]{1,0:T(8,128)(2,1)S(1)}, bf16[480,512]{1,0:T(8,128)(2,1)S(1)}, u32[]{:S(2)}, u32[]{:S(2)}) collective-permute-start(bf16[480,512]{1,0:T(8,128)(2,1)S(1)} %bitcast.159), channel_id=1, source_target_pairs={{0,4},{2,6},{4,0},{6,2},{8,12},{10,14},{12,8},{14,10},{16,20},{18,... | collective-permute-start | bytes 1474568 | tf_op jit(solution)/shard_map/ppermute | solution.py:61
  220.9 16.2 %collective-permute-start.59 = (bf16[480,512]{1,0:T(8,128)(2,1)S(1)}, bf16[480,512]{1,0:T(8,128)(2,1)S(1)}, u32[]{:S(2)}, u32[]{:S(2)}) collective-permute-start(bf16[480,512]{1,0:T(8,128)(2,1)S(1)} %bitcast.160), channel_id=1, source_target_pairs={{0,2},{2,0},{4,6},{6,4},{8,10},{10,8},{12,14},{14,12},{16,18},{18,... | collective-permute-start | bytes 1474568 | tf_op jit(solution)/shard_map/ppermute | solution.py:58
  234.4 8.2 %collective-permute-start.58 = (bf16[352,384]{1,0:T(8,128)(2,1)S(1)}, bf16[352,384]{1,0:T(8,128)(2,1)S(1)}, u32[]{:S(2)}, u32[]{:S(2)}) collective-permute-start(bf16[352,384]{1,0:T(8,128)(2,1)S(1)} %bitcast.171), channel_id=1, source_target_pairs={{0,4},{2,6},{4,0},{6,2},{8,12},{10,14},{12,8},{14,10},{16,20},{18,... | collective-permute-start | bytes 811016 | tf_op jit(solution)/shard_map/ppermute | solution.py:61
  234.8 13.4 %collective-permute-start.64 = (bf16[352,384]{1,0:T(8,128)(2,1)S(1)}, bf16[352,384]{1,0:T(8,128)(2,1)S(1)}, u32[]{:S(2)}, u32[]{:S(2)}) collective-permute-start(bf16[352,384]{1,0:T(8,128)(2,1)S(1)} %bitcast.172), channel_id=1, source_target_pairs={{0,2},{2,0},{4,6},{6,4},{8,10},{10,8},{12,14},{14,12},{16,18},{18,... | collective-permute-start | bytes 811016 | tf_op jit(solution)/shard_map/ppermute | solution.py:58
  243.4 11.2 %collective-permute-start.61 = (bf16[256,640]{1,0:T(8,128)(2,1)S(1)}, bf16[256,640]{1,0:T(8,128)(2,1)S(1)}, u32[]{:S(2)}, u32[]{:S(2)}) collective-permute-start(bf16[256,640]{1,0:T(8,128)(2,1)S(1)} %get-tuple-element.325), channel_id=1, source_target_pairs={{1,0},{2,1},{3,2},{4,3},{5,4},{6,5},{7,6},{8,7},{9,8},{10,9},{11,1... | collective-permute-start | bytes 983048 | tf_op jit(solution)/shard_map/ppermute | solution.py:72
  246.2 9.9 %collective-permute-start.63 = (bf16[256,640]{1,0:T(8,128)(2,1)S(1)}, bf16[256,640]{1,0:T(8,128)(2,1)S(1)}, u32[]{:S(2)}, u32[]{:S(2)}) collective-permute-start(bf16[256,640]{1,0:T(8,128)(2,1)S(1)} %get-tuple-element.326), channel_id=1, source_target_pairs={{2,0},{3,1},{4,2},{5,3},{6,4},{7,5},{8,6},{9,7},{10,8},{11,9},{12,... | collective-permute-start | bytes 983048 | tf_op jit(solution)/shard_map/ppermute | solution.py:72
  (61 other events, 446.0 us)
